TPU v7x, 32 devices: a whole 2x2x4 slice. The times are simulated.
32 devices in a mesh: row: 8 (over y, x, core), col: 4 (over z).
Axes of the slice: x: 2, y: 2, z: 4, core: 2. Of those that a mesh axis runs over, the one named last changes fastest.
Arguments:
- orbitals_in: float32 [4096, 256], P(('row', 'col')), may hold values from -6 to 6
- hblocks: bfloat16 [64, 32, 4096], P('row', 'col'), may hold values from -0.09375 to 0.09375
- block_cols: int32 [64, 32], P('row', 'col'), may hold values from 0 to 15, as said below
- live_counts: int32 [64, 4], P('row', 'col'), may hold values from 0 to 8, as said below
- onsite: bfloat16 [64, 4096], P(('row', 'col')), may hold values from -3 to 1, as said below
- cut_low: float32 [1], replicated, may hold values from -1.6 to -1
- top_bound: float32 [1], replicated, may hold values from 2.4 to 3.2
Outputs:
- orbitals: float32 [4096, 256], P(('row', 'col'))
- projected: float32 [256, 256], replicated
Inputs may be any that keep to these rules, and one draw needn't show every extreme that they name: `block_cols`: in block row b and column group c the first live_counts[b, c] slots name distinct block columns whose global block index exceeds b (strict upper triangle); the other slots are padding and are ignored. `live_counts`: block row 0 fills all 8 slots of every column group; the last block row has no live slot. `onsite`: every block is symmetric.
All inputs are finite; a program needn't handle non-finite values.
Results may differ from a plain program's by a relative error of at most 0.0008.
The roundings to bfloat16 on the way count: a program that leaves them out, or rounds other values in their place, can miss the bound.
Values may be sent and summed in bfloat16 or wider, within the bound.
No kernel may reach another device: no remote copies, remote signals or barrier semaphores. Data moves between devices by JAX's collectives and lax.ppermute only.
A program may use at most 128 MiB of HBM per device.

v0:
```python
import functools

import jax
import jax.numpy as jnp
from jax import lax
from jax.experimental import pallas as pl
from jax.experimental.pallas import tpu as pltpu
from jax.sharding import PartitionSpec as P

BS = 64
PB = 2
DEG = 3
LANES = 128
PANEL = 32
HI = lax.Precision.HIGHEST
VMEM = pl.BlockSpec(memory_space=pltpu.VMEM)
SMEM = pl.BlockSpec(memory_space=pltpu.SMEM)


def widen(x, width):
    return jnp.concatenate([x] * (width // LANES), 1) if width > LANES else x

def reciprocal(x):
    return pl.reciprocal(x, approx=True)


def finish_kernel(total_rows, packed_ref, diagonal_ref, y_ref, orbitals_ref, projected_ref, inverse_ref):
    k = packed_ref.shape[0]
    panels = k // PANEL
    packed = packed_ref[...]
    flipped = packed.T
    above = lax.broadcasted_iota(jnp.int32, (k, k), 0) - lax.broadcasted_iota(jnp.int32, (k, k), 1)
    gram = jnp.where(above <= 0, packed, flipped)
    cross = jnp.where(above > 0, packed, jnp.where(above < 0, flipped, diagonal_ref[...]))
    row_id = lax.broadcasted_iota(jnp.int32, (PANEL, LANES), 0)
    scale = 1.0 / total_rows
    upper = [gram[m * PANEL:(m + 1) * PANEL, :] * scale for m in range(panels)]
    inverse = []
    for m in range(panels):
        r = lax.broadcasted_iota(jnp.int32, (PANEL, k), 0) + m * PANEL
        inverse.append((r == lax.broadcasted_iota(jnp.int32, (PANEL, k), 1)).astype(jnp.float32))
    for p in range(panels):
        start = p * PANEL
        s_lo = start // LANES * LANES
        w_hi = (start + PANEL + LANES - 1) // LANES * LANES
        s, w = upper[p][:, s_lo:], inverse[p][:, :w_hi]
        columns = [
            jnp.broadcast_to(s[:, start - s_lo + t:start - s_lo + t + 1], (PANEL, LANES))
            for t in range(PANEL)
        ]
        pivots = jnp.zeros((PANEL, LANES), jnp.float32)
        for t in range(0, PANEL, 2):
            one, two = columns[t], columns[t + 1]
            a, b, d = one[t:t + 1, :], one[t + 1:t + 2, :], two[t + 1:t + 2, :]
            det = a * d - b * b
            det_inv = reciprocal(det)
            a_inv = reciprocal(a)
            pivots = jnp.where(row_id == t, a, pivots)
            pivots = jnp.where(row_id == t + 1, det * a_inv, pivots)
            one_below = jnp.where(row_id > t + 1, one, 0.0)
            two_below = jnp.where(row_id > t + 1, two, 0.0)
            for j in range(t + 2, PANEL):
                p1, p2 = one[j:j + 1, :], two[j:j + 1, :]
                columns[j] = (
                    columns[j]
                    - one_below * ((d * p1 - b * p2) * det_inv)
                    - two_below * ((a * p2 - b * p1) * det_inv)
                )
            first = (d * one_below - b * two_below) * det_inv
            first = jnp.where(row_id == t + 1, b * a_inv, first)
            second = (a * two_below - b * one_below) * det_inv
            s = (
                s
                - widen(first, s.shape[1]) * s[t:t + 1, :]
                - widen(second, s.shape[1]) * s[t + 1:t + 2, :]
            )
            w = (
                w
                - widen(first, w.shape[1]) * w[t:t + 1, :]
                - widen(second, w.shape[1]) * w[t + 1:t + 2, :]
            )
        root = lax.rsqrt(pivots)
        s = s * widen(root, s.shape[1])
        w = w * widen(root, w.shape[1])
        inverse_ref[start:start + PANEL, :w_hi] = w
        if w_hi < k:
            inverse_ref[start:start + PANEL, w_hi:] = jnp.zeros((PANEL, k - w_hi), jnp.float32)
        if p == panels - 1:
            break
        st = s.T
        for lo, hi in ((p + 1, p + 2), (p + 2, panels)):
            if lo >= hi:
                continue
            left = st[lo * PANEL - s_lo:hi * PANEL - s_lo, :]
            s_lo2 = lo * PANEL // LANES * LANES
            ds = jnp.dot(left, s[:, s_lo2 - s_lo:], precision=HI, preferred_element_type=jnp.float32)
            dw = jnp.dot(left, w, precision=HI, preferred_element_type=jnp.float32)
            for m in range(lo, hi):
                o = (m - lo) * PANEL
                a = upper[m][:, s_lo2:] - ds[o:o + PANEL, :]
                upper[m] = a if s_lo2 == 0 else jnp.concatenate([upper[m][:, :s_lo2], a], 1)
                b = inverse[m][:, :w_hi] - dw[o:o + PANEL, :]
                inverse[m] = b if w_hi == k else jnp.concatenate([b, inverse[m][:, w_hi:]], 1)
    inv = inverse_ref[...]
    nt = (((1,), (1,)), ((), ()))
    orbitals_ref[...] = lax.dot_general(y_ref[...], inv, nt, precision=HI, preferred_element_type=jnp.float32)
    half = jnp.dot(inv, cross, precision=HI, preferred_element_type=jnp.float32)
    full = lax.dot_general(half, inv, nt, precision=HI, preferred_element_type=jnp.float32)
    projected_ref[...] = full * (0.5 * scale)

def finish(packed, diagonal, y, total_rows):
    k = packed.shape[0]
    f32 = jnp.float32
    return pl.pallas_call(
        functools.partial(finish_kernel, total_rows),
        out_shape=(jax.ShapeDtypeStruct(y.shape, f32), jax.ShapeDtypeStruct((k, k), f32)),
        in_specs=[pl.BlockSpec(memory_space=pltpu.VMEM)] * 3,
        out_specs=(pl.BlockSpec(memory_space=pltpu.VMEM),) * 2,
        scratch_shapes=[pltpu.VMEM((k, k), f32)],
        compiler_params=pltpu.CompilerParams(vmem_limit_bytes=32 * 1024 * 1024),
        name="finish",
    )(packed, diagonal, y)


def exchanged(x, axis, size, apart):
    return lax.ppermute(x, axis, [(i, i ^ apart) for i in range(size)])


def shifted(x, axis, size, step):
    return lax.ppermute(x, axis, [(i, (i + step) % size) for i in range(size)])


def core_swap(x, rows):
    return exchanged(x, "row", rows, 1)


def chip_swap(x, rows, apart):
    return exchanged(x, "row", rows, 2 * apart)


def by_distance(x, index):
    size = x.shape[0]
    bit = 1
    while bit < size:
        pairs = x.reshape(size // (2 * bit), 2, bit, *x.shape[1:])
        flipped = jnp.stack([pairs[:, 1], pairs[:, 0]], 1).reshape(x.shape)
        x = jnp.where((index // bit) % 2 == 1, flipped, x)
        bit *= 2
    return x


def pack_kernel(col_ref, blocks_ref, places_ref, *piece_refs):
    cols = len(piece_refs)
    for s, piece in enumerate(piece_refs):
        owner = lax.rem(col_ref[0] + s, cols)
        piece[:, : BS * BS] = blocks_ref[owner]
        piece[:, BS * BS :] = places_ref[owner]


def pack(col, blocks, places):
    cols, height, _ = blocks.shape
    shape = jax.ShapeDtypeStruct((height, BS * BS + LANES), jnp.bfloat16)
    return pl.pallas_call(
        pack_kernel,
        out_shape=(shape,) * cols,
        in_specs=[SMEM, VMEM, VMEM],
        out_specs=(VMEM,) * cols,
        name="pack",
    )(col, blocks, places)


def unflatten(flat_ref, square_ref, groups):
    lower = lax.broadcasted_iota(jnp.int32, (groups, LANES), 1) < BS
    for h in range(BS * BS // LANES):
        even = flat_ref[:groups, h * LANES : (h + 1) * LANES]
        odd = flat_ref[groups:, h * LANES : (h + 1) * LANES]
        first = jnp.where(lower, even, pltpu.roll(odd, BS, 1))
        second = jnp.where(lower, pltpu.roll(even, BS, 1), odd)
        square_ref[pl.ds(2 * h, groups, stride=BS), :] = first
        square_ref[pl.ds(2 * h + 1, groups, stride=BS), :] = second


def mirror_kernel(key_ref, blocks_ref, onsite_ref, near_ref, far_ref, flat_ref, square_ref):
    height = near_ref.shape[1]
    groups = square_ref.shape[0] // BS
    places = lax.broadcasted_iota(jnp.int32, (2 * groups, key_ref.shape[1]), 0)
    chosen = (places == key_ref[...]).astype(jnp.float32).astype(jnp.bfloat16)
    flat_ref[...] = jnp.dot(chosen, blocks_ref[...], preferred_element_type=jnp.float32)
    for p in range(PB):
        at = p * groups + p
        flat_ref[at : at + 1, :] += onsite_ref[p : p + 1, :].astype(jnp.float32)
    unflatten(flat_ref, square_ref, groups)
    devices = square_ref.shape[0] // height
    for d in range(devices):
        out = near_ref if d < devices // 2 else far_ref
        at = d % (devices // 2) * LANES
        square = square_ref[d * height : (d + 1) * height, :]
        out[at : at + LANES, :] = square.T.astype(jnp.bfloat16)


def mirror(key, blocks, onsite, rows, row_blocks):
    half = (rows // 2 * PB * BS, row_blocks * BS)
    groups = rows * row_blocks
    return pl.pallas_call(
        mirror_kernel,
        out_shape=(jax.ShapeDtypeStruct(half, jnp.bfloat16),) * 2,
        in_specs=[VMEM, VMEM, VMEM],
        out_specs=(VMEM, VMEM),
        scratch_shapes=[
            pltpu.VMEM((2 * groups, BS * BS), jnp.float32),
            pltpu.VMEM((groups * BS, LANES), jnp.float32),
        ],
        compiler_params=pltpu.CompilerParams(vmem_limit_bytes=40 * 1024 * 1024),
        cost_estimate=pl.CostEstimate(
            flops=4 * groups * blocks.size, bytes_accessed=3 * blocks.size, transcendentals=0
        ),
        name="mirror",
    )(key, blocks, onsite)


def direct_kernel(rows, slots, *refs):
    cols = len(refs) - 2 - rows // 2
    piece_refs, out_refs, (flat_ref, square_ref) = refs[:cols], refs[cols:-2], refs[-2:]
    row_blocks = cols * PB
    groups = rows * row_blocks
    total = jnp.zeros((2 * groups, BS * BS), jnp.float32)
    for s, piece in enumerate(piece_refs):
        height = piece.shape[0]
        place = piece[0:1, BS * BS : BS * BS + height].astype(jnp.float32).astype(jnp.int32)
        block = lax.broadcasted_iota(jnp.int32, (1, height), 1) // slots
        key = place % 2 * groups + place // 2 * row_blocks + s * PB + block
        key = jnp.where(place < 0, -1, key)
        ids = lax.broadcasted_iota(jnp.int32, (2 * groups, height), 0)
        chosen = (ids == key).astype(jnp.float32).astype(jnp.bfloat16)
        total += jnp.dot(chosen, piece[:, : BS * BS], preferred_element_type=jnp.float32)
    flat_ref[...] = total
    unflatten(flat_ref, square_ref, groups)
    for chip, out in enumerate(out_refs):
        for g in range(2 * cols):
            at = (chip * 2 * cols + g) * LANES
            out[:, g * LANES : (g + 1) * LANES] = square_ref[at : at + LANES, :].astype(
                jnp.bfloat16
            )


def direct_rows(pieces, rows, slots):
    cols = len(pieces)
    groups = rows * cols * PB
    shape = jax.ShapeDtypeStruct((PB * BS, 2 * cols * LANES), jnp.bfloat16)
    return pl.pallas_call(
        functools.partial(direct_kernel, rows, slots),
        out_shape=(shape,) * (rows // 2),
        in_specs=[VMEM] * cols,
        out_specs=(VMEM,) * (rows // 2),
        scratch_shapes=[
            pltpu.VMEM((2 * groups, BS * BS), jnp.float32),
            pltpu.VMEM((groups * BS, LANES), jnp.float32),
        ],
        compiler_params=pltpu.CompilerParams(vmem_limit_bytes=48 * 1024 * 1024),
        name="direct_rows",
    )(*pieces)


def local(orbitals_in, hblocks, block_cols, live_counts, onsite, cut_low, top_bound):
    rows = lax.axis_size("row")
    cols = lax.axis_size("col")
    chips = rows // 2
    row = lax.axis_index("row")
    col = lax.axis_index("col")
    chip, core = row // 2, row % 2
    row_blocks, slots, _ = hblocks.shape
    k = orbitals_in.shape[1]
    local_rows = PB * BS
    total_rows = rows * cols * local_rows
    near_rows = cols * local_rows

    live = jnp.arange(slots, dtype=jnp.int32)[None, :] < live_counts
    device, block = block_cols // PB, block_cols % PB
    apart = (device % 2) ^ core
    distance = (device // 2) ^ chip
    places = jnp.where(live, (distance * 2 + apart) * PB + block, -1).astype(jnp.bfloat16)
    places = places.reshape(cols, 1, PB * slots)
    places = jnp.pad(places, ((0, 0), (0, PB * slots - 1), (0, LANES - PB * slots)))
    block_row = jnp.arange(row_blocks, dtype=jnp.int32)[:, None]
    near_row = (col - block_row // PB) % cols * PB + block_row % PB
    groups = rows * row_blocks
    key = block * groups + (apart * chips + distance) * row_blocks + near_row
    key = jnp.where(live, key, -1).reshape(1, row_blocks * slots)

    pieces = pack(col[None], hblocks.reshape(cols, PB * slots, BS * BS), places)
    key, pieces = lax.optimization_barrier((key, pieces))
    pieces = [shifted(pieces[s], "col", cols, s) if s else pieces[s] for s in range(cols)]

    def gather_near(v):
        return jnp.concatenate([v] + [shifted(v, "col", cols, s) for s in range(1, cols)], 0)

    def gather_rows(v):
        near = gather_near(v)
        return near, core_swap(near, rows)

    def dot(a, b):
        return jnp.dot(a, b, preferred_element_type=jnp.float32)

    near, far = mirror(
        key, hblocks.reshape(row_blocks * slots, BS * BS), onsite, rows, row_blocks
    )

    direct = direct_rows(pieces, rows, slots)
    far, direct = lax.optimization_barrier((far, direct))
    far = core_swap(far, rows)
    direct = [chip_swap(direct[s], rows, s) if s else direct[s] for s in range(chips)]
    first, far = lax.optimization_barrier((orbitals_in.astype(jnp.bfloat16), far))
    first_gathered = gather_rows(first)
    tile = jnp.concatenate([near, far], 1) + jnp.concatenate(direct, 0)
    tile_near, tile_far = tile[:, :near_rows], tile[:, near_rows:]

    def partial_product(gathered):
        near, far = gathered
        first, far = lax.optimization_barrier((dot(tile_near, near), far))
        return first + dot(tile_far, far)

    def apply(gathered):
        terms = partial_product(gathered).reshape(chips, local_rows, k)
        total = terms[0]
        for s in range(1, chips):
            total = total + chip_swap(terms[s], rows, s)
        return total

    centre = 0.5 * (top_bound[0] + cut_low[0])
    halfwidth = 0.5 * (top_bound[0] - cut_low[0])
    previous = orbitals_in
    current = (apply(first_gathered) - centre * orbitals_in) / halfwidth
    for degree in range(DEG - 1):
        gathered = gather_rows(current.astype(jnp.bfloat16))
        following = 2.0 * (apply(gathered) - centre * current) / halfwidth - previous
        previous, current = (current, following)

    rounded = current.astype(jnp.bfloat16)
    plane_rows = jnp.concatenate(
        [rounded] + [chip_swap(rounded, rows, s) for s in range(1, chips)], 0
    )
    near, plane_rows = lax.optimization_barrier((gather_near(rounded), plane_rows))
    gathered = near, core_swap(near, rows)
    contract = (((0,), (0,)), ((), ()))
    gram_part = lax.dot_general(
        gathered[0], gathered[0], contract, preferred_element_type=jnp.float32
    ) / cols
    cross_part = lax.dot_general(
        plane_rows.astype(jnp.float32), partial_product(gathered), contract, precision=HI
    )

    share = k // rows
    cross_part = cross_part + cross_part.T
    ids = jnp.arange(k, dtype=jnp.int32)
    packed = jnp.where(ids[:, None] <= ids[None, :], gram_part, cross_part)
    diagonal = jnp.sum(jnp.where(ids[:, None] == ids[None, :], cross_part, 0.0), 0)
    diagonal = jnp.broadcast_to(diagonal, (rows, 8, k))
    total = jnp.concatenate([packed.reshape(rows, share, k), diagonal], 1)
    total = total.reshape(chips, 2, share + 8, k)
    kept = jnp.where(core == 0, total[:, 0], total[:, 1])
    total = kept + core_swap(jnp.where(core == 0, total[:, 1], total[:, 0]), rows)
    total = by_distance(total, chip)
    total = sum([chip_swap(total[s], rows, s) for s in range(1, chips)], total[0])
    total = sum([shifted(total, "col", cols, s) for s in range(1, cols)], total)
    total = jnp.stack([total] + [chip_swap(total, rows, s) for s in range(1, chips)])
    total = by_distance(total, chip)
    other = core_swap(total, rows)
    pair = (jnp.where(core == 0, total, other), jnp.where(core == 0, other, total))
    total = jnp.stack(pair, 1).reshape(rows, share + 8, k)
    packed = total[:, :share].reshape(k, k)
    return finish(packed, total[0, share : share + 1], current, total_rows)


def solution(mesh):
    placed = (
        P(("row", "col"), None),
        P("row", "col", None),
        P("row", "col"),
        P("row", "col"),
        P(("row", "col"), None),
        P(),
        P(),
    )
    return jax.shard_map(
        local, mesh=mesh, in_specs=placed, out_specs=(P(("row", "col"), None), P()), check_vma=False
    )
```

profile of v0, /device:TPU:0, one launch (start us, length us, event | category | flops | bytes accessed | tf_op | source)
XLA Modules:
  0.0 139.1 jit_solution(14433297454526487537)
XLA Ops:
  2.2 1.9 %pack.1 = (bf16[16,4224]{1,0:T(8,128)(2,1)}, bf16[16,4224]{1,0:T(8,128)(2,1)}, bf16[16,4224]{1,0:T(8,128)(2,1)}, bf16[16,4224]{1,0:T(8,128)(2,1)}) custom-call(s32[1]{0:T(128)} %bitcast.1.col_ref, bf16[4,16,4096]{2,1,0:T(8,128)(2,1)} %bitcast.82, bf16[4,16,128]{2,1,0:T(8,128)(2,1)} %pad.4.places_ref), custom_call_target="tpu_custom_call" | custom-call | tf_op jit(solution)/shard_map/pack/pallas_call | solution.py:163
  4.1 3.0 %collective-permute-start = (bf16[16,4224]{1,0:T(8,128)(2,1)}, bf16[16,4224]{1,0:T(8,128)(2,1)S(1)}, u32[]{:S(2)}, u32[]{:S(2)}) collective-permute-start(bf16[16,4224]{1,0:T(8,128)(2,1)} %get-tuple-element.42), channel_id=1, source_target_pairs={{0,1},{1,2},{2,3},{3,0},{4,5},{5,6},{6,7},{7,4},{8,9},{9,10},{10,1... | collective-permute-start | bytes 405512 | tf_op jit(solution)/shard_map/ppermute | solution.py:130
  7.2 2.6 %collective-permute-start.1 = (bf16[16,4224]{1,0:T(8,128)(2,1)}, bf16[16,4224]{1,0:T(8,128)(2,1)S(1)}, u32[]{:S(2)}, u32[]{:S(2)}) collective-permute-start(bf16[16,4224]{1,0:T(8,128)(2,1)} %get-tuple-element.43), channel_id=1, source_target_pairs={{0,2},{1,3},{2,0},{3,1},{4,6},{5,7},{6,4},{7,5},{8,10},{9,11},{10,... | collective-permute-start | bytes 405512 | tf_op jit(solution)/shard_map/ppermute | solution.py:130
  9.7 1.3 collective-permute-start.2
  12.9 2.3 %mirror.1 = (bf16[512,512]{1,0:T(8,128)(2,1)S(1)}, bf16[512,512]{1,0:T(8,128)(2,1)S(1)}) custom-call(s32[1,64]{1,0:T(1,128)S(1)} %reshape.179.key_ref, bf16[64,4096]{1,0:T(8,128)(2,1)S(1)} %bitcast.83, bf16[2,4096]{1,0:T(2,128)(2,1)S(1)} %copy-done.2), custom_call_target="tpu_custom_call" | custom-call | flops 67108864 | bytes 786432 | tf_op jit(solution)/shard_map/mirror/pallas_call | solution.py:204
  15.1 3.7 %collective-permute-done.1.refs_2_ = bf16[16,4224]{1,0:T(8,128)(2,1)S(1)} collective-permute-done((bf16[16,4224]{1,0:T(8,128)(2,1)}, bf16[16,4224]{1,0:T(8,128)(2,1)S(1)}, u32[]{:S(2)}, u32[]{:S(2)}) %collective-permute-start.1) | collective-permute-done | bytes 135200 | tf_op jit(solution)/shard_map/ppermute | solution.py:130
  19.8 3.1 %direct_rows.1 = (bf16[128,1024]{1,0:T(8,128)(2,1)S(1)}, bf16[128,1024]{1,0:T(8,128)(2,1)S(1)}, bf16[128,1024]{1,0:T(8,128)(2,1)S(1)}, bf16[128,1024]{1,0:T(8,128)(2,1)S(1)}) custom-call(bf16[16,4224]{1,0:T(8,128)(2,1)S(1)} %copy-done.1, bf16[16,4224]{1,0:T(8,128)(2,1)S(1)} %collective-permute-done.refs_1_, ...), custom_call_target="tpu_custom_call" | custom-call | tf_op jit(solution)/shard_map/direct_rows/pallas_call | solution.py:250
  23.0 1.6 %collective-permute-start.4 = (bf16[128,1024]{1,0:T(8,128)(2,1)S(1)}, bf16[128,1024]{1,0:T(8,128)(2,1)S(1)}, u32[]{:S(2)}, u32[]{:S(2)}) collective-permute-start(bf16[128,1024]{1,0:T(8,128)(2,1)S(1)} %get-tuple-element.52), channel_id=1, source_target_pairs={{0,8},{4,12},{8,0},{12,4},{16,24},{20,28},{24,16},{28,20},{1,9},{5... | collective-permute-start | bytes 786440 | tf_op jit(solution)/shard_map/ppermute | solution.py:126
  24.5 1.5 %collective-permute-start.5 = (bf16[128,1024]{1,0:T(8,128)(2,1)S(1)}, bf16[128,1024]{1,0:T(8,128)(2,1)S(1)}, u32[]{:S(2)}, u32[]{:S(2)}) collective-permute-start(bf16[128,1024]{1,0:T(8,128)(2,1)S(1)} %get-tuple-element.53), channel_id=1, source_target_pairs={{0,16},{4,20},{8,24},{12,28},{16,0},{20,4},{24,8},{28,12},{1,17},{... | collective-permute-start | bytes 786440 | tf_op jit(solution)/shard_map/ppermute | solution.py:126
  26.5 3.4 %collective-permute-start.7 = (bf16[128,256]{1,0:T(8,128)(2,1)S(1)}, bf16[128,256]{1,0:T(8,128)(2,1)S(1)}, u32[]{:S(2)}, u32[]{:S(2)}) collective-permute-start(bf16[128,256]{1,0:T(8,128)(2,1)S(1)} %convert_element_type.19), channel_id=1, source_target_pairs={{0,1},{1,2},{2,3},{3,0},{4,5},{5,6},{6,7},{7,4},{8,9},{9,10},{10,1... | collective-permute-start | bytes 196616 | tf_op jit(solution)/shard_map/ppermute | solution.py:130
  29.9 1.6 %collective-permute-start.8 = (bf16[128,256]{1,0:T(8,128)(2,1)S(1)}, bf16[128,256]{1,0:T(8,128)(2,1)S(1)}, u32[]{:S(2)}, u32[]{:S(2)}) collective-permute-start(bf16[128,256]{1,0:T(8,128)(2,1)S(1)} %convert_element_type.19), channel_id=1, source_target_pairs={{0,2},{1,3},{2,0},{3,1},{4,6},{5,7},{6,4},{7,5},{8,10},{9,11},{10,... | collective-permute-start | bytes 196616 | tf_op jit(solution)/shard_map/ppermute | solution.py:130
  31.5 2.4 %collective-permute-done.7 = bf16[128,256]{1,0:T(8,128)(2,1)S(1)} collective-permute-done((bf16[128,256]{1,0:T(8,128)(2,1)S(1)}, bf16[128,256]{1,0:T(8,128)(2,1)S(1)}, u32[]{:S(2)}, u32[]{:S(2)}) %collective-permute-start.7) | collective-permute-done | bytes 65568 | tf_op jit(solution)/shard_map/ppermute | solution.py:130
  34.0 2.0 %collective-permute-start.9 = (bf16[128,256]{1,0:T(8,128)(2,1)S(1)}, bf16[128,256]{1,0:T(8,128)(2,1)S(1)}, u32[]{:S(2)}, u32[]{:S(2)}) collective-permute-start(bf16[128,256]{1,0:T(8,128)(2,1)S(1)} %convert_element_type.19), channel_id=1, source_target_pairs={{0,3},{1,0},{2,1},{3,2},{4,7},{5,4},{6,5},{7,6},{8,11},{9,8},{10,9... | collective-permute-start | bytes 196616 | tf_op jit(solution)/shard_map/ppermute | solution.py:130
  36.1 2.1 %collective-permute-done.9 = bf16[128,256]{1,0:T(8,128)(2,1)S(1)} collective-permute-done((bf16[128,256]{1,0:T(8,128)(2,1)S(1)}, bf16[128,256]{1,0:T(8,128)(2,1)S(1)}, u32[]{:S(2)}, u32[]{:S(2)}) %collective-permute-start.9) | collective-permute-done | bytes 65568 | tf_op jit(solution)/shard_map/ppermute | solution.py:130
  40.2 1.6 %collective-permute-start.11 = (f32[128,256]{1,0:T(8,128)S(1)}, f32[128,256]{1,0:T(8,128)S(1)}, u32[]{:S(2)}, u32[]{:S(2)}) collective-permute-start(f32[128,256]{1,0:T(8,128)S(1)} %get-tuple-element.78), channel_id=1, source_target_pairs={{0,8},{4,12},{8,0},{12,4},{16,24},{20,28},{24,16},{28,20},{1,9},{5... | collective-permute-start | bytes 393224 | tf_op jit(solution)/shard_map/ppermute | solution.py:126
  41.8 1.5 %collective-permute-start.12 = (f32[128,256]{1,0:T(8,128)S(1)}, f32[128,256]{1,0:T(8,128)S(1)}, u32[]{:S(2)}, u32[]{:S(2)}) collective-permute-start(f32[128,256]{1,0:T(8,128)S(1)} %get-tuple-element.80), channel_id=1, source_target_pairs={{0,16},{4,20},{8,24},{12,28},{16,0},{20,4},{24,8},{28,12},{1,17},{... | collective-permute-start | bytes 393224 | tf_op jit(solution)/shard_map/ppermute | solution.py:126
  46.1 3.7 %collective-permute-done.12 = f32[128,256]{1,0:T(8,128)S(1)} collective-permute-done((f32[128,256]{1,0:T(8,128)S(1)}, f32[128,256]{1,0:T(8,128)S(1)}, u32[]{:S(2)}, u32[]{:S(2)}) %collective-permute-start.12) | collective-permute-done | bytes 131104 | tf_op jit(solution)/shard_map/ppermute | solution.py:126
  49.9 2.2 %collective-permute-start.14 = (bf16[128,256]{1,0:T(8,128)(2,1)S(1)}, bf16[128,256]{1,0:T(8,128)(2,1)S(1)}, u32[]{:S(2)}, u32[]{:S(2)}) collective-permute-start(bf16[128,256]{1,0:T(8,128)(2,1)S(1)} %get-tuple-element.70), channel_id=1, source_target_pairs={{0,1},{1,2},{2,3},{3,0},{4,5},{5,6},{6,7},{7,4},{8,9},{9,10},{10,1... | collective-permute-start | bytes 196616 | tf_op jit(solution)/shard_map/ppermute | solution.py:130
  52.1 2.2 %collective-permute-start.15 = (bf16[128,256]{1,0:T(8,128)(2,1)S(1)}, bf16[128,256]{1,0:T(8,128)(2,1)S(1)}, u32[]{:S(2)}, u32[]{:S(2)}) collective-permute-start(bf16[128,256]{1,0:T(8,128)(2,1)S(1)} %get-tuple-element.70), channel_id=1, source_target_pairs={{0,2},{1,3},{2,0},{3,1},{4,6},{5,7},{6,4},{7,5},{8,10},{9,11},{10,... | collective-permute-start | bytes 196616 | tf_op jit(solution)/shard_map/ppermute | solution.py:130
  54.5 1.9 %collective-permute-done.14 = bf16[128,256]{1,0:T(8,128)(2,1)S(1)} collective-permute-done((bf16[128,256]{1,0:T(8,128)(2,1)S(1)}, bf16[128,256]{1,0:T(8,128)(2,1)S(1)}, u32[]{:S(2)}, u32[]{:S(2)}) %collective-permute-start.14) | collective-permute-done | bytes 65568 | tf_op jit(solution)/shard_map/ppermute | solution.py:130
  56.4 2.1 %collective-permute-done.15 = bf16[128,256]{1,0:T(8,128)(2,1)S(1)} collective-permute-done((bf16[128,256]{1,0:T(8,128)(2,1)S(1)}, bf16[128,256]{1,0:T(8,128)(2,1)S(1)}, u32[]{:S(2)}, u32[]{:S(2)}) %collective-permute-start.15) | collective-permute-done | bytes 65568 | tf_op jit(solution)/shard_map/ppermute | solution.py:130
  61.0 1.3 collective-permute-start.18
  63.2 1.4 collective-permute-start.20
  64.5 2.6 %collective-permute-done.18 = f32[128,256]{1,0:T(8,128)S(1)} collective-permute-done((f32[128,256]{1,0:T(8,128)S(1)}, f32[128,256]{1,0:T(8,128)S(1)}, u32[]{:S(2)}, u32[]{:S(2)}) %collective-permute-start.18) | collective-permute-done | bytes 131104 | tf_op jit(solution)/shard_map/ppermute | solution.py:126
  67.2 1.6 %collective-permute-done.19 = f32[128,256]{1,0:T(8,128)S(1)} collective-permute-done((f32[128,256]{1,0:T(8,128)S(1)}, f32[128,256]{1,0:T(8,128)S(1)}, u32[]{:S(2)}, u32[]{:S(2)}) %collective-permute-start.19) | collective-permute-done | bytes 131104 | tf_op jit(solution)/shard_map/ppermute | solution.py:126
  68.8 1.6 %collective-permute-done.20 = f32[128,256]{1,0:T(8,128)S(1)} collective-permute-done((f32[128,256]{1,0:T(8,128)S(1)}, f32[128,256]{1,0:T(8,128)S(1)}, u32[]{:S(2)}, u32[]{:S(2)}) %collective-permute-start.20) | collective-permute-done | bytes 131104 | tf_op jit(solution)/shard_map/ppermute | solution.py:126
  71.6 1.8 %collective-permute-start.22 = (bf16[128,256]{1,0:T(8,128)(2,1)S(1)}, bf16[128,256]{1,0:T(8,128)(2,1)S(1)}, u32[]{:S(2)}, u32[]{:S(2)}) collective-permute-start(bf16[128,256]{1,0:T(8,128)(2,1)S(1)} %get-tuple-element.68), channel_id=1, source_target_pairs={{0,2},{1,3},{2,0},{3,1},{4,6},{5,7},{6,4},{7,5},{8,10},{9,11},{10,... | collective-permute-start | bytes 196616 | tf_op jit(solution)/shard_map/ppermute | solution.py:130
  74.3 2.7 %collective-permute-done.21 = bf16[128,256]{1,0:T(8,128)(2,1)S(1)} collective-permute-done((bf16[128,256]{1,0:T(8,128)(2,1)S(1)}, bf16[128,256]{1,0:T(8,128)(2,1)S(1)}, u32[]{:S(2)}, u32[]{:S(2)}) %collective-permute-start.21) | collective-permute-done | bytes 65568 | tf_op jit(solution)/shard_map/ppermute | solution.py:130
  77.0 1.8 %collective-permute-done.22 = bf16[128,256]{1,0:T(8,128)(2,1)S(1)} collective-permute-done((bf16[128,256]{1,0:T(8,128)(2,1)S(1)}, bf16[128,256]{1,0:T(8,128)(2,1)S(1)}, u32[]{:S(2)}, u32[]{:S(2)}) %collective-permute-start.22) | collective-permute-done | bytes 65568 | tf_op jit(solution)/shard_map/ppermute | solution.py:130
  81.3 1.7 %collective-permute-start.26 = (f32[128,256]{1,0:T(8,128)S(1)}, f32[128,256]{1,0:T(8,128)S(1)}, u32[]{:S(2)}, u32[]{:S(2)}) collective-permute-start(f32[128,256]{1,0:T(8,128)S(1)} %get-tuple-element.74), channel_id=1, source_target_pairs={{0,16},{4,20},{8,24},{12,28},{16,0},{20,4},{24,8},{28,12},{1,17},{... | collective-permute-start | bytes 393224 | tf_op jit(solution)/shard_map/ppermute | solution.py:126
  83.0 1.4 %collective-permute-start.27 = (f32[128,256]{1,0:T(8,128)S(1)}, f32[128,256]{1,0:T(8,128)S(1)}, u32[]{:S(2)}, u32[]{:S(2)}) collective-permute-start(f32[128,256]{1,0:T(8,128)S(1)} %get-tuple-element.73), channel_id=1, source_target_pairs={{0,24},{4,28},{8,16},{12,20},{16,8},{20,12},{24,0},{28,4},{1,25},{... | collective-permute-start | bytes 393224 | tf_op jit(solution)/shard_map/ppermute | solution.py:126
  84.4 2.9 %collective-permute-done.25 = f32[128,256]{1,0:T(8,128)S(1)} collective-permute-done((f32[128,256]{1,0:T(8,128)S(1)}, f32[128,256]{1,0:T(8,128)S(1)}, u32[]{:S(2)}, u32[]{:S(2)}) %collective-permute-start.25) | collective-permute-done | bytes 131104 | tf_op jit(solution)/shard_map/ppermute | solution.py:126
  87.2 2.1 %collective-permute-done.26 = f32[128,256]{1,0:T(8,128)S(1)} collective-permute-done((f32[128,256]{1,0:T(8,128)S(1)}, f32[128,256]{1,0:T(8,128)S(1)}, u32[]{:S(2)}, u32[]{:S(2)}) %collective-permute-start.26) | collective-permute-done | bytes 131104 | tf_op jit(solution)/shard_map/ppermute | solution.py:126
  89.4 1.3 collective-permute-start.28
  90.7 1.7 %collective-permute-start.29 = (bf16[128,256]{1,0:T(8,128)(2,1)S(1)}, bf16[128,256]{1,0:T(8,128)(2,1)S(1)}, u32[]{:S(2)}, u32[]{:S(2)}) collective-permute-start(bf16[128,256]{1,0:T(8,128)(2,1)S(1)} %get-tuple-element.66), channel_id=1, source_target_pairs={{0,2},{1,3},{2,0},{3,1},{4,6},{5,7},{6,4},{7,5},{8,10},{9,11},{10,... | collective-permute-start | bytes 196616 | tf_op jit(solution)/shard_map/ppermute | solution.py:130
  93.3 1.6 %collective-permute-start.31 = (bf16[128,256]{1,0:T(8,128)(2,1)S(1)}, bf16[128,256]{1,0:T(8,128)(2,1)S(1)}, u32[]{:S(2)}, u32[]{:S(2)}) collective-permute-start(bf16[128,256]{1,0:T(8,128)(2,1)S(1)} %get-tuple-element.66), channel_id=1, source_target_pairs={{0,8},{4,12},{8,0},{12,4},{16,24},{20,28},{24,16},{28,20},{1,9},{5... | collective-permute-start | bytes 196616 | tf_op jit(solution)/shard_map/ppermute | solution.py:126
  95.7 1.4 %collective-permute-start.33 = (bf16[128,256]{1,0:T(8,128)(2,1)S(1)}, bf16[128,256]{1,0:T(8,128)(2,1)S(1)}, u32[]{:S(2)}, u32[]{:S(2)}) collective-permute-start(bf16[128,256]{1,0:T(8,128)(2,1)S(1)} %get-tuple-element.66), channel_id=1, source_target_pairs={{0,24},{4,28},{8,16},{12,20},{16,8},{20,12},{24,0},{28,4},{1,25},{... | collective-permute-start | bytes 196616 | tf_op jit(solution)/shard_map/ppermute | solution.py:126
  99.2 1.7 %collective-permute-done.33 = bf16[128,256]{1,0:T(8,128)(2,1)S(1)} collective-permute-done((bf16[128,256]{1,0:T(8,128)(2,1)S(1)}, bf16[128,256]{1,0:T(8,128)(2,1)S(1)}, u32[]{:S(2)}, u32[]{:S(2)}) %collective-permute-start.33) | collective-permute-done | bytes 65568 | tf_op jit(solution)/shard_map/ppermute | solution.py:126
  105.4 1.8 %collective-permute-start.36 = (f32[40,256]{1,0:T(8,128)S(1)}, f32[40,256]{1,0:T(8,128)S(1)}, u32[]{:S(2)}, u32[]{:S(2)}) collective-permute-start(f32[40,256]{1,0:T(8,128)S(1)} %get-tuple-element.87), channel_id=1, source_target_pairs={{0,8},{4,12},{8,0},{12,4},{16,24},{20,28},{24,16},{28,20},{1,9},{5... | collective-permute-start | bytes 122888 | tf_op jit(solution)/shard_map/ppermute | solution.py:126
  107.5 1.5 %collective-permute-start.38 = (f32[40,256]{1,0:T(8,128)S(1)}, f32[40,256]{1,0:T(8,128)S(1)}, u32[]{:S(2)}, u32[]{:S(2)}) collective-permute-start(f32[40,256]{1,0:T(8,128)S(1)} %get-tuple-element.88), channel_id=1, source_target_pairs={{0,24},{4,28},{8,16},{12,20},{16,8},{20,12},{24,0},{28,4},{1,25},{... | collective-permute-start | bytes 122888 | tf_op jit(solution)/shard_map/ppermute | solution.py:126
  109.5 2.1 %collective-permute-done.37 = f32[40,256]{1,0:T(8,128)S(1)} collective-permute-done((f32[40,256]{1,0:T(8,128)S(1)}, f32[40,256]{1,0:T(8,128)S(1)}, u32[]{:S(2)}, u32[]{:S(2)}) %collective-permute-start.37) | collective-permute-done | bytes 40992 | tf_op jit(solution)/shard_map/ppermute | solution.py:126
  114.5 2.6 %collective-permute-start.41 = (f32[40,256]{1,0:T(8,128)S(1)}, f32[40,256]{1,0:T(8,128)S(1)}, u32[]{:S(2)}, u32[]{:S(2)}) collective-permute-start(f32[40,256]{1,0:T(8,128)S(1)} %fusion.45), channel_id=1, source_target_pairs={{0,3},{1,0},{2,1},{3,2},{4,7},{5,4},{6,5},{7,6},{8,11},{9,8},{10,9... | collective-permute-start | bytes 122888 | tf_op jit(solution)/shard_map/ppermute | solution.py:130
  119.1 1.6 %collective-permute-start.42 = (f32[40,256]{1,0:T(8,128)S(1)}, f32[40,256]{1,0:T(8,128)S(1)}, u32[]{:S(2)}, u32[]{:S(2)}) collective-permute-start(f32[40,256]{1,0:T(8,128)S(1)} %add_add_fusion), channel_id=1, source_target_pairs={{0,8},{4,12},{8,0},{12,4},{16,24},{20,28},{24,16},{28,20},{1,9},{5... | collective-permute-start | bytes 122888 | tf_op jit(solution)/shard_map/ppermute | solution.py:126
  121.3 1.4 collective-permute-start.44
  123.2 1.6 %collective-permute-done.43 = f32[40,256]{1,0:T(8,128)S(1)} collective-permute-done((f32[40,256]{1,0:T(8,128)S(1)}, f32[40,256]{1,0:T(8,128)S(1)}, u32[]{:S(2)}, u32[]{:S(2)}) %collective-permute-start.43) | collective-permute-done | bytes 40992 | tf_op jit(solution)/shard_map/ppermute | solution.py:126
  124.7 1.5 %collective-permute-done.44 = f32[40,256]{1,0:T(8,128)S(1)} collective-permute-done((f32[40,256]{1,0:T(8,128)S(1)}, f32[40,256]{1,0:T(8,128)S(1)}, u32[]{:S(2)}, u32[]{:S(2)}) %collective-permute-start.44) | collective-permute-done | bytes 40992 | tf_op jit(solution)/shard_map/ppermute | solution.py:126
  126.4 1.4 collective-permute-done.45
  128.0 11.1 %finish.1 = (f32[128,256]{1,0:T(8,128)}, f32[256,256]{1,0:T(8,128)}) custom-call(f32[256,256]{1,0:T(8,128)S(1)} %bitcast.84, f32[1,256]{1,0:T(1,128)S(1)} %slice_bitcast_fusion.4.diagonal_ref, f32[128,256]{1,0:T(8,128)S(1)} %get-tuple-element.67.y_ref), custom_call_target="tpu_custom_call" | custom-call | tf_op jit(solution)/shard_map/finish/pallas_call | solution.py:114
  (115 shorter events, 31.7 us)
Async XLA Ops:
  0.6 22.3 %copy-start.3 = (f32[128,256]{1,0:T(8,128)S(1)}, f32[128,256]{1,0:T(8,128)}, u32[]{:S(2)}) copy-start(f32[128,256]{1,0:T(8,128)} %param.7) | copy-start | bytes 393220
  4.1 11.0 %collective-permute-start = (bf16[16,4224]{1,0:T(8,128)(2,1)}, bf16[16,4224]{1,0:T(8,128)(2,1)S(1)}, u32[]{:S(2)}, u32[]{:S(2)}) collective-permute-start(bf16[16,4224]{1,0:T(8,128)(2,1)} %get-tuple-element.42), channel_id=1, source_target_pairs={{0,1},{1,2},{2,3},{3,0},{4,5},{5,6},{6,7},{7,4},{8,9},{9,10},{10,1... | collective-permute-start | bytes 405512 | tf_op jit(solution)/shard_map/ppermute | solution.py:130
  7.2 11.7 %collective-permute-start.1 = (bf16[16,4224]{1,0:T(8,128)(2,1)}, bf16[16,4224]{1,0:T(8,128)(2,1)S(1)}, u32[]{:S(2)}, u32[]{:S(2)}) collective-permute-start(bf16[16,4224]{1,0:T(8,128)(2,1)} %get-tuple-element.43), channel_id=1, source_target_pairs={{0,2},{1,3},{2,0},{3,1},{4,6},{5,7},{6,4},{7,5},{8,10},{9,11},{10,... | collective-permute-start | bytes 405512 | tf_op jit(solution)/shard_map/ppermute | solution.py:130
  9.7 9.1 %collective-permute-start.2 = (bf16[16,4224]{1,0:T(8,128)(2,1)}, bf16[16,4224]{1,0:T(8,128)(2,1)S(1)}, u32[]{:S(2)}, u32[]{:S(2)}) collective-permute-start(bf16[16,4224]{1,0:T(8,128)(2,1)} %get-tuple-element.44), channel_id=1, source_target_pairs={{0,3},{1,0},{2,1},{3,2},{4,7},{5,4},{6,5},{7,6},{8,11},{9,8},{10,9... | collective-permute-start | bytes 405512 | tf_op jit(solution)/shard_map/ppermute | solution.py:130
  11.1 1.0 copy-start
  22.9 3.7 %collective-permute-start.3 = (bf16[512,512]{1,0:T(8,128)(2,1)S(1)}, bf16[512,512]{1,0:T(8,128)(2,1)S(1)}, u32[]{:S(2)}, u32[]{:S(2)}) collective-permute-start(bf16[512,512]{1,0:T(8,128)(2,1)S(1)} %get-tuple-element.49), channel_id=1, source_target_pairs={{0,4},{4,0},{8,12},{12,8},{16,20},{20,16},{24,28},{28,24},{1,5},{5... | collective-permute-start | bytes 1572872 | tf_op jit(solution)/shard_map/ppermute | solution.py:126
  23.0 15.3 %collective-permute-start.4 = (bf16[128,1024]{1,0:T(8,128)(2,1)S(1)}, bf16[128,1024]{1,0:T(8,128)(2,1)S(1)}, u32[]{:S(2)}, u32[]{:S(2)}) collective-permute-start(bf16[128,1024]{1,0:T(8,128)(2,1)S(1)} %get-tuple-element.52), channel_id=1, source_target_pairs={{0,8},{4,12},{8,0},{12,4},{16,24},{20,28},{24,16},{28,20},{1,9},{5... | collective-permute-start | bytes 786440 | tf_op jit(solution)/shard_map/ppermute | solution.py:126
  24.5 14.0 %collective-permute-start.5 = (bf16[128,1024]{1,0:T(8,128)(2,1)S(1)}, bf16[128,1024]{1,0:T(8,128)(2,1)S(1)}, u32[]{:S(2)}, u32[]{:S(2)}) collective-permute-start(bf16[128,1024]{1,0:T(8,128)(2,1)S(1)} %get-tuple-element.53), channel_id=1, source_target_pairs={{0,16},{4,20},{8,24},{12,28},{16,0},{20,4},{24,8},{28,12},{1,17},{... | collective-permute-start | bytes 786440 | tf_op jit(solution)/shard_map/ppermute | solution.py:126
  26.1 12.5 %collective-permute-start.6 = (bf16[128,1024]{1,0:T(8,128)(2,1)S(1)}, bf16[128,1024]{1,0:T(8,128)(2,1)S(1)}, u32[]{:S(2)}, u32[]{:S(2)}) collective-permute-start(bf16[128,1024]{1,0:T(8,128)(2,1)S(1)} %get-tuple-element.54), channel_id=1, source_target_pairs={{0,24},{4,28},{8,16},{12,20},{16,8},{20,12},{24,0},{28,4},{1,25},{... | collective-permute-start | bytes 786440 | tf_op jit(solution)/shard_map/ppermute | solution.py:126
  26.5 7.4 %collective-permute-start.7 = (bf16[128,256]{1,0:T(8,128)(2,1)S(1)}, bf16[128,256]{1,0:T(8,128)(2,1)S(1)}, u32[]{:S(2)}, u32[]{:S(2)}) collective-permute-start(bf16[128,256]{1,0:T(8,128)(2,1)S(1)} %convert_element_type.19), channel_id=1, source_target_pairs={{0,1},{1,2},{2,3},{3,0},{4,5},{5,6},{6,7},{7,4},{8,9},{9,10},{10,1... | collective-permute-start | bytes 196616 | tf_op jit(solution)/shard_map/ppermute | solution.py:130
  29.9 6.2 %collective-permute-start.8 = (bf16[128,256]{1,0:T(8,128)(2,1)S(1)}, bf16[128,256]{1,0:T(8,128)(2,1)S(1)}, u32[]{:S(2)}, u32[]{:S(2)}) collective-permute-start(bf16[128,256]{1,0:T(8,128)(2,1)S(1)} %convert_element_type.19), channel_id=1, source_target_pairs={{0,2},{1,3},{2,0},{3,1},{4,6},{5,7},{6,4},{7,5},{8,10},{9,11},{10,... | collective-permute-start | bytes 196616 | tf_op jit(solution)/shard_map/ppermute | solution.py:130
  34.0 4.3 %collective-permute-start.9 = (bf16[128,256]{1,0:T(8,128)(2,1)S(1)}, bf16[128,256]{1,0:T(8,128)(2,1)S(1)}, u32[]{:S(2)}, u32[]{:S(2)}) collective-permute-start(bf16[128,256]{1,0:T(8,128)(2,1)S(1)} %convert_element_type.19), channel_id=1, source_target_pairs={{0,3},{1,0},{2,1},{3,2},{4,7},{5,4},{6,5},{7,6},{8,11},{9,8},{10,9... | collective-permute-start | bytes 196616 | tf_op jit(solution)/shard_map/ppermute | solution.py:130
  38.3 1.5 %collective-permute-start.10 = (bf16[512,256]{1,0:T(8,128)(2,1)S(1)}, bf16[512,256]{1,0:T(8,128)(2,1)S(1)}, u32[]{:S(2)}, u32[]{:S(2)}) collective-permute-start(bf16[512,256]{1,0:T(8,128)(2,1)S(1)} %constant_dynamic-update-slice_fusion), channel_id=1, source_target_pairs={{0,4},{4,0},{8,12},{12,8},{16,20},{20,16},{24,28},{28,24},{1,5},{5... | collective-permute-start | bytes 786440 | tf_op jit(solution)/shard_map/ppermute | solution.py:126
  40.2 5.9 %collective-permute-start.11 = (f32[128,256]{1,0:T(8,128)S(1)}, f32[128,256]{1,0:T(8,128)S(1)}, u32[]{:S(2)}, u32[]{:S(2)}) collective-permute-start(f32[128,256]{1,0:T(8,128)S(1)} %get-tuple-element.78), channel_id=1, source_target_pairs={{0,8},{4,12},{8,0},{12,4},{16,24},{20,28},{24,16},{28,20},{1,9},{5... | collective-permute-start | bytes 393224 | tf_op jit(solution)/shard_map/ppermute | solution.py:126
  41.8 8.1 %collective-permute-start.12 = (f32[128,256]{1,0:T(8,128)S(1)}, f32[128,256]{1,0:T(8,128)S(1)}, u32[]{:S(2)}, u32[]{:S(2)}) collective-permute-start(f32[128,256]{1,0:T(8,128)S(1)} %get-tuple-element.80), channel_id=1, source_target_pairs={{0,16},{4,20},{8,24},{12,28},{16,0},{20,4},{24,8},{28,12},{1,17},{... | collective-permute-start | bytes 393224 | tf_op jit(solution)/shard_map/ppermute | solution.py:126
  43.3 6.6 %collective-permute-start.13 = (f32[128,256]{1,0:T(8,128)S(1)}, f32[128,256]{1,0:T(8,128)S(1)}, u32[]{:S(2)}, u32[]{:S(2)}) collective-permute-start(f32[128,256]{1,0:T(8,128)S(1)} %get-tuple-element.79), channel_id=1, source_target_pairs={{0,24},{4,28},{8,16},{12,20},{16,8},{20,12},{24,0},{28,4},{1,25},{... | collective-permute-start | bytes 393224 | tf_op jit(solution)/shard_map/ppermute | solution.py:126
  49.9 6.5 %collective-permute-start.14 = (bf16[128,256]{1,0:T(8,128)(2,1)S(1)}, bf16[128,256]{1,0:T(8,128)(2,1)S(1)}, u32[]{:S(2)}, u32[]{:S(2)}) collective-permute-start(bf16[128,256]{1,0:T(8,128)(2,1)S(1)} %get-tuple-element.70), channel_id=1, source_target_pairs={{0,1},{1,2},{2,3},{3,0},{4,5},{5,6},{6,7},{7,4},{8,9},{9,10},{10,1... | collective-permute-start | bytes 196616 | tf_op jit(solution)/shard_map/ppermute | solution.py:130
  52.1 6.4 %collective-permute-start.15 = (bf16[128,256]{1,0:T(8,128)(2,1)S(1)}, bf16[128,256]{1,0:T(8,128)(2,1)S(1)}, u32[]{:S(2)}, u32[]{:S(2)}) collective-permute-start(bf16[128,256]{1,0:T(8,128)(2,1)S(1)} %get-tuple-element.70), channel_id=1, source_target_pairs={{0,2},{1,3},{2,0},{3,1},{4,6},{5,7},{6,4},{7,5},{8,10},{9,11},{10,... | collective-permute-start | bytes 196616 | tf_op jit(solution)/shard_map/ppermute | solution.py:130
  54.3 4.6 %collective-permute-start.16 = (bf16[128,256]{1,0:T(8,128)(2,1)S(1)}, bf16[128,256]{1,0:T(8,128)(2,1)S(1)}, u32[]{:S(2)}, u32[]{:S(2)}) collective-permute-start(bf16[128,256]{1,0:T(8,128)(2,1)S(1)} %get-tuple-element.70), channel_id=1, source_target_pairs={{0,3},{1,0},{2,1},{3,2},{4,7},{5,4},{6,5},{7,6},{8,11},{9,8},{10,9... | collective-permute-start | bytes 196616 | tf_op jit(solution)/shard_map/ppermute | solution.py:130
  59.0 1.6 %collective-permute-start.17 = (bf16[512,256]{1,0:T(8,128)(2,1)S(1)}, bf16[512,256]{1,0:T(8,128)(2,1)S(1)}, u32[]{:S(2)}, u32[]{:S(2)}) collective-permute-start(bf16[512,256]{1,0:T(8,128)(2,1)S(1)} %pad_maximum_fusion.3), channel_id=1, source_target_pairs={{0,4},{4,0},{8,12},{12,8},{16,20},{20,16},{24,28},{28,24},{1,5},{5... | collective-permute-start | bytes 786440 | tf_op jit(solution)/shard_map/ppermute | solution.py:126
  61.0 6.2 %collective-permute-start.18 = (f32[128,256]{1,0:T(8,128)S(1)}, f32[128,256]{1,0:T(8,128)S(1)}, u32[]{:S(2)}, u32[]{:S(2)}) collective-permute-start(f32[128,256]{1,0:T(8,128)S(1)} %get-tuple-element.75), channel_id=1, source_target_pairs={{0,8},{4,12},{8,0},{12,4},{16,24},{20,28},{24,16},{28,20},{1,9},{5... | collective-permute-start | bytes 393224 | tf_op jit(solution)/shard_map/ppermute | solution.py:126
  62.3 6.5 %collective-permute-start.19 = (f32[128,256]{1,0:T(8,128)S(1)}, f32[128,256]{1,0:T(8,128)S(1)}, u32[]{:S(2)}, u32[]{:S(2)}) collective-permute-start(f32[128,256]{1,0:T(8,128)S(1)} %get-tuple-element.77), channel_id=1, source_target_pairs={{0,16},{4,20},{8,24},{12,28},{16,0},{20,4},{24,8},{28,12},{1,17},{... | collective-permute-start | bytes 393224 | tf_op jit(solution)/shard_map/ppermute | solution.py:126
  63.2 7.2 %collective-permute-start.20 = (f32[128,256]{1,0:T(8,128)S(1)}, f32[128,256]{1,0:T(8,128)S(1)}, u32[]{:S(2)}, u32[]{:S(2)}) collective-permute-start(f32[128,256]{1,0:T(8,128)S(1)} %get-tuple-element.76), channel_id=1, source_target_pairs={{0,24},{4,28},{8,16},{12,20},{16,8},{20,12},{24,0},{28,4},{1,25},{... | collective-permute-start | bytes 393224 | tf_op jit(solution)/shard_map/ppermute | solution.py:126
  70.4 6.6 %collective-permute-start.21 = (bf16[128,256]{1,0:T(8,128)(2,1)S(1)}, bf16[128,256]{1,0:T(8,128)(2,1)S(1)}, u32[]{:S(2)}, u32[]{:S(2)}) collective-permute-start(bf16[128,256]{1,0:T(8,128)(2,1)S(1)} %get-tuple-element.68), channel_id=1, source_target_pairs={{0,1},{1,2},{2,3},{3,0},{4,5},{5,6},{6,7},{7,4},{8,9},{9,10},{10,1... | collective-permute-start | bytes 196616 | tf_op jit(solution)/shard_map/ppermute | solution.py:130
  71.6 7.2 %collective-permute-start.22 = (bf16[128,256]{1,0:T(8,128)(2,1)S(1)}, bf16[128,256]{1,0:T(8,128)(2,1)S(1)}, u32[]{:S(2)}, u32[]{:S(2)}) collective-permute-start(bf16[128,256]{1,0:T(8,128)(2,1)S(1)} %get-tuple-element.68), channel_id=1, source_target_pairs={{0,2},{1,3},{2,0},{3,1},{4,6},{5,7},{6,4},{7,5},{8,10},{9,11},{10,... | collective-permute-start | bytes 196616 | tf_op jit(solution)/shard_map/ppermute | solution.py:130
  73.5 5.3 %collective-permute-start.23 = (bf16[128,256]{1,0:T(8,128)(2,1)S(1)}, bf16[128,256]{1,0:T(8,128)(2,1)S(1)}, u32[]{:S(2)}, u32[]{:S(2)}) collective-permute-start(bf16[128,256]{1,0:T(8,128)(2,1)S(1)} %get-tuple-element.68), channel_id=1, source_target_pairs={{0,3},{1,0},{2,1},{3,2},{4,7},{5,4},{6,5},{7,6},{8,11},{9,8},{10,9... | collective-permute-start | bytes 196616 | tf_op jit(solution)/shard_map/ppermute | solution.py:130
  78.8 1.6 %collective-permute-start.24 = (bf16[512,256]{1,0:T(8,128)(2,1)S(1)}, bf16[512,256]{1,0:T(8,128)(2,1)S(1)}, u32[]{:S(2)}, u32[]{:S(2)}) collective-permute-start(bf16[512,256]{1,0:T(8,128)(2,1)S(1)} %pad_maximum_fusion.4), channel_id=1, source_target_pairs={{0,4},{4,0},{8,12},{12,8},{16,20},{20,16},{24,28},{28,24},{1,5},{5... | collective-permute-start | bytes 786440 | tf_op jit(solution)/shard_map/ppermute | solution.py:126
  80.8 6.4 %collective-permute-start.25 = (f32[128,256]{1,0:T(8,128)S(1)}, f32[128,256]{1,0:T(8,128)S(1)}, u32[]{:S(2)}, u32[]{:S(2)}) collective-permute-start(f32[128,256]{1,0:T(8,128)S(1)} %get-tuple-element.72), channel_id=1, source_target_pairs={{0,8},{4,12},{8,0},{12,4},{16,24},{20,28},{24,16},{28,20},{1,9},{5... | collective-permute-start | bytes 393224 | tf_op jit(solution)/shard_map/ppermute | solution.py:126
  81.3 8.1 %collective-permute-start.26 = (f32[128,256]{1,0:T(8,128)S(1)}, f32[128,256]{1,0:T(8,128)S(1)}, u32[]{:S(2)}, u32[]{:S(2)}) collective-permute-start(f32[128,256]{1,0:T(8,128)S(1)} %get-tuple-element.74), channel_id=1, source_target_pairs={{0,16},{4,20},{8,24},{12,28},{16,0},{20,4},{24,8},{28,12},{1,17},{... | collective-permute-start | bytes 393224 | tf_op jit(solution)/shard_map/ppermute | solution.py:126
  83.0 6.4 %collective-permute-start.27 = (f32[128,256]{1,0:T(8,128)S(1)}, f32[128,256]{1,0:T(8,128)S(1)}, u32[]{:S(2)}, u32[]{:S(2)}) collective-permute-start(f32[128,256]{1,0:T(8,128)S(1)} %get-tuple-element.73), channel_id=1, source_target_pairs={{0,24},{4,28},{8,16},{12,20},{16,8},{20,12},{24,0},{28,4},{1,25},{... | collective-permute-start | bytes 393224 | tf_op jit(solution)/shard_map/ppermute | solution.py:126
  89.4 6.3 %collective-permute-start.28 = (bf16[128,256]{1,0:T(8,128)(2,1)S(1)}, bf16[128,256]{1,0:T(8,128)(2,1)S(1)}, u32[]{:S(2)}, u32[]{:S(2)}) collective-permute-start(bf16[128,256]{1,0:T(8,128)(2,1)S(1)} %get-tuple-element.66), channel_id=1, source_target_pairs={{0,1},{1,2},{2,3},{3,0},{4,5},{5,6},{6,7},{7,4},{8,9},{9,10},{10,1... | collective-permute-start | bytes 196616 | tf_op jit(solution)/shard_map/ppermute | solution.py:130
  90.7 6.7 %collective-permute-start.29 = (bf16[128,256]{1,0:T(8,128)(2,1)S(1)}, bf16[128,256]{1,0:T(8,128)(2,1)S(1)}, u32[]{:S(2)}, u32[]{:S(2)}) collective-permute-start(bf16[128,256]{1,0:T(8,128)(2,1)S(1)} %get-tuple-element.66), channel_id=1, source_target_pairs={{0,2},{1,3},{2,0},{3,1},{4,6},{5,7},{6,4},{7,5},{8,10},{9,11},{10,... | collective-permute-start | bytes 196616 | tf_op jit(solution)/shard_map/ppermute | solution.py:130
  92.4 5.0 %collective-permute-start.30 = (bf16[128,256]{1,0:T(8,128)(2,1)S(1)}, bf16[128,256]{1,0:T(8,128)(2,1)S(1)}, u32[]{:S(2)}, u32[]{:S(2)}) collective-permute-start(bf16[128,256]{1,0:T(8,128)(2,1)S(1)} %get-tuple-element.66), channel_id=1, source_target_pairs={{0,3},{1,0},{2,1},{3,2},{4,7},{5,4},{6,5},{7,6},{8,11},{9,8},{10,9... | collective-permute-start | bytes 196616 | tf_op jit(solution)/shard_map/ppermute | solution.py:130
  93.3 4.7 %collective-permute-start.31 = (bf16[128,256]{1,0:T(8,128)(2,1)S(1)}, bf16[128,256]{1,0:T(8,128)(2,1)S(1)}, u32[]{:S(2)}, u32[]{:S(2)}) collective-permute-start(bf16[128,256]{1,0:T(8,128)(2,1)S(1)} %get-tuple-element.66), channel_id=1, source_target_pairs={{0,8},{4,12},{8,0},{12,4},{16,24},{20,28},{24,16},{28,20},{1,9},{5... | collective-permute-start | bytes 196616 | tf_op jit(solution)/shard_map/ppermute | solution.py:126
  94.9 4.3 %collective-permute-start.32 = (bf16[128,256]{1,0:T(8,128)(2,1)S(1)}, bf16[128,256]{1,0:T(8,128)(2,1)S(1)}, u32[]{:S(2)}, u32[]{:S(2)}) collective-permute-start(bf16[128,256]{1,0:T(8,128)(2,1)S(1)} %get-tuple-element.66), channel_id=1, source_target_pairs={{0,16},{4,20},{8,24},{12,28},{16,0},{20,4},{24,8},{28,12},{1,17},{... | collective-permute-start | bytes 196616 | tf_op jit(solution)/shard_map/ppermute | solution.py:126
  95.7 5.2 %collective-permute-start.33 = (bf16[128,256]{1,0:T(8,128)(2,1)S(1)}, bf16[128,256]{1,0:T(8,128)(2,1)S(1)}, u32[]{:S(2)}, u32[]{:S(2)}) collective-permute-start(bf16[128,256]{1,0:T(8,128)(2,1)S(1)} %get-tuple-element.66), channel_id=1, source_target_pairs={{0,24},{4,28},{8,16},{12,20},{16,8},{20,12},{24,0},{28,4},{1,25},{... | collective-permute-start | bytes 196616 | tf_op jit(solution)/shard_map/ppermute | solution.py:126
  100.9 1.6 %collective-permute-start.34 = (bf16[512,256]{1,0:T(8,128)(2,1)S(1)}, bf16[512,256]{1,0:T(8,128)(2,1)S(1)}, u32[]{:S(2)}, u32[]{:S(2)}) collective-permute-start(bf16[512,256]{1,0:T(8,128)(2,1)S(1)} %get-tuple-element.62), channel_id=1, source_target_pairs={{0,4},{4,0},{8,12},{12,8},{16,20},{20,16},{24,28},{28,24},{1,5},{5... | collective-permute-start | bytes 786440 | tf_op jit(solution)/shard_map/ppermute | solution.py:126
  103.8 1.5 %collective-permute-start.35 = (f32[4,40,256]{2,1,0:T(8,128)S(1)}, f32[4,40,256]{2,1,0:T(8,128)S(1)}, u32[]{:S(2)}, u32[]{:S(2)}) collective-permute-start(f32[4,40,256]{2,1,0:T(8,128)S(1)} %select_bitcast_fusion.2), channel_id=1, source_target_pairs={{0,4},{4,0},{8,12},{12,8},{16,20},{20,16},{24,28},{28,24},{1,5},{5... | collective-permute-start | bytes 491528 | tf_op jit(solution)/shard_map/ppermute | solution.py:126
  105.4 4.1 %collective-permute-start.36 = (f32[40,256]{1,0:T(8,128)S(1)}, f32[40,256]{1,0:T(8,128)S(1)}, u32[]{:S(2)}, u32[]{:S(2)}) collective-permute-start(f32[40,256]{1,0:T(8,128)S(1)} %get-tuple-element.87), channel_id=1, source_target_pairs={{0,8},{4,12},{8,0},{12,4},{16,24},{20,28},{24,16},{28,20},{1,9},{5... | collective-permute-start | bytes 122888 | tf_op jit(solution)/shard_map/ppermute | solution.py:126
  107.2 4.4 %collective-permute-start.37 = (f32[40,256]{1,0:T(8,128)S(1)}, f32[40,256]{1,0:T(8,128)S(1)}, u32[]{:S(2)}, u32[]{:S(2)}) collective-permute-start(f32[40,256]{1,0:T(8,128)S(1)} %get-tuple-element.89), channel_id=1, source_target_pairs={{0,16},{4,20},{8,24},{12,28},{16,0},{20,4},{24,8},{28,12},{1,17},{... | collective-permute-start | bytes 122888 | tf_op jit(solution)/shard_map/ppermute | solution.py:126
  107.5 4.9 %collective-permute-start.38 = (f32[40,256]{1,0:T(8,128)S(1)}, f32[40,256]{1,0:T(8,128)S(1)}, u32[]{:S(2)}, u32[]{:S(2)}) collective-permute-start(f32[40,256]{1,0:T(8,128)S(1)} %get-tuple-element.88), channel_id=1, source_target_pairs={{0,24},{4,28},{8,16},{12,20},{16,8},{20,12},{24,0},{28,4},{1,25},{... | collective-permute-start | bytes 122888 | tf_op jit(solution)/shard_map/ppermute | solution.py:126
  112.4 6.0 %collective-permute-start.39 = (f32[40,256]{1,0:T(8,128)S(1)}, f32[40,256]{1,0:T(8,128)S(1)}, u32[]{:S(2)}, u32[]{:S(2)}) collective-permute-start(f32[40,256]{1,0:T(8,128)S(1)} %fusion.45), channel_id=1, source_target_pairs={{0,1},{1,2},{2,3},{3,0},{4,5},{5,6},{6,7},{7,4},{8,9},{9,10},{10,1... | collective-permute-start | bytes 122888 | tf_op jit(solution)/shard_map/ppermute | solution.py:130
  113.3 5.8 %collective-permute-start.40 = (f32[40,256]{1,0:T(8,128)S(1)}, f32[40,256]{1,0:T(8,128)S(1)}, u32[]{:S(2)}, u32[]{:S(2)}) collective-permute-start(f32[40,256]{1,0:T(8,128)S(1)} %fusion.45), channel_id=1, source_target_pairs={{0,2},{1,3},{2,0},{3,1},{4,6},{5,7},{6,4},{7,5},{8,10},{9,11},{10,... | collective-permute-start | bytes 122888 | tf_op jit(solution)/shard_map/ppermute | solution.py:130
  114.5 4.6 %collective-permute-start.41 = (f32[40,256]{1,0:T(8,128)S(1)}, f32[40,256]{1,0:T(8,128)S(1)}, u32[]{:S(2)}, u32[]{:S(2)}) collective-permute-start(f32[40,256]{1,0:T(8,128)S(1)} %fusion.45), channel_id=1, source_target_pairs={{0,3},{1,0},{2,1},{3,2},{4,7},{5,4},{6,5},{7,6},{8,11},{9,8},{10,9... | collective-permute-start | bytes 122888 | tf_op jit(solution)/shard_map/ppermute | solution.py:130
  119.1 4.1 %collective-permute-start.42 = (f32[40,256]{1,0:T(8,128)S(1)}, f32[40,256]{1,0:T(8,128)S(1)}, u32[]{:S(2)}, u32[]{:S(2)}) collective-permute-start(f32[40,256]{1,0:T(8,128)S(1)} %add_add_fusion), channel_id=1, source_target_pairs={{0,8},{4,12},{8,0},{12,4},{16,24},{20,28},{24,16},{28,20},{1,9},{5... | collective-permute-start | bytes 122888 | tf_op jit(solution)/shard_map/ppermute | solution.py:126
  120.7 4.0 %collective-permute-start.43 = (f32[40,256]{1,0:T(8,128)S(1)}, f32[40,256]{1,0:T(8,128)S(1)}, u32[]{:S(2)}, u32[]{:S(2)}) collective-permute-start(f32[40,256]{1,0:T(8,128)S(1)} %add_add_fusion), channel_id=1, source_target_pairs={{0,16},{4,20},{8,24},{12,28},{16,0},{20,4},{24,8},{28,12},{1,17},{... | collective-permute-start | bytes 122888 | tf_op jit(solution)/shard_map/ppermute | solution.py:126
  121.3 4.9 %collective-permute-start.44 = (f32[40,256]{1,0:T(8,128)S(1)}, f32[40,256]{1,0:T(8,128)S(1)}, u32[]{:S(2)}, u32[]{:S(2)}) collective-permute-start(f32[40,256]{1,0:T(8,128)S(1)} %add_add_fusion), channel_id=1, source_target_pairs={{0,24},{4,28},{8,16},{12,20},{16,8},{20,12},{24,0},{28,4},{1,25},{... | collective-permute-start | bytes 122888 | tf_op jit(solution)/shard_map/ppermute | solution.py:126
  126.4 1.5 %collective-permute-start.45 = (f32[4,40,256]{2,1,0:T(8,128)S(1)}, f32[4,40,256]{2,1,0:T(8,128)S(1)}, u32[]{:S(2)}, u32[]{:S(2)}) collective-permute-start(f32[4,40,256]{2,1,0:T(8,128)S(1)} %fusion.26), channel_id=1, source_target_pairs={{0,4},{4,0},{8,12},{12,8},{16,20},{20,16},{24,28},{28,24},{1,5},{5... | collective-permute-start | bytes 491528 | tf_op jit(solution)/shard_map/ppermute | solution.py:126
  (2 other events, 1.6 us)
where the time goes:
time: 139 us
  starting transfers between devices  56.4 us (41%)
  waiting for transfers between devices  53 us (38%)
  Pallas kernels  18.4 us (13%)
  local copies, waits for them, and re-layouts  3.8 us (3%)
  matrix products  3.13 us (2%)
  between operations  2.43 us (2%)
  other arithmetic  1.97 us (1%)
    ppermute x28, waiting for transfers between devices, exchanged(): return lax.ppermute(x, axis, [(i, i ^ apart) for i in range(size)])  33 us
    ppermute x18, starting transfers between devices, shifted(): return lax.ppermute(x, axis, [(i, (i + step) % size) for i in range(size)])  31.1 us
    ppermute x28, starting transfers between devices, exchanged(): return lax.ppermute(x, axis, [(i, i ^ apart) for i in range(size)])  25.3 us
    ppermute x18, waiting for transfers between devices, shifted(): return lax.ppermute(x, axis, [(i, (i + step) % size) for i in range(size)])  19.9 us
    pallas_call x1, Pallas kernels, finish(): pl.pallas_call(functools.partial(finish_kernel, total_rows), out_shape=(j...  11.1 us
    pallas_call x1, Pallas kernels, direct_rows(): pl.pallas_call(functools.partial(direct_kernel, rows, slots), out_shape=(...  3.1 us
  transfers between devices with their start and end apart: 46, of which 36 were waited for; matrix products, arithmetic and copies ran while one was open for 1% of the time, Pallas kernels for 2%

commit v1 on v0

--- a/solution.py
+++ b/solution.py
@@ -48,40 +48,49 @@
             jnp.broadcast_to(s[:, start - s_lo + t:start - s_lo + t + 1], (PANEL, LANES))
             for t in range(PANEL)
         ]
-        pivots = jnp.zeros((PANEL, LANES), jnp.float32)
-        for t in range(0, PANEL, 2):
-            one, two = columns[t], columns[t + 1]
-            a, b, d = one[t:t + 1, :], one[t + 1:t + 2, :], two[t + 1:t + 2, :]
-            det = a * d - b * b
-            det_inv = reciprocal(det)
-            a_inv = reciprocal(a)
-            pivots = jnp.where(row_id == t, a, pivots)
-            pivots = jnp.where(row_id == t + 1, det * a_inv, pivots)
-            one_below = jnp.where(row_id > t + 1, one, 0.0)
-            two_below = jnp.where(row_id > t + 1, two, 0.0)
-            for j in range(t + 2, PANEL):
-                p1, p2 = one[j:j + 1, :], two[j:j + 1, :]
-                columns[j] = (
-                    columns[j]
-                    - one_below * ((d * p1 - b * p2) * det_inv)
-                    - two_below * ((a * p2 - b * p1) * det_inv)
+        s_done, w_done = [], []
+        for base in range(0, PANEL, 8):
+            ids = row_id[: PANEL - base]
+            pivots = jnp.zeros((8, LANES), jnp.float32)
+            for t in range(base, base + 8, 2):
+                at = t - base
+                one, two = columns[t], columns[t + 1]
+                a, b, d = one[at:at + 1, :], one[at + 1:at + 2, :], two[at + 1:at + 2, :]
+                det = a * d - b * b
+                det_inv = reciprocal(det)
+                a_inv = reciprocal(a)
+                pivots = jnp.where(ids[:8] == at, a, pivots)
+                pivots = jnp.where(ids[:8] == at + 1, det * a_inv, pivots)
+                below = ids > at + 1
+                one_below = jnp.where(below, one, 0.0)
+                two_below = jnp.where(below, two, 0.0)
+                first = (d * one - b * two) * det_inv
+                second = (a * two - b * one) * det_inv
+                for j in range(t + 2, PANEL):
+                    r = j - base
+                    if j < t + 4:
+                        p1, p2 = one[r:r + 1, :], two[r:r + 1, :]
+                        m1, m2 = (d * p1 - b * p2) * det_inv, (a * p2 - b * p1) * det_inv
+                    else:
+                        m1, m2 = first[r:r + 1, :], second[r:r + 1, :]
+                    columns[j] = columns[j] - (one_below * m1 + two_below * m2)
+                first = jnp.where(below, first, jnp.where(ids == at + 1, b * a_inv, 0.0))
+                second = jnp.where(below, second, 0.0)
+                s = s - (
+                    widen(first, s.shape[1]) * s[at:at + 1, :]
+                    + widen(second, s.shape[1]) * s[at + 1:at + 2, :]
                 )
-            first = (d * one_below - b * two_below) * det_inv
-            first = jnp.where(row_id == t + 1, b * a_inv, first)
-            second = (a * two_below - b * one_below) * det_inv
-            s = (
-                s
-                - widen(first, s.shape[1]) * s[t:t + 1, :]
-                - widen(second, s.shape[1]) * s[t + 1:t + 2, :]
-            )
-            w = (
-                w
-                - widen(first, w.shape[1]) * w[t:t + 1, :]
-                - widen(second, w.shape[1]) * w[t + 1:t + 2, :]
-            )
-        root = lax.rsqrt(pivots)
-        s = s * widen(root, s.shape[1])
-        w = w * widen(root, w.shape[1])
+                w = w - (
+                    widen(first, w.shape[1]) * w[at:at + 1, :]
+                    + widen(second, w.shape[1]) * w[at + 1:at + 2, :]
+                )
+            root = lax.rsqrt(pivots)
+            s_done.append(s[:8] * widen(root, s.shape[1]))
+            w_done.append(w[:8] * widen(root, w.shape[1]))
+            s, w = s[8:], w[8:]
+            columns = [c[8:] for c in columns]
+        s = jnp.concatenate(s_done, 0)
+        w = jnp.concatenate(w_done, 0)
         inverse_ref[start:start + PANEL, :w_hi] = w
         if w_hi < k:
             inverse_ref[start:start + PANEL, w_hi:] = jnp.zeros((PANEL, k - w_hi), jnp.float32)
@@ -149,12 +158,19 @@
     return x
 
 
+def places_of(places_ref, owner):
+    ids = lax.broadcasted_iota(jnp.int32, places_ref.shape, 0)
+    return jnp.sum(jnp.where(ids == owner, places_ref[...], 0.0), 0, keepdims=True)
+
+
 def pack_kernel(col_ref, blocks_ref, places_ref, *piece_refs):
-    cols = len(piece_refs)
-    for s, piece in enumerate(piece_refs):
+    cols = len(piece_refs) + 1
+    for s, piece in enumerate(piece_refs, 1):
         owner = lax.rem(col_ref[0] + s, cols)
         piece[:, : BS * BS] = blocks_ref[owner]
-        piece[:, BS * BS :] = places_ref[owner]
+        count = places_ref.shape[1]
+        row = jnp.broadcast_to(places_of(places_ref, owner), (piece.shape[0], count))
+        piece[:, BS * BS : BS * BS + count] = row.astype(jnp.bfloat16)
 
 
 def pack(col, blocks, places):
@@ -162,9 +178,9 @@
     shape = jax.ShapeDtypeStruct((height, BS * BS + LANES), jnp.bfloat16)
     return pl.pallas_call(
         pack_kernel,
-        out_shape=(shape,) * cols,
+        out_shape=(shape,) * (cols - 1),
         in_specs=[SMEM, VMEM, VMEM],
-        out_specs=(VMEM,) * cols,
+        out_specs=(VMEM,) * (cols - 1),
         name="pack",
     )(col, blocks, places)
 
@@ -218,21 +234,28 @@
     )(key, blocks, onsite)
 
 
-def direct_kernel(rows, slots, *refs):
-    cols = len(refs) - 2 - rows // 2
-    piece_refs, out_refs, (flat_ref, square_ref) = refs[:cols], refs[cols:-2], refs[-2:]
+def direct_kernel(rows, slots, col_ref, blocks_ref, places_ref, *refs):
+    cols = blocks_ref.shape[0]
+    piece_refs, out_refs = refs[: cols - 1], refs[cols - 1 : -2]
+    flat_ref, square_ref = refs[-2:]
     row_blocks = cols * PB
     groups = rows * row_blocks
     total = jnp.zeros((2 * groups, BS * BS), jnp.float32)
-    for s, piece in enumerate(piece_refs):
-        height = piece.shape[0]
-        place = piece[0:1, BS * BS : BS * BS + height].astype(jnp.float32).astype(jnp.int32)
+    height = blocks_ref.shape[1]
+    for s in range(cols):
+        if s == 0:
+            place, blocks = places_of(places_ref, col_ref[0]), blocks_ref[col_ref[0]]
+        else:
+            piece = piece_refs[s - 1]
+            place = piece[0:1, BS * BS : BS * BS + height].astype(jnp.float32)
+            blocks = piece[:, : BS * BS]
+        place = place.astype(jnp.int32)
         block = lax.broadcasted_iota(jnp.int32, (1, height), 1) // slots
         key = place % 2 * groups + place // 2 * row_blocks + s * PB + block
         key = jnp.where(place < 0, -1, key)
         ids = lax.broadcasted_iota(jnp.int32, (2 * groups, height), 0)
         chosen = (ids == key).astype(jnp.float32).astype(jnp.bfloat16)
-        total += jnp.dot(chosen, piece[:, : BS * BS], preferred_element_type=jnp.float32)
+        total += jnp.dot(chosen, blocks, preferred_element_type=jnp.float32)
     flat_ref[...] = total
     unflatten(flat_ref, square_ref, groups)
     for chip, out in enumerate(out_refs):
@@ -243,14 +266,14 @@
             )
 
 
-def direct_rows(pieces, rows, slots):
-    cols = len(pieces)
+def direct_rows(col, blocks, places, pieces, rows, slots):
+    cols = blocks.shape[0]
     groups = rows * cols * PB
     shape = jax.ShapeDtypeStruct((PB * BS, 2 * cols * LANES), jnp.bfloat16)
     return pl.pallas_call(
         functools.partial(direct_kernel, rows, slots),
         out_shape=(shape,) * (rows // 2),
-        in_specs=[VMEM] * cols,
+        in_specs=[SMEM] + [VMEM] * (cols + 1),
         out_specs=(VMEM,) * (rows // 2),
         scratch_shapes=[
             pltpu.VMEM((2 * groups, BS * BS), jnp.float32),
@@ -258,7 +281,7 @@
         ],
         compiler_params=pltpu.CompilerParams(vmem_limit_bytes=48 * 1024 * 1024),
         name="direct_rows",
-    )(*pieces)
+    )(col, blocks, places, *pieces)
 
 
 def local(orbitals_in, hblocks, block_cols, live_counts, onsite, cut_low, top_bound):
@@ -278,18 +301,18 @@
     device, block = block_cols // PB, block_cols % PB
     apart = (device % 2) ^ core
     distance = (device // 2) ^ chip
-    places = jnp.where(live, (distance * 2 + apart) * PB + block, -1).astype(jnp.bfloat16)
-    places = places.reshape(cols, 1, PB * slots)
-    places = jnp.pad(places, ((0, 0), (0, PB * slots - 1), (0, LANES - PB * slots)))
+    places = jnp.where(live, (distance * 2 + apart) * PB + block, -1).astype(jnp.float32)
+    places = places.reshape(cols, PB * slots)
     block_row = jnp.arange(row_blocks, dtype=jnp.int32)[:, None]
     near_row = (col - block_row // PB) % cols * PB + block_row % PB
     groups = rows * row_blocks
     key = block * groups + (apart * chips + distance) * row_blocks + near_row
     key = jnp.where(live, key, -1).reshape(1, row_blocks * slots)
 
-    pieces = pack(col[None], hblocks.reshape(cols, PB * slots, BS * BS), places)
+    by_owner = hblocks.reshape(cols, PB * slots, BS * BS)
+    pieces = pack(col[None], by_owner, places)
     key, pieces = lax.optimization_barrier((key, pieces))
-    pieces = [shifted(pieces[s], "col", cols, s) if s else pieces[s] for s in range(cols)]
+    pieces = [shifted(piece, "col", cols, s) for s, piece in enumerate(pieces, 1)]
 
     def gather_near(v):
         return jnp.concatenate([v] + [shifted(v, "col", cols, s) for s in range(1, cols)], 0)
@@ -305,7 +328,7 @@
         key, hblocks.reshape(row_blocks * slots, BS * BS), onsite, rows, row_blocks
     )
 
-    direct = direct_rows(pieces, rows, slots)
+    direct = direct_rows(col[None], by_owner, places, pieces, rows, slots)
     far, direct = lax.optimization_barrier((far, direct))
     far = core_swap(far, rows)
     direct = [chip_swap(direct[s], rows, s) if s else direct[s] for s in range(chips)]

time: 139 us -> 136 us (0.978)
  Pallas kernels: 18.4 us -> 16 us
    pallas_call x1, Pallas kernels: 11.1 us -> 8.8 us  [finish(): pl.pallas_call(functools.partial(finish_kernel, total_rows), out_shape=(j...]
where the time goes in v1:
time: 136 us
  starting transfers between devices  56.4 us (41%)
  waiting for transfers between devices  53 us (39%)
  Pallas kernels  16 us (12%)
  matrix products  3.13 us (2%)
  local copies, waits for them, and re-layouts  2.85 us (2%)
  between operations  2.43 us (2%)
  other arithmetic  2.02 us (1%)
    ppermute x28, waiting for transfers between devices, exchanged(): return lax.ppermute(x, axis, [(i, i ^ apart) for i in range(size)])  33 us
    ppermute x18, starting transfers between devices, shifted(): return lax.ppermute(x, axis, [(i, (i + step) % size) for i in range(size)])  31.1 us
    ppermute x28, starting transfers between devices, exchanged(): return lax.ppermute(x, axis, [(i, i ^ apart) for i in range(size)])  25.3 us
    ppermute x18, waiting for transfers between devices, shifted(): return lax.ppermute(x, axis, [(i, (i + step) % size) for i in range(size)])  20 us
    pallas_call x1, Pallas kernels, finish(): pl.pallas_call(functools.partial(finish_kernel, total_rows), out_shape=(j...  8.8 us
    pallas_call x1, Pallas kernels, direct_rows(): pl.pallas_call(functools.partial(direct_kernel, rows, slots), out_shape=(...  3.09 us
  transfers between devices with their start and end apart: 46, of which 36 were waited for; matrix products, arithmetic and copies ran while one was open for 1% of the time, Pallas kernels for 2%

profile of v1, /device:TPU:0, one launch (start us, length us, event | category | flops | bytes accessed | tf_op | source)
XLA Modules:
  0.0 135.8 jit_solution(10120827455732901231)
XLA Ops:
  2.3 1.8 %pack.1 = (bf16[16,4224]{1,0:T(8,128)(2,1)}, bf16[16,4224]{1,0:T(8,128)(2,1)}, bf16[16,4224]{1,0:T(8,128)(2,1)}) custom-call(s32[1]{0:T(128)} %bitcast.1.col_ref, bf16[4,16,4096]{2,1,0:T(8,128)(2,1)} %bitcast.82, f32[4,16]{1,0:T(4,128)} %reshape.181.places_ref), custom_call_target="tpu_custom_call" | custom-call | tf_op jit(solution)/shard_map/pack/pallas_call | solution.py:179
  4.1 3.0 %collective-permute-start = (bf16[16,4224]{1,0:T(8,128)(2,1)}, bf16[16,4224]{1,0:T(8,128)(2,1)S(1)}, u32[]{:S(2)}, u32[]{:S(2)}) collective-permute-start(bf16[16,4224]{1,0:T(8,128)(2,1)} %get-tuple-element.38), channel_id=1, source_target_pairs={{0,1},{1,2},{2,3},{3,0},{4,5},{5,6},{6,7},{7,4},{8,9},{9,10},{10,1... | collective-permute-start | bytes 405512 | tf_op jit(solution)/shard_map/ppermute | solution.py:139
  7.1 2.6 %collective-permute-start.1 = (bf16[16,4224]{1,0:T(8,128)(2,1)}, bf16[16,4224]{1,0:T(8,128)(2,1)S(1)}, u32[]{:S(2)}, u32[]{:S(2)}) collective-permute-start(bf16[16,4224]{1,0:T(8,128)(2,1)} %get-tuple-element.39), channel_id=1, source_target_pairs={{0,2},{1,3},{2,0},{3,1},{4,6},{5,7},{6,4},{7,5},{8,10},{9,11},{10,... | collective-permute-start | bytes 405512 | tf_op jit(solution)/shard_map/ppermute | solution.py:139
  9.7 1.3 collective-permute-start.2
  12.8 2.3 %mirror.1 = (bf16[512,512]{1,0:T(8,128)(2,1)S(1)}, bf16[512,512]{1,0:T(8,128)(2,1)S(1)}) custom-call(s32[1,64]{1,0:T(1,128)S(1)} %reshape.179.key_ref, bf16[64,4096]{1,0:T(8,128)(2,1)S(1)} %bitcast.83, bf16[2,4096]{1,0:T(2,128)(2,1)S(1)} %copy-done.3), custom_call_target="tpu_custom_call" | custom-call | flops 67108864 | bytes 786432 | tf_op jit(solution)/shard_map/mirror/pallas_call | solution.py:220
  15.1 3.7 %collective-permute-done.1.refs_1_ = bf16[16,4224]{1,0:T(8,128)(2,1)S(1)} collective-permute-done((bf16[16,4224]{1,0:T(8,128)(2,1)}, bf16[16,4224]{1,0:T(8,128)(2,1)S(1)}, u32[]{:S(2)}, u32[]{:S(2)}) %collective-permute-start.1) | collective-permute-done | bytes 135200 | tf_op jit(solution)/shard_map/ppermute | solution.py:139
  18.8 3.1 %direct_rows.1 = (bf16[128,1024]{1,0:T(8,128)(2,1)S(1)}, bf16[128,1024]{1,0:T(8,128)(2,1)S(1)}, bf16[128,1024]{1,0:T(8,128)(2,1)S(1)}, bf16[128,1024]{1,0:T(8,128)(2,1)S(1)}) custom-call(s32[1]{0:T(128)} %bitcast.1.col_ref, bf16[4,16,4096]{2,1,0:T(8,128)(2,1)S(1)} %bitcast.84, f32[4,16]{1,0:T(4,128)S(1)} %copy-done.2, ...), custom_call_target="tpu_custom_call" | custom-call | tf_op jit(solution)/shard_map/direct_rows/pallas_call | solution.py:273
  22.0 1.6 %collective-permute-start.4 = (bf16[128,1024]{1,0:T(8,128)(2,1)S(1)}, bf16[128,1024]{1,0:T(8,128)(2,1)S(1)}, u32[]{:S(2)}, u32[]{:S(2)}) collective-permute-start(bf16[128,1024]{1,0:T(8,128)(2,1)S(1)} %get-tuple-element.48), channel_id=1, source_target_pairs={{0,8},{4,12},{8,0},{12,4},{16,24},{20,28},{24,16},{28,20},{1,9},{5... | collective-permute-start | bytes 786440 | tf_op jit(solution)/shard_map/ppermute | solution.py:135
  23.6 1.5 %collective-permute-start.5 = (bf16[128,1024]{1,0:T(8,128)(2,1)S(1)}, bf16[128,1024]{1,0:T(8,128)(2,1)S(1)}, u32[]{:S(2)}, u32[]{:S(2)}) collective-permute-start(bf16[128,1024]{1,0:T(8,128)(2,1)S(1)} %get-tuple-element.49), channel_id=1, source_target_pairs={{0,16},{4,20},{8,24},{12,28},{16,0},{20,4},{24,8},{28,12},{1,17},{... | collective-permute-start | bytes 786440 | tf_op jit(solution)/shard_map/ppermute | solution.py:135
  25.6 3.4 %collective-permute-start.7 = (bf16[128,256]{1,0:T(8,128)(2,1)S(1)}, bf16[128,256]{1,0:T(8,128)(2,1)S(1)}, u32[]{:S(2)}, u32[]{:S(2)}) collective-permute-start(bf16[128,256]{1,0:T(8,128)(2,1)S(1)} %convert_element_type.17), channel_id=1, source_target_pairs={{0,1},{1,2},{2,3},{3,0},{4,5},{5,6},{6,7},{7,4},{8,9},{9,10},{10,1... | collective-permute-start | bytes 196616 | tf_op jit(solution)/shard_map/ppermute | solution.py:139
  28.9 1.6 %collective-permute-start.8 = (bf16[128,256]{1,0:T(8,128)(2,1)S(1)}, bf16[128,256]{1,0:T(8,128)(2,1)S(1)}, u32[]{:S(2)}, u32[]{:S(2)}) collective-permute-start(bf16[128,256]{1,0:T(8,128)(2,1)S(1)} %convert_element_type.17), channel_id=1, source_target_pairs={{0,2},{1,3},{2,0},{3,1},{4,6},{5,7},{6,4},{7,5},{8,10},{9,11},{10,... | collective-permute-start | bytes 196616 | tf_op jit(solution)/shard_map/ppermute | solution.py:139
  30.6 2.4 %collective-permute-done.7 = bf16[128,256]{1,0:T(8,128)(2,1)S(1)} collective-permute-done((bf16[128,256]{1,0:T(8,128)(2,1)S(1)}, bf16[128,256]{1,0:T(8,128)(2,1)S(1)}, u32[]{:S(2)}, u32[]{:S(2)}) %collective-permute-start.7) | collective-permute-done | bytes 65568 | tf_op jit(solution)/shard_map/ppermute | solution.py:139
  33.0 2.0 %collective-permute-start.9 = (bf16[128,256]{1,0:T(8,128)(2,1)S(1)}, bf16[128,256]{1,0:T(8,128)(2,1)S(1)}, u32[]{:S(2)}, u32[]{:S(2)}) collective-permute-start(bf16[128,256]{1,0:T(8,128)(2,1)S(1)} %convert_element_type.17), channel_id=1, source_target_pairs={{0,3},{1,0},{2,1},{3,2},{4,7},{5,4},{6,5},{7,6},{8,11},{9,8},{10,9... | collective-permute-start | bytes 196616 | tf_op jit(solution)/shard_map/ppermute | solution.py:139
  35.2 2.1 %collective-permute-done.9 = bf16[128,256]{1,0:T(8,128)(2,1)S(1)} collective-permute-done((bf16[128,256]{1,0:T(8,128)(2,1)S(1)}, bf16[128,256]{1,0:T(8,128)(2,1)S(1)}, u32[]{:S(2)}, u32[]{:S(2)}) %collective-permute-start.9) | collective-permute-done | bytes 65568 | tf_op jit(solution)/shard_map/ppermute | solution.py:139
  39.2 1.6 %collective-permute-start.11 = (f32[128,256]{1,0:T(8,128)S(1)}, f32[128,256]{1,0:T(8,128)S(1)}, u32[]{:S(2)}, u32[]{:S(2)}) collective-permute-start(f32[128,256]{1,0:T(8,128)S(1)} %get-tuple-element.74), channel_id=1, source_target_pairs={{0,8},{4,12},{8,0},{12,4},{16,24},{20,28},{24,16},{28,20},{1,9},{5... | collective-permute-start | bytes 393224 | tf_op jit(solution)/shard_map/ppermute | solution.py:135
  40.8 1.5 %collective-permute-start.12 = (f32[128,256]{1,0:T(8,128)S(1)}, f32[128,256]{1,0:T(8,128)S(1)}, u32[]{:S(2)}, u32[]{:S(2)}) collective-permute-start(f32[128,256]{1,0:T(8,128)S(1)} %get-tuple-element.76), channel_id=1, source_target_pairs={{0,16},{4,20},{8,24},{12,28},{16,0},{20,4},{24,8},{28,12},{1,17},{... | collective-permute-start | bytes 393224 | tf_op jit(solution)/shard_map/ppermute | solution.py:135
  45.2 3.7 %collective-permute-done.12 = f32[128,256]{1,0:T(8,128)S(1)} collective-permute-done((f32[128,256]{1,0:T(8,128)S(1)}, f32[128,256]{1,0:T(8,128)S(1)}, u32[]{:S(2)}, u32[]{:S(2)}) %collective-permute-start.12) | collective-permute-done | bytes 131104 | tf_op jit(solution)/shard_map/ppermute | solution.py:135
  48.9 2.2 %collective-permute-start.14 = (bf16[128,256]{1,0:T(8,128)(2,1)S(1)}, bf16[128,256]{1,0:T(8,128)(2,1)S(1)}, u32[]{:S(2)}, u32[]{:S(2)}) collective-permute-start(bf16[128,256]{1,0:T(8,128)(2,1)S(1)} %get-tuple-element.66), channel_id=1, source_target_pairs={{0,1},{1,2},{2,3},{3,0},{4,5},{5,6},{6,7},{7,4},{8,9},{9,10},{10,1... | collective-permute-start | bytes 196616 | tf_op jit(solution)/shard_map/ppermute | solution.py:139
  51.1 2.2 %collective-permute-start.15 = (bf16[128,256]{1,0:T(8,128)(2,1)S(1)}, bf16[128,256]{1,0:T(8,128)(2,1)S(1)}, u32[]{:S(2)}, u32[]{:S(2)}) collective-permute-start(bf16[128,256]{1,0:T(8,128)(2,1)S(1)} %get-tuple-element.66), channel_id=1, source_target_pairs={{0,2},{1,3},{2,0},{3,1},{4,6},{5,7},{6,4},{7,5},{8,10},{9,11},{10,... | collective-permute-start | bytes 196616 | tf_op jit(solution)/shard_map/ppermute | solution.py:139
  53.6 1.9 %collective-permute-done.14 = bf16[128,256]{1,0:T(8,128)(2,1)S(1)} collective-permute-done((bf16[128,256]{1,0:T(8,128)(2,1)S(1)}, bf16[128,256]{1,0:T(8,128)(2,1)S(1)}, u32[]{:S(2)}, u32[]{:S(2)}) %collective-permute-start.14) | collective-permute-done | bytes 65568 | tf_op jit(solution)/shard_map/ppermute | solution.py:139
  55.5 2.1 %collective-permute-done.15 = bf16[128,256]{1,0:T(8,128)(2,1)S(1)} collective-permute-done((bf16[128,256]{1,0:T(8,128)(2,1)S(1)}, bf16[128,256]{1,0:T(8,128)(2,1)S(1)}, u32[]{:S(2)}, u32[]{:S(2)}) %collective-permute-start.15) | collective-permute-done | bytes 65568 | tf_op jit(solution)/shard_map/ppermute | solution.py:139
  60.0 1.3 collective-permute-start.18
  62.2 1.4 %collective-permute-start.20 = (f32[128,256]{1,0:T(8,128)S(1)}, f32[128,256]{1,0:T(8,128)S(1)}, u32[]{:S(2)}, u32[]{:S(2)}) collective-permute-start(f32[128,256]{1,0:T(8,128)S(1)} %get-tuple-element.72), channel_id=1, source_target_pairs={{0,24},{4,28},{8,16},{12,20},{16,8},{20,12},{24,0},{28,4},{1,25},{... | collective-permute-start | bytes 393224 | tf_op jit(solution)/shard_map/ppermute | solution.py:135
  63.6 2.7 %collective-permute-done.18 = f32[128,256]{1,0:T(8,128)S(1)} collective-permute-done((f32[128,256]{1,0:T(8,128)S(1)}, f32[128,256]{1,0:T(8,128)S(1)}, u32[]{:S(2)}, u32[]{:S(2)}) %collective-permute-start.18) | collective-permute-done | bytes 131104 | tf_op jit(solution)/shard_map/ppermute | solution.py:135
  66.2 1.6 %collective-permute-done.19 = f32[128,256]{1,0:T(8,128)S(1)} collective-permute-done((f32[128,256]{1,0:T(8,128)S(1)}, f32[128,256]{1,0:T(8,128)S(1)}, u32[]{:S(2)}, u32[]{:S(2)}) %collective-permute-start.19) | collective-permute-done | bytes 131104 | tf_op jit(solution)/shard_map/ppermute | solution.py:135
  67.8 1.6 %collective-permute-done.20 = f32[128,256]{1,0:T(8,128)S(1)} collective-permute-done((f32[128,256]{1,0:T(8,128)S(1)}, f32[128,256]{1,0:T(8,128)S(1)}, u32[]{:S(2)}, u32[]{:S(2)}) %collective-permute-start.20) | collective-permute-done | bytes 131104 | tf_op jit(solution)/shard_map/ppermute | solution.py:135
  70.7 1.8 %collective-permute-start.22 = (bf16[128,256]{1,0:T(8,128)(2,1)S(1)}, bf16[128,256]{1,0:T(8,128)(2,1)S(1)}, u32[]{:S(2)}, u32[]{:S(2)}) collective-permute-start(bf16[128,256]{1,0:T(8,128)(2,1)S(1)} %get-tuple-element.64), channel_id=1, source_target_pairs={{0,2},{1,3},{2,0},{3,1},{4,6},{5,7},{6,4},{7,5},{8,10},{9,11},{10,... | collective-permute-start | bytes 196616 | tf_op jit(solution)/shard_map/ppermute | solution.py:139
  73.4 2.7 %collective-permute-done.21 = bf16[128,256]{1,0:T(8,128)(2,1)S(1)} collective-permute-done((bf16[128,256]{1,0:T(8,128)(2,1)S(1)}, bf16[128,256]{1,0:T(8,128)(2,1)S(1)}, u32[]{:S(2)}, u32[]{:S(2)}) %collective-permute-start.21) | collective-permute-done | bytes 65568 | tf_op jit(solution)/shard_map/ppermute | solution.py:139
  76.0 1.8 %collective-permute-done.22 = bf16[128,256]{1,0:T(8,128)(2,1)S(1)} collective-permute-done((bf16[128,256]{1,0:T(8,128)(2,1)S(1)}, bf16[128,256]{1,0:T(8,128)(2,1)S(1)}, u32[]{:S(2)}, u32[]{:S(2)}) %collective-permute-start.22) | collective-permute-done | bytes 65568 | tf_op jit(solution)/shard_map/ppermute | solution.py:139
  80.3 1.7 %collective-permute-start.26 = (f32[128,256]{1,0:T(8,128)S(1)}, f32[128,256]{1,0:T(8,128)S(1)}, u32[]{:S(2)}, u32[]{:S(2)}) collective-permute-start(f32[128,256]{1,0:T(8,128)S(1)} %get-tuple-element.70), channel_id=1, source_target_pairs={{0,16},{4,20},{8,24},{12,28},{16,0},{20,4},{24,8},{28,12},{1,17},{... | collective-permute-start | bytes 393224 | tf_op jit(solution)/shard_map/ppermute | solution.py:135
  82.0 1.4 %collective-permute-start.27 = (f32[128,256]{1,0:T(8,128)S(1)}, f32[128,256]{1,0:T(8,128)S(1)}, u32[]{:S(2)}, u32[]{:S(2)}) collective-permute-start(f32[128,256]{1,0:T(8,128)S(1)} %get-tuple-element.69), channel_id=1, source_target_pairs={{0,24},{4,28},{8,16},{12,20},{16,8},{20,12},{24,0},{28,4},{1,25},{... | collective-permute-start | bytes 393224 | tf_op jit(solution)/shard_map/ppermute | solution.py:135
  83.4 2.9 %collective-permute-done.25 = f32[128,256]{1,0:T(8,128)S(1)} collective-permute-done((f32[128,256]{1,0:T(8,128)S(1)}, f32[128,256]{1,0:T(8,128)S(1)}, u32[]{:S(2)}, u32[]{:S(2)}) %collective-permute-start.25) | collective-permute-done | bytes 131104 | tf_op jit(solution)/shard_map/ppermute | solution.py:135
  86.3 2.1 %collective-permute-done.26 = f32[128,256]{1,0:T(8,128)S(1)} collective-permute-done((f32[128,256]{1,0:T(8,128)S(1)}, f32[128,256]{1,0:T(8,128)S(1)}, u32[]{:S(2)}, u32[]{:S(2)}) %collective-permute-start.26) | collective-permute-done | bytes 131104 | tf_op jit(solution)/shard_map/ppermute | solution.py:135
  88.5 1.3 collective-permute-start.28
  89.8 1.7 %collective-permute-start.29 = (bf16[128,256]{1,0:T(8,128)(2,1)S(1)}, bf16[128,256]{1,0:T(8,128)(2,1)S(1)}, u32[]{:S(2)}, u32[]{:S(2)}) collective-permute-start(bf16[128,256]{1,0:T(8,128)(2,1)S(1)} %get-tuple-element.62), channel_id=1, source_target_pairs={{0,2},{1,3},{2,0},{3,1},{4,6},{5,7},{6,4},{7,5},{8,10},{9,11},{10,... | collective-permute-start | bytes 196616 | tf_op jit(solution)/shard_map/ppermute | solution.py:139
  92.4 1.6 %collective-permute-start.31 = (bf16[128,256]{1,0:T(8,128)(2,1)S(1)}, bf16[128,256]{1,0:T(8,128)(2,1)S(1)}, u32[]{:S(2)}, u32[]{:S(2)}) collective-permute-start(bf16[128,256]{1,0:T(8,128)(2,1)S(1)} %get-tuple-element.62), channel_id=1, source_target_pairs={{0,8},{4,12},{8,0},{12,4},{16,24},{20,28},{24,16},{28,20},{1,9},{5... | collective-permute-start | bytes 196616 | tf_op jit(solution)/shard_map/ppermute | solution.py:135
  94.7 1.4 %collective-permute-start.33 = (bf16[128,256]{1,0:T(8,128)(2,1)S(1)}, bf16[128,256]{1,0:T(8,128)(2,1)S(1)}, u32[]{:S(2)}, u32[]{:S(2)}) collective-permute-start(bf16[128,256]{1,0:T(8,128)(2,1)S(1)} %get-tuple-element.62), channel_id=1, source_target_pairs={{0,24},{4,28},{8,16},{12,20},{16,8},{20,12},{24,0},{28,4},{1,25},{... | collective-permute-start | bytes 196616 | tf_op jit(solution)/shard_map/ppermute | solution.py:135
  98.2 1.7 %collective-permute-done.33 = bf16[128,256]{1,0:T(8,128)(2,1)S(1)} collective-permute-done((bf16[128,256]{1,0:T(8,128)(2,1)S(1)}, bf16[128,256]{1,0:T(8,128)(2,1)S(1)}, u32[]{:S(2)}, u32[]{:S(2)}) %collective-permute-start.33) | collective-permute-done | bytes 65568 | tf_op jit(solution)/shard_map/ppermute | solution.py:135
  104.5 1.8 %collective-permute-start.36 = (f32[40,256]{1,0:T(8,128)S(1)}, f32[40,256]{1,0:T(8,128)S(1)}, u32[]{:S(2)}, u32[]{:S(2)}) collective-permute-start(f32[40,256]{1,0:T(8,128)S(1)} %get-tuple-element.83), channel_id=1, source_target_pairs={{0,8},{4,12},{8,0},{12,4},{16,24},{20,28},{24,16},{28,20},{1,9},{5... | collective-permute-start | bytes 122888 | tf_op jit(solution)/shard_map/ppermute | solution.py:135
  106.5 1.5 %collective-permute-start.38 = (f32[40,256]{1,0:T(8,128)S(1)}, f32[40,256]{1,0:T(8,128)S(1)}, u32[]{:S(2)}, u32[]{:S(2)}) collective-permute-start(f32[40,256]{1,0:T(8,128)S(1)} %get-tuple-element.84), channel_id=1, source_target_pairs={{0,24},{4,28},{8,16},{12,20},{16,8},{20,12},{24,0},{28,4},{1,25},{... | collective-permute-start | bytes 122888 | tf_op jit(solution)/shard_map/ppermute | solution.py:135
  108.6 2.1 %collective-permute-done.37 = f32[40,256]{1,0:T(8,128)S(1)} collective-permute-done((f32[40,256]{1,0:T(8,128)S(1)}, f32[40,256]{1,0:T(8,128)S(1)}, u32[]{:S(2)}, u32[]{:S(2)}) %collective-permute-start.37) | collective-permute-done | bytes 40992 | tf_op jit(solution)/shard_map/ppermute | solution.py:135
  113.6 2.6 %collective-permute-start.41 = (f32[40,256]{1,0:T(8,128)S(1)}, f32[40,256]{1,0:T(8,128)S(1)}, u32[]{:S(2)}, u32[]{:S(2)}) collective-permute-start(f32[40,256]{1,0:T(8,128)S(1)} %fusion.45), channel_id=1, source_target_pairs={{0,3},{1,0},{2,1},{3,2},{4,7},{5,4},{6,5},{7,6},{8,11},{9,8},{10,9... | collective-permute-start | bytes 122888 | tf_op jit(solution)/shard_map/ppermute | solution.py:139
  118.2 1.6 %collective-permute-start.42 = (f32[40,256]{1,0:T(8,128)S(1)}, f32[40,256]{1,0:T(8,128)S(1)}, u32[]{:S(2)}, u32[]{:S(2)}) collective-permute-start(f32[40,256]{1,0:T(8,128)S(1)} %add_add_fusion), channel_id=1, source_target_pairs={{0,8},{4,12},{8,0},{12,4},{16,24},{20,28},{24,16},{28,20},{1,9},{5... | collective-permute-start | bytes 122888 | tf_op jit(solution)/shard_map/ppermute | solution.py:135
  120.4 1.4 %collective-permute-start.44 = (f32[40,256]{1,0:T(8,128)S(1)}, f32[40,256]{1,0:T(8,128)S(1)}, u32[]{:S(2)}, u32[]{:S(2)}) collective-permute-start(f32[40,256]{1,0:T(8,128)S(1)} %add_add_fusion), channel_id=1, source_target_pairs={{0,24},{4,28},{8,16},{12,20},{16,8},{20,12},{24,0},{28,4},{1,25},{... | collective-permute-start | bytes 122888 | tf_op jit(solution)/shard_map/ppermute | solution.py:135
  122.3 1.5 %collective-permute-done.43 = f32[40,256]{1,0:T(8,128)S(1)} collective-permute-done((f32[40,256]{1,0:T(8,128)S(1)}, f32[40,256]{1,0:T(8,128)S(1)}, u32[]{:S(2)}, u32[]{:S(2)}) %collective-permute-start.43) | collective-permute-done | bytes 40992 | tf_op jit(solution)/shard_map/ppermute | solution.py:135
  123.8 1.5 %collective-permute-done.44 = f32[40,256]{1,0:T(8,128)S(1)} collective-permute-done((f32[40,256]{1,0:T(8,128)S(1)}, f32[40,256]{1,0:T(8,128)S(1)}, u32[]{:S(2)}, u32[]{:S(2)}) %collective-permute-start.44) | collective-permute-done | bytes 40992 | tf_op jit(solution)/shard_map/ppermute | solution.py:135
  125.5 1.4 %collective-permute-done.45 = f32[4,40,256]{2,1,0:T(8,128)S(1)} collective-permute-done((f32[4,40,256]{2,1,0:T(8,128)S(1)}, f32[4,40,256]{2,1,0:T(8,128)S(1)}, u32[]{:S(2)}, u32[]{:S(2)}) %collective-permute-start.45) | collective-permute-done | bytes 163872 | tf_op jit(solution)/shard_map/ppermute | solution.py:135
  127.0 8.8 %finish.1 = (f32[128,256]{1,0:T(8,128)}, f32[256,256]{1,0:T(8,128)}) custom-call(f32[256,256]{1,0:T(8,128)S(1)} %bitcast.85, f32[1,256]{1,0:T(1,128)S(1)} %slice_bitcast_fusion.4.diagonal_ref, f32[128,256]{1,0:T(8,128)S(1)} %get-tuple-element.63.y_ref), custom_call_target="tpu_custom_call" | custom-call | tf_op jit(solution)/shard_map/finish/pallas_call | solution.py:123
  (116 shorter events, 31.0 us)
Async XLA Ops:
  0.6 18.2 %copy-start.1 = (bf16[8,8,4096]{2,1,0:T(8,128)(2,1)S(1)}, bf16[8,8,4096]{2,1,0:T(8,128)(2,1)}, u32[]{:S(2)}) copy-start(bf16[8,8,4096]{2,1,0:T(8,128)(2,1)} %param.8) | copy-start | bytes 1572868
  2.2 16.6 %copy-start.2 = (f32[4,16]{1,0:T(4,128)S(1)}, f32[4,16]{1,0:T(4,128)}, u32[]{:S(2)}) copy-start(f32[4,16]{1,0:T(4,128)} %reshape.181.places_ref) | copy-start | bytes 772
  4.1 11.0 %collective-permute-start = (bf16[16,4224]{1,0:T(8,128)(2,1)}, bf16[16,4224]{1,0:T(8,128)(2,1)S(1)}, u32[]{:S(2)}, u32[]{:S(2)}) collective-permute-start(bf16[16,4224]{1,0:T(8,128)(2,1)} %get-tuple-element.38), channel_id=1, source_target_pairs={{0,1},{1,2},{2,3},{3,0},{4,5},{5,6},{6,7},{7,4},{8,9},{9,10},{10,1... | collective-permute-start | bytes 405512 | tf_op jit(solution)/shard_map/ppermute | solution.py:139
  7.1 11.7 %collective-permute-start.1 = (bf16[16,4224]{1,0:T(8,128)(2,1)}, bf16[16,4224]{1,0:T(8,128)(2,1)S(1)}, u32[]{:S(2)}, u32[]{:S(2)}) collective-permute-start(bf16[16,4224]{1,0:T(8,128)(2,1)} %get-tuple-element.39), channel_id=1, source_target_pairs={{0,2},{1,3},{2,0},{3,1},{4,6},{5,7},{6,4},{7,5},{8,10},{9,11},{10,... | collective-permute-start | bytes 405512 | tf_op jit(solution)/shard_map/ppermute | solution.py:139
  9.7 9.1 %collective-permute-start.2 = (bf16[16,4224]{1,0:T(8,128)(2,1)}, bf16[16,4224]{1,0:T(8,128)(2,1)S(1)}, u32[]{:S(2)}, u32[]{:S(2)}) collective-permute-start(bf16[16,4224]{1,0:T(8,128)(2,1)} %get-tuple-element.40), channel_id=1, source_target_pairs={{0,3},{1,0},{2,1},{3,2},{4,7},{5,4},{6,5},{7,6},{8,11},{9,8},{10,9... | collective-permute-start | bytes 405512 | tf_op jit(solution)/shard_map/ppermute | solution.py:139
  21.9 3.7 %collective-permute-start.3 = (bf16[512,512]{1,0:T(8,128)(2,1)S(1)}, bf16[512,512]{1,0:T(8,128)(2,1)S(1)}, u32[]{:S(2)}, u32[]{:S(2)}) collective-permute-start(bf16[512,512]{1,0:T(8,128)(2,1)S(1)} %get-tuple-element.45), channel_id=1, source_target_pairs={{0,4},{4,0},{8,12},{12,8},{16,20},{20,16},{24,28},{28,24},{1,5},{5... | collective-permute-start | bytes 1572872 | tf_op jit(solution)/shard_map/ppermute | solution.py:135
  22.0 15.3 %collective-permute-start.4 = (bf16[128,1024]{1,0:T(8,128)(2,1)S(1)}, bf16[128,1024]{1,0:T(8,128)(2,1)S(1)}, u32[]{:S(2)}, u32[]{:S(2)}) collective-permute-start(bf16[128,1024]{1,0:T(8,128)(2,1)S(1)} %get-tuple-element.48), channel_id=1, source_target_pairs={{0,8},{4,12},{8,0},{12,4},{16,24},{20,28},{24,16},{28,20},{1,9},{5... | collective-permute-start | bytes 786440 | tf_op jit(solution)/shard_map/ppermute | solution.py:135
  23.6 14.0 %collective-permute-start.5 = (bf16[128,1024]{1,0:T(8,128)(2,1)S(1)}, bf16[128,1024]{1,0:T(8,128)(2,1)S(1)}, u32[]{:S(2)}, u32[]{:S(2)}) collective-permute-start(bf16[128,1024]{1,0:T(8,128)(2,1)S(1)} %get-tuple-element.49), channel_id=1, source_target_pairs={{0,16},{4,20},{8,24},{12,28},{16,0},{20,4},{24,8},{28,12},{1,17},{... | collective-permute-start | bytes 786440 | tf_op jit(solution)/shard_map/ppermute | solution.py:135
  25.1 12.5 %collective-permute-start.6 = (bf16[128,1024]{1,0:T(8,128)(2,1)S(1)}, bf16[128,1024]{1,0:T(8,128)(2,1)S(1)}, u32[]{:S(2)}, u32[]{:S(2)}) collective-permute-start(bf16[128,1024]{1,0:T(8,128)(2,1)S(1)} %get-tuple-element.50), channel_id=1, source_target_pairs={{0,24},{4,28},{8,16},{12,20},{16,8},{20,12},{24,0},{28,4},{1,25},{... | collective-permute-start | bytes 786440 | tf_op jit(solution)/shard_map/ppermute | solution.py:135
  25.6 7.5 %collective-permute-start.7 = (bf16[128,256]{1,0:T(8,128)(2,1)S(1)}, bf16[128,256]{1,0:T(8,128)(2,1)S(1)}, u32[]{:S(2)}, u32[]{:S(2)}) collective-permute-start(bf16[128,256]{1,0:T(8,128)(2,1)S(1)} %convert_element_type.17), channel_id=1, source_target_pairs={{0,1},{1,2},{2,3},{3,0},{4,5},{5,6},{6,7},{7,4},{8,9},{9,10},{10,1... | collective-permute-start | bytes 196616 | tf_op jit(solution)/shard_map/ppermute | solution.py:139
  28.9 6.2 %collective-permute-start.8 = (bf16[128,256]{1,0:T(8,128)(2,1)S(1)}, bf16[128,256]{1,0:T(8,128)(2,1)S(1)}, u32[]{:S(2)}, u32[]{:S(2)}) collective-permute-start(bf16[128,256]{1,0:T(8,128)(2,1)S(1)} %convert_element_type.17), channel_id=1, source_target_pairs={{0,2},{1,3},{2,0},{3,1},{4,6},{5,7},{6,4},{7,5},{8,10},{9,11},{10,... | collective-permute-start | bytes 196616 | tf_op jit(solution)/shard_map/ppermute | solution.py:139
  33.0 4.3 %collective-permute-start.9 = (bf16[128,256]{1,0:T(8,128)(2,1)S(1)}, bf16[128,256]{1,0:T(8,128)(2,1)S(1)}, u32[]{:S(2)}, u32[]{:S(2)}) collective-permute-start(bf16[128,256]{1,0:T(8,128)(2,1)S(1)} %convert_element_type.17), channel_id=1, source_target_pairs={{0,3},{1,0},{2,1},{3,2},{4,7},{5,4},{6,5},{7,6},{8,11},{9,8},{10,9... | collective-permute-start | bytes 196616 | tf_op jit(solution)/shard_map/ppermute | solution.py:139
  37.3 1.5 %collective-permute-start.10 = (bf16[512,256]{1,0:T(8,128)(2,1)S(1)}, bf16[512,256]{1,0:T(8,128)(2,1)S(1)}, u32[]{:S(2)}, u32[]{:S(2)}) collective-permute-start(bf16[512,256]{1,0:T(8,128)(2,1)S(1)} %constant_dynamic-update-slice_fusion), channel_id=1, source_target_pairs={{0,4},{4,0},{8,12},{12,8},{16,20},{20,16},{24,28},{28,24},{1,5},{5... | collective-permute-start | bytes 786440 | tf_op jit(solution)/shard_map/ppermute | solution.py:135
  39.2 5.9 %collective-permute-start.11 = (f32[128,256]{1,0:T(8,128)S(1)}, f32[128,256]{1,0:T(8,128)S(1)}, u32[]{:S(2)}, u32[]{:S(2)}) collective-permute-start(f32[128,256]{1,0:T(8,128)S(1)} %get-tuple-element.74), channel_id=1, source_target_pairs={{0,8},{4,12},{8,0},{12,4},{16,24},{20,28},{24,16},{28,20},{1,9},{5... | collective-permute-start | bytes 393224 | tf_op jit(solution)/shard_map/ppermute | solution.py:135
  40.8 8.1 %collective-permute-start.12 = (f32[128,256]{1,0:T(8,128)S(1)}, f32[128,256]{1,0:T(8,128)S(1)}, u32[]{:S(2)}, u32[]{:S(2)}) collective-permute-start(f32[128,256]{1,0:T(8,128)S(1)} %get-tuple-element.76), channel_id=1, source_target_pairs={{0,16},{4,20},{8,24},{12,28},{16,0},{20,4},{24,8},{28,12},{1,17},{... | collective-permute-start | bytes 393224 | tf_op jit(solution)/shard_map/ppermute | solution.py:135
  42.3 6.6 %collective-permute-start.13 = (f32[128,256]{1,0:T(8,128)S(1)}, f32[128,256]{1,0:T(8,128)S(1)}, u32[]{:S(2)}, u32[]{:S(2)}) collective-permute-start(f32[128,256]{1,0:T(8,128)S(1)} %get-tuple-element.75), channel_id=1, source_target_pairs={{0,24},{4,28},{8,16},{12,20},{16,8},{20,12},{24,0},{28,4},{1,25},{... | collective-permute-start | bytes 393224 | tf_op jit(solution)/shard_map/ppermute | solution.py:135
  48.9 6.5 %collective-permute-start.14 = (bf16[128,256]{1,0:T(8,128)(2,1)S(1)}, bf16[128,256]{1,0:T(8,128)(2,1)S(1)}, u32[]{:S(2)}, u32[]{:S(2)}) collective-permute-start(bf16[128,256]{1,0:T(8,128)(2,1)S(1)} %get-tuple-element.66), channel_id=1, source_target_pairs={{0,1},{1,2},{2,3},{3,0},{4,5},{5,6},{6,7},{7,4},{8,9},{9,10},{10,1... | collective-permute-start | bytes 196616 | tf_op jit(solution)/shard_map/ppermute | solution.py:139
  51.1 6.4 %collective-permute-start.15 = (bf16[128,256]{1,0:T(8,128)(2,1)S(1)}, bf16[128,256]{1,0:T(8,128)(2,1)S(1)}, u32[]{:S(2)}, u32[]{:S(2)}) collective-permute-start(bf16[128,256]{1,0:T(8,128)(2,1)S(1)} %get-tuple-element.66), channel_id=1, source_target_pairs={{0,2},{1,3},{2,0},{3,1},{4,6},{5,7},{6,4},{7,5},{8,10},{9,11},{10,... | collective-permute-start | bytes 196616 | tf_op jit(solution)/shard_map/ppermute | solution.py:139
  53.4 4.6 %collective-permute-start.16 = (bf16[128,256]{1,0:T(8,128)(2,1)S(1)}, bf16[128,256]{1,0:T(8,128)(2,1)S(1)}, u32[]{:S(2)}, u32[]{:S(2)}) collective-permute-start(bf16[128,256]{1,0:T(8,128)(2,1)S(1)} %get-tuple-element.66), channel_id=1, source_target_pairs={{0,3},{1,0},{2,1},{3,2},{4,7},{5,4},{6,5},{7,6},{8,11},{9,8},{10,9... | collective-permute-start | bytes 196616 | tf_op jit(solution)/shard_map/ppermute | solution.py:139
  58.0 1.6 %collective-permute-start.17 = (bf16[512,256]{1,0:T(8,128)(2,1)S(1)}, bf16[512,256]{1,0:T(8,128)(2,1)S(1)}, u32[]{:S(2)}, u32[]{:S(2)}) collective-permute-start(bf16[512,256]{1,0:T(8,128)(2,1)S(1)} %pad_maximum_fusion.3), channel_id=1, source_target_pairs={{0,4},{4,0},{8,12},{12,8},{16,20},{20,16},{24,28},{28,24},{1,5},{5... | collective-permute-start | bytes 786440 | tf_op jit(solution)/shard_map/ppermute | solution.py:135
  60.0 6.2 %collective-permute-start.18 = (f32[128,256]{1,0:T(8,128)S(1)}, f32[128,256]{1,0:T(8,128)S(1)}, u32[]{:S(2)}, u32[]{:S(2)}) collective-permute-start(f32[128,256]{1,0:T(8,128)S(1)} %get-tuple-element.71), channel_id=1, source_target_pairs={{0,8},{4,12},{8,0},{12,4},{16,24},{20,28},{24,16},{28,20},{1,9},{5... | collective-permute-start | bytes 393224 | tf_op jit(solution)/shard_map/ppermute | solution.py:135
  61.3 6.5 %collective-permute-start.19 = (f32[128,256]{1,0:T(8,128)S(1)}, f32[128,256]{1,0:T(8,128)S(1)}, u32[]{:S(2)}, u32[]{:S(2)}) collective-permute-start(f32[128,256]{1,0:T(8,128)S(1)} %get-tuple-element.73), channel_id=1, source_target_pairs={{0,16},{4,20},{8,24},{12,28},{16,0},{20,4},{24,8},{28,12},{1,17},{... | collective-permute-start | bytes 393224 | tf_op jit(solution)/shard_map/ppermute | solution.py:135
  62.2 7.2 %collective-permute-start.20 = (f32[128,256]{1,0:T(8,128)S(1)}, f32[128,256]{1,0:T(8,128)S(1)}, u32[]{:S(2)}, u32[]{:S(2)}) collective-permute-start(f32[128,256]{1,0:T(8,128)S(1)} %get-tuple-element.72), channel_id=1, source_target_pairs={{0,24},{4,28},{8,16},{12,20},{16,8},{20,12},{24,0},{28,4},{1,25},{... | collective-permute-start | bytes 393224 | tf_op jit(solution)/shard_map/ppermute | solution.py:135
  69.5 6.5 %collective-permute-start.21 = (bf16[128,256]{1,0:T(8,128)(2,1)S(1)}, bf16[128,256]{1,0:T(8,128)(2,1)S(1)}, u32[]{:S(2)}, u32[]{:S(2)}) collective-permute-start(bf16[128,256]{1,0:T(8,128)(2,1)S(1)} %get-tuple-element.64), channel_id=1, source_target_pairs={{0,1},{1,2},{2,3},{3,0},{4,5},{5,6},{6,7},{7,4},{8,9},{9,10},{10,1... | collective-permute-start | bytes 196616 | tf_op jit(solution)/shard_map/ppermute | solution.py:139
  70.7 7.2 %collective-permute-start.22 = (bf16[128,256]{1,0:T(8,128)(2,1)S(1)}, bf16[128,256]{1,0:T(8,128)(2,1)S(1)}, u32[]{:S(2)}, u32[]{:S(2)}) collective-permute-start(bf16[128,256]{1,0:T(8,128)(2,1)S(1)} %get-tuple-element.64), channel_id=1, source_target_pairs={{0,2},{1,3},{2,0},{3,1},{4,6},{5,7},{6,4},{7,5},{8,10},{9,11},{10,... | collective-permute-start | bytes 196616 | tf_op jit(solution)/shard_map/ppermute | solution.py:139
  72.5 5.3 %collective-permute-start.23 = (bf16[128,256]{1,0:T(8,128)(2,1)S(1)}, bf16[128,256]{1,0:T(8,128)(2,1)S(1)}, u32[]{:S(2)}, u32[]{:S(2)}) collective-permute-start(bf16[128,256]{1,0:T(8,128)(2,1)S(1)} %get-tuple-element.64), channel_id=1, source_target_pairs={{0,3},{1,0},{2,1},{3,2},{4,7},{5,4},{6,5},{7,6},{8,11},{9,8},{10,9... | collective-permute-start | bytes 196616 | tf_op jit(solution)/shard_map/ppermute | solution.py:139
  77.9 1.6 %collective-permute-start.24 = (bf16[512,256]{1,0:T(8,128)(2,1)S(1)}, bf16[512,256]{1,0:T(8,128)(2,1)S(1)}, u32[]{:S(2)}, u32[]{:S(2)}) collective-permute-start(bf16[512,256]{1,0:T(8,128)(2,1)S(1)} %pad_maximum_fusion.4), channel_id=1, source_target_pairs={{0,4},{4,0},{8,12},{12,8},{16,20},{20,16},{24,28},{28,24},{1,5},{5... | collective-permute-start | bytes 786440 | tf_op jit(solution)/shard_map/ppermute | solution.py:135
  79.9 6.4 %collective-permute-start.25 = (f32[128,256]{1,0:T(8,128)S(1)}, f32[128,256]{1,0:T(8,128)S(1)}, u32[]{:S(2)}, u32[]{:S(2)}) collective-permute-start(f32[128,256]{1,0:T(8,128)S(1)} %get-tuple-element.68), channel_id=1, source_target_pairs={{0,8},{4,12},{8,0},{12,4},{16,24},{20,28},{24,16},{28,20},{1,9},{5... | collective-permute-start | bytes 393224 | tf_op jit(solution)/shard_map/ppermute | solution.py:135
  80.3 8.1 %collective-permute-start.26 = (f32[128,256]{1,0:T(8,128)S(1)}, f32[128,256]{1,0:T(8,128)S(1)}, u32[]{:S(2)}, u32[]{:S(2)}) collective-permute-start(f32[128,256]{1,0:T(8,128)S(1)} %get-tuple-element.70), channel_id=1, source_target_pairs={{0,16},{4,20},{8,24},{12,28},{16,0},{20,4},{24,8},{28,12},{1,17},{... | collective-permute-start | bytes 393224 | tf_op jit(solution)/shard_map/ppermute | solution.py:135
  82.0 6.4 %collective-permute-start.27 = (f32[128,256]{1,0:T(8,128)S(1)}, f32[128,256]{1,0:T(8,128)S(1)}, u32[]{:S(2)}, u32[]{:S(2)}) collective-permute-start(f32[128,256]{1,0:T(8,128)S(1)} %get-tuple-element.69), channel_id=1, source_target_pairs={{0,24},{4,28},{8,16},{12,20},{16,8},{20,12},{24,0},{28,4},{1,25},{... | collective-permute-start | bytes 393224 | tf_op jit(solution)/shard_map/ppermute | solution.py:135
  88.5 6.3 %collective-permute-start.28 = (bf16[128,256]{1,0:T(8,128)(2,1)S(1)}, bf16[128,256]{1,0:T(8,128)(2,1)S(1)}, u32[]{:S(2)}, u32[]{:S(2)}) collective-permute-start(bf16[128,256]{1,0:T(8,128)(2,1)S(1)} %get-tuple-element.62), channel_id=1, source_target_pairs={{0,1},{1,2},{2,3},{3,0},{4,5},{5,6},{6,7},{7,4},{8,9},{9,10},{10,1... | collective-permute-start | bytes 196616 | tf_op jit(solution)/shard_map/ppermute | solution.py:139
  89.8 6.7 %collective-permute-start.29 = (bf16[128,256]{1,0:T(8,128)(2,1)S(1)}, bf16[128,256]{1,0:T(8,128)(2,1)S(1)}, u32[]{:S(2)}, u32[]{:S(2)}) collective-permute-start(bf16[128,256]{1,0:T(8,128)(2,1)S(1)} %get-tuple-element.62), channel_id=1, source_target_pairs={{0,2},{1,3},{2,0},{3,1},{4,6},{5,7},{6,4},{7,5},{8,10},{9,11},{10,... | collective-permute-start | bytes 196616 | tf_op jit(solution)/shard_map/ppermute | solution.py:139
  91.5 5.0 %collective-permute-start.30 = (bf16[128,256]{1,0:T(8,128)(2,1)S(1)}, bf16[128,256]{1,0:T(8,128)(2,1)S(1)}, u32[]{:S(2)}, u32[]{:S(2)}) collective-permute-start(bf16[128,256]{1,0:T(8,128)(2,1)S(1)} %get-tuple-element.62), channel_id=1, source_target_pairs={{0,3},{1,0},{2,1},{3,2},{4,7},{5,4},{6,5},{7,6},{8,11},{9,8},{10,9... | collective-permute-start | bytes 196616 | tf_op jit(solution)/shard_map/ppermute | solution.py:139
  92.4 4.7 %collective-permute-start.31 = (bf16[128,256]{1,0:T(8,128)(2,1)S(1)}, bf16[128,256]{1,0:T(8,128)(2,1)S(1)}, u32[]{:S(2)}, u32[]{:S(2)}) collective-permute-start(bf16[128,256]{1,0:T(8,128)(2,1)S(1)} %get-tuple-element.62), channel_id=1, source_target_pairs={{0,8},{4,12},{8,0},{12,4},{16,24},{20,28},{24,16},{28,20},{1,9},{5... | collective-permute-start | bytes 196616 | tf_op jit(solution)/shard_map/ppermute | solution.py:135
  94.0 4.3 %collective-permute-start.32 = (bf16[128,256]{1,0:T(8,128)(2,1)S(1)}, bf16[128,256]{1,0:T(8,128)(2,1)S(1)}, u32[]{:S(2)}, u32[]{:S(2)}) collective-permute-start(bf16[128,256]{1,0:T(8,128)(2,1)S(1)} %get-tuple-element.62), channel_id=1, source_target_pairs={{0,16},{4,20},{8,24},{12,28},{16,0},{20,4},{24,8},{28,12},{1,17},{... | collective-permute-start | bytes 196616 | tf_op jit(solution)/shard_map/ppermute | solution.py:135
  94.7 5.2 %collective-permute-start.33 = (bf16[128,256]{1,0:T(8,128)(2,1)S(1)}, bf16[128,256]{1,0:T(8,128)(2,1)S(1)}, u32[]{:S(2)}, u32[]{:S(2)}) collective-permute-start(bf16[128,256]{1,0:T(8,128)(2,1)S(1)} %get-tuple-element.62), channel_id=1, source_target_pairs={{0,24},{4,28},{8,16},{12,20},{16,8},{20,12},{24,0},{28,4},{1,25},{... | collective-permute-start | bytes 196616 | tf_op jit(solution)/shard_map/ppermute | solution.py:135
  100.0 1.6 %collective-permute-start.34 = (bf16[512,256]{1,0:T(8,128)(2,1)S(1)}, bf16[512,256]{1,0:T(8,128)(2,1)S(1)}, u32[]{:S(2)}, u32[]{:S(2)}) collective-permute-start(bf16[512,256]{1,0:T(8,128)(2,1)S(1)} %get-tuple-element.58), channel_id=1, source_target_pairs={{0,4},{4,0},{8,12},{12,8},{16,20},{20,16},{24,28},{28,24},{1,5},{5... | collective-permute-start | bytes 786440 | tf_op jit(solution)/shard_map/ppermute | solution.py:135
  102.9 1.5 %collective-permute-start.35 = (f32[4,40,256]{2,1,0:T(8,128)S(1)}, f32[4,40,256]{2,1,0:T(8,128)S(1)}, u32[]{:S(2)}, u32[]{:S(2)}) collective-permute-start(f32[4,40,256]{2,1,0:T(8,128)S(1)} %select_bitcast_fusion.2), channel_id=1, source_target_pairs={{0,4},{4,0},{8,12},{12,8},{16,20},{20,16},{24,28},{28,24},{1,5},{5... | collective-permute-start | bytes 491528 | tf_op jit(solution)/shard_map/ppermute | solution.py:135
  104.5 4.1 %collective-permute-start.36 = (f32[40,256]{1,0:T(8,128)S(1)}, f32[40,256]{1,0:T(8,128)S(1)}, u32[]{:S(2)}, u32[]{:S(2)}) collective-permute-start(f32[40,256]{1,0:T(8,128)S(1)} %get-tuple-element.83), channel_id=1, source_target_pairs={{0,8},{4,12},{8,0},{12,4},{16,24},{20,28},{24,16},{28,20},{1,9},{5... | collective-permute-start | bytes 122888 | tf_op jit(solution)/shard_map/ppermute | solution.py:135
  106.3 4.4 %collective-permute-start.37 = (f32[40,256]{1,0:T(8,128)S(1)}, f32[40,256]{1,0:T(8,128)S(1)}, u32[]{:S(2)}, u32[]{:S(2)}) collective-permute-start(f32[40,256]{1,0:T(8,128)S(1)} %get-tuple-element.85), channel_id=1, source_target_pairs={{0,16},{4,20},{8,24},{12,28},{16,0},{20,4},{24,8},{28,12},{1,17},{... | collective-permute-start | bytes 122888 | tf_op jit(solution)/shard_map/ppermute | solution.py:135
  106.5 4.9 %collective-permute-start.38 = (f32[40,256]{1,0:T(8,128)S(1)}, f32[40,256]{1,0:T(8,128)S(1)}, u32[]{:S(2)}, u32[]{:S(2)}) collective-permute-start(f32[40,256]{1,0:T(8,128)S(1)} %get-tuple-element.84), channel_id=1, source_target_pairs={{0,24},{4,28},{8,16},{12,20},{16,8},{20,12},{24,0},{28,4},{1,25},{... | collective-permute-start | bytes 122888 | tf_op jit(solution)/shard_map/ppermute | solution.py:135
  111.4 6.0 %collective-permute-start.39 = (f32[40,256]{1,0:T(8,128)S(1)}, f32[40,256]{1,0:T(8,128)S(1)}, u32[]{:S(2)}, u32[]{:S(2)}) collective-permute-start(f32[40,256]{1,0:T(8,128)S(1)} %fusion.45), channel_id=1, source_target_pairs={{0,1},{1,2},{2,3},{3,0},{4,5},{5,6},{6,7},{7,4},{8,9},{9,10},{10,1... | collective-permute-start | bytes 122888 | tf_op jit(solution)/shard_map/ppermute | solution.py:139
  112.4 5.8 %collective-permute-start.40 = (f32[40,256]{1,0:T(8,128)S(1)}, f32[40,256]{1,0:T(8,128)S(1)}, u32[]{:S(2)}, u32[]{:S(2)}) collective-permute-start(f32[40,256]{1,0:T(8,128)S(1)} %fusion.45), channel_id=1, source_target_pairs={{0,2},{1,3},{2,0},{3,1},{4,6},{5,7},{6,4},{7,5},{8,10},{9,11},{10,... | collective-permute-start | bytes 122888 | tf_op jit(solution)/shard_map/ppermute | solution.py:139
  113.6 4.6 %collective-permute-start.41 = (f32[40,256]{1,0:T(8,128)S(1)}, f32[40,256]{1,0:T(8,128)S(1)}, u32[]{:S(2)}, u32[]{:S(2)}) collective-permute-start(f32[40,256]{1,0:T(8,128)S(1)} %fusion.45), channel_id=1, source_target_pairs={{0,3},{1,0},{2,1},{3,2},{4,7},{5,4},{6,5},{7,6},{8,11},{9,8},{10,9... | collective-permute-start | bytes 122888 | tf_op jit(solution)/shard_map/ppermute | solution.py:139
  118.2 4.1 %collective-permute-start.42 = (f32[40,256]{1,0:T(8,128)S(1)}, f32[40,256]{1,0:T(8,128)S(1)}, u32[]{:S(2)}, u32[]{:S(2)}) collective-permute-start(f32[40,256]{1,0:T(8,128)S(1)} %add_add_fusion), channel_id=1, source_target_pairs={{0,8},{4,12},{8,0},{12,4},{16,24},{20,28},{24,16},{28,20},{1,9},{5... | collective-permute-start | bytes 122888 | tf_op jit(solution)/shard_map/ppermute | solution.py:135
  119.8 4.0 %collective-permute-start.43 = (f32[40,256]{1,0:T(8,128)S(1)}, f32[40,256]{1,0:T(8,128)S(1)}, u32[]{:S(2)}, u32[]{:S(2)}) collective-permute-start(f32[40,256]{1,0:T(8,128)S(1)} %add_add_fusion), channel_id=1, source_target_pairs={{0,16},{4,20},{8,24},{12,28},{16,0},{20,4},{24,8},{28,12},{1,17},{... | collective-permute-start | bytes 122888 | tf_op jit(solution)/shard_map/ppermute | solution.py:135
  120.4 4.9 %collective-permute-start.44 = (f32[40,256]{1,0:T(8,128)S(1)}, f32[40,256]{1,0:T(8,128)S(1)}, u32[]{:S(2)}, u32[]{:S(2)}) collective-permute-start(f32[40,256]{1,0:T(8,128)S(1)} %add_add_fusion), channel_id=1, source_target_pairs={{0,24},{4,28},{8,16},{12,20},{16,8},{20,12},{24,0},{28,4},{1,25},{... | collective-permute-start | bytes 122888 | tf_op jit(solution)/shard_map/ppermute | solution.py:135
  125.4 1.5 %collective-permute-start.45 = (f32[4,40,256]{2,1,0:T(8,128)S(1)}, f32[4,40,256]{2,1,0:T(8,128)S(1)}, u32[]{:S(2)}, u32[]{:S(2)}) collective-permute-start(f32[4,40,256]{2,1,0:T(8,128)S(1)} %fusion.26), channel_id=1, source_target_pairs={{0,4},{4,0},{8,12},{12,8},{16,20},{20,16},{24,28},{28,24},{1,5},{5... | collective-permute-start | bytes 491528 | tf_op jit(solution)/shard_map/ppermute | solution.py:135
  (3 other events, 11.0 us)

commit v2 on v1

--- a/solution.py
+++ b/solution.py
@@ -24,17 +24,12 @@
     return pl.reciprocal(x, approx=True)
 
 
-def finish_kernel(total_rows, packed_ref, diagonal_ref, y_ref, orbitals_ref, projected_ref, inverse_ref):
-    k = packed_ref.shape[0]
+def finish_kernel(total_rows, gram_ref, cross_ref, y_ref, orbitals_ref, projected_ref, inverse_ref):
+    k = gram_ref.shape[0]
     panels = k // PANEL
-    packed = packed_ref[...]
-    flipped = packed.T
-    above = lax.broadcasted_iota(jnp.int32, (k, k), 0) - lax.broadcasted_iota(jnp.int32, (k, k), 1)
-    gram = jnp.where(above <= 0, packed, flipped)
-    cross = jnp.where(above > 0, packed, jnp.where(above < 0, flipped, diagonal_ref[...]))
     row_id = lax.broadcasted_iota(jnp.int32, (PANEL, LANES), 0)
     scale = 1.0 / total_rows
-    upper = [gram[m * PANEL:(m + 1) * PANEL, :] * scale for m in range(panels)]
+    upper = [gram_ref[m * PANEL:(m + 1) * PANEL, :] * scale for m in range(panels)]
     inverse = []
     for m in range(panels):
         r = lax.broadcasted_iota(jnp.int32, (PANEL, k), 0) + m * PANEL
@@ -113,12 +108,12 @@
     inv = inverse_ref[...]
     nt = (((1,), (1,)), ((), ()))
     orbitals_ref[...] = lax.dot_general(y_ref[...], inv, nt, precision=HI, preferred_element_type=jnp.float32)
-    half = jnp.dot(inv, cross, precision=HI, preferred_element_type=jnp.float32)
+    half = jnp.dot(inv, cross_ref[...], precision=HI, preferred_element_type=jnp.float32)
     full = lax.dot_general(half, inv, nt, precision=HI, preferred_element_type=jnp.float32)
-    projected_ref[...] = full * (0.5 * scale)
-
-def finish(packed, diagonal, y, total_rows):
-    k = packed.shape[0]
+    projected_ref[...] = (full + full.T) * (0.5 * scale)
+
+def finish(gram, cross, y, total_rows):
+    k = gram.shape[0]
     f32 = jnp.float32
     return pl.pallas_call(
         functools.partial(finish_kernel, total_rows),
@@ -128,7 +123,7 @@
         scratch_shapes=[pltpu.VMEM((k, k), f32)],
         compiler_params=pltpu.CompilerParams(vmem_limit_bytes=32 * 1024 * 1024),
         name="finish",
-    )(packed, diagonal, y)
+    )(gram, cross, y)
 
 
 def exchanged(x, axis, size, apart):
@@ -196,8 +191,8 @@
         square_ref[pl.ds(2 * h + 1, groups, stride=BS), :] = second
 
 
-def mirror_kernel(key_ref, blocks_ref, onsite_ref, near_ref, far_ref, flat_ref, square_ref):
-    height = near_ref.shape[1]
+def mirror_kernel(key_ref, blocks_ref, onsite_ref, out_ref, flat_ref, square_ref):
+    height = out_ref.shape[2]
     groups = square_ref.shape[0] // BS
     places = lax.broadcasted_iota(jnp.int32, (2 * groups, key_ref.shape[1]), 0)
     chosen = (places == key_ref[...]).astype(jnp.float32).astype(jnp.bfloat16)
@@ -208,20 +203,19 @@
     unflatten(flat_ref, square_ref, groups)
     devices = square_ref.shape[0] // height
     for d in range(devices):
-        out = near_ref if d < devices // 2 else far_ref
-        at = d % (devices // 2) * LANES
+        which, at = d // (devices // 2), d % (devices // 2) * LANES
         square = square_ref[d * height : (d + 1) * height, :]
-        out[at : at + LANES, :] = square.T.astype(jnp.bfloat16)
+        out_ref[which, at : at + LANES, :] = square.T.astype(jnp.bfloat16)
 
 
 def mirror(key, blocks, onsite, rows, row_blocks):
-    half = (rows // 2 * PB * BS, row_blocks * BS)
+    shape = (2, rows // 2 * PB * BS, row_blocks * BS)
     groups = rows * row_blocks
     return pl.pallas_call(
         mirror_kernel,
-        out_shape=(jax.ShapeDtypeStruct(half, jnp.bfloat16),) * 2,
+        out_shape=jax.ShapeDtypeStruct(shape, jnp.bfloat16),
         in_specs=[VMEM, VMEM, VMEM],
-        out_specs=(VMEM, VMEM),
+        out_specs=VMEM,
         scratch_shapes=[
             pltpu.VMEM((2 * groups, BS * BS), jnp.float32),
             pltpu.VMEM((groups * BS, LANES), jnp.float32),
@@ -261,9 +255,8 @@
     for chip, out in enumerate(out_refs):
         for g in range(2 * cols):
             at = (chip * 2 * cols + g) * LANES
-            out[:, g * LANES : (g + 1) * LANES] = square_ref[at : at + LANES, :].astype(
-                jnp.bfloat16
-            )
+            lane = (g % cols * 2 + g // cols) * LANES
+            out[:, lane : lane + LANES] = square_ref[at : at + LANES, :].astype(jnp.bfloat16)
 
 
 def direct_rows(col, blocks, places, pieces, rows, slots):
@@ -284,6 +277,40 @@
     )(col, blocks, places, *pieces)
 
 
+def assemble_kernel(mirrored, mirrored_other, *refs):
+    chips = (len(refs) - 1) // 2
+    tile = refs[-1]
+    size = PB * BS
+    cols = mirrored.shape[2] // size
+    for chip in range(chips):
+        for j in range(2):
+            sources = mirrored.at[j], mirrored_other.at[1 - j]
+            direct = refs[j * chips + chip]
+            rows = slice(chip * size, (chip + 1) * size)
+            out_rows = slice((2 * chip + j) * size, (2 * chip + j + 1) * size)
+            for s in range(cols):
+                for i in range(2):
+                    taken = (2 * s + (i ^ j)) * size
+                    lane = (2 * s + i) * size
+                    tile[out_rows, lane : lane + size] = (
+                        sources[i][rows, s * size : (s + 1) * size]
+                        + direct[:, taken : taken + size]
+                    )
+
+
+def assemble(mirrored, mirrored_other, direct, direct_other):
+    _, height, width = mirrored.shape
+    args = (mirrored, mirrored_other, *direct, *direct_other)
+    return pl.pallas_call(
+        assemble_kernel,
+        out_shape=jax.ShapeDtypeStruct((2 * height, 2 * width), jnp.bfloat16),
+        in_specs=[VMEM] * len(args),
+        out_specs=VMEM,
+        compiler_params=pltpu.CompilerParams(vmem_limit_bytes=40 * 1024 * 1024),
+        name="assemble",
+    )(*args)
+
+
 def local(orbitals_in, hblocks, block_cols, live_counts, onsite, cut_low, top_bound):
     rows = lax.axis_size("row")
     cols = lax.axis_size("col")
@@ -295,7 +322,6 @@
     k = orbitals_in.shape[1]
     local_rows = PB * BS
     total_rows = rows * cols * local_rows
-    near_rows = cols * local_rows
 
     live = jnp.arange(slots, dtype=jnp.int32)[None, :] < live_counts
     device, block = block_cols // PB, block_cols % PB
@@ -309,41 +335,56 @@
     key = block * groups + (apart * chips + distance) * row_blocks + near_row
     key = jnp.where(live, key, -1).reshape(1, row_blocks * slots)
 
+    half = k // 2
+    first_core = core == 0
+
+    def halves(x):
+        low, high = x[:, :half], x[:, half:]
+        return jnp.where(first_core, low, high), jnp.where(first_core, high, low)
+
+    def joined(own, other, axis):
+        ordered = jnp.concatenate([own, other], axis), jnp.concatenate([other, own], axis)
+        return jnp.where(first_core, *ordered)
+
+    own, other = halves(orbitals_in)
+    start = jnp.concatenate([own, core_swap(other, rows)], 0)
+
     by_owner = hblocks.reshape(cols, PB * slots, BS * BS)
     pieces = pack(col[None], by_owner, places)
-    key, pieces = lax.optimization_barrier((key, pieces))
+    key, pieces, start = lax.optimization_barrier((key, pieces, start))
     pieces = [shifted(piece, "col", cols, s) for s, piece in enumerate(pieces, 1)]
 
-    def gather_near(v):
+    def gather(v):
         return jnp.concatenate([v] + [shifted(v, "col", cols, s) for s in range(1, cols)], 0)
 
-    def gather_rows(v):
-        near = gather_near(v)
-        return near, core_swap(near, rows)
-
-    def dot(a, b):
-        return jnp.dot(a, b, preferred_element_type=jnp.float32)
-
-    near, far = mirror(
+    def plane_gather(v):
+        return jnp.concatenate([v] + [chip_swap(v, rows, s) for s in range(1, chips)], 0)
+
+    def from_other_core(v):
+        blocks = core_swap(v, rows).reshape(-1, 2, local_rows, half)
+        return jnp.stack([blocks[:, 1], blocks[:, 0]], 1).reshape(v.shape)
+
+    mirrored = mirror(
         key, hblocks.reshape(row_blocks * slots, BS * BS), onsite, rows, row_blocks
     )
 
     direct = direct_rows(col[None], by_owner, places, pieces, rows, slots)
-    far, direct = lax.optimization_barrier((far, direct))
-    far = core_swap(far, rows)
+    mirrored, direct = lax.optimization_barrier((mirrored, direct))
+    mirrored_other = core_swap(mirrored, rows)
     direct = [chip_swap(direct[s], rows, s) if s else direct[s] for s in range(chips)]
-    first, far = lax.optimization_barrier((orbitals_in.astype(jnp.bfloat16), far))
-    first_gathered = gather_rows(first)
-    tile = jnp.concatenate([near, far], 1) + jnp.concatenate(direct, 0)
-    tile_near, tile_far = tile[:, :near_rows], tile[:, near_rows:]
+    first, mirrored_other = lax.optimization_barrier(
+        (start.astype(jnp.bfloat16), mirrored_other)
+    )
+    first_gathered, direct = lax.optimization_barrier((gather(first), direct))
+    direct_other = [core_swap(rows_of_chip, rows) for rows_of_chip in direct]
+
+    tile = assemble(mirrored, mirrored_other, direct, direct_other)
 
     def partial_product(gathered):
-        near, far = gathered
-        first, far = lax.optimization_barrier((dot(tile_near, near), far))
-        return first + dot(tile_far, far)
+        return jnp.dot(tile, gathered, preferred_element_type=jnp.float32)
 
     def apply(gathered):
-        terms = partial_product(gathered).reshape(chips, local_rows, k)
+        terms = partial_product(gathered).reshape(chips, 2 * local_rows, half)
         total = terms[0]
         for s in range(1, chips):
             total = total + chip_swap(terms[s], rows, s)
@@ -351,47 +392,42 @@
 
     centre = 0.5 * (top_bound[0] + cut_low[0])
     halfwidth = 0.5 * (top_bound[0] - cut_low[0])
-    previous = orbitals_in
-    current = (apply(first_gathered) - centre * orbitals_in) / halfwidth
+    previous = start
+    current = (apply(first_gathered) - centre * start) / halfwidth
     for degree in range(DEG - 1):
-        gathered = gather_rows(current.astype(jnp.bfloat16))
+        gathered = gather(current.astype(jnp.bfloat16))
         following = 2.0 * (apply(gathered) - centre * current) / halfwidth - previous
         previous, current = (current, following)
 
     rounded = current.astype(jnp.bfloat16)
-    plane_rows = jnp.concatenate(
-        [rounded] + [chip_swap(rounded, rows, s) for s in range(1, chips)], 0
-    )
-    near, plane_rows = lax.optimization_barrier((gather_near(rounded), plane_rows))
-    gathered = near, core_swap(near, rows)
+    plane_rows = plane_gather(rounded)
+    gathered, plane_rows = lax.optimization_barrier((gather(rounded), plane_rows))
+    gathered_other = from_other_core(gathered)
+    plane_other = from_other_core(plane_rows)
+    filtered = joined(current[:local_rows], core_swap(current[local_rows:], rows), 1)
     contract = (((0,), (0,)), ((), ()))
-    gram_part = lax.dot_general(
-        gathered[0], gathered[0], contract, preferred_element_type=jnp.float32
-    ) / cols
-    cross_part = lax.dot_general(
-        plane_rows.astype(jnp.float32), partial_product(gathered), contract, precision=HI
-    )
-
-    share = k // rows
-    cross_part = cross_part + cross_part.T
-    ids = jnp.arange(k, dtype=jnp.int32)
-    packed = jnp.where(ids[:, None] <= ids[None, :], gram_part, cross_part)
-    diagonal = jnp.sum(jnp.where(ids[:, None] == ids[None, :], cross_part, 0.0), 0)
-    diagonal = jnp.broadcast_to(diagonal, (rows, 8, k))
-    total = jnp.concatenate([packed.reshape(rows, share, k), diagonal], 1)
-    total = total.reshape(chips, 2, share + 8, k)
-    kept = jnp.where(core == 0, total[:, 0], total[:, 1])
-    total = kept + core_swap(jnp.where(core == 0, total[:, 1], total[:, 0]), rows)
-    total = by_distance(total, chip)
-    total = sum([chip_swap(total[s], rows, s) for s in range(1, chips)], total[0])
-    total = sum([shifted(total, "col", cols, s) for s in range(1, cols)], total)
+
+    def gram_rows(g):
+        return lax.dot_general(g, gathered, contract, preferred_element_type=jnp.float32)
+
+    image = partial_product(gathered)
+
+    def cross_rows(g):
+        return lax.dot_general(g.astype(jnp.float32), image, contract, precision=HI)
+
+    gram_part = jnp.concatenate([gram_rows(gathered), gram_rows(gathered_other)], 0)
+    cross_part = jnp.concatenate([cross_rows(plane_rows), cross_rows(plane_other)], 0)
+    share = k // chips
+    parts = [x.reshape(chips, share, half) for x in (gram_part, cross_part)]
+    parts = by_distance(jnp.stack(parts, 1), chip)
+    total = sum([chip_swap(parts[s], rows, s) for s in range(1, chips)], parts[0])
+    cross_share = sum([shifted(total[1], "col", cols, s) for s in range(1, cols)], total[1])
+    total = jnp.stack([total[0], cross_share])
     total = jnp.stack([total] + [chip_swap(total, rows, s) for s in range(1, chips)])
-    total = by_distance(total, chip)
-    other = core_swap(total, rows)
-    pair = (jnp.where(core == 0, total, other), jnp.where(core == 0, other, total))
-    total = jnp.stack(pair, 1).reshape(rows, share + 8, k)
-    packed = total[:, :share].reshape(k, k)
-    return finish(packed, total[0, share : share + 1], current, total_rows)
+    total = by_distance(total, chip).swapaxes(0, 1).reshape(2, k, half)
+    total = joined(total[:, :half], total[:, half:], 1)
+    total = joined(total, core_swap(total, rows), 2)
+    return finish(total[0], total[1], filtered, total_rows)
 
 
 def solution(mesh):

time: 136 us -> 136 us (level)
  waiting for transfers between devices: 53 us -> 46.6 us
  starting transfers between devices: 56.4 us -> 60.2 us
    ppermute x28 -> x31, waiting for transfers between devices: 33 us -> 28 us  [exchanged(): return lax.ppermute(x, axis, [(i, i ^ apart) for i in range(size)])]
    ppermute x28 -> x31, starting transfers between devices: 25.3 us -> 27.7 us  [exchanged(): return lax.ppermute(x, axis, [(i, i ^ apart) for i in range(size)])]
    ppermute x18, waiting for transfers between devices: 20 us -> 18.7 us  [shifted(): return lax.ppermute(x, axis, [(i, (i + step) % size) for i in range(size)])]
    ppermute x18, starting transfers between devices: 31.1 us -> 32.5 us  [shifted(): return lax.ppermute(x, axis, [(i, (i + step) % size) for i in range(size)])]
    dot_general x10 -> x8, matrix products: 3.13 us -> 4.24 us  [the longest x4 2.82 us: partial_product(): return jnp.dot(tile, gathered, preferred_element_type=jnp.float32)]
    pallas_call x1 -> x2, Pallas kernels: 2.27 us -> 2.87 us  [the longest x1 2.26 us: mirror(): pl.pallas_call(mirror_kernel, out_shape=jax.ShapeDtypeStruct(shape, jnp.b...]
  transfers between devices with their start and end apart: 46 -> 49, of which waited for: 36 -> 34; matrix products, arithmetic and copies ran while one was open for 1% -> 2% of each run, Pallas kernels for 2% -> 3%
where the time goes in v2:
time: 136 us; the launch traced here: 135 us
  starting transfers between devices  60.2 us (44%)
  waiting for transfers between devices  46.6 us (34%)
  Pallas kernels  16.5 us (12%)
  matrix products  4.24 us (3%)
  local copies, waits for them, and re-layouts  2.8 us (2%)
  between operations  2.45 us (2%)
  other arithmetic  2.38 us (2%)
    ppermute x18, starting transfers between devices, shifted(): return lax.ppermute(x, axis, [(i, (i + step) % size) for i in range(size)])  32.5 us
    ppermute x31, waiting for transfers between devices, exchanged(): return lax.ppermute(x, axis, [(i, i ^ apart) for i in range(size)])  28 us
    ppermute x31, starting transfers between devices, exchanged(): return lax.ppermute(x, axis, [(i, i ^ apart) for i in range(size)])  27.7 us
    ppermute x18, waiting for transfers between devices, shifted(): return lax.ppermute(x, axis, [(i, (i + step) % size) for i in range(size)])  18.7 us
    pallas_call x1, Pallas kernels, finish(): pl.pallas_call(functools.partial(finish_kernel, total_rows), out_shape=(j...  8.78 us
    pallas_call x1, Pallas kernels, direct_rows(): pl.pallas_call(functools.partial(direct_kernel, rows, slots), out_shape=(...  3.08 us
    dot_general x4, matrix products, partial_product(): return jnp.dot(tile, gathered, preferred_element_type=jnp.float32)  2.82 us
  transfers between devices with their start and end apart: 49, of which 34 were waited for; matrix products, arithmetic and copies ran while one was open for 2% of the time, Pallas kernels for 3%

profile of v2, /device:TPU:0, one launch (start us, length us, event | category | flops | bytes accessed | tf_op | source)
XLA Modules:
  0.0 135.3 jit_solution(1454651508746282118)
XLA Ops:
  3.7 1.8 %pack.1 = (bf16[16,4224]{1,0:T(8,128)(2,1)}, bf16[16,4224]{1,0:T(8,128)(2,1)}, bf16[16,4224]{1,0:T(8,128)(2,1)}) custom-call(s32[1]{0:T(128)} %bitcast.1.col_ref, bf16[4,16,4096]{2,1,0:T(8,128)(2,1)} %bitcast.85, f32[4,16]{1,0:T(4,128)} %reshape.221.places_ref), custom_call_target="tpu_custom_call" | custom-call | tf_op jit(solution)/shard_map/pack/pallas_call | solution.py:174
  5.5 2.7 %collective-permute-start.1 = (bf16[16,4224]{1,0:T(8,128)(2,1)}, bf16[16,4224]{1,0:T(8,128)(2,1)S(1)}, u32[]{:S(2)}, u32[]{:S(2)}) collective-permute-start(bf16[16,4224]{1,0:T(8,128)(2,1)} %get-tuple-element.32), channel_id=1, source_target_pairs={{0,1},{1,2},{2,3},{3,0},{4,5},{5,6},{6,7},{7,4},{8,9},{9,10},{10,1... | collective-permute-start | bytes 405512 | tf_op jit(solution)/shard_map/ppermute | solution.py:134
  8.2 2.6 %collective-permute-start.2 = (bf16[16,4224]{1,0:T(8,128)(2,1)}, bf16[16,4224]{1,0:T(8,128)(2,1)S(1)}, u32[]{:S(2)}, u32[]{:S(2)}) collective-permute-start(bf16[16,4224]{1,0:T(8,128)(2,1)} %get-tuple-element.33), channel_id=1, source_target_pairs={{0,2},{1,3},{2,0},{3,1},{4,6},{5,7},{6,4},{7,5},{8,10},{9,11},{10,... | collective-permute-start | bytes 405512 | tf_op jit(solution)/shard_map/ppermute | solution.py:134
  10.7 1.3 collective-permute-start.3
  13.9 2.3 %mirror.1.mirrored = bf16[2,512,512]{2,1,0:T(8,128)(2,1)S(1)} custom-call(s32[1,64]{1,0:T(1,128)S(1)} %reshape.219.key_ref, bf16[64,4096]{1,0:T(8,128)(2,1)S(1)} %bitcast.86, bf16[2,4096]{1,0:T(2,128)(2,1)S(1)} %copy-done.3), custom_call_target="tpu_custom_call" | custom-call | flops 67108864 | bytes 786432 | tf_op jit(solution)/shard_map/mirror/pallas_call | solution.py:214
  16.1 4.3 %collective-permute-done.2.refs_1_ = bf16[16,4224]{1,0:T(8,128)(2,1)S(1)} collective-permute-done((bf16[16,4224]{1,0:T(8,128)(2,1)}, bf16[16,4224]{1,0:T(8,128)(2,1)S(1)}, u32[]{:S(2)}, u32[]{:S(2)}) %collective-permute-start.2) | collective-permute-done | bytes 135200 | tf_op jit(solution)/shard_map/ppermute | solution.py:134
  20.5 3.1 %direct_rows.1 = (bf16[128,1024]{1,0:T(8,128)(2,1)S(1)}, bf16[128,1024]{1,0:T(8,128)(2,1)S(1)}, bf16[128,1024]{1,0:T(8,128)(2,1)S(1)}, bf16[128,1024]{1,0:T(8,128)(2,1)S(1)}) custom-call(s32[1]{0:T(128)} %bitcast.1.col_ref, bf16[4,16,4096]{2,1,0:T(8,128)(2,1)S(1)} %bitcast.87, f32[4,16]{1,0:T(4,128)S(1)} %copy-done.2, ...), custom_call_target="tpu_custom_call" | custom-call | tf_op jit(solution)/shard_map/direct_rows/pallas_call | solution.py:266
  23.7 2.5 %collective-permute-start.10 = (bf16[128,1024]{1,0:T(8,128)(2,1)S(1)}, bf16[128,1024]{1,0:T(8,128)(2,1)S(1)}, u32[]{:S(2)}, u32[]{:S(2)}) collective-permute-start(bf16[128,1024]{1,0:T(8,128)(2,1)S(1)} %get-tuple-element.46), channel_id=1, source_target_pairs={{0,24},{4,28},{8,16},{12,20},{16,8},{20,12},{24,0},{28,4},{1,25},{... | collective-permute-start | bytes 786440 | tf_op jit(solution)/shard_map/ppermute | solution.py:130
  27.2 3.4 %collective-permute-start.5 = (bf16[256,128]{1,0:T(8,128)(2,1)S(1)}, bf16[256,128]{1,0:T(8,128)(2,1)S(1)}, u32[]{:S(2)}, u32[]{:S(2)}) collective-permute-start(bf16[256,128]{1,0:T(8,128)(2,1)S(1)} %convert_element_type.18), channel_id=1, source_target_pairs={{0,1},{1,2},{2,3},{3,0},{4,5},{5,6},{6,7},{7,4},{8,9},{9,10},{10,1... | collective-permute-start | bytes 196616 | tf_op jit(solution)/shard_map/ppermute | solution.py:134
  30.7 1.6 %collective-permute-start.6 = (bf16[256,128]{1,0:T(8,128)(2,1)S(1)}, bf16[256,128]{1,0:T(8,128)(2,1)S(1)}, u32[]{:S(2)}, u32[]{:S(2)}) collective-permute-start(bf16[256,128]{1,0:T(8,128)(2,1)S(1)} %convert_element_type.18), channel_id=1, source_target_pairs={{0,2},{1,3},{2,0},{3,1},{4,6},{5,7},{6,4},{7,5},{8,10},{9,11},{10,... | collective-permute-start | bytes 196616 | tf_op jit(solution)/shard_map/ppermute | solution.py:134
  32.3 2.5 %collective-permute-done.5 = bf16[256,128]{1,0:T(8,128)(2,1)S(1)} collective-permute-done((bf16[256,128]{1,0:T(8,128)(2,1)S(1)}, bf16[256,128]{1,0:T(8,128)(2,1)S(1)}, u32[]{:S(2)}, u32[]{:S(2)}) %collective-permute-start.5) | collective-permute-done | bytes 65568 | tf_op jit(solution)/shard_map/ppermute | solution.py:134
  34.8 1.9 %collective-permute-start.7 = (bf16[256,128]{1,0:T(8,128)(2,1)S(1)}, bf16[256,128]{1,0:T(8,128)(2,1)S(1)}, u32[]{:S(2)}, u32[]{:S(2)}) collective-permute-start(bf16[256,128]{1,0:T(8,128)(2,1)S(1)} %convert_element_type.18), channel_id=1, source_target_pairs={{0,3},{1,0},{2,1},{3,2},{4,7},{5,4},{6,5},{7,6},{8,11},{9,8},{10,9... | collective-permute-start | bytes 196616 | tf_op jit(solution)/shard_map/ppermute | solution.py:134
  36.9 2.1 %collective-permute-done.7 = bf16[256,128]{1,0:T(8,128)(2,1)S(1)} collective-permute-done((bf16[256,128]{1,0:T(8,128)(2,1)S(1)}, bf16[256,128]{1,0:T(8,128)(2,1)S(1)}, u32[]{:S(2)}, u32[]{:S(2)}) %collective-permute-start.7) | collective-permute-done | bytes 65568 | tf_op jit(solution)/shard_map/ppermute | solution.py:134
  43.2 1.6 %collective-permute-start.15 = (f32[256,128]{1,0:T(8,128)S(1)}, f32[256,128]{1,0:T(8,128)S(1)}, u32[]{:S(2)}, u32[]{:S(2)}) collective-permute-start(f32[256,128]{1,0:T(8,128)S(1)} %get-tuple-element.70), channel_id=1, source_target_pairs={{0,8},{4,12},{8,0},{12,4},{16,24},{20,28},{24,16},{28,20},{1,9},{5... | collective-permute-start | bytes 393224 | tf_op jit(solution)/shard_map/ppermute | solution.py:130
  44.8 1.5 %collective-permute-start.16 = (f32[256,128]{1,0:T(8,128)S(1)}, f32[256,128]{1,0:T(8,128)S(1)}, u32[]{:S(2)}, u32[]{:S(2)}) collective-permute-start(f32[256,128]{1,0:T(8,128)S(1)} %get-tuple-element.72), channel_id=1, source_target_pairs={{0,16},{4,20},{8,24},{12,28},{16,0},{20,4},{24,8},{28,12},{1,17},{... | collective-permute-start | bytes 393224 | tf_op jit(solution)/shard_map/ppermute | solution.py:130
  49.1 3.7 %collective-permute-done.16 = f32[256,128]{1,0:T(8,128)S(1)} collective-permute-done((f32[256,128]{1,0:T(8,128)S(1)}, f32[256,128]{1,0:T(8,128)S(1)}, u32[]{:S(2)}, u32[]{:S(2)}) %collective-permute-start.16) | collective-permute-done | bytes 131104 | tf_op jit(solution)/shard_map/ppermute | solution.py:130
  52.9 3.3 %collective-permute-start.18 = (bf16[256,128]{1,0:T(8,128)(2,1)S(1)}, bf16[256,128]{1,0:T(8,128)(2,1)S(1)}, u32[]{:S(2)}, u32[]{:S(2)}) collective-permute-start(bf16[256,128]{1,0:T(8,128)(2,1)S(1)} %get-tuple-element.60), channel_id=1, source_target_pairs={{0,1},{1,2},{2,3},{3,0},{4,5},{5,6},{6,7},{7,4},{8,9},{9,10},{10,1... | collective-permute-start | bytes 196616 | tf_op jit(solution)/shard_map/ppermute | solution.py:134
  56.1 1.6 %collective-permute-start.19 = (bf16[256,128]{1,0:T(8,128)(2,1)S(1)}, bf16[256,128]{1,0:T(8,128)(2,1)S(1)}, u32[]{:S(2)}, u32[]{:S(2)}) collective-permute-start(bf16[256,128]{1,0:T(8,128)(2,1)S(1)} %get-tuple-element.60), channel_id=1, source_target_pairs={{0,2},{1,3},{2,0},{3,1},{4,6},{5,7},{6,4},{7,5},{8,10},{9,11},{10,... | collective-permute-start | bytes 196616 | tf_op jit(solution)/shard_map/ppermute | solution.py:134
  58.6 1.2 collective-permute-done.18
  59.7 2.5 %collective-permute-done.19 = bf16[256,128]{1,0:T(8,128)(2,1)S(1)} collective-permute-done((bf16[256,128]{1,0:T(8,128)(2,1)S(1)}, bf16[256,128]{1,0:T(8,128)(2,1)S(1)}, u32[]{:S(2)}, u32[]{:S(2)}) %collective-permute-start.19) | collective-permute-done | bytes 65568 | tf_op jit(solution)/shard_map/ppermute | solution.py:134
  63.3 1.3 collective-permute-start.21
  65.4 1.5 %collective-permute-start.23 = (f32[256,128]{1,0:T(8,128)S(1)}, f32[256,128]{1,0:T(8,128)S(1)}, u32[]{:S(2)}, u32[]{:S(2)}) collective-permute-start(f32[256,128]{1,0:T(8,128)S(1)} %get-tuple-element.68), channel_id=1, source_target_pairs={{0,24},{4,28},{8,16},{12,20},{16,8},{20,12},{24,0},{28,4},{1,25},{... | collective-permute-start | bytes 393224 | tf_op jit(solution)/shard_map/ppermute | solution.py:130
  66.8 2.8 %collective-permute-done.21 = f32[256,128]{1,0:T(8,128)S(1)} collective-permute-done((f32[256,128]{1,0:T(8,128)S(1)}, f32[256,128]{1,0:T(8,128)S(1)}, u32[]{:S(2)}, u32[]{:S(2)}) %collective-permute-start.21) | collective-permute-done | bytes 131104 | tf_op jit(solution)/shard_map/ppermute | solution.py:130
  69.7 1.9 %collective-permute-done.22 = f32[256,128]{1,0:T(8,128)S(1)} collective-permute-done((f32[256,128]{1,0:T(8,128)S(1)}, f32[256,128]{1,0:T(8,128)S(1)}, u32[]{:S(2)}, u32[]{:S(2)}) %collective-permute-start.22) | collective-permute-done | bytes 131104 | tf_op jit(solution)/shard_map/ppermute | solution.py:130
  71.6 1.9 %collective-permute-start.24 = (bf16[256,128]{1,0:T(8,128)(2,1)S(1)}, bf16[256,128]{1,0:T(8,128)(2,1)S(1)}, u32[]{:S(2)}, u32[]{:S(2)}) collective-permute-start(bf16[256,128]{1,0:T(8,128)(2,1)S(1)} %get-tuple-element.58), channel_id=1, source_target_pairs={{0,1},{1,2},{2,3},{3,0},{4,5},{5,6},{6,7},{7,4},{8,9},{9,10},{10,1... | collective-permute-start | bytes 196616 | tf_op jit(solution)/shard_map/ppermute | solution.py:134
  74.1 1.8 %collective-permute-start.26 = (bf16[256,128]{1,0:T(8,128)(2,1)S(1)}, bf16[256,128]{1,0:T(8,128)(2,1)S(1)}, u32[]{:S(2)}, u32[]{:S(2)}) collective-permute-start(bf16[256,128]{1,0:T(8,128)(2,1)S(1)} %get-tuple-element.58), channel_id=1, source_target_pairs={{0,3},{1,0},{2,1},{3,2},{4,7},{5,4},{6,5},{7,6},{8,11},{9,8},{10,9... | collective-permute-start | bytes 196616 | tf_op jit(solution)/shard_map/ppermute | solution.py:134
  75.9 1.8 %collective-permute-done.24 = bf16[256,128]{1,0:T(8,128)(2,1)S(1)} collective-permute-done((bf16[256,128]{1,0:T(8,128)(2,1)S(1)}, bf16[256,128]{1,0:T(8,128)(2,1)S(1)}, u32[]{:S(2)}, u32[]{:S(2)}) %collective-permute-start.24) | collective-permute-done | bytes 65568 | tf_op jit(solution)/shard_map/ppermute | solution.py:134
  77.7 1.4 %collective-permute-done.25 = bf16[256,128]{1,0:T(8,128)(2,1)S(1)} collective-permute-done((bf16[256,128]{1,0:T(8,128)(2,1)S(1)}, bf16[256,128]{1,0:T(8,128)(2,1)S(1)}, u32[]{:S(2)}, u32[]{:S(2)}) %collective-permute-start.25) | collective-permute-done | bytes 65568 | tf_op jit(solution)/shard_map/ppermute | solution.py:134
  79.8 1.3 collective-permute-start.27
  81.8 1.6 %collective-permute-start.29 = (f32[256,128]{1,0:T(8,128)S(1)}, f32[256,128]{1,0:T(8,128)S(1)}, u32[]{:S(2)}, u32[]{:S(2)}) collective-permute-start(f32[256,128]{1,0:T(8,128)S(1)} %get-tuple-element.65), channel_id=1, source_target_pairs={{0,24},{4,28},{8,16},{12,20},{16,8},{20,12},{24,0},{28,4},{1,25},{... | collective-permute-start | bytes 393224 | tf_op jit(solution)/shard_map/ppermute | solution.py:130
  83.4 1.5 %collective-permute-done.27 = f32[256,128]{1,0:T(8,128)S(1)} collective-permute-done((f32[256,128]{1,0:T(8,128)S(1)}, f32[256,128]{1,0:T(8,128)S(1)}, u32[]{:S(2)}, u32[]{:S(2)}) %collective-permute-start.27) | collective-permute-done | bytes 131104 | tf_op jit(solution)/shard_map/ppermute | solution.py:130
  84.9 1.2 collective-permute-done.28
  86.1 1.6 %collective-permute-done.29 = f32[256,128]{1,0:T(8,128)S(1)} collective-permute-done((f32[256,128]{1,0:T(8,128)S(1)}, f32[256,128]{1,0:T(8,128)S(1)}, u32[]{:S(2)}, u32[]{:S(2)}) %collective-permute-start.29) | collective-permute-done | bytes 131104 | tf_op jit(solution)/shard_map/ppermute | solution.py:130
  87.7 1.2 collective-permute-start.30
  88.9 2.1 %collective-permute-start.31 = (bf16[256,128]{1,0:T(8,128)(2,1)S(1)}, bf16[256,128]{1,0:T(8,128)(2,1)S(1)}, u32[]{:S(2)}, u32[]{:S(2)}) collective-permute-start(bf16[256,128]{1,0:T(8,128)(2,1)S(1)} %get-tuple-element.56), channel_id=1, source_target_pairs={{0,2},{1,3},{2,0},{3,1},{4,6},{5,7},{6,4},{7,5},{8,10},{9,11},{10,... | collective-permute-start | bytes 196616 | tf_op jit(solution)/shard_map/ppermute | solution.py:134
  92.1 1.2 collective-permute-start.33
  94.4 1.2 collective-permute-start.35
  96.4 1.2 collective-permute-done.34
  97.6 2.0 %collective-permute-done.35 = bf16[256,128]{1,0:T(8,128)(2,1)S(1)} collective-permute-done((bf16[256,128]{1,0:T(8,128)(2,1)S(1)}, bf16[256,128]{1,0:T(8,128)(2,1)S(1)}, u32[]{:S(2)}, u32[]{:S(2)}) %collective-permute-start.35) | collective-permute-done | bytes 65568 | tf_op jit(solution)/shard_map/ppermute | solution.py:130
  105.0 1.8 %collective-permute-start.40 = (f32[2,64,128]{2,1,0:T(8,128)S(1)}, f32[2,64,128]{2,1,0:T(8,128)S(1)}, u32[]{:S(2)}, u32[]{:S(2)}) collective-permute-start(f32[2,64,128]{2,1,0:T(8,128)S(1)} %get-tuple-element.80), channel_id=1, source_target_pairs={{0,24},{4,28},{8,16},{12,20},{16,8},{20,12},{24,0},{28,4},{1,25},{... | collective-permute-start | bytes 196616 | tf_op jit(solution)/shard_map/ppermute | solution.py:130
  107.7 1.6 %collective-permute-done.39 = f32[2,64,128]{2,1,0:T(8,128)S(1)} collective-permute-done((f32[2,64,128]{2,1,0:T(8,128)S(1)}, f32[2,64,128]{2,1,0:T(8,128)S(1)}, u32[]{:S(2)}, u32[]{:S(2)}) %collective-permute-start.39) | collective-permute-done | bytes 65568 | tf_op jit(solution)/shard_map/ppermute | solution.py:130
  112.1 2.7 %collective-permute-start.43 = (f32[64,128]{1,0:T(8,128)S(1)}, f32[64,128]{1,0:T(8,128)S(1)}, u32[]{:S(2)}, u32[]{:S(2)}) collective-permute-start(f32[64,128]{1,0:T(8,128)S(1)} %get-tuple-element.95), channel_id=1, source_target_pairs={{0,3},{1,0},{2,1},{3,2},{4,7},{5,4},{6,5},{7,6},{8,11},{9,8},{10,9... | collective-permute-start | bytes 98312 | tf_op jit(solution)/shard_map/ppermute | solution.py:134
  114.7 1.3 collective-permute-done.41
  116.7 1.3 collective-permute-start.44
  118.0 1.2 collective-permute-start.45
  121.1 1.2 collective-permute-done.45
  122.3 2.1 %collective-permute-done.46 = f32[2,64,128]{2,1,0:T(8,128)S(1)} collective-permute-done((f32[2,64,128]{2,1,0:T(8,128)S(1)}, f32[2,64,128]{2,1,0:T(8,128)S(1)}, u32[]{:S(2)}, u32[]{:S(2)}) %collective-permute-start.46) | collective-permute-done | bytes 65568 | tf_op jit(solution)/shard_map/ppermute | solution.py:130
  126.5 8.8 %finish.1 = (f32[128,256]{1,0:T(8,128)}, f32[256,256]{1,0:T(8,128)}) custom-call(f32[256,256]{1,0:T(8,128)S(1)} %get-tuple-element.63.gram_ref, f32[256,256]{1,0:T(8,128)S(1)} %get-tuple-element.62.cross_ref, f32[128,256]{1,0:T(8,128)S(1)} %maximum_select_fusion.4.y_ref), custom_call_target="tpu_custom_call" | custom-call | tf_op jit(solution)/shard_map/finish/pallas_call | solution.py:118
  (117 shorter events, 33.0 us)
Async XLA Ops:
  1.6 3.9 %collective-permute-start = (f32[128,128]{1,0:T(8,128)S(1)}, f32[128,128]{1,0:T(8,128)S(1)}, u32[]{:S(2)}, u32[]{:S(2)}) collective-permute-start(f32[128,128]{1,0:T(8,128)S(1)} %get-tuple-element.91), channel_id=1, source_target_pairs={{0,4},{4,0},{8,12},{12,8},{16,20},{20,16},{24,28},{28,24},{1,5},{5... | collective-permute-start | bytes 196616 | tf_op jit(solution)/shard_map/ppermute | solution.py:130
  5.5 10.6 %collective-permute-start.1 = (bf16[16,4224]{1,0:T(8,128)(2,1)}, bf16[16,4224]{1,0:T(8,128)(2,1)S(1)}, u32[]{:S(2)}, u32[]{:S(2)}) collective-permute-start(bf16[16,4224]{1,0:T(8,128)(2,1)} %get-tuple-element.32), channel_id=1, source_target_pairs={{0,1},{1,2},{2,3},{3,0},{4,5},{5,6},{6,7},{7,4},{8,9},{9,10},{10,1... | collective-permute-start | bytes 405512 | tf_op jit(solution)/shard_map/ppermute | solution.py:134
  8.2 12.3 %collective-permute-start.2 = (bf16[16,4224]{1,0:T(8,128)(2,1)}, bf16[16,4224]{1,0:T(8,128)(2,1)S(1)}, u32[]{:S(2)}, u32[]{:S(2)}) collective-permute-start(bf16[16,4224]{1,0:T(8,128)(2,1)} %get-tuple-element.33), channel_id=1, source_target_pairs={{0,2},{1,3},{2,0},{3,1},{4,6},{5,7},{6,4},{7,5},{8,10},{9,11},{10,... | collective-permute-start | bytes 405512 | tf_op jit(solution)/shard_map/ppermute | solution.py:134
  10.7 9.7 %collective-permute-start.3 = (bf16[16,4224]{1,0:T(8,128)(2,1)}, bf16[16,4224]{1,0:T(8,128)(2,1)S(1)}, u32[]{:S(2)}, u32[]{:S(2)}) collective-permute-start(bf16[16,4224]{1,0:T(8,128)(2,1)} %get-tuple-element.34), channel_id=1, source_target_pairs={{0,3},{1,0},{2,1},{3,2},{4,7},{5,4},{6,5},{7,6},{8,11},{9,8},{10,9... | collective-permute-start | bytes 405512 | tf_op jit(solution)/shard_map/ppermute | solution.py:134
  23.6 3.6 %collective-permute-start.4 = (bf16[2,512,512]{2,1,0:T(8,128)(2,1)S(1)}, bf16[2,512,512]{2,1,0:T(8,128)(2,1)S(1)}, u32[]{:S(2)}, u32[]{:S(2)}) collective-permute-start(bf16[2,512,512]{2,1,0:T(8,128)(2,1)S(1)} %mirror.1.mirrored), channel_id=1, source_target_pairs={{0,4},{4,0},{8,12},{12,8},{16,20},{20,16},{24,28},{28,24},{1,5},{5... | collective-permute-start | bytes 3145736 | tf_op jit(solution)/shard_map/ppermute | solution.py:130
  23.7 15.4 %collective-permute-start.10 = (bf16[128,1024]{1,0:T(8,128)(2,1)S(1)}, bf16[128,1024]{1,0:T(8,128)(2,1)S(1)}, u32[]{:S(2)}, u32[]{:S(2)}) collective-permute-start(bf16[128,1024]{1,0:T(8,128)(2,1)S(1)} %get-tuple-element.46), channel_id=1, source_target_pairs={{0,24},{4,28},{8,16},{12,20},{16,8},{20,12},{24,0},{28,4},{1,25},{... | collective-permute-start | bytes 786440 | tf_op jit(solution)/shard_map/ppermute | solution.py:130
  26.2 12.9 %collective-permute-start.8 = (bf16[128,1024]{1,0:T(8,128)(2,1)S(1)}, bf16[128,1024]{1,0:T(8,128)(2,1)S(1)}, u32[]{:S(2)}, u32[]{:S(2)}) collective-permute-start(bf16[128,1024]{1,0:T(8,128)(2,1)S(1)} %get-tuple-element.44), channel_id=1, source_target_pairs={{0,8},{4,12},{8,0},{12,4},{16,24},{20,28},{24,16},{28,20},{1,9},{5... | collective-permute-start | bytes 786440 | tf_op jit(solution)/shard_map/ppermute | solution.py:130
  26.7 12.4 %collective-permute-start.9 = (bf16[128,1024]{1,0:T(8,128)(2,1)S(1)}, bf16[128,1024]{1,0:T(8,128)(2,1)S(1)}, u32[]{:S(2)}, u32[]{:S(2)}) collective-permute-start(bf16[128,1024]{1,0:T(8,128)(2,1)S(1)} %get-tuple-element.45), channel_id=1, source_target_pairs={{0,16},{4,20},{8,24},{12,28},{16,0},{20,4},{24,8},{28,12},{1,17},{... | collective-permute-start | bytes 786440 | tf_op jit(solution)/shard_map/ppermute | solution.py:130
  27.2 7.6 %collective-permute-start.5 = (bf16[256,128]{1,0:T(8,128)(2,1)S(1)}, bf16[256,128]{1,0:T(8,128)(2,1)S(1)}, u32[]{:S(2)}, u32[]{:S(2)}) collective-permute-start(bf16[256,128]{1,0:T(8,128)(2,1)S(1)} %convert_element_type.18), channel_id=1, source_target_pairs={{0,1},{1,2},{2,3},{3,0},{4,5},{5,6},{6,7},{7,4},{8,9},{9,10},{10,1... | collective-permute-start | bytes 196616 | tf_op jit(solution)/shard_map/ppermute | solution.py:134
  30.7 6.3 %collective-permute-start.6 = (bf16[256,128]{1,0:T(8,128)(2,1)S(1)}, bf16[256,128]{1,0:T(8,128)(2,1)S(1)}, u32[]{:S(2)}, u32[]{:S(2)}) collective-permute-start(bf16[256,128]{1,0:T(8,128)(2,1)S(1)} %convert_element_type.18), channel_id=1, source_target_pairs={{0,2},{1,3},{2,0},{3,1},{4,6},{5,7},{6,4},{7,5},{8,10},{9,11},{10,... | collective-permute-start | bytes 196616 | tf_op jit(solution)/shard_map/ppermute | solution.py:134
  34.8 4.3 %collective-permute-start.7 = (bf16[256,128]{1,0:T(8,128)(2,1)S(1)}, bf16[256,128]{1,0:T(8,128)(2,1)S(1)}, u32[]{:S(2)}, u32[]{:S(2)}) collective-permute-start(bf16[256,128]{1,0:T(8,128)(2,1)S(1)} %convert_element_type.18), channel_id=1, source_target_pairs={{0,3},{1,0},{2,1},{3,2},{4,7},{5,4},{6,5},{7,6},{8,11},{9,8},{10,9... | collective-permute-start | bytes 196616 | tf_op jit(solution)/shard_map/ppermute | solution.py:134
  39.1 1.6 %collective-permute-start.11 = (bf16[128,1024]{1,0:T(8,128)(2,1)S(1)}, bf16[128,1024]{1,0:T(8,128)(2,1)S(1)}, u32[]{:S(2)}, u32[]{:S(2)}) collective-permute-start(bf16[128,1024]{1,0:T(8,128)(2,1)S(1)} %get-tuple-element.47.refs_0_), channel_id=1, source_target_pairs={{0,4},{4,0},{8,12},{12,8},{16,20},{20,16},{24,28},{28,24},{1,5},{5... | collective-permute-start | bytes 786440 | tf_op jit(solution)/shard_map/ppermute | solution.py:130
  39.2 1.9 %collective-permute-start.12 = (bf16[128,1024]{1,0:T(8,128)(2,1)S(1)}, bf16[128,1024]{1,0:T(8,128)(2,1)S(1)}, u32[]{:S(2)}, u32[]{:S(2)}) collective-permute-start(bf16[128,1024]{1,0:T(8,128)(2,1)S(1)} %collective-permute-done.8.refs_1_), channel_id=1, source_target_pairs={{0,4},{4,0},{8,12},{12,8},{16,20},{20,16},{24,28},{28,24},{1,5},{5... | collective-permute-start | bytes 786440 | tf_op jit(solution)/shard_map/ppermute | solution.py:130
  39.7 1.8 %collective-permute-start.13 = (bf16[128,1024]{1,0:T(8,128)(2,1)S(1)}, bf16[128,1024]{1,0:T(8,128)(2,1)S(1)}, u32[]{:S(2)}, u32[]{:S(2)}) collective-permute-start(bf16[128,1024]{1,0:T(8,128)(2,1)S(1)} %collective-permute-done.9.refs_2_), channel_id=1, source_target_pairs={{0,4},{4,0},{8,12},{12,8},{16,20},{20,16},{24,28},{28,24},{1,5},{5... | collective-permute-start | bytes 786440 | tf_op jit(solution)/shard_map/ppermute | solution.py:130
  39.8 2.1 %collective-permute-start.14 = (bf16[128,1024]{1,0:T(8,128)(2,1)S(1)}, bf16[128,1024]{1,0:T(8,128)(2,1)S(1)}, u32[]{:S(2)}, u32[]{:S(2)}) collective-permute-start(bf16[128,1024]{1,0:T(8,128)(2,1)S(1)} %collective-permute-done.10.refs_3_), channel_id=1, source_target_pairs={{0,4},{4,0},{8,12},{12,8},{16,20},{20,16},{24,28},{28,24},{1,5},{5... | collective-permute-start | bytes 786440 | tf_op jit(solution)/shard_map/ppermute | solution.py:130
  43.2 5.9 %collective-permute-start.15 = (f32[256,128]{1,0:T(8,128)S(1)}, f32[256,128]{1,0:T(8,128)S(1)}, u32[]{:S(2)}, u32[]{:S(2)}) collective-permute-start(f32[256,128]{1,0:T(8,128)S(1)} %get-tuple-element.70), channel_id=1, source_target_pairs={{0,8},{4,12},{8,0},{12,4},{16,24},{20,28},{24,16},{28,20},{1,9},{5... | collective-permute-start | bytes 393224 | tf_op jit(solution)/shard_map/ppermute | solution.py:130
  44.8 8.1 %collective-permute-start.16 = (f32[256,128]{1,0:T(8,128)S(1)}, f32[256,128]{1,0:T(8,128)S(1)}, u32[]{:S(2)}, u32[]{:S(2)}) collective-permute-start(f32[256,128]{1,0:T(8,128)S(1)} %get-tuple-element.72), channel_id=1, source_target_pairs={{0,16},{4,20},{8,24},{12,28},{16,0},{20,4},{24,8},{28,12},{1,17},{... | collective-permute-start | bytes 393224 | tf_op jit(solution)/shard_map/ppermute | solution.py:130
  46.3 6.6 %collective-permute-start.17 = (f32[256,128]{1,0:T(8,128)S(1)}, f32[256,128]{1,0:T(8,128)S(1)}, u32[]{:S(2)}, u32[]{:S(2)}) collective-permute-start(f32[256,128]{1,0:T(8,128)S(1)} %get-tuple-element.71), channel_id=1, source_target_pairs={{0,24},{4,28},{8,16},{12,20},{16,8},{20,12},{24,0},{28,4},{1,25},{... | collective-permute-start | bytes 393224 | tf_op jit(solution)/shard_map/ppermute | solution.py:130
  52.9 6.9 %collective-permute-start.18 = (bf16[256,128]{1,0:T(8,128)(2,1)S(1)}, bf16[256,128]{1,0:T(8,128)(2,1)S(1)}, u32[]{:S(2)}, u32[]{:S(2)}) collective-permute-start(bf16[256,128]{1,0:T(8,128)(2,1)S(1)} %get-tuple-element.60), channel_id=1, source_target_pairs={{0,1},{1,2},{2,3},{3,0},{4,5},{5,6},{6,7},{7,4},{8,9},{9,10},{10,1... | collective-permute-start | bytes 196616 | tf_op jit(solution)/shard_map/ppermute | solution.py:134
  56.1 6.1 %collective-permute-start.19 = (bf16[256,128]{1,0:T(8,128)(2,1)S(1)}, bf16[256,128]{1,0:T(8,128)(2,1)S(1)}, u32[]{:S(2)}, u32[]{:S(2)}) collective-permute-start(bf16[256,128]{1,0:T(8,128)(2,1)S(1)} %get-tuple-element.60), channel_id=1, source_target_pairs={{0,2},{1,3},{2,0},{3,1},{4,6},{5,7},{6,4},{7,5},{8,10},{9,11},{10,... | collective-permute-start | bytes 196616 | tf_op jit(solution)/shard_map/ppermute | solution.py:134
  57.8 4.8 %collective-permute-start.20 = (bf16[256,128]{1,0:T(8,128)(2,1)S(1)}, bf16[256,128]{1,0:T(8,128)(2,1)S(1)}, u32[]{:S(2)}, u32[]{:S(2)}) collective-permute-start(bf16[256,128]{1,0:T(8,128)(2,1)S(1)} %get-tuple-element.60), channel_id=1, source_target_pairs={{0,3},{1,0},{2,1},{3,2},{4,7},{5,4},{6,5},{7,6},{8,11},{9,8},{10,9... | collective-permute-start | bytes 196616 | tf_op jit(solution)/shard_map/ppermute | solution.py:134
  63.3 6.4 %collective-permute-start.21 = (f32[256,128]{1,0:T(8,128)S(1)}, f32[256,128]{1,0:T(8,128)S(1)}, u32[]{:S(2)}, u32[]{:S(2)}) collective-permute-start(f32[256,128]{1,0:T(8,128)S(1)} %get-tuple-element.67), channel_id=1, source_target_pairs={{0,8},{4,12},{8,0},{12,4},{16,24},{20,28},{24,16},{28,20},{1,9},{5... | collective-permute-start | bytes 393224 | tf_op jit(solution)/shard_map/ppermute | solution.py:130
  64.6 6.9 %collective-permute-start.22 = (f32[256,128]{1,0:T(8,128)S(1)}, f32[256,128]{1,0:T(8,128)S(1)}, u32[]{:S(2)}, u32[]{:S(2)}) collective-permute-start(f32[256,128]{1,0:T(8,128)S(1)} %get-tuple-element.69), channel_id=1, source_target_pairs={{0,16},{4,20},{8,24},{12,28},{16,0},{20,4},{24,8},{28,12},{1,17},{... | collective-permute-start | bytes 393224 | tf_op jit(solution)/shard_map/ppermute | solution.py:130
  65.4 6.2 %collective-permute-start.23 = (f32[256,128]{1,0:T(8,128)S(1)}, f32[256,128]{1,0:T(8,128)S(1)}, u32[]{:S(2)}, u32[]{:S(2)}) collective-permute-start(f32[256,128]{1,0:T(8,128)S(1)} %get-tuple-element.68), channel_id=1, source_target_pairs={{0,24},{4,28},{8,16},{12,20},{16,8},{20,12},{24,0},{28,4},{1,25},{... | collective-permute-start | bytes 393224 | tf_op jit(solution)/shard_map/ppermute | solution.py:130
  71.6 6.1 %collective-permute-start.24 = (bf16[256,128]{1,0:T(8,128)(2,1)S(1)}, bf16[256,128]{1,0:T(8,128)(2,1)S(1)}, u32[]{:S(2)}, u32[]{:S(2)}) collective-permute-start(bf16[256,128]{1,0:T(8,128)(2,1)S(1)} %get-tuple-element.58), channel_id=1, source_target_pairs={{0,1},{1,2},{2,3},{3,0},{4,5},{5,6},{6,7},{7,4},{8,9},{9,10},{10,1... | collective-permute-start | bytes 196616 | tf_op jit(solution)/shard_map/ppermute | solution.py:134
  73.5 5.6 %collective-permute-start.25 = (bf16[256,128]{1,0:T(8,128)(2,1)S(1)}, bf16[256,128]{1,0:T(8,128)(2,1)S(1)}, u32[]{:S(2)}, u32[]{:S(2)}) collective-permute-start(bf16[256,128]{1,0:T(8,128)(2,1)S(1)} %get-tuple-element.58), channel_id=1, source_target_pairs={{0,2},{1,3},{2,0},{3,1},{4,6},{5,7},{6,4},{7,5},{8,10},{9,11},{10,... | collective-permute-start | bytes 196616 | tf_op jit(solution)/shard_map/ppermute | solution.py:134
  74.1 5.0 %collective-permute-start.26 = (bf16[256,128]{1,0:T(8,128)(2,1)S(1)}, bf16[256,128]{1,0:T(8,128)(2,1)S(1)}, u32[]{:S(2)}, u32[]{:S(2)}) collective-permute-start(bf16[256,128]{1,0:T(8,128)(2,1)S(1)} %get-tuple-element.58), channel_id=1, source_target_pairs={{0,3},{1,0},{2,1},{3,2},{4,7},{5,4},{6,5},{7,6},{8,11},{9,8},{10,9... | collective-permute-start | bytes 196616 | tf_op jit(solution)/shard_map/ppermute | solution.py:134
  79.8 5.0 %collective-permute-start.27 = (f32[256,128]{1,0:T(8,128)S(1)}, f32[256,128]{1,0:T(8,128)S(1)}, u32[]{:S(2)}, u32[]{:S(2)}) collective-permute-start(f32[256,128]{1,0:T(8,128)S(1)} %get-tuple-element.64), channel_id=1, source_target_pairs={{0,8},{4,12},{8,0},{12,4},{16,24},{20,28},{24,16},{28,20},{1,9},{5... | collective-permute-start | bytes 393224 | tf_op jit(solution)/shard_map/ppermute | solution.py:130
  81.1 5.0 %collective-permute-start.28 = (f32[256,128]{1,0:T(8,128)S(1)}, f32[256,128]{1,0:T(8,128)S(1)}, u32[]{:S(2)}, u32[]{:S(2)}) collective-permute-start(f32[256,128]{1,0:T(8,128)S(1)} %get-tuple-element.66), channel_id=1, source_target_pairs={{0,16},{4,20},{8,24},{12,28},{16,0},{20,4},{24,8},{28,12},{1,17},{... | collective-permute-start | bytes 393224 | tf_op jit(solution)/shard_map/ppermute | solution.py:130
  81.8 5.9 %collective-permute-start.29 = (f32[256,128]{1,0:T(8,128)S(1)}, f32[256,128]{1,0:T(8,128)S(1)}, u32[]{:S(2)}, u32[]{:S(2)}) collective-permute-start(f32[256,128]{1,0:T(8,128)S(1)} %get-tuple-element.65), channel_id=1, source_target_pairs={{0,24},{4,28},{8,16},{12,20},{16,8},{20,12},{24,0},{28,4},{1,25},{... | collective-permute-start | bytes 393224 | tf_op jit(solution)/shard_map/ppermute | solution.py:130
  87.7 6.7 %collective-permute-start.30 = (bf16[256,128]{1,0:T(8,128)(2,1)S(1)}, bf16[256,128]{1,0:T(8,128)(2,1)S(1)}, u32[]{:S(2)}, u32[]{:S(2)}) collective-permute-start(bf16[256,128]{1,0:T(8,128)(2,1)S(1)} %get-tuple-element.56), channel_id=1, source_target_pairs={{0,1},{1,2},{2,3},{3,0},{4,5},{5,6},{6,7},{7,4},{8,9},{9,10},{10,1... | collective-permute-start | bytes 196616 | tf_op jit(solution)/shard_map/ppermute | solution.py:134
  88.9 6.7 %collective-permute-start.31 = (bf16[256,128]{1,0:T(8,128)(2,1)S(1)}, bf16[256,128]{1,0:T(8,128)(2,1)S(1)}, u32[]{:S(2)}, u32[]{:S(2)}) collective-permute-start(bf16[256,128]{1,0:T(8,128)(2,1)S(1)} %get-tuple-element.56), channel_id=1, source_target_pairs={{0,2},{1,3},{2,0},{3,1},{4,6},{5,7},{6,4},{7,5},{8,10},{9,11},{10,... | collective-permute-start | bytes 196616 | tf_op jit(solution)/shard_map/ppermute | solution.py:134
  91.1 4.9 %collective-permute-start.32 = (bf16[256,128]{1,0:T(8,128)(2,1)S(1)}, bf16[256,128]{1,0:T(8,128)(2,1)S(1)}, u32[]{:S(2)}, u32[]{:S(2)}) collective-permute-start(bf16[256,128]{1,0:T(8,128)(2,1)S(1)} %get-tuple-element.56), channel_id=1, source_target_pairs={{0,3},{1,0},{2,1},{3,2},{4,7},{5,4},{6,5},{7,6},{8,11},{9,8},{10,9... | collective-permute-start | bytes 196616 | tf_op jit(solution)/shard_map/ppermute | solution.py:134
  92.1 4.3 %collective-permute-start.33 = (bf16[256,128]{1,0:T(8,128)(2,1)S(1)}, bf16[256,128]{1,0:T(8,128)(2,1)S(1)}, u32[]{:S(2)}, u32[]{:S(2)}) collective-permute-start(bf16[256,128]{1,0:T(8,128)(2,1)S(1)} %get-tuple-element.56), channel_id=1, source_target_pairs={{0,8},{4,12},{8,0},{12,4},{16,24},{20,28},{24,16},{28,20},{1,9},{5... | collective-permute-start | bytes 196616 | tf_op jit(solution)/shard_map/ppermute | solution.py:130
  93.3 4.3 %collective-permute-start.34 = (bf16[256,128]{1,0:T(8,128)(2,1)S(1)}, bf16[256,128]{1,0:T(8,128)(2,1)S(1)}, u32[]{:S(2)}, u32[]{:S(2)}) collective-permute-start(bf16[256,128]{1,0:T(8,128)(2,1)S(1)} %get-tuple-element.56), channel_id=1, source_target_pairs={{0,16},{4,20},{8,24},{12,28},{16,0},{20,4},{24,8},{28,12},{1,17},{... | collective-permute-start | bytes 196616 | tf_op jit(solution)/shard_map/ppermute | solution.py:130
  94.4 5.2 %collective-permute-start.35 = (bf16[256,128]{1,0:T(8,128)(2,1)S(1)}, bf16[256,128]{1,0:T(8,128)(2,1)S(1)}, u32[]{:S(2)}, u32[]{:S(2)}) collective-permute-start(bf16[256,128]{1,0:T(8,128)(2,1)S(1)} %get-tuple-element.56), channel_id=1, source_target_pairs={{0,24},{4,28},{8,16},{12,20},{16,8},{20,12},{24,0},{28,4},{1,25},{... | collective-permute-start | bytes 196616 | tf_op jit(solution)/shard_map/ppermute | solution.py:130
  99.6 2.1 %collective-permute-start.36 = (bf16[1024,128]{1,0:T(8,128)(2,1)S(1)}, bf16[1024,128]{1,0:T(8,128)(2,1)S(1)}, u32[]{:S(2)}, u32[]{:S(2)}) collective-permute-start(bf16[1024,128]{1,0:T(8,128)(2,1)S(1)} %get-tuple-element.52), channel_id=1, source_target_pairs={{0,4},{4,0},{8,12},{12,8},{16,20},{20,16},{24,28},{28,24},{1,5},{5... | collective-permute-start | bytes 786440 | tf_op jit(solution)/shard_map/ppermute | solution.py:130
  100.7 1.7 %collective-permute-start.37 = (bf16[1024,128]{1,0:T(8,128)(2,1)S(1)}, bf16[1024,128]{1,0:T(8,128)(2,1)S(1)}, u32[]{:S(2)}, u32[]{:S(2)}) collective-permute-start(bf16[1024,128]{1,0:T(8,128)(2,1)S(1)} %get-tuple-element.53), channel_id=1, source_target_pairs={{0,4},{4,0},{8,12},{12,8},{16,20},{20,16},{24,28},{28,24},{1,5},{5... | collective-permute-start | bytes 786440 | tf_op jit(solution)/shard_map/ppermute | solution.py:130
  103.2 4.4 %collective-permute-start.38 = (f32[2,64,128]{2,1,0:T(8,128)S(1)}, f32[2,64,128]{2,1,0:T(8,128)S(1)}, u32[]{:S(2)}, u32[]{:S(2)}) collective-permute-start(f32[2,64,128]{2,1,0:T(8,128)S(1)} %get-tuple-element.79), channel_id=1, source_target_pairs={{0,8},{4,12},{8,0},{12,4},{16,24},{20,28},{24,16},{28,20},{1,9},{5... | collective-permute-start | bytes 196616 | tf_op jit(solution)/shard_map/ppermute | solution.py:130
  104.3 5.0 %collective-permute-start.39 = (f32[2,64,128]{2,1,0:T(8,128)S(1)}, f32[2,64,128]{2,1,0:T(8,128)S(1)}, u32[]{:S(2)}, u32[]{:S(2)}) collective-permute-start(f32[2,64,128]{2,1,0:T(8,128)S(1)} %get-tuple-element.81), channel_id=1, source_target_pairs={{0,16},{4,20},{8,24},{12,28},{16,0},{20,4},{24,8},{28,12},{1,17},{... | collective-permute-start | bytes 196616 | tf_op jit(solution)/shard_map/ppermute | solution.py:130
  105.0 5.2 %collective-permute-start.40 = (f32[2,64,128]{2,1,0:T(8,128)S(1)}, f32[2,64,128]{2,1,0:T(8,128)S(1)}, u32[]{:S(2)}, u32[]{:S(2)}) collective-permute-start(f32[2,64,128]{2,1,0:T(8,128)S(1)} %get-tuple-element.80), channel_id=1, source_target_pairs={{0,24},{4,28},{8,16},{12,20},{16,8},{20,12},{24,0},{28,4},{1,25},{... | collective-permute-start | bytes 196616 | tf_op jit(solution)/shard_map/ppermute | solution.py:130
  110.2 5.8 %collective-permute-start.41 = (f32[64,128]{1,0:T(8,128)S(1)}, f32[64,128]{1,0:T(8,128)S(1)}, u32[]{:S(2)}, u32[]{:S(2)}) collective-permute-start(f32[64,128]{1,0:T(8,128)S(1)} %get-tuple-element.95), channel_id=1, source_target_pairs={{0,1},{1,2},{2,3},{3,0},{4,5},{5,6},{6,7},{7,4},{8,9},{9,10},{10,1... | collective-permute-start | bytes 98312 | tf_op jit(solution)/shard_map/ppermute | solution.py:134
  111.3 5.4 %collective-permute-start.42 = (f32[64,128]{1,0:T(8,128)S(1)}, f32[64,128]{1,0:T(8,128)S(1)}, u32[]{:S(2)}, u32[]{:S(2)}) collective-permute-start(f32[64,128]{1,0:T(8,128)S(1)} %get-tuple-element.95), channel_id=1, source_target_pairs={{0,2},{1,3},{2,0},{3,1},{4,6},{5,7},{6,4},{7,5},{8,10},{9,11},{10,... | collective-permute-start | bytes 98312 | tf_op jit(solution)/shard_map/ppermute | solution.py:134
  112.1 4.6 %collective-permute-start.43 = (f32[64,128]{1,0:T(8,128)S(1)}, f32[64,128]{1,0:T(8,128)S(1)}, u32[]{:S(2)}, u32[]{:S(2)}) collective-permute-start(f32[64,128]{1,0:T(8,128)S(1)} %get-tuple-element.95), channel_id=1, source_target_pairs={{0,3},{1,0},{2,1},{3,2},{4,7},{5,4},{6,5},{7,6},{8,11},{9,8},{10,9... | collective-permute-start | bytes 98312 | tf_op jit(solution)/shard_map/ppermute | solution.py:134
  116.7 4.3 %collective-permute-start.44 = (f32[2,64,128]{2,1,0:T(8,128)S(1)}, f32[2,64,128]{2,1,0:T(8,128)S(1)}, u32[]{:S(2)}, u32[]{:S(2)}) collective-permute-start(f32[2,64,128]{2,1,0:T(8,128)S(1)} %get-tuple-element.93), channel_id=1, source_target_pairs={{0,8},{4,12},{8,0},{12,4},{16,24},{20,28},{24,16},{28,20},{1,9},{5... | collective-permute-start | bytes 196616 | tf_op jit(solution)/shard_map/ppermute | solution.py:130
  118.0 4.3 %collective-permute-start.45 = (f32[2,64,128]{2,1,0:T(8,128)S(1)}, f32[2,64,128]{2,1,0:T(8,128)S(1)}, u32[]{:S(2)}, u32[]{:S(2)}) collective-permute-start(f32[2,64,128]{2,1,0:T(8,128)S(1)} %get-tuple-element.93), channel_id=1, source_target_pairs={{0,16},{4,20},{8,24},{12,28},{16,0},{20,4},{24,8},{28,12},{1,17},{... | collective-permute-start | bytes 196616 | tf_op jit(solution)/shard_map/ppermute | solution.py:130
  119.2 5.2 %collective-permute-start.46 = (f32[2,64,128]{2,1,0:T(8,128)S(1)}, f32[2,64,128]{2,1,0:T(8,128)S(1)}, u32[]{:S(2)}, u32[]{:S(2)}) collective-permute-start(f32[2,64,128]{2,1,0:T(8,128)S(1)} %get-tuple-element.93), channel_id=1, source_target_pairs={{0,24},{4,28},{8,16},{12,20},{16,8},{20,12},{24,0},{28,4},{1,25},{... | collective-permute-start | bytes 196616 | tf_op jit(solution)/shard_map/ppermute | solution.py:130
  124.7 1.7 %collective-permute-start.47 = (f32[2,256,128]{2,1,0:T(8,128)S(1)}, f32[2,256,128]{2,1,0:T(8,128)S(1)}, u32[]{:S(2)}, u32[]{:S(2)}) collective-permute-start(f32[2,256,128]{2,1,0:T(8,128)S(1)} %maximum_select_fusion.3), channel_id=1, source_target_pairs={{0,4},{4,0},{8,12},{12,8},{16,20},{20,16},{24,28},{28,24},{1,5},{5... | collective-permute-start | bytes 786440 | tf_op jit(solution)/shard_map/ppermute | solution.py:130
  (5 other events, 40.1 us)

commit v3 on v2

--- a/solution.py
+++ b/solution.py
@@ -375,10 +375,26 @@
     first, mirrored_other = lax.optimization_barrier(
         (start.astype(jnp.bfloat16), mirrored_other)
     )
-    first_gathered, direct = lax.optimization_barrier((gather(first), direct))
+    def last_piece(v, of_core):
+        return lax.ppermute(
+            v,
+            ("row", "col"),
+            [
+                (r * cols + i, r * cols + (i + cols - 1) % cols)
+                for r in range(of_core, rows, 2)
+                for i in range(cols)
+            ],
+        )
+
+    early = [shifted(first, "col", cols, s) for s in range(1, cols - 1)] + [last_piece(first, 0)]
+    early, direct = lax.optimization_barrier((early, direct))
     direct_other = [core_swap(rows_of_chip, rows) for rows_of_chip in direct]
 
     tile = assemble(mirrored, mirrored_other, direct, direct_other)
+
+    tile, first = lax.optimization_barrier((tile, first))
+    last = jnp.where(first_core, early[-1], last_piece(first, 1))
+    first_gathered = jnp.concatenate([first] + early[:-1] + [last], 0)
 
     def partial_product(gathered):
         return jnp.dot(tile, gathered, preferred_element_type=jnp.float32)

time: 136 us -> 142 us (1.044)
  starting transfers between devices: 60.2 us -> 64.2 us
  waiting for transfers between devices: 46.6 us -> 48.5 us
    ppermute x0 -> x2, starting transfers between devices: none -> 7.01 us  [last_piece(): lax.ppermute(v, ('row', 'col'), [(r * cols + i, r * cols + (i + cols - 1)...]
    ppermute x18 -> x17, starting transfers between devices: 32.5 us -> 29.5 us  [shifted(): return lax.ppermute(x, axis, [(i, (i + step) % size) for i in range(size)])]
    ppermute x0 -> x2, waiting for transfers between devices: none -> 1.84 us  [last_piece(): lax.ppermute(v, ('row', 'col'), [(r * cols + i, r * cols + (i + cols - 1)...]
    ppermute x18 -> x17, waiting for transfers between devices: 18.7 us -> 17.5 us  [shifted(): return lax.ppermute(x, axis, [(i, (i + step) % size) for i in range(size)])]
  transfers between devices with their start and end apart: 49 -> 50, of which waited for: 34 -> 37; matrix products, arithmetic and copies ran while one was open for 2% -> 2% of each run, Pallas kernels for 3% -> 3%
where the time goes in v3:
time: 142 us; the launch traced here: 141 us
  starting transfers between devices  64.2 us (45%)
  waiting for transfers between devices  48.5 us (34%)
  Pallas kernels  16.5 us (12%)
  matrix products  4.23 us (3%)
  local copies, waits for them, and re-layouts  2.8 us (2%)
  between operations  2.49 us (2%)
  other arithmetic  2.38 us (2%)
    ppermute x17, starting transfers between devices, shifted(): return lax.ppermute(x, axis, [(i, (i + step) % size) for i in range(size)])  29.5 us
    ppermute x31, waiting for transfers between devices, exchanged(): return lax.ppermute(x, axis, [(i, i ^ apart) for i in range(size)])  29.2 us
    ppermute x31, starting transfers between devices, exchanged(): return lax.ppermute(x, axis, [(i, i ^ apart) for i in range(size)])  27.7 us
    ppermute x17, waiting for transfers between devices, shifted(): return lax.ppermute(x, axis, [(i, (i + step) % size) for i in range(size)])  17.5 us
    pallas_call x1, Pallas kernels, finish(): pl.pallas_call(functools.partial(finish_kernel, total_rows), out_shape=(j...  8.78 us
    ppermute x2, starting transfers between devices, last_piece(): lax.ppermute(v, ('row', 'col'), [(r * cols + i, r * cols + (i + cols - 1)...  7.01 us
    pallas_call x1, Pallas kernels, direct_rows(): pl.pallas_call(functools.partial(direct_kernel, rows, slots), out_shape=(...  3.08 us
  transfers between devices with their start and end apart: 50, of which 37 were waited for; matrix products, arithmetic and copies ran while one was open for 2% of the time, Pallas kernels for 3%

profile of v3, /device:TPU:0, one launch (start us, length us, event | category | flops | bytes accessed | tf_op | source)
XLA Modules:
  0.0 141.2 jit_solution(14081646327407246126)
XLA Ops:
  3.7 1.8 %pack.1 = (bf16[16,4224]{1,0:T(8,128)(2,1)}, bf16[16,4224]{1,0:T(8,128)(2,1)}, bf16[16,4224]{1,0:T(8,128)(2,1)}) custom-call(s32[1]{0:T(128)} %bitcast.1.col_ref, bf16[4,16,4096]{2,1,0:T(8,128)(2,1)} %bitcast.84, f32[4,16]{1,0:T(4,128)} %reshape.221.places_ref), custom_call_target="tpu_custom_call" | custom-call | tf_op jit(solution)/shard_map/pack/pallas_call | solution.py:174
  5.5 2.7 %collective-permute-start.1 = (bf16[16,4224]{1,0:T(8,128)(2,1)}, bf16[16,4224]{1,0:T(8,128)(2,1)S(1)}, u32[]{:S(2)}, u32[]{:S(2)}) collective-permute-start(bf16[16,4224]{1,0:T(8,128)(2,1)} %get-tuple-element.36), channel_id=1, source_target_pairs={{0,1},{1,2},{2,3},{3,0},{4,5},{5,6},{6,7},{7,4},{8,9},{9,10},{10,1... | collective-permute-start | bytes 405512 | tf_op jit(solution)/shard_map/ppermute | solution.py:134
  8.1 2.6 %collective-permute-start.2 = (bf16[16,4224]{1,0:T(8,128)(2,1)}, bf16[16,4224]{1,0:T(8,128)(2,1)S(1)}, u32[]{:S(2)}, u32[]{:S(2)}) collective-permute-start(bf16[16,4224]{1,0:T(8,128)(2,1)} %get-tuple-element.37), channel_id=1, source_target_pairs={{0,2},{1,3},{2,0},{3,1},{4,6},{5,7},{6,4},{7,5},{8,10},{9,11},{10,... | collective-permute-start | bytes 405512 | tf_op jit(solution)/shard_map/ppermute | solution.py:134
  10.7 1.3 collective-permute-start.3
  13.8 2.3 %mirror.1.mirrored = bf16[2,512,512]{2,1,0:T(8,128)(2,1)S(1)} custom-call(s32[1,64]{1,0:T(1,128)S(1)} %reshape.219.key_ref, bf16[64,4096]{1,0:T(8,128)(2,1)S(1)} %bitcast.85, bf16[2,4096]{1,0:T(2,128)(2,1)S(1)} %copy-done.3), custom_call_target="tpu_custom_call" | custom-call | flops 67108864 | bytes 786432 | tf_op jit(solution)/shard_map/mirror/pallas_call | solution.py:214
  16.1 4.3 %collective-permute-done.2.refs_1_ = bf16[16,4224]{1,0:T(8,128)(2,1)S(1)} collective-permute-done((bf16[16,4224]{1,0:T(8,128)(2,1)}, bf16[16,4224]{1,0:T(8,128)(2,1)S(1)}, u32[]{:S(2)}, u32[]{:S(2)}) %collective-permute-start.2) | collective-permute-done | bytes 135200 | tf_op jit(solution)/shard_map/ppermute | solution.py:134
  20.5 3.1 %direct_rows.1 = (bf16[128,1024]{1,0:T(8,128)(2,1)S(1)}, bf16[128,1024]{1,0:T(8,128)(2,1)S(1)}, bf16[128,1024]{1,0:T(8,128)(2,1)S(1)}, bf16[128,1024]{1,0:T(8,128)(2,1)S(1)}) custom-call(s32[1]{0:T(128)} %bitcast.1.col_ref, bf16[4,16,4096]{2,1,0:T(8,128)(2,1)S(1)} %bitcast.86, f32[4,16]{1,0:T(4,128)S(1)} %copy-done.2, ...), custom_call_target="tpu_custom_call" | custom-call | tf_op jit(solution)/shard_map/direct_rows/pallas_call | solution.py:266
  23.6 2.5 %collective-permute-start.10 = (bf16[128,1024]{1,0:T(8,128)(2,1)S(1)}, bf16[128,1024]{1,0:T(8,128)(2,1)S(1)}, u32[]{:S(2)}, u32[]{:S(2)}) collective-permute-start(bf16[128,1024]{1,0:T(8,128)(2,1)S(1)} %get-tuple-element.50), channel_id=1, source_target_pairs={{0,24},{4,28},{8,16},{12,20},{16,8},{20,12},{24,0},{28,4},{1,25},{... | collective-permute-start | bytes 786440 | tf_op jit(solution)/shard_map/ppermute | solution.py:130
  27.2 3.4 %collective-permute-start.5 = (bf16[256,128]{1,0:T(8,128)(2,1)S(1)}, bf16[256,128]{1,0:T(8,128)(2,1)S(1)}, u32[]{:S(2)}, u32[]{:S(2)}) collective-permute-start(bf16[256,128]{1,0:T(8,128)(2,1)S(1)} %convert_element_type.18), channel_id=1, source_target_pairs={{0,1},{1,2},{2,3},{3,0},{4,5},{5,6},{6,7},{7,4},{8,9},{9,10},{10,1... | collective-permute-start | bytes 196616 | tf_op jit(solution)/shard_map/ppermute | solution.py:134
  30.7 1.6 %collective-permute-start.6 = (bf16[256,128]{1,0:T(8,128)(2,1)S(1)}, bf16[256,128]{1,0:T(8,128)(2,1)S(1)}, u32[]{:S(2)}, u32[]{:S(2)}) collective-permute-start(bf16[256,128]{1,0:T(8,128)(2,1)S(1)} %convert_element_type.18), channel_id=1, source_target_pairs={{0,2},{1,3},{2,0},{3,1},{4,6},{5,7},{6,4},{7,5},{8,10},{9,11},{10,... | collective-permute-start | bytes 196616 | tf_op jit(solution)/shard_map/ppermute | solution.py:134
  32.3 1.5 %collective-permute-done.10.refs_3_ = bf16[128,1024]{1,0:T(8,128)(2,1)S(1)} collective-permute-done((bf16[128,1024]{1,0:T(8,128)(2,1)S(1)}, bf16[128,1024]{1,0:T(8,128)(2,1)S(1)}, u32[]{:S(2)}, u32[]{:S(2)}) %collective-permute-start.10) | collective-permute-done | bytes 262176 | tf_op jit(solution)/shard_map/ppermute | solution.py:130
  33.8 6.3 %collective-permute-start.7 = (bf16[256,128]{1,0:T(8,128)(2,1)S(1)}, bf16[256,128]{1,0:T(8,128)(2,1)S(1)}, u32[]{:S(2)}, u32[]{:S(2)}) collective-permute-start(bf16[256,128]{1,0:T(8,128)(2,1)S(1)} %convert_element_type.18), channel_id=1, source_target_pairs={{0,3},{1,0},{2,1},{3,2},{8,11},{9,8},{10,9},{11,10},{16,19},{17,16... | collective-permute-start | bytes 196616 | tf_op jit(solution)/shard_map/ppermute | solution.py:379
  40.2 1.8 %collective-permute-done.7 = bf16[256,128]{1,0:T(8,128)(2,1)S(1)} collective-permute-done((bf16[256,128]{1,0:T(8,128)(2,1)S(1)}, bf16[256,128]{1,0:T(8,128)(2,1)S(1)}, u32[]{:S(2)}, u32[]{:S(2)}) %collective-permute-start.7) | collective-permute-done | bytes 65568 | tf_op jit(solution)/shard_map/ppermute | solution.py:379
  46.7 1.6 %collective-permute-start.16 = (f32[256,128]{1,0:T(8,128)S(1)}, f32[256,128]{1,0:T(8,128)S(1)}, u32[]{:S(2)}, u32[]{:S(2)}) collective-permute-start(f32[256,128]{1,0:T(8,128)S(1)} %get-tuple-element.78), channel_id=1, source_target_pairs={{0,8},{4,12},{8,0},{12,4},{16,24},{20,28},{24,16},{28,20},{1,9},{5... | collective-permute-start | bytes 393224 | tf_op jit(solution)/shard_map/ppermute | solution.py:130
  48.3 1.5 %collective-permute-start.17 = (f32[256,128]{1,0:T(8,128)S(1)}, f32[256,128]{1,0:T(8,128)S(1)}, u32[]{:S(2)}, u32[]{:S(2)}) collective-permute-start(f32[256,128]{1,0:T(8,128)S(1)} %get-tuple-element.80), channel_id=1, source_target_pairs={{0,16},{4,20},{8,24},{12,28},{16,0},{20,4},{24,8},{28,12},{1,17},{... | collective-permute-start | bytes 393224 | tf_op jit(solution)/shard_map/ppermute | solution.py:130
  51.8 1.5 %collective-permute-done.17 = f32[256,128]{1,0:T(8,128)S(1)} collective-permute-done((f32[256,128]{1,0:T(8,128)S(1)}, f32[256,128]{1,0:T(8,128)S(1)}, u32[]{:S(2)}, u32[]{:S(2)}) %collective-permute-start.17) | collective-permute-done | bytes 131104 | tf_op jit(solution)/shard_map/ppermute | solution.py:130
  53.2 2.4 %collective-permute-done.18 = f32[256,128]{1,0:T(8,128)S(1)} collective-permute-done((f32[256,128]{1,0:T(8,128)S(1)}, f32[256,128]{1,0:T(8,128)S(1)}, u32[]{:S(2)}, u32[]{:S(2)}) %collective-permute-start.18) | collective-permute-done | bytes 131104 | tf_op jit(solution)/shard_map/ppermute | solution.py:130
  55.7 1.9 %collective-permute-start.19 = (bf16[256,128]{1,0:T(8,128)(2,1)S(1)}, bf16[256,128]{1,0:T(8,128)(2,1)S(1)}, u32[]{:S(2)}, u32[]{:S(2)}) collective-permute-start(bf16[256,128]{1,0:T(8,128)(2,1)S(1)} %get-tuple-element.68), channel_id=1, source_target_pairs={{0,1},{1,2},{2,3},{3,0},{4,5},{5,6},{6,7},{7,4},{8,9},{9,10},{10,1... | collective-permute-start | bytes 196616 | tf_op jit(solution)/shard_map/ppermute | solution.py:134
  57.6 2.8 %collective-permute-start.20 = (bf16[256,128]{1,0:T(8,128)(2,1)S(1)}, bf16[256,128]{1,0:T(8,128)(2,1)S(1)}, u32[]{:S(2)}, u32[]{:S(2)}) collective-permute-start(bf16[256,128]{1,0:T(8,128)(2,1)S(1)} %get-tuple-element.68), channel_id=1, source_target_pairs={{0,2},{1,3},{2,0},{3,1},{4,6},{5,7},{6,4},{7,5},{8,10},{9,11},{10,... | collective-permute-start | bytes 196616 | tf_op jit(solution)/shard_map/ppermute | solution.py:134
  60.5 1.7 %collective-permute-done.19 = bf16[256,128]{1,0:T(8,128)(2,1)S(1)} collective-permute-done((bf16[256,128]{1,0:T(8,128)(2,1)S(1)}, bf16[256,128]{1,0:T(8,128)(2,1)S(1)}, u32[]{:S(2)}, u32[]{:S(2)}) %collective-permute-start.19) | collective-permute-done | bytes 65568 | tf_op jit(solution)/shard_map/ppermute | solution.py:134
  62.2 1.4 collective-permute-done.20
  63.6 1.2 collective-permute-done.21
  66.6 2.5 %collective-permute-start.24 = (f32[256,128]{1,0:T(8,128)S(1)}, f32[256,128]{1,0:T(8,128)S(1)}, u32[]{:S(2)}, u32[]{:S(2)}) collective-permute-start(f32[256,128]{1,0:T(8,128)S(1)} %get-tuple-element.76), channel_id=1, source_target_pairs={{0,24},{4,28},{8,16},{12,20},{16,8},{20,12},{24,0},{28,4},{1,25},{... | collective-permute-start | bytes 393224 | tf_op jit(solution)/shard_map/ppermute | solution.py:130
  69.1 1.5 %collective-permute-done.22 = f32[256,128]{1,0:T(8,128)S(1)} collective-permute-done((f32[256,128]{1,0:T(8,128)S(1)}, f32[256,128]{1,0:T(8,128)S(1)}, u32[]{:S(2)}, u32[]{:S(2)}) %collective-permute-start.22) | collective-permute-done | bytes 131104 | tf_op jit(solution)/shard_map/ppermute | solution.py:130
  71.1 2.0 %collective-permute-done.24 = f32[256,128]{1,0:T(8,128)S(1)} collective-permute-done((f32[256,128]{1,0:T(8,128)S(1)}, f32[256,128]{1,0:T(8,128)S(1)}, u32[]{:S(2)}, u32[]{:S(2)}) %collective-permute-start.24) | collective-permute-done | bytes 131104 | tf_op jit(solution)/shard_map/ppermute | solution.py:130
  73.2 3.9 %collective-permute-start.26 = (bf16[256,128]{1,0:T(8,128)(2,1)S(1)}, bf16[256,128]{1,0:T(8,128)(2,1)S(1)}, u32[]{:S(2)}, u32[]{:S(2)}) collective-permute-start(bf16[256,128]{1,0:T(8,128)(2,1)S(1)} %get-tuple-element.66), channel_id=1, source_target_pairs={{0,2},{1,3},{2,0},{3,1},{4,6},{5,7},{6,4},{7,5},{8,10},{9,11},{10,... | collective-permute-start | bytes 196616 | tf_op jit(solution)/shard_map/ppermute | solution.py:134
  77.9 1.4 collective-permute-done.25
  79.3 3.4 %collective-permute-done.26 = bf16[256,128]{1,0:T(8,128)(2,1)S(1)} collective-permute-done((bf16[256,128]{1,0:T(8,128)(2,1)S(1)}, bf16[256,128]{1,0:T(8,128)(2,1)S(1)}, u32[]{:S(2)}, u32[]{:S(2)}) %collective-permute-start.26) | collective-permute-done | bytes 65568 | tf_op jit(solution)/shard_map/ppermute | solution.py:134
  85.1 1.2 collective-permute-start.29
  86.3 1.5 %collective-permute-start.30 = (f32[256,128]{1,0:T(8,128)S(1)}, f32[256,128]{1,0:T(8,128)S(1)}, u32[]{:S(2)}, u32[]{:S(2)}) collective-permute-start(f32[256,128]{1,0:T(8,128)S(1)} %get-tuple-element.73), channel_id=1, source_target_pairs={{0,24},{4,28},{8,16},{12,20},{16,8},{20,12},{24,0},{28,4},{1,25},{... | collective-permute-start | bytes 393224 | tf_op jit(solution)/shard_map/ppermute | solution.py:130
  87.8 2.6 %collective-permute-done.28 = f32[256,128]{1,0:T(8,128)S(1)} collective-permute-done((f32[256,128]{1,0:T(8,128)S(1)}, f32[256,128]{1,0:T(8,128)S(1)}, u32[]{:S(2)}, u32[]{:S(2)}) %collective-permute-start.28) | collective-permute-done | bytes 131104 | tf_op jit(solution)/shard_map/ppermute | solution.py:130
  90.4 3.3 %collective-permute-done.29 = f32[256,128]{1,0:T(8,128)S(1)} collective-permute-done((f32[256,128]{1,0:T(8,128)S(1)}, f32[256,128]{1,0:T(8,128)S(1)}, u32[]{:S(2)}, u32[]{:S(2)}) %collective-permute-start.29) | collective-permute-done | bytes 131104 | tf_op jit(solution)/shard_map/ppermute | solution.py:130
  93.7 1.5 %collective-permute-start.31 = (bf16[256,128]{1,0:T(8,128)(2,1)S(1)}, bf16[256,128]{1,0:T(8,128)(2,1)S(1)}, u32[]{:S(2)}, u32[]{:S(2)}) collective-permute-start(bf16[256,128]{1,0:T(8,128)(2,1)S(1)} %get-tuple-element.64), channel_id=1, source_target_pairs={{0,1},{1,2},{2,3},{3,0},{4,5},{5,6},{6,7},{7,4},{8,9},{9,10},{10,1... | collective-permute-start | bytes 196616 | tf_op jit(solution)/shard_map/ppermute | solution.py:134
  95.1 2.2 %collective-permute-start.32 = (bf16[256,128]{1,0:T(8,128)(2,1)S(1)}, bf16[256,128]{1,0:T(8,128)(2,1)S(1)}, u32[]{:S(2)}, u32[]{:S(2)}) collective-permute-start(bf16[256,128]{1,0:T(8,128)(2,1)S(1)} %get-tuple-element.64), channel_id=1, source_target_pairs={{0,2},{1,3},{2,0},{3,1},{4,6},{5,7},{6,4},{7,5},{8,10},{9,11},{10,... | collective-permute-start | bytes 196616 | tf_op jit(solution)/shard_map/ppermute | solution.py:134
  97.6 1.1 collective-permute-start.34
  100.0 1.7 %collective-permute-start.36 = (bf16[256,128]{1,0:T(8,128)(2,1)S(1)}, bf16[256,128]{1,0:T(8,128)(2,1)S(1)}, u32[]{:S(2)}, u32[]{:S(2)}) collective-permute-start(bf16[256,128]{1,0:T(8,128)(2,1)S(1)} %get-tuple-element.64), channel_id=1, source_target_pairs={{0,24},{4,28},{8,16},{12,20},{16,8},{20,12},{24,0},{28,4},{1,25},{... | collective-permute-start | bytes 196616 | tf_op jit(solution)/shard_map/ppermute | solution.py:130
  103.1 2.0 %collective-permute-done.36 = bf16[256,128]{1,0:T(8,128)(2,1)S(1)} collective-permute-done((bf16[256,128]{1,0:T(8,128)(2,1)S(1)}, bf16[256,128]{1,0:T(8,128)(2,1)S(1)}, u32[]{:S(2)}, u32[]{:S(2)}) %collective-permute-start.36) | collective-permute-done | bytes 65568 | tf_op jit(solution)/shard_map/ppermute | solution.py:130
  108.8 1.4 %collective-permute-start.39 = (f32[2,64,128]{2,1,0:T(8,128)S(1)}, f32[2,64,128]{2,1,0:T(8,128)S(1)}, u32[]{:S(2)}, u32[]{:S(2)}) collective-permute-start(f32[2,64,128]{2,1,0:T(8,128)S(1)} %get-tuple-element.87), channel_id=1, source_target_pairs={{0,8},{4,12},{8,0},{12,4},{16,24},{20,28},{24,16},{28,20},{1,9},{5... | collective-permute-start | bytes 196616 | tf_op jit(solution)/shard_map/ppermute | solution.py:130
  111.1 1.2 collective-permute-start.41
  113.2 1.3 collective-permute-done.40
  114.5 1.8 %collective-permute-done.41 = f32[2,64,128]{2,1,0:T(8,128)S(1)} collective-permute-done((f32[2,64,128]{2,1,0:T(8,128)S(1)}, f32[2,64,128]{2,1,0:T(8,128)S(1)}, u32[]{:S(2)}, u32[]{:S(2)}) %collective-permute-start.41) | collective-permute-done | bytes 65568 | tf_op jit(solution)/shard_map/ppermute | solution.py:130
  116.3 1.4 collective-permute-start.42
  118.4 2.3 %collective-permute-start.44 = (f32[64,128]{1,0:T(8,128)S(1)}, f32[64,128]{1,0:T(8,128)S(1)}, u32[]{:S(2)}, u32[]{:S(2)}) collective-permute-start(f32[64,128]{1,0:T(8,128)S(1)} %get-tuple-element.103), channel_id=1, source_target_pairs={{0,3},{1,0},{2,1},{3,2},{4,7},{5,4},{6,5},{7,6},{8,11},{9,8},{10,9... | collective-permute-start | bytes 98312 | tf_op jit(solution)/shard_map/ppermute | solution.py:134
  120.7 1.4 collective-permute-done.42
  122.9 1.2 collective-permute-start.45
  125.1 1.3 collective-permute-start.47
  128.3 1.9 %collective-permute-done.47 = f32[2,64,128]{2,1,0:T(8,128)S(1)} collective-permute-done((f32[2,64,128]{2,1,0:T(8,128)S(1)}, f32[2,64,128]{2,1,0:T(8,128)S(1)}, u32[]{:S(2)}, u32[]{:S(2)}) %collective-permute-start.47) | collective-permute-done | bytes 65568 | tf_op jit(solution)/shard_map/ppermute | solution.py:130
  132.4 8.8 %finish.1 = (f32[128,256]{1,0:T(8,128)}, f32[256,256]{1,0:T(8,128)}) custom-call(f32[256,256]{1,0:T(8,128)S(1)} %get-tuple-element.71.gram_ref, f32[256,256]{1,0:T(8,128)S(1)} %get-tuple-element.70.cross_ref, f32[128,256]{1,0:T(8,128)S(1)} %maximum_select_fusion.4.y_ref), custom_call_target="tpu_custom_call" | custom-call | tf_op jit(solution)/shard_map/finish/pallas_call | solution.py:118
  (119 shorter events, 31.5 us)
Async XLA Ops:
  1.6 3.9 %collective-permute-start = (f32[128,128]{1,0:T(8,128)S(1)}, f32[128,128]{1,0:T(8,128)S(1)}, u32[]{:S(2)}, u32[]{:S(2)}) collective-permute-start(f32[128,128]{1,0:T(8,128)S(1)} %get-tuple-element.99), channel_id=1, source_target_pairs={{0,4},{4,0},{8,12},{12,8},{16,20},{20,16},{24,28},{28,24},{1,5},{5... | collective-permute-start | bytes 196616 | tf_op jit(solution)/shard_map/ppermute | solution.py:130
  5.5 10.6 %collective-permute-start.1 = (bf16[16,4224]{1,0:T(8,128)(2,1)}, bf16[16,4224]{1,0:T(8,128)(2,1)S(1)}, u32[]{:S(2)}, u32[]{:S(2)}) collective-permute-start(bf16[16,4224]{1,0:T(8,128)(2,1)} %get-tuple-element.36), channel_id=1, source_target_pairs={{0,1},{1,2},{2,3},{3,0},{4,5},{5,6},{6,7},{7,4},{8,9},{9,10},{10,1... | collective-permute-start | bytes 405512 | tf_op jit(solution)/shard_map/ppermute | solution.py:134
  8.1 12.3 %collective-permute-start.2 = (bf16[16,4224]{1,0:T(8,128)(2,1)}, bf16[16,4224]{1,0:T(8,128)(2,1)S(1)}, u32[]{:S(2)}, u32[]{:S(2)}) collective-permute-start(bf16[16,4224]{1,0:T(8,128)(2,1)} %get-tuple-element.37), channel_id=1, source_target_pairs={{0,2},{1,3},{2,0},{3,1},{4,6},{5,7},{6,4},{7,5},{8,10},{9,11},{10,... | collective-permute-start | bytes 405512 | tf_op jit(solution)/shard_map/ppermute | solution.py:134
  10.7 9.7 %collective-permute-start.3 = (bf16[16,4224]{1,0:T(8,128)(2,1)}, bf16[16,4224]{1,0:T(8,128)(2,1)S(1)}, u32[]{:S(2)}, u32[]{:S(2)}) collective-permute-start(bf16[16,4224]{1,0:T(8,128)(2,1)} %get-tuple-element.38), channel_id=1, source_target_pairs={{0,3},{1,0},{2,1},{3,2},{4,7},{5,4},{6,5},{7,6},{8,11},{9,8},{10,9... | collective-permute-start | bytes 405512 | tf_op jit(solution)/shard_map/ppermute | solution.py:134
  23.6 3.6 %collective-permute-start.4 = (bf16[2,512,512]{2,1,0:T(8,128)(2,1)S(1)}, bf16[2,512,512]{2,1,0:T(8,128)(2,1)S(1)}, u32[]{:S(2)}, u32[]{:S(2)}) collective-permute-start(bf16[2,512,512]{2,1,0:T(8,128)(2,1)S(1)} %mirror.1.mirrored), channel_id=1, source_target_pairs={{0,4},{4,0},{8,12},{12,8},{16,20},{20,16},{24,28},{28,24},{1,5},{5... | collective-permute-start | bytes 3145736 | tf_op jit(solution)/shard_map/ppermute | solution.py:130
  23.6 10.1 %collective-permute-start.10 = (bf16[128,1024]{1,0:T(8,128)(2,1)S(1)}, bf16[128,1024]{1,0:T(8,128)(2,1)S(1)}, u32[]{:S(2)}, u32[]{:S(2)}) collective-permute-start(bf16[128,1024]{1,0:T(8,128)(2,1)S(1)} %get-tuple-element.50), channel_id=1, source_target_pairs={{0,24},{4,28},{8,16},{12,20},{16,8},{20,12},{24,0},{28,4},{1,25},{... | collective-permute-start | bytes 786440 | tf_op jit(solution)/shard_map/ppermute | solution.py:130
  26.2 14.0 %collective-permute-start.8 = (bf16[128,1024]{1,0:T(8,128)(2,1)S(1)}, bf16[128,1024]{1,0:T(8,128)(2,1)S(1)}, u32[]{:S(2)}, u32[]{:S(2)}) collective-permute-start(bf16[128,1024]{1,0:T(8,128)(2,1)S(1)} %get-tuple-element.48), channel_id=1, source_target_pairs={{0,8},{4,12},{8,0},{12,4},{16,24},{20,28},{24,16},{28,20},{1,9},{5... | collective-permute-start | bytes 786440 | tf_op jit(solution)/shard_map/ppermute | solution.py:130
  26.7 13.4 %collective-permute-start.9 = (bf16[128,1024]{1,0:T(8,128)(2,1)S(1)}, bf16[128,1024]{1,0:T(8,128)(2,1)S(1)}, u32[]{:S(2)}, u32[]{:S(2)}) collective-permute-start(bf16[128,1024]{1,0:T(8,128)(2,1)S(1)} %get-tuple-element.49), channel_id=1, source_target_pairs={{0,16},{4,20},{8,24},{12,28},{16,0},{20,4},{24,8},{28,12},{1,17},{... | collective-permute-start | bytes 786440 | tf_op jit(solution)/shard_map/ppermute | solution.py:130
  27.2 12.9 %collective-permute-start.5 = (bf16[256,128]{1,0:T(8,128)(2,1)S(1)}, bf16[256,128]{1,0:T(8,128)(2,1)S(1)}, u32[]{:S(2)}, u32[]{:S(2)}) collective-permute-start(bf16[256,128]{1,0:T(8,128)(2,1)S(1)} %convert_element_type.18), channel_id=1, source_target_pairs={{0,1},{1,2},{2,3},{3,0},{4,5},{5,6},{6,7},{7,4},{8,9},{9,10},{10,1... | collective-permute-start | bytes 196616 | tf_op jit(solution)/shard_map/ppermute | solution.py:134
  30.7 9.5 %collective-permute-start.6 = (bf16[256,128]{1,0:T(8,128)(2,1)S(1)}, bf16[256,128]{1,0:T(8,128)(2,1)S(1)}, u32[]{:S(2)}, u32[]{:S(2)}) collective-permute-start(bf16[256,128]{1,0:T(8,128)(2,1)S(1)} %convert_element_type.18), channel_id=1, source_target_pairs={{0,2},{1,3},{2,0},{3,1},{4,6},{5,7},{6,4},{7,5},{8,10},{9,11},{10,... | collective-permute-start | bytes 196616 | tf_op jit(solution)/shard_map/ppermute | solution.py:134
  33.8 8.2 %collective-permute-start.7 = (bf16[256,128]{1,0:T(8,128)(2,1)S(1)}, bf16[256,128]{1,0:T(8,128)(2,1)S(1)}, u32[]{:S(2)}, u32[]{:S(2)}) collective-permute-start(bf16[256,128]{1,0:T(8,128)(2,1)S(1)} %convert_element_type.18), channel_id=1, source_target_pairs={{0,3},{1,0},{2,1},{3,2},{8,11},{9,8},{10,9},{11,10},{16,19},{17,16... | collective-permute-start | bytes 196616 | tf_op jit(solution)/shard_map/ppermute | solution.py:379
  42.0 1.9 %collective-permute-start.12 = (bf16[128,1024]{1,0:T(8,128)(2,1)S(1)}, bf16[128,1024]{1,0:T(8,128)(2,1)S(1)}, u32[]{:S(2)}, u32[]{:S(2)}) collective-permute-start(bf16[128,1024]{1,0:T(8,128)(2,1)S(1)} %collective-permute-done.8.refs_1_), channel_id=1, source_target_pairs={{0,4},{4,0},{8,12},{12,8},{16,20},{20,16},{24,28},{28,24},{1,5},{5... | collective-permute-start | bytes 786440 | tf_op jit(solution)/shard_map/ppermute | solution.py:130
  42.5 1.8 %collective-permute-start.13 = (bf16[128,1024]{1,0:T(8,128)(2,1)S(1)}, bf16[128,1024]{1,0:T(8,128)(2,1)S(1)}, u32[]{:S(2)}, u32[]{:S(2)}) collective-permute-start(bf16[128,1024]{1,0:T(8,128)(2,1)S(1)} %collective-permute-done.9.refs_2_), channel_id=1, source_target_pairs={{0,4},{4,0},{8,12},{12,8},{16,20},{20,16},{24,28},{28,24},{1,5},{5... | collective-permute-start | bytes 786440 | tf_op jit(solution)/shard_map/ppermute | solution.py:130
  42.5 2.1 %collective-permute-start.14 = (bf16[128,1024]{1,0:T(8,128)(2,1)S(1)}, bf16[128,1024]{1,0:T(8,128)(2,1)S(1)}, u32[]{:S(2)}, u32[]{:S(2)}) collective-permute-start(bf16[128,1024]{1,0:T(8,128)(2,1)S(1)} %collective-permute-done.10.refs_3_), channel_id=1, source_target_pairs={{0,4},{4,0},{8,12},{12,8},{16,20},{20,16},{24,28},{28,24},{1,5},{5... | collective-permute-start | bytes 786440 | tf_op jit(solution)/shard_map/ppermute | solution.py:130
  46.7 5.0 %collective-permute-start.16 = (f32[256,128]{1,0:T(8,128)S(1)}, f32[256,128]{1,0:T(8,128)S(1)}, u32[]{:S(2)}, u32[]{:S(2)}) collective-permute-start(f32[256,128]{1,0:T(8,128)S(1)} %get-tuple-element.78), channel_id=1, source_target_pairs={{0,8},{4,12},{8,0},{12,4},{16,24},{20,28},{24,16},{28,20},{1,9},{5... | collective-permute-start | bytes 393224 | tf_op jit(solution)/shard_map/ppermute | solution.py:130
  48.3 5.0 %collective-permute-start.17 = (f32[256,128]{1,0:T(8,128)S(1)}, f32[256,128]{1,0:T(8,128)S(1)}, u32[]{:S(2)}, u32[]{:S(2)}) collective-permute-start(f32[256,128]{1,0:T(8,128)S(1)} %get-tuple-element.80), channel_id=1, source_target_pairs={{0,16},{4,20},{8,24},{12,28},{16,0},{20,4},{24,8},{28,12},{1,17},{... | collective-permute-start | bytes 393224 | tf_op jit(solution)/shard_map/ppermute | solution.py:130
  49.8 5.9 %collective-permute-start.18 = (f32[256,128]{1,0:T(8,128)S(1)}, f32[256,128]{1,0:T(8,128)S(1)}, u32[]{:S(2)}, u32[]{:S(2)}) collective-permute-start(f32[256,128]{1,0:T(8,128)S(1)} %get-tuple-element.79), channel_id=1, source_target_pairs={{0,24},{4,28},{8,16},{12,20},{16,8},{20,12},{24,0},{28,4},{1,25},{... | collective-permute-start | bytes 393224 | tf_op jit(solution)/shard_map/ppermute | solution.py:130
  55.7 6.5 %collective-permute-start.19 = (bf16[256,128]{1,0:T(8,128)(2,1)S(1)}, bf16[256,128]{1,0:T(8,128)(2,1)S(1)}, u32[]{:S(2)}, u32[]{:S(2)}) collective-permute-start(bf16[256,128]{1,0:T(8,128)(2,1)S(1)} %get-tuple-element.68), channel_id=1, source_target_pairs={{0,1},{1,2},{2,3},{3,0},{4,5},{5,6},{6,7},{7,4},{8,9},{9,10},{10,1... | collective-permute-start | bytes 196616 | tf_op jit(solution)/shard_map/ppermute | solution.py:134
  57.6 5.9 %collective-permute-start.20 = (bf16[256,128]{1,0:T(8,128)(2,1)S(1)}, bf16[256,128]{1,0:T(8,128)(2,1)S(1)}, u32[]{:S(2)}, u32[]{:S(2)}) collective-permute-start(bf16[256,128]{1,0:T(8,128)(2,1)S(1)} %get-tuple-element.68), channel_id=1, source_target_pairs={{0,2},{1,3},{2,0},{3,1},{4,6},{5,7},{6,4},{7,5},{8,10},{9,11},{10,... | collective-permute-start | bytes 196616 | tf_op jit(solution)/shard_map/ppermute | solution.py:134
  60.5 4.3 %collective-permute-start.21 = (bf16[256,128]{1,0:T(8,128)(2,1)S(1)}, bf16[256,128]{1,0:T(8,128)(2,1)S(1)}, u32[]{:S(2)}, u32[]{:S(2)}) collective-permute-start(bf16[256,128]{1,0:T(8,128)(2,1)S(1)} %get-tuple-element.68), channel_id=1, source_target_pairs={{0,3},{1,0},{2,1},{3,2},{4,7},{5,4},{6,5},{7,6},{8,11},{9,8},{10,9... | collective-permute-start | bytes 196616 | tf_op jit(solution)/shard_map/ppermute | solution.py:134
  65.5 5.0 %collective-permute-start.22 = (f32[256,128]{1,0:T(8,128)S(1)}, f32[256,128]{1,0:T(8,128)S(1)}, u32[]{:S(2)}, u32[]{:S(2)}) collective-permute-start(f32[256,128]{1,0:T(8,128)S(1)} %get-tuple-element.75), channel_id=1, source_target_pairs={{0,8},{4,12},{8,0},{12,4},{16,24},{20,28},{24,16},{28,20},{1,9},{5... | collective-permute-start | bytes 393224 | tf_op jit(solution)/shard_map/ppermute | solution.py:130
  66.1 5.0 %collective-permute-start.23 = (f32[256,128]{1,0:T(8,128)S(1)}, f32[256,128]{1,0:T(8,128)S(1)}, u32[]{:S(2)}, u32[]{:S(2)}) collective-permute-start(f32[256,128]{1,0:T(8,128)S(1)} %get-tuple-element.77), channel_id=1, source_target_pairs={{0,16},{4,20},{8,24},{12,28},{16,0},{20,4},{24,8},{28,12},{1,17},{... | collective-permute-start | bytes 393224 | tf_op jit(solution)/shard_map/ppermute | solution.py:130
  66.6 6.5 %collective-permute-start.24 = (f32[256,128]{1,0:T(8,128)S(1)}, f32[256,128]{1,0:T(8,128)S(1)}, u32[]{:S(2)}, u32[]{:S(2)}) collective-permute-start(f32[256,128]{1,0:T(8,128)S(1)} %get-tuple-element.76), channel_id=1, source_target_pairs={{0,24},{4,28},{8,16},{12,20},{16,8},{20,12},{24,0},{28,4},{1,25},{... | collective-permute-start | bytes 393224 | tf_op jit(solution)/shard_map/ppermute | solution.py:130
  73.2 6.2 %collective-permute-start.25 = (bf16[256,128]{1,0:T(8,128)(2,1)S(1)}, bf16[256,128]{1,0:T(8,128)(2,1)S(1)}, u32[]{:S(2)}, u32[]{:S(2)}) collective-permute-start(bf16[256,128]{1,0:T(8,128)(2,1)S(1)} %get-tuple-element.66), channel_id=1, source_target_pairs={{0,1},{1,2},{2,3},{3,0},{4,5},{5,6},{6,7},{7,4},{8,9},{9,10},{10,1... | collective-permute-start | bytes 196616 | tf_op jit(solution)/shard_map/ppermute | solution.py:134
  73.2 9.6 %collective-permute-start.26 = (bf16[256,128]{1,0:T(8,128)(2,1)S(1)}, bf16[256,128]{1,0:T(8,128)(2,1)S(1)}, u32[]{:S(2)}, u32[]{:S(2)}) collective-permute-start(bf16[256,128]{1,0:T(8,128)(2,1)S(1)} %get-tuple-element.66), channel_id=1, source_target_pairs={{0,2},{1,3},{2,0},{3,1},{4,6},{5,7},{6,4},{7,5},{8,10},{9,11},{10,... | collective-permute-start | bytes 196616 | tf_op jit(solution)/shard_map/ppermute | solution.py:134
  77.2 6.3 %collective-permute-start.27 = (bf16[256,128]{1,0:T(8,128)(2,1)S(1)}, bf16[256,128]{1,0:T(8,128)(2,1)S(1)}, u32[]{:S(2)}, u32[]{:S(2)}) collective-permute-start(bf16[256,128]{1,0:T(8,128)(2,1)S(1)} %get-tuple-element.66), channel_id=1, source_target_pairs={{0,3},{1,0},{2,1},{3,2},{4,7},{5,4},{6,5},{7,6},{8,11},{9,8},{10,9... | collective-permute-start | bytes 196616 | tf_op jit(solution)/shard_map/ppermute | solution.py:134
  84.2 6.1 %collective-permute-start.28 = (f32[256,128]{1,0:T(8,128)S(1)}, f32[256,128]{1,0:T(8,128)S(1)}, u32[]{:S(2)}, u32[]{:S(2)}) collective-permute-start(f32[256,128]{1,0:T(8,128)S(1)} %get-tuple-element.72), channel_id=1, source_target_pairs={{0,8},{4,12},{8,0},{12,4},{16,24},{20,28},{24,16},{28,20},{1,9},{5... | collective-permute-start | bytes 393224 | tf_op jit(solution)/shard_map/ppermute | solution.py:130
  85.1 8.6 %collective-permute-start.29 = (f32[256,128]{1,0:T(8,128)S(1)}, f32[256,128]{1,0:T(8,128)S(1)}, u32[]{:S(2)}, u32[]{:S(2)}) collective-permute-start(f32[256,128]{1,0:T(8,128)S(1)} %get-tuple-element.74), channel_id=1, source_target_pairs={{0,16},{4,20},{8,24},{12,28},{16,0},{20,4},{24,8},{28,12},{1,17},{... | collective-permute-start | bytes 393224 | tf_op jit(solution)/shard_map/ppermute | solution.py:130
  86.3 7.4 %collective-permute-start.30 = (f32[256,128]{1,0:T(8,128)S(1)}, f32[256,128]{1,0:T(8,128)S(1)}, u32[]{:S(2)}, u32[]{:S(2)}) collective-permute-start(f32[256,128]{1,0:T(8,128)S(1)} %get-tuple-element.73), channel_id=1, source_target_pairs={{0,24},{4,28},{8,16},{12,20},{16,8},{20,12},{24,0},{28,4},{1,25},{... | collective-permute-start | bytes 393224 | tf_op jit(solution)/shard_map/ppermute | solution.py:130
  93.7 6.3 %collective-permute-start.31 = (bf16[256,128]{1,0:T(8,128)(2,1)S(1)}, bf16[256,128]{1,0:T(8,128)(2,1)S(1)}, u32[]{:S(2)}, u32[]{:S(2)}) collective-permute-start(bf16[256,128]{1,0:T(8,128)(2,1)S(1)} %get-tuple-element.64), channel_id=1, source_target_pairs={{0,1},{1,2},{2,3},{3,0},{4,5},{5,6},{6,7},{7,4},{8,9},{9,10},{10,1... | collective-permute-start | bytes 196616 | tf_op jit(solution)/shard_map/ppermute | solution.py:134
  95.1 6.6 %collective-permute-start.32 = (bf16[256,128]{1,0:T(8,128)(2,1)S(1)}, bf16[256,128]{1,0:T(8,128)(2,1)S(1)}, u32[]{:S(2)}, u32[]{:S(2)}) collective-permute-start(bf16[256,128]{1,0:T(8,128)(2,1)S(1)} %get-tuple-element.64), channel_id=1, source_target_pairs={{0,2},{1,3},{2,0},{3,1},{4,6},{5,7},{6,4},{7,5},{8,10},{9,11},{10,... | collective-permute-start | bytes 196616 | tf_op jit(solution)/shard_map/ppermute | solution.py:134
  97.3 4.9 %collective-permute-start.33 = (bf16[256,128]{1,0:T(8,128)(2,1)S(1)}, bf16[256,128]{1,0:T(8,128)(2,1)S(1)}, u32[]{:S(2)}, u32[]{:S(2)}) collective-permute-start(bf16[256,128]{1,0:T(8,128)(2,1)S(1)} %get-tuple-element.64), channel_id=1, source_target_pairs={{0,3},{1,0},{2,1},{3,2},{4,7},{5,4},{6,5},{7,6},{8,11},{9,8},{10,9... | collective-permute-start | bytes 196616 | tf_op jit(solution)/shard_map/ppermute | solution.py:134
  97.6 4.8 %collective-permute-start.34 = (bf16[256,128]{1,0:T(8,128)(2,1)S(1)}, bf16[256,128]{1,0:T(8,128)(2,1)S(1)}, u32[]{:S(2)}, u32[]{:S(2)}) collective-permute-start(bf16[256,128]{1,0:T(8,128)(2,1)S(1)} %get-tuple-element.64), channel_id=1, source_target_pairs={{0,8},{4,12},{8,0},{12,4},{16,24},{20,28},{24,16},{28,20},{1,9},{5... | collective-permute-start | bytes 196616 | tf_op jit(solution)/shard_map/ppermute | solution.py:130
  98.7 4.4 %collective-permute-start.35 = (bf16[256,128]{1,0:T(8,128)(2,1)S(1)}, bf16[256,128]{1,0:T(8,128)(2,1)S(1)}, u32[]{:S(2)}, u32[]{:S(2)}) collective-permute-start(bf16[256,128]{1,0:T(8,128)(2,1)S(1)} %get-tuple-element.64), channel_id=1, source_target_pairs={{0,16},{4,20},{8,24},{12,28},{16,0},{20,4},{24,8},{28,12},{1,17},{... | collective-permute-start | bytes 196616 | tf_op jit(solution)/shard_map/ppermute | solution.py:130
  100.0 5.2 %collective-permute-start.36 = (bf16[256,128]{1,0:T(8,128)(2,1)S(1)}, bf16[256,128]{1,0:T(8,128)(2,1)S(1)}, u32[]{:S(2)}, u32[]{:S(2)}) collective-permute-start(bf16[256,128]{1,0:T(8,128)(2,1)S(1)} %get-tuple-element.64), channel_id=1, source_target_pairs={{0,24},{4,28},{8,16},{12,20},{16,8},{20,12},{24,0},{28,4},{1,25},{... | collective-permute-start | bytes 196616 | tf_op jit(solution)/shard_map/ppermute | solution.py:130
  105.2 2.1 %collective-permute-start.37 = (bf16[1024,128]{1,0:T(8,128)(2,1)S(1)}, bf16[1024,128]{1,0:T(8,128)(2,1)S(1)}, u32[]{:S(2)}, u32[]{:S(2)}) collective-permute-start(bf16[1024,128]{1,0:T(8,128)(2,1)S(1)} %get-tuple-element.60), channel_id=1, source_target_pairs={{0,4},{4,0},{8,12},{12,8},{16,20},{20,16},{24,28},{28,24},{1,5},{5... | collective-permute-start | bytes 786440 | tf_op jit(solution)/shard_map/ppermute | solution.py:130
  106.2 1.7 %collective-permute-start.38 = (bf16[1024,128]{1,0:T(8,128)(2,1)S(1)}, bf16[1024,128]{1,0:T(8,128)(2,1)S(1)}, u32[]{:S(2)}, u32[]{:S(2)}) collective-permute-start(bf16[1024,128]{1,0:T(8,128)(2,1)S(1)} %get-tuple-element.61), channel_id=1, source_target_pairs={{0,4},{4,0},{8,12},{12,8},{16,20},{20,16},{24,28},{28,24},{1,5},{5... | collective-permute-start | bytes 786440 | tf_op jit(solution)/shard_map/ppermute | solution.py:130
  108.8 4.4 %collective-permute-start.39 = (f32[2,64,128]{2,1,0:T(8,128)S(1)}, f32[2,64,128]{2,1,0:T(8,128)S(1)}, u32[]{:S(2)}, u32[]{:S(2)}) collective-permute-start(f32[2,64,128]{2,1,0:T(8,128)S(1)} %get-tuple-element.87), channel_id=1, source_target_pairs={{0,8},{4,12},{8,0},{12,4},{16,24},{20,28},{24,16},{28,20},{1,9},{5... | collective-permute-start | bytes 196616 | tf_op jit(solution)/shard_map/ppermute | solution.py:130
  110.2 4.3 %collective-permute-start.40 = (f32[2,64,128]{2,1,0:T(8,128)S(1)}, f32[2,64,128]{2,1,0:T(8,128)S(1)}, u32[]{:S(2)}, u32[]{:S(2)}) collective-permute-start(f32[2,64,128]{2,1,0:T(8,128)S(1)} %get-tuple-element.89), channel_id=1, source_target_pairs={{0,16},{4,20},{8,24},{12,28},{16,0},{20,4},{24,8},{28,12},{1,17},{... | collective-permute-start | bytes 196616 | tf_op jit(solution)/shard_map/ppermute | solution.py:130
  111.1 5.2 %collective-permute-start.41 = (f32[2,64,128]{2,1,0:T(8,128)S(1)}, f32[2,64,128]{2,1,0:T(8,128)S(1)}, u32[]{:S(2)}, u32[]{:S(2)}) collective-permute-start(f32[2,64,128]{2,1,0:T(8,128)S(1)} %get-tuple-element.88), channel_id=1, source_target_pairs={{0,24},{4,28},{8,16},{12,20},{16,8},{20,12},{24,0},{28,4},{1,25},{... | collective-permute-start | bytes 196616 | tf_op jit(solution)/shard_map/ppermute | solution.py:130
  116.3 5.8 %collective-permute-start.42 = (f32[64,128]{1,0:T(8,128)S(1)}, f32[64,128]{1,0:T(8,128)S(1)}, u32[]{:S(2)}, u32[]{:S(2)}) collective-permute-start(f32[64,128]{1,0:T(8,128)S(1)} %get-tuple-element.103), channel_id=1, source_target_pairs={{0,1},{1,2},{2,3},{3,0},{4,5},{5,6},{6,7},{7,4},{8,9},{9,10},{10,1... | collective-permute-start | bytes 98312 | tf_op jit(solution)/shard_map/ppermute | solution.py:134
  117.7 5.2 %collective-permute-start.43 = (f32[64,128]{1,0:T(8,128)S(1)}, f32[64,128]{1,0:T(8,128)S(1)}, u32[]{:S(2)}, u32[]{:S(2)}) collective-permute-start(f32[64,128]{1,0:T(8,128)S(1)} %get-tuple-element.103), channel_id=1, source_target_pairs={{0,2},{1,3},{2,0},{3,1},{4,6},{5,7},{6,4},{7,5},{8,10},{9,11},{10,... | collective-permute-start | bytes 98312 | tf_op jit(solution)/shard_map/ppermute | solution.py:134
  118.4 4.5 %collective-permute-start.44 = (f32[64,128]{1,0:T(8,128)S(1)}, f32[64,128]{1,0:T(8,128)S(1)}, u32[]{:S(2)}, u32[]{:S(2)}) collective-permute-start(f32[64,128]{1,0:T(8,128)S(1)} %get-tuple-element.103), channel_id=1, source_target_pairs={{0,3},{1,0},{2,1},{3,2},{4,7},{5,4},{6,5},{7,6},{8,11},{9,8},{10,9... | collective-permute-start | bytes 98312 | tf_op jit(solution)/shard_map/ppermute | solution.py:134
  122.9 4.3 %collective-permute-start.45 = (f32[2,64,128]{2,1,0:T(8,128)S(1)}, f32[2,64,128]{2,1,0:T(8,128)S(1)}, u32[]{:S(2)}, u32[]{:S(2)}) collective-permute-start(f32[2,64,128]{2,1,0:T(8,128)S(1)} %get-tuple-element.101), channel_id=1, source_target_pairs={{0,8},{4,12},{8,0},{12,4},{16,24},{20,28},{24,16},{28,20},{1,9},{5... | collective-permute-start | bytes 196616 | tf_op jit(solution)/shard_map/ppermute | solution.py:130
  124.1 4.3 %collective-permute-start.46 = (f32[2,64,128]{2,1,0:T(8,128)S(1)}, f32[2,64,128]{2,1,0:T(8,128)S(1)}, u32[]{:S(2)}, u32[]{:S(2)}) collective-permute-start(f32[2,64,128]{2,1,0:T(8,128)S(1)} %get-tuple-element.101), channel_id=1, source_target_pairs={{0,16},{4,20},{8,24},{12,28},{16,0},{20,4},{24,8},{28,12},{1,17},{... | collective-permute-start | bytes 196616 | tf_op jit(solution)/shard_map/ppermute | solution.py:130
  125.1 5.2 %collective-permute-start.47 = (f32[2,64,128]{2,1,0:T(8,128)S(1)}, f32[2,64,128]{2,1,0:T(8,128)S(1)}, u32[]{:S(2)}, u32[]{:S(2)}) collective-permute-start(f32[2,64,128]{2,1,0:T(8,128)S(1)} %get-tuple-element.101), channel_id=1, source_target_pairs={{0,24},{4,28},{8,16},{12,20},{16,8},{20,12},{24,0},{28,4},{1,25},{... | collective-permute-start | bytes 196616 | tf_op jit(solution)/shard_map/ppermute | solution.py:130
  130.6 1.7 %collective-permute-start.48 = (f32[2,256,128]{2,1,0:T(8,128)S(1)}, f32[2,256,128]{2,1,0:T(8,128)S(1)}, u32[]{:S(2)}, u32[]{:S(2)}) collective-permute-start(f32[2,256,128]{2,1,0:T(8,128)S(1)} %maximum_select_fusion.3), channel_id=1, source_target_pairs={{0,4},{4,0},{8,12},{12,8},{16,20},{20,16},{24,28},{28,24},{1,5},{5... | collective-permute-start | bytes 786440 | tf_op jit(solution)/shard_map/ppermute | solution.py:130
  130.7 1.6 %collective-permute-start.49 = (f32[128,128]{1,0:T(8,128)S(1)}, f32[128,128]{1,0:T(8,128)S(1)}, u32[]{:S(2)}, u32[]{:S(2)}) collective-permute-start(f32[128,128]{1,0:T(8,128)S(1)} %get-tuple-element.97), channel_id=1, source_target_pairs={{0,4},{4,0},{8,12},{12,8},{16,20},{20,16},{24,28},{28,24},{1,5},{5... | collective-permute-start | bytes 196616 | tf_op jit(solution)/shard_map/ppermute | solution.py:130
  (6 other events, 40.7 us)

commit v4 on v2

--- a/solution.py
+++ b/solution.py
@@ -24,7 +24,7 @@
     return pl.reciprocal(x, approx=True)
 
 
-def finish_kernel(total_rows, gram_ref, cross_ref, y_ref, orbitals_ref, projected_ref, inverse_ref):
+def factor_kernel(total_rows, gram_ref, y_ref, orbitals_ref, inverse_ref):
     k = gram_ref.shape[0]
     panels = k // PANEL
     row_id = lax.broadcasted_iota(jnp.int32, (PANEL, LANES), 0)
@@ -108,22 +108,41 @@
     inv = inverse_ref[...]
     nt = (((1,), (1,)), ((), ()))
     orbitals_ref[...] = lax.dot_general(y_ref[...], inv, nt, precision=HI, preferred_element_type=jnp.float32)
+
+
+def project_kernel(total_rows, inverse_ref, cross_ref, projected_ref):
+    inv = inverse_ref[...]
+    nt = (((1,), (1,)), ((), ()))
     half = jnp.dot(inv, cross_ref[...], precision=HI, preferred_element_type=jnp.float32)
     full = lax.dot_general(half, inv, nt, precision=HI, preferred_element_type=jnp.float32)
-    projected_ref[...] = (full + full.T) * (0.5 * scale)
-
-def finish(gram, cross, y, total_rows):
+    projected_ref[...] = (full + full.T) * (0.5 / total_rows)
+
+
+def factorize(gram, y, total_rows):
     k = gram.shape[0]
     f32 = jnp.float32
     return pl.pallas_call(
-        functools.partial(finish_kernel, total_rows),
+        functools.partial(factor_kernel, total_rows),
         out_shape=(jax.ShapeDtypeStruct(y.shape, f32), jax.ShapeDtypeStruct((k, k), f32)),
-        in_specs=[pl.BlockSpec(memory_space=pltpu.VMEM)] * 3,
-        out_specs=(pl.BlockSpec(memory_space=pltpu.VMEM),) * 2,
-        scratch_shapes=[pltpu.VMEM((k, k), f32)],
+        in_specs=[VMEM] * 2,
+        out_specs=(VMEM,) * 2,
         compiler_params=pltpu.CompilerParams(vmem_limit_bytes=32 * 1024 * 1024),
-        name="finish",
-    )(gram, cross, y)
+        cost_estimate=pl.CostEstimate(
+            flops=0, bytes_accessed=80 * gram.size, transcendentals=0
+        ),
+        name="factorize",
+    )(gram, y)
+
+
+def project(inverse, cross, total_rows):
+    return pl.pallas_call(
+        functools.partial(project_kernel, total_rows),
+        out_shape=jax.ShapeDtypeStruct(cross.shape, jnp.float32),
+        in_specs=[VMEM] * 2,
+        out_specs=VMEM,
+        compiler_params=pltpu.CompilerParams(vmem_limit_bytes=32 * 1024 * 1024),
+        name="project",
+    )(inverse, cross)
 
 
 def exchanged(x, axis, size, apart):
@@ -347,12 +366,13 @@
         return jnp.where(first_core, *ordered)
 
     own, other = halves(orbitals_in)
-    start = jnp.concatenate([own, core_swap(other, rows)], 0)
 
     by_owner = hblocks.reshape(cols, PB * slots, BS * BS)
     pieces = pack(col[None], by_owner, places)
-    key, pieces, start = lax.optimization_barrier((key, pieces, start))
+    key, pieces, other = lax.optimization_barrier((key, pieces, other))
+    start = jnp.concatenate([own, core_swap(other, rows)], 0)
     pieces = [shifted(piece, "col", cols, s) for s, piece in enumerate(pieces, 1)]
+    pieces, start = lax.optimization_barrier((pieces, start))
 
     def gather(v):
         return jnp.concatenate([v] + [shifted(v, "col", cols, s) for s in range(1, cols)], 0)
@@ -421,13 +441,19 @@
     parts = [x.reshape(chips, share, half) for x in (gram_part, cross_part)]
     parts = by_distance(jnp.stack(parts, 1), chip)
     total = sum([chip_swap(parts[s], rows, s) for s in range(1, chips)], parts[0])
+
+    def chip_shares(x):
+        return [x] + [chip_swap(x, rows, s) for s in range(1, chips)]
+
+    def whole(shares):
+        x = by_distance(jnp.stack(shares), chip).reshape(k, half)
+        x = joined(x[:half], x[half:], 0)
+        return joined(x, core_swap(x, rows), 1)
+
     cross_share = sum([shifted(total[1], "col", cols, s) for s in range(1, cols)], total[1])
-    total = jnp.stack([total[0], cross_share])
-    total = jnp.stack([total] + [chip_swap(total, rows, s) for s in range(1, chips)])
-    total = by_distance(total, chip).swapaxes(0, 1).reshape(2, k, half)
-    total = joined(total[:, :half], total[:, half:], 1)
-    total = joined(total, core_swap(total, rows), 2)
-    return finish(total[0], total[1], filtered, total_rows)
+    orbitals, inverse = factorize(whole(chip_shares(total[0])), filtered, total_rows)
+    inverse, shares = lax.optimization_barrier((inverse, chip_shares(cross_share)))
+    return orbitals, project(inverse, whole(shares), total_rows)
 
 
 def solution(mesh):

time: 136 us -> 135 us (level)
  waiting for transfers between devices: 46.6 us -> 42.3 us
  starting transfers between devices: 60.2 us -> 63.3 us
    ppermute x31 -> x35, waiting for transfers between devices: 28 us -> 23.9 us  [exchanged(): return lax.ppermute(x, axis, [(i, i ^ apart) for i in range(size)])]
    ppermute x31 -> x35, starting transfers between devices: 27.7 us -> 30.8 us  [exchanged(): return lax.ppermute(x, axis, [(i, i ^ apart) for i in range(size)])]
    pallas_call x1 -> x2, Pallas kernels: 8.78 us -> 9.72 us  [the longest x1 7.94 us: factorize(): pl.pallas_call(functools.partial(factor_kernel, total_rows), out_shape=(j...]
  transfers between devices with their start and end apart: 49 -> 53, of which waited for: 34 -> 31; matrix products, arithmetic and copies ran while one was open for 2% -> 1% of each run, Pallas kernels for 3% -> 8%
where the time goes in v4:
time: 135 us
  starting transfers between devices  63.3 us (47%)
  waiting for transfers between devices  42.3 us (31%)
  Pallas kernels  17.5 us (13%)
  matrix products  4.23 us (3%)
  local copies, waits for them, and re-layouts  2.78 us (2%)
  between operations  2.53 us (2%)
  other arithmetic  2.39 us (2%)
    ppermute x18, starting transfers between devices, shifted(): return lax.ppermute(x, axis, [(i, (i + step) % size) for i in range(size)])  32.5 us
    ppermute x35, starting transfers between devices, exchanged(): return lax.ppermute(x, axis, [(i, i ^ apart) for i in range(size)])  30.8 us
    ppermute x35, waiting for transfers between devices, exchanged(): return lax.ppermute(x, axis, [(i, i ^ apart) for i in range(size)])  23.9 us
    ppermute x18, waiting for transfers between devices, shifted(): return lax.ppermute(x, axis, [(i, (i + step) % size) for i in range(size)])  18.4 us
    pallas_call x1, Pallas kernels, factorize(): pl.pallas_call(functools.partial(factor_kernel, total_rows), out_shape=(j...  7.94 us
    pallas_call x1, Pallas kernels, direct_rows(): pl.pallas_call(functools.partial(direct_kernel, rows, slots), out_shape=(...  3.08 us
    dot_general x4, matrix products, partial_product(): return jnp.dot(tile, gathered, preferred_element_type=jnp.float32)  2.82 us
  transfers between devices with their start and end apart: 53, of which 31 were waited for; matrix products, arithmetic and copies ran while one was open for 1% of the time, Pallas kernels for 8%

profile of v4, /device:TPU:0, one launch (start us, length us, event | category | flops | bytes accessed | tf_op | source)
XLA Modules:
  0.0 135.1 jit_solution(14285184972879546188)
XLA Ops:
  3.1 1.8 %pack.1 = (bf16[16,4224]{1,0:T(8,128)(2,1)}, bf16[16,4224]{1,0:T(8,128)(2,1)}, bf16[16,4224]{1,0:T(8,128)(2,1)}) custom-call(s32[1]{0:T(128)} %bitcast.1.col_ref, bf16[4,16,4096]{2,1,0:T(8,128)(2,1)} %bitcast.91, f32[4,16]{1,0:T(4,128)} %reshape.253.places_ref), custom_call_target="tpu_custom_call" | custom-call | tf_op jit(solution)/shard_map/pack/pallas_call | solution.py:193
  5.4 2.6 %collective-permute-start = (bf16[16,4224]{1,0:T(8,128)(2,1)}, bf16[16,4224]{1,0:T(8,128)(2,1)S(1)}, u32[]{:S(2)}, u32[]{:S(2)}) collective-permute-start(bf16[16,4224]{1,0:T(8,128)(2,1)} %get-tuple-element.43), channel_id=1, source_target_pairs={{0,1},{1,2},{2,3},{3,0},{4,5},{5,6},{6,7},{7,4},{8,9},{9,10},{10,1... | collective-permute-start | bytes 405512 | tf_op jit(solution)/shard_map/ppermute | solution.py:153
  8.0 2.6 %collective-permute-start.1 = (bf16[16,4224]{1,0:T(8,128)(2,1)}, bf16[16,4224]{1,0:T(8,128)(2,1)S(1)}, u32[]{:S(2)}, u32[]{:S(2)}) collective-permute-start(bf16[16,4224]{1,0:T(8,128)(2,1)} %get-tuple-element.44), channel_id=1, source_target_pairs={{0,2},{1,3},{2,0},{3,1},{4,6},{5,7},{6,4},{7,5},{8,10},{9,11},{10,... | collective-permute-start | bytes 405512 | tf_op jit(solution)/shard_map/ppermute | solution.py:153
  10.6 1.3 collective-permute-start.2
  13.7 2.3 %mirror.1.mirrored = bf16[2,512,512]{2,1,0:T(8,128)(2,1)S(1)} custom-call(s32[1,64]{1,0:T(1,128)S(1)} %reshape.251.key_ref, bf16[64,4096]{1,0:T(8,128)(2,1)S(1)} %bitcast.92, bf16[2,4096]{1,0:T(2,128)(2,1)S(1)} %copy-done.3), custom_call_target="tpu_custom_call" | custom-call | flops 67108864 | bytes 786432 | tf_op jit(solution)/shard_map/mirror/pallas_call | solution.py:233
  16.0 4.3 %collective-permute-done.1.refs_1_ = bf16[16,4224]{1,0:T(8,128)(2,1)S(1)} collective-permute-done((bf16[16,4224]{1,0:T(8,128)(2,1)}, bf16[16,4224]{1,0:T(8,128)(2,1)S(1)}, u32[]{:S(2)}, u32[]{:S(2)}) %collective-permute-start.1) | collective-permute-done | bytes 135200 | tf_op jit(solution)/shard_map/ppermute | solution.py:153
  20.3 3.1 %direct_rows.1 = (bf16[128,1024]{1,0:T(8,128)(2,1)S(1)}, bf16[128,1024]{1,0:T(8,128)(2,1)S(1)}, bf16[128,1024]{1,0:T(8,128)(2,1)S(1)}, bf16[128,1024]{1,0:T(8,128)(2,1)S(1)}) custom-call(s32[1]{0:T(128)} %bitcast.1.col_ref, bf16[4,16,4096]{2,1,0:T(8,128)(2,1)S(1)} %bitcast.93, f32[4,16]{1,0:T(4,128)S(1)} %copy-done.2, ...), custom_call_target="tpu_custom_call" | custom-call | tf_op jit(solution)/shard_map/direct_rows/pallas_call | solution.py:285
  23.5 2.5 %collective-permute-start.10 = (bf16[128,1024]{1,0:T(8,128)(2,1)S(1)}, bf16[128,1024]{1,0:T(8,128)(2,1)S(1)}, u32[]{:S(2)}, u32[]{:S(2)}) collective-permute-start(bf16[128,1024]{1,0:T(8,128)(2,1)S(1)} %get-tuple-element.61), channel_id=1, source_target_pairs={{0,24},{4,28},{8,16},{12,20},{16,8},{20,12},{24,0},{28,4},{1,25},{... | collective-permute-start | bytes 786440 | tf_op jit(solution)/shard_map/ppermute | solution.py:149
  27.1 3.4 %collective-permute-start.5 = (bf16[256,128]{1,0:T(8,128)(2,1)S(1)}, bf16[256,128]{1,0:T(8,128)(2,1)S(1)}, u32[]{:S(2)}, u32[]{:S(2)}) collective-permute-start(bf16[256,128]{1,0:T(8,128)(2,1)S(1)} %convert_element_type.18), channel_id=1, source_target_pairs={{0,1},{1,2},{2,3},{3,0},{4,5},{5,6},{6,7},{7,4},{8,9},{9,10},{10,1... | collective-permute-start | bytes 196616 | tf_op jit(solution)/shard_map/ppermute | solution.py:153
  30.5 1.6 %collective-permute-start.6 = (bf16[256,128]{1,0:T(8,128)(2,1)S(1)}, bf16[256,128]{1,0:T(8,128)(2,1)S(1)}, u32[]{:S(2)}, u32[]{:S(2)}) collective-permute-start(bf16[256,128]{1,0:T(8,128)(2,1)S(1)} %convert_element_type.18), channel_id=1, source_target_pairs={{0,2},{1,3},{2,0},{3,1},{4,6},{5,7},{6,4},{7,5},{8,10},{9,11},{10,... | collective-permute-start | bytes 196616 | tf_op jit(solution)/shard_map/ppermute | solution.py:153
  32.2 2.5 %collective-permute-done.5 = bf16[256,128]{1,0:T(8,128)(2,1)S(1)} collective-permute-done((bf16[256,128]{1,0:T(8,128)(2,1)S(1)}, bf16[256,128]{1,0:T(8,128)(2,1)S(1)}, u32[]{:S(2)}, u32[]{:S(2)}) %collective-permute-start.5) | collective-permute-done | bytes 65568 | tf_op jit(solution)/shard_map/ppermute | solution.py:153
  34.6 1.9 %collective-permute-start.7 = (bf16[256,128]{1,0:T(8,128)(2,1)S(1)}, bf16[256,128]{1,0:T(8,128)(2,1)S(1)}, u32[]{:S(2)}, u32[]{:S(2)}) collective-permute-start(bf16[256,128]{1,0:T(8,128)(2,1)S(1)} %convert_element_type.18), channel_id=1, source_target_pairs={{0,3},{1,0},{2,1},{3,2},{4,7},{5,4},{6,5},{7,6},{8,11},{9,8},{10,9... | collective-permute-start | bytes 196616 | tf_op jit(solution)/shard_map/ppermute | solution.py:153
  36.8 2.1 %collective-permute-done.7 = bf16[256,128]{1,0:T(8,128)(2,1)S(1)} collective-permute-done((bf16[256,128]{1,0:T(8,128)(2,1)S(1)}, bf16[256,128]{1,0:T(8,128)(2,1)S(1)}, u32[]{:S(2)}, u32[]{:S(2)}) %collective-permute-start.7) | collective-permute-done | bytes 65568 | tf_op jit(solution)/shard_map/ppermute | solution.py:153
  43.0 1.6 %collective-permute-start.15 = (f32[256,128]{1,0:T(8,128)S(1)}, f32[256,128]{1,0:T(8,128)S(1)}, u32[]{:S(2)}, u32[]{:S(2)}) collective-permute-start(f32[256,128]{1,0:T(8,128)S(1)} %get-tuple-element.90), channel_id=1, source_target_pairs={{0,8},{4,12},{8,0},{12,4},{16,24},{20,28},{24,16},{28,20},{1,9},{5... | collective-permute-start | bytes 393224 | tf_op jit(solution)/shard_map/ppermute | solution.py:149
  44.6 1.5 %collective-permute-start.16 = (f32[256,128]{1,0:T(8,128)S(1)}, f32[256,128]{1,0:T(8,128)S(1)}, u32[]{:S(2)}, u32[]{:S(2)}) collective-permute-start(f32[256,128]{1,0:T(8,128)S(1)} %get-tuple-element.92), channel_id=1, source_target_pairs={{0,16},{4,20},{8,24},{12,28},{16,0},{20,4},{24,8},{28,12},{1,17},{... | collective-permute-start | bytes 393224 | tf_op jit(solution)/shard_map/ppermute | solution.py:149
  49.0 3.6 %collective-permute-done.16 = f32[256,128]{1,0:T(8,128)S(1)} collective-permute-done((f32[256,128]{1,0:T(8,128)S(1)}, f32[256,128]{1,0:T(8,128)S(1)}, u32[]{:S(2)}, u32[]{:S(2)}) %collective-permute-start.16) | collective-permute-done | bytes 131104 | tf_op jit(solution)/shard_map/ppermute | solution.py:149
  52.7 3.3 %collective-permute-start.18 = (bf16[256,128]{1,0:T(8,128)(2,1)S(1)}, bf16[256,128]{1,0:T(8,128)(2,1)S(1)}, u32[]{:S(2)}, u32[]{:S(2)}) collective-permute-start(bf16[256,128]{1,0:T(8,128)(2,1)S(1)} %get-tuple-element.82), channel_id=1, source_target_pairs={{0,1},{1,2},{2,3},{3,0},{4,5},{5,6},{6,7},{7,4},{8,9},{9,10},{10,1... | collective-permute-start | bytes 196616 | tf_op jit(solution)/shard_map/ppermute | solution.py:153
  56.0 1.6 %collective-permute-start.19 = (bf16[256,128]{1,0:T(8,128)(2,1)S(1)}, bf16[256,128]{1,0:T(8,128)(2,1)S(1)}, u32[]{:S(2)}, u32[]{:S(2)}) collective-permute-start(bf16[256,128]{1,0:T(8,128)(2,1)S(1)} %get-tuple-element.82), channel_id=1, source_target_pairs={{0,2},{1,3},{2,0},{3,1},{4,6},{5,7},{6,4},{7,5},{8,10},{9,11},{10,... | collective-permute-start | bytes 196616 | tf_op jit(solution)/shard_map/ppermute | solution.py:153
  58.4 1.2 collective-permute-done.18
  59.6 2.5 %collective-permute-done.19 = bf16[256,128]{1,0:T(8,128)(2,1)S(1)} collective-permute-done((bf16[256,128]{1,0:T(8,128)(2,1)S(1)}, bf16[256,128]{1,0:T(8,128)(2,1)S(1)}, u32[]{:S(2)}, u32[]{:S(2)}) %collective-permute-start.19) | collective-permute-done | bytes 65568 | tf_op jit(solution)/shard_map/ppermute | solution.py:153
  63.1 1.3 collective-permute-start.21
  65.2 1.5 %collective-permute-start.23 = (f32[256,128]{1,0:T(8,128)S(1)}, f32[256,128]{1,0:T(8,128)S(1)}, u32[]{:S(2)}, u32[]{:S(2)}) collective-permute-start(f32[256,128]{1,0:T(8,128)S(1)} %get-tuple-element.88), channel_id=1, source_target_pairs={{0,24},{4,28},{8,16},{12,20},{16,8},{20,12},{24,0},{28,4},{1,25},{... | collective-permute-start | bytes 393224 | tf_op jit(solution)/shard_map/ppermute | solution.py:149
  66.7 2.9 %collective-permute-done.21 = f32[256,128]{1,0:T(8,128)S(1)} collective-permute-done((f32[256,128]{1,0:T(8,128)S(1)}, f32[256,128]{1,0:T(8,128)S(1)}, u32[]{:S(2)}, u32[]{:S(2)}) %collective-permute-start.21) | collective-permute-done | bytes 131104 | tf_op jit(solution)/shard_map/ppermute | solution.py:149
  69.5 1.7 %collective-permute-done.22 = f32[256,128]{1,0:T(8,128)S(1)} collective-permute-done((f32[256,128]{1,0:T(8,128)S(1)}, f32[256,128]{1,0:T(8,128)S(1)}, u32[]{:S(2)}, u32[]{:S(2)}) %collective-permute-start.22) | collective-permute-done | bytes 131104 | tf_op jit(solution)/shard_map/ppermute | solution.py:149
  71.3 2.0 %collective-permute-start.24 = (bf16[256,128]{1,0:T(8,128)(2,1)S(1)}, bf16[256,128]{1,0:T(8,128)(2,1)S(1)}, u32[]{:S(2)}, u32[]{:S(2)}) collective-permute-start(bf16[256,128]{1,0:T(8,128)(2,1)S(1)} %get-tuple-element.80), channel_id=1, source_target_pairs={{0,1},{1,2},{2,3},{3,0},{4,5},{5,6},{6,7},{7,4},{8,9},{9,10},{10,1... | collective-permute-start | bytes 196616 | tf_op jit(solution)/shard_map/ppermute | solution.py:153
  74.0 1.8 %collective-permute-start.26 = (bf16[256,128]{1,0:T(8,128)(2,1)S(1)}, bf16[256,128]{1,0:T(8,128)(2,1)S(1)}, u32[]{:S(2)}, u32[]{:S(2)}) collective-permute-start(bf16[256,128]{1,0:T(8,128)(2,1)S(1)} %get-tuple-element.80), channel_id=1, source_target_pairs={{0,3},{1,0},{2,1},{3,2},{4,7},{5,4},{6,5},{7,6},{8,11},{9,8},{10,9... | collective-permute-start | bytes 196616 | tf_op jit(solution)/shard_map/ppermute | solution.py:153
  75.7 1.7 %collective-permute-done.24 = bf16[256,128]{1,0:T(8,128)(2,1)S(1)} collective-permute-done((bf16[256,128]{1,0:T(8,128)(2,1)S(1)}, bf16[256,128]{1,0:T(8,128)(2,1)S(1)}, u32[]{:S(2)}, u32[]{:S(2)}) %collective-permute-start.24) | collective-permute-done | bytes 65568 | tf_op jit(solution)/shard_map/ppermute | solution.py:153
  77.4 1.5 %collective-permute-done.25 = bf16[256,128]{1,0:T(8,128)(2,1)S(1)} collective-permute-done((bf16[256,128]{1,0:T(8,128)(2,1)S(1)}, bf16[256,128]{1,0:T(8,128)(2,1)S(1)}, u32[]{:S(2)}, u32[]{:S(2)}) %collective-permute-start.25) | collective-permute-done | bytes 65568 | tf_op jit(solution)/shard_map/ppermute | solution.py:153
  79.7 1.3 collective-permute-start.27
  81.7 1.6 %collective-permute-start.29 = (f32[256,128]{1,0:T(8,128)S(1)}, f32[256,128]{1,0:T(8,128)S(1)}, u32[]{:S(2)}, u32[]{:S(2)}) collective-permute-start(f32[256,128]{1,0:T(8,128)S(1)} %get-tuple-element.85), channel_id=1, source_target_pairs={{0,24},{4,28},{8,16},{12,20},{16,8},{20,12},{24,0},{28,4},{1,25},{... | collective-permute-start | bytes 393224 | tf_op jit(solution)/shard_map/ppermute | solution.py:149
  83.2 1.5 %collective-permute-done.27 = f32[256,128]{1,0:T(8,128)S(1)} collective-permute-done((f32[256,128]{1,0:T(8,128)S(1)}, f32[256,128]{1,0:T(8,128)S(1)}, u32[]{:S(2)}, u32[]{:S(2)}) %collective-permute-start.27) | collective-permute-done | bytes 131104 | tf_op jit(solution)/shard_map/ppermute | solution.py:149
  84.7 1.2 collective-permute-done.28
  85.9 1.6 %collective-permute-done.29 = f32[256,128]{1,0:T(8,128)S(1)} collective-permute-done((f32[256,128]{1,0:T(8,128)S(1)}, f32[256,128]{1,0:T(8,128)S(1)}, u32[]{:S(2)}, u32[]{:S(2)}) %collective-permute-start.29) | collective-permute-done | bytes 131104 | tf_op jit(solution)/shard_map/ppermute | solution.py:149
  87.6 1.2 collective-permute-start.30
  88.8 2.1 %collective-permute-start.31 = (bf16[256,128]{1,0:T(8,128)(2,1)S(1)}, bf16[256,128]{1,0:T(8,128)(2,1)S(1)}, u32[]{:S(2)}, u32[]{:S(2)}) collective-permute-start(bf16[256,128]{1,0:T(8,128)(2,1)S(1)} %get-tuple-element.78), channel_id=1, source_target_pairs={{0,2},{1,3},{2,0},{3,1},{4,6},{5,7},{6,4},{7,5},{8,10},{9,11},{10,... | collective-permute-start | bytes 196616 | tf_op jit(solution)/shard_map/ppermute | solution.py:153
  91.9 1.2 collective-permute-start.33
  94.2 1.2 collective-permute-start.35
  96.2 1.2 collective-permute-done.34
  97.4 2.0 %collective-permute-done.35 = bf16[256,128]{1,0:T(8,128)(2,1)S(1)} collective-permute-done((bf16[256,128]{1,0:T(8,128)(2,1)S(1)}, bf16[256,128]{1,0:T(8,128)(2,1)S(1)}, u32[]{:S(2)}, u32[]{:S(2)}) %collective-permute-start.35) | collective-permute-done | bytes 65568 | tf_op jit(solution)/shard_map/ppermute | solution.py:149
  104.9 1.8 %collective-permute-start.40 = (f32[2,64,128]{2,1,0:T(8,128)S(1)}, f32[2,64,128]{2,1,0:T(8,128)S(1)}, u32[]{:S(2)}, u32[]{:S(2)}) collective-permute-start(f32[2,64,128]{2,1,0:T(8,128)S(1)} %get-tuple-element.94), channel_id=1, source_target_pairs={{0,24},{4,28},{8,16},{12,20},{16,8},{20,12},{24,0},{28,4},{1,25},{... | collective-permute-start | bytes 196616 | tf_op jit(solution)/shard_map/ppermute | solution.py:149
  107.5 1.6 %collective-permute-done.39 = f32[2,64,128]{2,1,0:T(8,128)S(1)} collective-permute-done((f32[2,64,128]{2,1,0:T(8,128)S(1)}, f32[2,64,128]{2,1,0:T(8,128)S(1)}, u32[]{:S(2)}, u32[]{:S(2)}) %collective-permute-start.39) | collective-permute-done | bytes 65568 | tf_op jit(solution)/shard_map/ppermute | solution.py:149
  110.1 1.3 collective-permute-start.41
  115.5 2.7 %collective-permute-start.48 = (f32[64,128]{1,0:T(8,128)S(1)}, f32[64,128]{1,0:T(8,128)S(1)}, u32[]{:S(2)}, u32[]{:S(2)}) collective-permute-start(f32[64,128]{1,0:T(8,128)S(1)} %get-tuple-element.118), channel_id=1, source_target_pairs={{0,3},{1,0},{2,1},{3,2},{4,7},{5,4},{6,5},{7,6},{8,11},{9,8},{10,9... | collective-permute-start | bytes 98312 | tf_op jit(solution)/shard_map/ppermute | solution.py:153
  120.1 1.3 collective-permute-start.49
  121.4 1.2 collective-permute-start.50
  123.7 7.9 %factorize.1 = (f32[128,256]{1,0:T(8,128)}, f32[256,256]{1,0:T(8,128)S(1)}) custom-call(f32[256,256]{1,0:T(8,128)S(1)} %maximum_select_fusion.2.gram_ref, f32[128,256]{1,0:T(8,128)S(1)} %maximum_select_fusion.5.y_ref), custom_call_target="tpu_custom_call" | custom-call | bytes 5242880 | tf_op jit(solution)/shard_map/factorize/pallas_call | solution.py:124
  131.9 1.3 collective-permute-done.52
  133.3 1.8 %project.1 = f32[256,256]{1,0:T(8,128)} custom-call(f32[256,256]{1,0:T(8,128)S(1)} %get-tuple-element.71.inverse_ref, f32[256,256]{1,0:T(8,128)S(1)} %maximum_select_fusion.3.cross_ref), custom_call_target="tpu_custom_call" | custom-call | tf_op jit(solution)/shard_map/project/pallas_call | solution.py:138
  (134 shorter events, 34.0 us)
Async XLA Ops:
  4.9 11.0 %collective-permute-start.3 = (f32[128,128]{1,0:T(8,128)S(1)}, f32[128,128]{1,0:T(8,128)S(1)}, u32[]{:S(2)}, u32[]{:S(2)}) collective-permute-start(f32[128,128]{1,0:T(8,128)S(1)} %get-tuple-element.46), channel_id=1, source_target_pairs={{0,4},{4,0},{8,12},{12,8},{16,20},{20,16},{24,28},{28,24},{1,5},{5... | collective-permute-start | bytes 196616 | tf_op jit(solution)/shard_map/ppermute | solution.py:149
  5.4 10.6 %collective-permute-start = (bf16[16,4224]{1,0:T(8,128)(2,1)}, bf16[16,4224]{1,0:T(8,128)(2,1)S(1)}, u32[]{:S(2)}, u32[]{:S(2)}) collective-permute-start(bf16[16,4224]{1,0:T(8,128)(2,1)} %get-tuple-element.43), channel_id=1, source_target_pairs={{0,1},{1,2},{2,3},{3,0},{4,5},{5,6},{6,7},{7,4},{8,9},{9,10},{10,1... | collective-permute-start | bytes 405512 | tf_op jit(solution)/shard_map/ppermute | solution.py:153
  8.0 12.3 %collective-permute-start.1 = (bf16[16,4224]{1,0:T(8,128)(2,1)}, bf16[16,4224]{1,0:T(8,128)(2,1)S(1)}, u32[]{:S(2)}, u32[]{:S(2)}) collective-permute-start(bf16[16,4224]{1,0:T(8,128)(2,1)} %get-tuple-element.44), channel_id=1, source_target_pairs={{0,2},{1,3},{2,0},{3,1},{4,6},{5,7},{6,4},{7,5},{8,10},{9,11},{10,... | collective-permute-start | bytes 405512 | tf_op jit(solution)/shard_map/ppermute | solution.py:153
  10.6 9.8 %collective-permute-start.2 = (bf16[16,4224]{1,0:T(8,128)(2,1)}, bf16[16,4224]{1,0:T(8,128)(2,1)S(1)}, u32[]{:S(2)}, u32[]{:S(2)}) collective-permute-start(bf16[16,4224]{1,0:T(8,128)(2,1)} %get-tuple-element.45), channel_id=1, source_target_pairs={{0,3},{1,0},{2,1},{3,2},{4,7},{5,4},{6,5},{7,6},{8,11},{9,8},{10,9... | collective-permute-start | bytes 405512 | tf_op jit(solution)/shard_map/ppermute | solution.py:153
  23.4 3.6 %collective-permute-start.4 = (bf16[2,512,512]{2,1,0:T(8,128)(2,1)S(1)}, bf16[2,512,512]{2,1,0:T(8,128)(2,1)S(1)}, u32[]{:S(2)}, u32[]{:S(2)}) collective-permute-start(bf16[2,512,512]{2,1,0:T(8,128)(2,1)S(1)} %mirror.1.mirrored), channel_id=1, source_target_pairs={{0,4},{4,0},{8,12},{12,8},{16,20},{20,16},{24,28},{28,24},{1,5},{5... | collective-permute-start | bytes 3145736 | tf_op jit(solution)/shard_map/ppermute | solution.py:149
  23.5 15.4 %collective-permute-start.10 = (bf16[128,1024]{1,0:T(8,128)(2,1)S(1)}, bf16[128,1024]{1,0:T(8,128)(2,1)S(1)}, u32[]{:S(2)}, u32[]{:S(2)}) collective-permute-start(bf16[128,1024]{1,0:T(8,128)(2,1)S(1)} %get-tuple-element.61), channel_id=1, source_target_pairs={{0,24},{4,28},{8,16},{12,20},{16,8},{20,12},{24,0},{28,4},{1,25},{... | collective-permute-start | bytes 786440 | tf_op jit(solution)/shard_map/ppermute | solution.py:149
  26.0 12.9 %collective-permute-start.8 = (bf16[128,1024]{1,0:T(8,128)(2,1)S(1)}, bf16[128,1024]{1,0:T(8,128)(2,1)S(1)}, u32[]{:S(2)}, u32[]{:S(2)}) collective-permute-start(bf16[128,1024]{1,0:T(8,128)(2,1)S(1)} %get-tuple-element.59), channel_id=1, source_target_pairs={{0,8},{4,12},{8,0},{12,4},{16,24},{20,28},{24,16},{28,20},{1,9},{5... | collective-permute-start | bytes 786440 | tf_op jit(solution)/shard_map/ppermute | solution.py:149
  26.5 12.4 %collective-permute-start.9 = (bf16[128,1024]{1,0:T(8,128)(2,1)S(1)}, bf16[128,1024]{1,0:T(8,128)(2,1)S(1)}, u32[]{:S(2)}, u32[]{:S(2)}) collective-permute-start(bf16[128,1024]{1,0:T(8,128)(2,1)S(1)} %get-tuple-element.60), channel_id=1, source_target_pairs={{0,16},{4,20},{8,24},{12,28},{16,0},{20,4},{24,8},{28,12},{1,17},{... | collective-permute-start | bytes 786440 | tf_op jit(solution)/shard_map/ppermute | solution.py:149
  27.1 7.6 %collective-permute-start.5 = (bf16[256,128]{1,0:T(8,128)(2,1)S(1)}, bf16[256,128]{1,0:T(8,128)(2,1)S(1)}, u32[]{:S(2)}, u32[]{:S(2)}) collective-permute-start(bf16[256,128]{1,0:T(8,128)(2,1)S(1)} %convert_element_type.18), channel_id=1, source_target_pairs={{0,1},{1,2},{2,3},{3,0},{4,5},{5,6},{6,7},{7,4},{8,9},{9,10},{10,1... | collective-permute-start | bytes 196616 | tf_op jit(solution)/shard_map/ppermute | solution.py:153
  30.5 6.3 %collective-permute-start.6 = (bf16[256,128]{1,0:T(8,128)(2,1)S(1)}, bf16[256,128]{1,0:T(8,128)(2,1)S(1)}, u32[]{:S(2)}, u32[]{:S(2)}) collective-permute-start(bf16[256,128]{1,0:T(8,128)(2,1)S(1)} %convert_element_type.18), channel_id=1, source_target_pairs={{0,2},{1,3},{2,0},{3,1},{4,6},{5,7},{6,4},{7,5},{8,10},{9,11},{10,... | collective-permute-start | bytes 196616 | tf_op jit(solution)/shard_map/ppermute | solution.py:153
  34.6 4.3 %collective-permute-start.7 = (bf16[256,128]{1,0:T(8,128)(2,1)S(1)}, bf16[256,128]{1,0:T(8,128)(2,1)S(1)}, u32[]{:S(2)}, u32[]{:S(2)}) collective-permute-start(bf16[256,128]{1,0:T(8,128)(2,1)S(1)} %convert_element_type.18), channel_id=1, source_target_pairs={{0,3},{1,0},{2,1},{3,2},{4,7},{5,4},{6,5},{7,6},{8,11},{9,8},{10,9... | collective-permute-start | bytes 196616 | tf_op jit(solution)/shard_map/ppermute | solution.py:153
  39.6 2.1 %collective-permute-start.14 = (bf16[128,1024]{1,0:T(8,128)(2,1)S(1)}, bf16[128,1024]{1,0:T(8,128)(2,1)S(1)}, u32[]{:S(2)}, u32[]{:S(2)}) collective-permute-start(bf16[128,1024]{1,0:T(8,128)(2,1)S(1)} %collective-permute-done.10.refs_3_), channel_id=1, source_target_pairs={{0,4},{4,0},{8,12},{12,8},{16,20},{20,16},{24,28},{28,24},{1,5},{5... | collective-permute-start | bytes 786440 | tf_op jit(solution)/shard_map/ppermute | solution.py:149
  43.0 6.0 %collective-permute-start.15 = (f32[256,128]{1,0:T(8,128)S(1)}, f32[256,128]{1,0:T(8,128)S(1)}, u32[]{:S(2)}, u32[]{:S(2)}) collective-permute-start(f32[256,128]{1,0:T(8,128)S(1)} %get-tuple-element.90), channel_id=1, source_target_pairs={{0,8},{4,12},{8,0},{12,4},{16,24},{20,28},{24,16},{28,20},{1,9},{5... | collective-permute-start | bytes 393224 | tf_op jit(solution)/shard_map/ppermute | solution.py:149
  44.6 8.1 %collective-permute-start.16 = (f32[256,128]{1,0:T(8,128)S(1)}, f32[256,128]{1,0:T(8,128)S(1)}, u32[]{:S(2)}, u32[]{:S(2)}) collective-permute-start(f32[256,128]{1,0:T(8,128)S(1)} %get-tuple-element.92), channel_id=1, source_target_pairs={{0,16},{4,20},{8,24},{12,28},{16,0},{20,4},{24,8},{28,12},{1,17},{... | collective-permute-start | bytes 393224 | tf_op jit(solution)/shard_map/ppermute | solution.py:149
  46.1 6.5 %collective-permute-start.17 = (f32[256,128]{1,0:T(8,128)S(1)}, f32[256,128]{1,0:T(8,128)S(1)}, u32[]{:S(2)}, u32[]{:S(2)}) collective-permute-start(f32[256,128]{1,0:T(8,128)S(1)} %get-tuple-element.91), channel_id=1, source_target_pairs={{0,24},{4,28},{8,16},{12,20},{16,8},{20,12},{24,0},{28,4},{1,25},{... | collective-permute-start | bytes 393224 | tf_op jit(solution)/shard_map/ppermute | solution.py:149
  52.7 6.9 %collective-permute-start.18 = (bf16[256,128]{1,0:T(8,128)(2,1)S(1)}, bf16[256,128]{1,0:T(8,128)(2,1)S(1)}, u32[]{:S(2)}, u32[]{:S(2)}) collective-permute-start(bf16[256,128]{1,0:T(8,128)(2,1)S(1)} %get-tuple-element.82), channel_id=1, source_target_pairs={{0,1},{1,2},{2,3},{3,0},{4,5},{5,6},{6,7},{7,4},{8,9},{9,10},{10,1... | collective-permute-start | bytes 196616 | tf_op jit(solution)/shard_map/ppermute | solution.py:153
  56.0 6.1 %collective-permute-start.19 = (bf16[256,128]{1,0:T(8,128)(2,1)S(1)}, bf16[256,128]{1,0:T(8,128)(2,1)S(1)}, u32[]{:S(2)}, u32[]{:S(2)}) collective-permute-start(bf16[256,128]{1,0:T(8,128)(2,1)S(1)} %get-tuple-element.82), channel_id=1, source_target_pairs={{0,2},{1,3},{2,0},{3,1},{4,6},{5,7},{6,4},{7,5},{8,10},{9,11},{10,... | collective-permute-start | bytes 196616 | tf_op jit(solution)/shard_map/ppermute | solution.py:153
  57.6 4.8 %collective-permute-start.20 = (bf16[256,128]{1,0:T(8,128)(2,1)S(1)}, bf16[256,128]{1,0:T(8,128)(2,1)S(1)}, u32[]{:S(2)}, u32[]{:S(2)}) collective-permute-start(bf16[256,128]{1,0:T(8,128)(2,1)S(1)} %get-tuple-element.82), channel_id=1, source_target_pairs={{0,3},{1,0},{2,1},{3,2},{4,7},{5,4},{6,5},{7,6},{8,11},{9,8},{10,9... | collective-permute-start | bytes 196616 | tf_op jit(solution)/shard_map/ppermute | solution.py:153
  63.1 6.4 %collective-permute-start.21 = (f32[256,128]{1,0:T(8,128)S(1)}, f32[256,128]{1,0:T(8,128)S(1)}, u32[]{:S(2)}, u32[]{:S(2)}) collective-permute-start(f32[256,128]{1,0:T(8,128)S(1)} %get-tuple-element.87), channel_id=1, source_target_pairs={{0,8},{4,12},{8,0},{12,4},{16,24},{20,28},{24,16},{28,20},{1,9},{5... | collective-permute-start | bytes 393224 | tf_op jit(solution)/shard_map/ppermute | solution.py:149
  64.4 6.8 %collective-permute-start.22 = (f32[256,128]{1,0:T(8,128)S(1)}, f32[256,128]{1,0:T(8,128)S(1)}, u32[]{:S(2)}, u32[]{:S(2)}) collective-permute-start(f32[256,128]{1,0:T(8,128)S(1)} %get-tuple-element.89), channel_id=1, source_target_pairs={{0,16},{4,20},{8,24},{12,28},{16,0},{20,4},{24,8},{28,12},{1,17},{... | collective-permute-start | bytes 393224 | tf_op jit(solution)/shard_map/ppermute | solution.py:149
  65.2 6.0 %collective-permute-start.23 = (f32[256,128]{1,0:T(8,128)S(1)}, f32[256,128]{1,0:T(8,128)S(1)}, u32[]{:S(2)}, u32[]{:S(2)}) collective-permute-start(f32[256,128]{1,0:T(8,128)S(1)} %get-tuple-element.88), channel_id=1, source_target_pairs={{0,24},{4,28},{8,16},{12,20},{16,8},{20,12},{24,0},{28,4},{1,25},{... | collective-permute-start | bytes 393224 | tf_op jit(solution)/shard_map/ppermute | solution.py:149
  71.3 6.1 %collective-permute-start.24 = (bf16[256,128]{1,0:T(8,128)(2,1)S(1)}, bf16[256,128]{1,0:T(8,128)(2,1)S(1)}, u32[]{:S(2)}, u32[]{:S(2)}) collective-permute-start(bf16[256,128]{1,0:T(8,128)(2,1)S(1)} %get-tuple-element.80), channel_id=1, source_target_pairs={{0,1},{1,2},{2,3},{3,0},{4,5},{5,6},{6,7},{7,4},{8,9},{9,10},{10,1... | collective-permute-start | bytes 196616 | tf_op jit(solution)/shard_map/ppermute | solution.py:153
  73.3 5.6 %collective-permute-start.25 = (bf16[256,128]{1,0:T(8,128)(2,1)S(1)}, bf16[256,128]{1,0:T(8,128)(2,1)S(1)}, u32[]{:S(2)}, u32[]{:S(2)}) collective-permute-start(bf16[256,128]{1,0:T(8,128)(2,1)S(1)} %get-tuple-element.80), channel_id=1, source_target_pairs={{0,2},{1,3},{2,0},{3,1},{4,6},{5,7},{6,4},{7,5},{8,10},{9,11},{10,... | collective-permute-start | bytes 196616 | tf_op jit(solution)/shard_map/ppermute | solution.py:153
  74.0 5.0 %collective-permute-start.26 = (bf16[256,128]{1,0:T(8,128)(2,1)S(1)}, bf16[256,128]{1,0:T(8,128)(2,1)S(1)}, u32[]{:S(2)}, u32[]{:S(2)}) collective-permute-start(bf16[256,128]{1,0:T(8,128)(2,1)S(1)} %get-tuple-element.80), channel_id=1, source_target_pairs={{0,3},{1,0},{2,1},{3,2},{4,7},{5,4},{6,5},{7,6},{8,11},{9,8},{10,9... | collective-permute-start | bytes 196616 | tf_op jit(solution)/shard_map/ppermute | solution.py:153
  79.7 5.0 %collective-permute-start.27 = (f32[256,128]{1,0:T(8,128)S(1)}, f32[256,128]{1,0:T(8,128)S(1)}, u32[]{:S(2)}, u32[]{:S(2)}) collective-permute-start(f32[256,128]{1,0:T(8,128)S(1)} %get-tuple-element.84), channel_id=1, source_target_pairs={{0,8},{4,12},{8,0},{12,4},{16,24},{20,28},{24,16},{28,20},{1,9},{5... | collective-permute-start | bytes 393224 | tf_op jit(solution)/shard_map/ppermute | solution.py:149
  81.0 5.0 %collective-permute-start.28 = (f32[256,128]{1,0:T(8,128)S(1)}, f32[256,128]{1,0:T(8,128)S(1)}, u32[]{:S(2)}, u32[]{:S(2)}) collective-permute-start(f32[256,128]{1,0:T(8,128)S(1)} %get-tuple-element.86), channel_id=1, source_target_pairs={{0,16},{4,20},{8,24},{12,28},{16,0},{20,4},{24,8},{28,12},{1,17},{... | collective-permute-start | bytes 393224 | tf_op jit(solution)/shard_map/ppermute | solution.py:149
  81.7 5.9 %collective-permute-start.29 = (f32[256,128]{1,0:T(8,128)S(1)}, f32[256,128]{1,0:T(8,128)S(1)}, u32[]{:S(2)}, u32[]{:S(2)}) collective-permute-start(f32[256,128]{1,0:T(8,128)S(1)} %get-tuple-element.85), channel_id=1, source_target_pairs={{0,24},{4,28},{8,16},{12,20},{16,8},{20,12},{24,0},{28,4},{1,25},{... | collective-permute-start | bytes 393224 | tf_op jit(solution)/shard_map/ppermute | solution.py:149
  87.6 6.7 %collective-permute-start.30 = (bf16[256,128]{1,0:T(8,128)(2,1)S(1)}, bf16[256,128]{1,0:T(8,128)(2,1)S(1)}, u32[]{:S(2)}, u32[]{:S(2)}) collective-permute-start(bf16[256,128]{1,0:T(8,128)(2,1)S(1)} %get-tuple-element.78), channel_id=1, source_target_pairs={{0,1},{1,2},{2,3},{3,0},{4,5},{5,6},{6,7},{7,4},{8,9},{9,10},{10,1... | collective-permute-start | bytes 196616 | tf_op jit(solution)/shard_map/ppermute | solution.py:153
  88.8 6.7 %collective-permute-start.31 = (bf16[256,128]{1,0:T(8,128)(2,1)S(1)}, bf16[256,128]{1,0:T(8,128)(2,1)S(1)}, u32[]{:S(2)}, u32[]{:S(2)}) collective-permute-start(bf16[256,128]{1,0:T(8,128)(2,1)S(1)} %get-tuple-element.78), channel_id=1, source_target_pairs={{0,2},{1,3},{2,0},{3,1},{4,6},{5,7},{6,4},{7,5},{8,10},{9,11},{10,... | collective-permute-start | bytes 196616 | tf_op jit(solution)/shard_map/ppermute | solution.py:153
  90.9 4.9 %collective-permute-start.32 = (bf16[256,128]{1,0:T(8,128)(2,1)S(1)}, bf16[256,128]{1,0:T(8,128)(2,1)S(1)}, u32[]{:S(2)}, u32[]{:S(2)}) collective-permute-start(bf16[256,128]{1,0:T(8,128)(2,1)S(1)} %get-tuple-element.78), channel_id=1, source_target_pairs={{0,3},{1,0},{2,1},{3,2},{4,7},{5,4},{6,5},{7,6},{8,11},{9,8},{10,9... | collective-permute-start | bytes 196616 | tf_op jit(solution)/shard_map/ppermute | solution.py:153
  91.9 4.3 %collective-permute-start.33 = (bf16[256,128]{1,0:T(8,128)(2,1)S(1)}, bf16[256,128]{1,0:T(8,128)(2,1)S(1)}, u32[]{:S(2)}, u32[]{:S(2)}) collective-permute-start(bf16[256,128]{1,0:T(8,128)(2,1)S(1)} %get-tuple-element.78), channel_id=1, source_target_pairs={{0,8},{4,12},{8,0},{12,4},{16,24},{20,28},{24,16},{28,20},{1,9},{5... | collective-permute-start | bytes 196616 | tf_op jit(solution)/shard_map/ppermute | solution.py:149
  93.2 4.3 %collective-permute-start.34 = (bf16[256,128]{1,0:T(8,128)(2,1)S(1)}, bf16[256,128]{1,0:T(8,128)(2,1)S(1)}, u32[]{:S(2)}, u32[]{:S(2)}) collective-permute-start(bf16[256,128]{1,0:T(8,128)(2,1)S(1)} %get-tuple-element.78), channel_id=1, source_target_pairs={{0,16},{4,20},{8,24},{12,28},{16,0},{20,4},{24,8},{28,12},{1,17},{... | collective-permute-start | bytes 196616 | tf_op jit(solution)/shard_map/ppermute | solution.py:149
  94.2 5.2 %collective-permute-start.35 = (bf16[256,128]{1,0:T(8,128)(2,1)S(1)}, bf16[256,128]{1,0:T(8,128)(2,1)S(1)}, u32[]{:S(2)}, u32[]{:S(2)}) collective-permute-start(bf16[256,128]{1,0:T(8,128)(2,1)S(1)} %get-tuple-element.78), channel_id=1, source_target_pairs={{0,24},{4,28},{8,16},{12,20},{16,8},{20,12},{24,0},{28,4},{1,25},{... | collective-permute-start | bytes 196616 | tf_op jit(solution)/shard_map/ppermute | solution.py:149
  99.5 2.1 %collective-permute-start.36 = (bf16[1024,128]{1,0:T(8,128)(2,1)S(1)}, bf16[1024,128]{1,0:T(8,128)(2,1)S(1)}, u32[]{:S(2)}, u32[]{:S(2)}) collective-permute-start(bf16[1024,128]{1,0:T(8,128)(2,1)S(1)} %get-tuple-element.67), channel_id=1, source_target_pairs={{0,4},{4,0},{8,12},{12,8},{16,20},{20,16},{24,28},{28,24},{1,5},{5... | collective-permute-start | bytes 786440 | tf_op jit(solution)/shard_map/ppermute | solution.py:149
  103.0 4.4 %collective-permute-start.38 = (f32[2,64,128]{2,1,0:T(8,128)S(1)}, f32[2,64,128]{2,1,0:T(8,128)S(1)}, u32[]{:S(2)}, u32[]{:S(2)}) collective-permute-start(f32[2,64,128]{2,1,0:T(8,128)S(1)} %get-tuple-element.93), channel_id=1, source_target_pairs={{0,8},{4,12},{8,0},{12,4},{16,24},{20,28},{24,16},{28,20},{1,9},{5... | collective-permute-start | bytes 196616 | tf_op jit(solution)/shard_map/ppermute | solution.py:149
  104.1 5.0 %collective-permute-start.39 = (f32[2,64,128]{2,1,0:T(8,128)S(1)}, f32[2,64,128]{2,1,0:T(8,128)S(1)}, u32[]{:S(2)}, u32[]{:S(2)}) collective-permute-start(f32[2,64,128]{2,1,0:T(8,128)S(1)} %get-tuple-element.95), channel_id=1, source_target_pairs={{0,16},{4,20},{8,24},{12,28},{16,0},{20,4},{24,8},{28,12},{1,17},{... | collective-permute-start | bytes 196616 | tf_op jit(solution)/shard_map/ppermute | solution.py:149
  104.9 5.2 %collective-permute-start.40 = (f32[2,64,128]{2,1,0:T(8,128)S(1)}, f32[2,64,128]{2,1,0:T(8,128)S(1)}, u32[]{:S(2)}, u32[]{:S(2)}) collective-permute-start(f32[2,64,128]{2,1,0:T(8,128)S(1)} %get-tuple-element.94), channel_id=1, source_target_pairs={{0,24},{4,28},{8,16},{12,20},{16,8},{20,12},{24,0},{28,4},{1,25},{... | collective-permute-start | bytes 196616 | tf_op jit(solution)/shard_map/ppermute | solution.py:149
  106.6 7.0 %collective-permute-start.45 = (f32[128,128]{1,0:T(8,128)S(1)}, f32[128,128]{1,0:T(8,128)S(1)}, u32[]{:S(2)}, u32[]{:S(2)}) collective-permute-start(f32[128,128]{1,0:T(8,128)S(1)} %get-tuple-element.109), channel_id=1, source_target_pairs={{0,4},{4,0},{8,12},{12,8},{16,20},{20,16},{24,28},{28,24},{1,5},{5... | collective-permute-start | bytes 196616 | tf_op jit(solution)/shard_map/ppermute | solution.py:149
  110.1 5.4 %collective-permute-start.41 = (f32[64,128]{1,0:T(8,128)S(1)}, f32[64,128]{1,0:T(8,128)S(1)}, u32[]{:S(2)}, u32[]{:S(2)}) collective-permute-start(f32[64,128]{1,0:T(8,128)S(1)} %get-tuple-element.119), channel_id=1, source_target_pairs={{0,8},{4,12},{8,0},{12,4},{16,24},{20,28},{24,16},{28,20},{1,9},{5... | collective-permute-start | bytes 98312 | tf_op jit(solution)/shard_map/ppermute | solution.py:149
  111.3 6.8 %collective-permute-start.42 = (f32[64,128]{1,0:T(8,128)S(1)}, f32[64,128]{1,0:T(8,128)S(1)}, u32[]{:S(2)}, u32[]{:S(2)}) collective-permute-start(f32[64,128]{1,0:T(8,128)S(1)} %get-tuple-element.119), channel_id=1, source_target_pairs={{0,16},{4,20},{8,24},{12,28},{16,0},{20,4},{24,8},{28,12},{1,17},{... | collective-permute-start | bytes 98312 | tf_op jit(solution)/shard_map/ppermute | solution.py:149
  112.4 5.7 %collective-permute-start.43 = (f32[64,128]{1,0:T(8,128)S(1)}, f32[64,128]{1,0:T(8,128)S(1)}, u32[]{:S(2)}, u32[]{:S(2)}) collective-permute-start(f32[64,128]{1,0:T(8,128)S(1)} %get-tuple-element.119), channel_id=1, source_target_pairs={{0,24},{4,28},{8,16},{12,20},{16,8},{20,12},{24,0},{28,4},{1,25},{... | collective-permute-start | bytes 98312 | tf_op jit(solution)/shard_map/ppermute | solution.py:149
  113.6 5.8 %collective-permute-start.46 = (f32[64,128]{1,0:T(8,128)S(1)}, f32[64,128]{1,0:T(8,128)S(1)}, u32[]{:S(2)}, u32[]{:S(2)}) collective-permute-start(f32[64,128]{1,0:T(8,128)S(1)} %get-tuple-element.118), channel_id=1, source_target_pairs={{0,1},{1,2},{2,3},{3,0},{4,5},{5,6},{6,7},{7,4},{8,9},{9,10},{10,1... | collective-permute-start | bytes 98312 | tf_op jit(solution)/shard_map/ppermute | solution.py:153
  114.7 5.4 %collective-permute-start.47 = (f32[64,128]{1,0:T(8,128)S(1)}, f32[64,128]{1,0:T(8,128)S(1)}, u32[]{:S(2)}, u32[]{:S(2)}) collective-permute-start(f32[64,128]{1,0:T(8,128)S(1)} %get-tuple-element.118), channel_id=1, source_target_pairs={{0,2},{1,3},{2,0},{3,1},{4,6},{5,7},{6,4},{7,5},{8,10},{9,11},{10,... | collective-permute-start | bytes 98312 | tf_op jit(solution)/shard_map/ppermute | solution.py:153
  115.5 4.6 %collective-permute-start.48 = (f32[64,128]{1,0:T(8,128)S(1)}, f32[64,128]{1,0:T(8,128)S(1)}, u32[]{:S(2)}, u32[]{:S(2)}) collective-permute-start(f32[64,128]{1,0:T(8,128)S(1)} %get-tuple-element.118), channel_id=1, source_target_pairs={{0,3},{1,0},{2,1},{3,2},{4,7},{5,4},{6,5},{7,6},{8,11},{9,8},{10,9... | collective-permute-start | bytes 98312 | tf_op jit(solution)/shard_map/ppermute | solution.py:153
  118.4 5.3 %collective-permute-start.44 = (f32[256,128]{1,0:T(8,128)S(1)}, f32[256,128]{1,0:T(8,128)S(1)}, u32[]{:S(2)}, u32[]{:S(2)}) collective-permute-start(f32[256,128]{1,0:T(8,128)S(1)} %maximum_select_fusion.4), channel_id=1, source_target_pairs={{0,4},{4,0},{8,12},{12,8},{16,20},{20,16},{24,28},{28,24},{1,5},{5... | collective-permute-start | bytes 393224 | tf_op jit(solution)/shard_map/ppermute | solution.py:149
  120.1 11.5 %collective-permute-start.49 = (f32[64,128]{1,0:T(8,128)S(1)}, f32[64,128]{1,0:T(8,128)S(1)}, u32[]{:S(2)}, u32[]{:S(2)}) collective-permute-start(f32[64,128]{1,0:T(8,128)S(1)} %add_add_fusion), channel_id=1, source_target_pairs={{0,8},{4,12},{8,0},{12,4},{16,24},{20,28},{24,16},{28,20},{1,9},{5... | collective-permute-start | bytes 98312 | tf_op jit(solution)/shard_map/ppermute | solution.py:149
  121.4 10.2 %collective-permute-start.50 = (f32[64,128]{1,0:T(8,128)S(1)}, f32[64,128]{1,0:T(8,128)S(1)}, u32[]{:S(2)}, u32[]{:S(2)}) collective-permute-start(f32[64,128]{1,0:T(8,128)S(1)} %add_add_fusion), channel_id=1, source_target_pairs={{0,16},{4,20},{8,24},{12,28},{16,0},{20,4},{24,8},{28,12},{1,17},{... | collective-permute-start | bytes 98312 | tf_op jit(solution)/shard_map/ppermute | solution.py:149
  122.6 9.1 %collective-permute-start.51 = (f32[64,128]{1,0:T(8,128)S(1)}, f32[64,128]{1,0:T(8,128)S(1)}, u32[]{:S(2)}, u32[]{:S(2)}) collective-permute-start(f32[64,128]{1,0:T(8,128)S(1)} %add_add_fusion), channel_id=1, source_target_pairs={{0,24},{4,28},{8,16},{12,20},{16,8},{20,12},{24,0},{28,4},{1,25},{... | collective-permute-start | bytes 98312 | tf_op jit(solution)/shard_map/ppermute | solution.py:149
  (9 other events, 48.0 us)

commit v5 on v4

--- a/solution.py
+++ b/solution.py
@@ -365,14 +365,17 @@
         ordered = jnp.concatenate([own, other], axis), jnp.concatenate([other, own], axis)
         return jnp.where(first_core, *ordered)
 
-    own, other = halves(orbitals_in)
-
     by_owner = hblocks.reshape(cols, PB * slots, BS * BS)
     pieces = pack(col[None], by_owner, places)
-    key, pieces, other = lax.optimization_barrier((key, pieces, other))
+    key, pieces, orbitals_in = lax.optimization_barrier((key, pieces, orbitals_in))
+    own, other = halves(orbitals_in)
     start = jnp.concatenate([own, core_swap(other, rows)], 0)
     pieces = [shifted(piece, "col", cols, s) for s, piece in enumerate(pieces, 1)]
-    pieces, start = lax.optimization_barrier((pieces, start))
+    mirrored = mirror(
+        key, hblocks.reshape(row_blocks * slots, BS * BS), onsite, rows, row_blocks
+    )
+
+    pieces, start, mirrored = lax.optimization_barrier((pieces, start, mirrored))
 
     def gather(v):
         return jnp.concatenate([v] + [shifted(v, "col", cols, s) for s in range(1, cols)], 0)
@@ -384,18 +387,17 @@
         blocks = core_swap(v, rows).reshape(-1, 2, local_rows, half)
         return jnp.stack([blocks[:, 1], blocks[:, 0]], 1).reshape(v.shape)
 
-    mirrored = mirror(
-        key, hblocks.reshape(row_blocks * slots, BS * BS), onsite, rows, row_blocks
-    )
-
     direct = direct_rows(col[None], by_owner, places, pieces, rows, slots)
-    mirrored, direct = lax.optimization_barrier((mirrored, direct))
+    first = start.astype(jnp.bfloat16)
+    second = shifted(first, "col", cols, 1)
+    mirrored, direct, second = lax.optimization_barrier((mirrored, direct, second))
     mirrored_other = core_swap(mirrored, rows)
     direct = [chip_swap(direct[s], rows, s) if s else direct[s] for s in range(chips)]
-    first, mirrored_other = lax.optimization_barrier(
-        (start.astype(jnp.bfloat16), mirrored_other)
+    first, mirrored_other = lax.optimization_barrier((first, mirrored_other))
+    first_gathered = jnp.concatenate(
+        [first, second] + [shifted(first, "col", cols, s) for s in range(2, cols)], 0
     )
-    first_gathered, direct = lax.optimization_barrier((gather(first), direct))
+    first_gathered, direct = lax.optimization_barrier((first_gathered, direct))
     direct_other = [core_swap(rows_of_chip, rows) for rows_of_chip in direct]
 
     tile = assemble(mirrored, mirrored_other, direct, direct_other)

time: 135 us -> 138 us (1.022)
  waiting for transfers between devices: 42.3 us -> 46 us
    ppermute x35, waiting for transfers between devices: 23.9 us -> 29.6 us  [exchanged(): return lax.ppermute(x, axis, [(i, i ^ apart) for i in range(size)])]
    ppermute x18, waiting for transfers between devices: 18.4 us -> 16.4 us  [shifted(): return lax.ppermute(x, axis, [(i, (i + step) % size) for i in range(size)])]
    ppermute x18, starting transfers between devices: 32.5 us -> 31 us  [shifted(): return lax.ppermute(x, axis, [(i, (i + step) % size) for i in range(size)])]
  transfers between devices with their start and end apart: 53 -> 53, of which waited for: 31 -> 31; matrix products, arithmetic and copies ran while one was open for 1% -> 1% of each run, Pallas kernels for 8% -> 10%
where the time goes in v5:
time: 138 us; the launch traced here: 137 us
  starting transfers between devices  62.1 us (45%)
  waiting for transfers between devices  46 us (33%)
  Pallas kernels  17.5 us (13%)
  matrix products  4.24 us (3%)
  local copies, waits for them, and re-layouts  2.78 us (2%)
  between operations  2.5 us (2%)
  other arithmetic  2.39 us (2%)
    ppermute x35, starting transfers between devices, exchanged(): return lax.ppermute(x, axis, [(i, i ^ apart) for i in range(size)])  31.1 us
    ppermute x18, starting transfers between devices, shifted(): return lax.ppermute(x, axis, [(i, (i + step) % size) for i in range(size)])  31 us
    ppermute x35, waiting for transfers between devices, exchanged(): return lax.ppermute(x, axis, [(i, i ^ apart) for i in range(size)])  29.6 us
    ppermute x18, waiting for transfers between devices, shifted(): return lax.ppermute(x, axis, [(i, (i + step) % size) for i in range(size)])  16.4 us
    pallas_call x1, Pallas kernels, factorize(): pl.pallas_call(functools.partial(factor_kernel, total_rows), out_shape=(j...  7.94 us
    pallas_call x1, Pallas kernels, direct_rows(): pl.pallas_call(functools.partial(direct_kernel, rows, slots), out_shape=(...  3.07 us
    dot_general x4, matrix products, partial_product(): return jnp.dot(tile, gathered, preferred_element_type=jnp.float32)  2.82 us
  transfers between devices with their start and end apart: 53, of which 31 were waited for; matrix products, arithmetic and copies ran while one was open for 1% of the time, Pallas kernels for 10%

profile of v5, /device:TPU:0, one launch (start us, length us, event | category | flops | bytes accessed | tf_op | source)
XLA Modules:
  0.0 137.4 jit_solution(15739787826888751136)
XLA Ops:
  2.3 1.8 %pack.1 = (bf16[16,4224]{1,0:T(8,128)(2,1)}, bf16[16,4224]{1,0:T(8,128)(2,1)}, bf16[16,4224]{1,0:T(8,128)(2,1)}) custom-call(s32[1]{0:T(128)} %bitcast.1.col_ref, bf16[4,16,4096]{2,1,0:T(8,128)(2,1)} %bitcast.91, f32[4,16]{1,0:T(4,128)} %reshape.253.places_ref), custom_call_target="tpu_custom_call" | custom-call | tf_op jit(solution)/shard_map/pack/pallas_call | solution.py:193
  5.5 2.6 %collective-permute-start = (bf16[16,4224]{1,0:T(8,128)(2,1)}, bf16[16,4224]{1,0:T(8,128)(2,1)S(1)}, u32[]{:S(2)}, u32[]{:S(2)}) collective-permute-start(bf16[16,4224]{1,0:T(8,128)(2,1)} %get-tuple-element.44), channel_id=1, source_target_pairs={{0,1},{1,2},{2,3},{3,0},{4,5},{5,6},{6,7},{7,4},{8,9},{9,10},{10,1... | collective-permute-start | bytes 405512 | tf_op jit(solution)/shard_map/ppermute | solution.py:153
  8.1 2.6 %collective-permute-start.1 = (bf16[16,4224]{1,0:T(8,128)(2,1)}, bf16[16,4224]{1,0:T(8,128)(2,1)S(1)}, u32[]{:S(2)}, u32[]{:S(2)}) collective-permute-start(bf16[16,4224]{1,0:T(8,128)(2,1)} %get-tuple-element.45), channel_id=1, source_target_pairs={{0,2},{1,3},{2,0},{3,1},{4,6},{5,7},{6,4},{7,5},{8,10},{9,11},{10,... | collective-permute-start | bytes 405512 | tf_op jit(solution)/shard_map/ppermute | solution.py:153
  10.7 1.3 collective-permute-start.2
  13.8 2.3 %mirror.1.mirrored = bf16[2,512,512]{2,1,0:T(8,128)(2,1)S(1)} custom-call(s32[1,64]{1,0:T(1,128)S(1)} %reshape.251.key_ref, bf16[64,4096]{1,0:T(8,128)(2,1)S(1)} %bitcast.92, bf16[2,4096]{1,0:T(2,128)(2,1)S(1)} %copy-done.3), custom_call_target="tpu_custom_call" | custom-call | flops 67108864 | bytes 786432 | tf_op jit(solution)/shard_map/mirror/pallas_call | solution.py:233
  16.1 4.3 %collective-permute-done.1.refs_1_ = bf16[16,4224]{1,0:T(8,128)(2,1)S(1)} collective-permute-done((bf16[16,4224]{1,0:T(8,128)(2,1)}, bf16[16,4224]{1,0:T(8,128)(2,1)S(1)}, u32[]{:S(2)}, u32[]{:S(2)}) %collective-permute-start.1) | collective-permute-done | bytes 135200 | tf_op jit(solution)/shard_map/ppermute | solution.py:153
  20.4 3.4 %collective-permute-start.4 = (bf16[256,128]{1,0:T(8,128)(2,1)S(1)}, bf16[256,128]{1,0:T(8,128)(2,1)S(1)}, u32[]{:S(2)}, u32[]{:S(2)}) collective-permute-start(bf16[256,128]{1,0:T(8,128)(2,1)S(1)} %convert_element_type.18), channel_id=1, source_target_pairs={{0,1},{1,2},{2,3},{3,0},{4,5},{5,6},{6,7},{7,4},{8,9},{9,10},{10,1... | collective-permute-start | bytes 196616 | tf_op jit(solution)/shard_map/ppermute | solution.py:153
  23.9 3.1 %direct_rows.1 = (bf16[128,1024]{1,0:T(8,128)(2,1)S(1)}, bf16[128,1024]{1,0:T(8,128)(2,1)S(1)}, bf16[128,1024]{1,0:T(8,128)(2,1)S(1)}, bf16[128,1024]{1,0:T(8,128)(2,1)S(1)}) custom-call(s32[1]{0:T(128)} %bitcast.1.col_ref, bf16[4,16,4096]{2,1,0:T(8,128)(2,1)S(1)} %bitcast.93, f32[4,16]{1,0:T(4,128)S(1)} %copy-done.2, ...), custom_call_target="tpu_custom_call" | custom-call | tf_op jit(solution)/shard_map/direct_rows/pallas_call | solution.py:285
  27.2 2.4 %collective-permute-start.10 = (bf16[128,1024]{1,0:T(8,128)(2,1)S(1)}, bf16[128,1024]{1,0:T(8,128)(2,1)S(1)}, u32[]{:S(2)}, u32[]{:S(2)}) collective-permute-start(bf16[128,1024]{1,0:T(8,128)(2,1)S(1)} %get-tuple-element.65), channel_id=1, source_target_pairs={{0,24},{4,28},{8,16},{12,20},{16,8},{20,12},{24,0},{28,4},{1,25},{... | collective-permute-start | bytes 786440 | tf_op jit(solution)/shard_map/ppermute | solution.py:149
  30.7 1.6 %collective-permute-start.6 = (bf16[256,128]{1,0:T(8,128)(2,1)S(1)}, bf16[256,128]{1,0:T(8,128)(2,1)S(1)}, u32[]{:S(2)}, u32[]{:S(2)}) collective-permute-start(bf16[256,128]{1,0:T(8,128)(2,1)S(1)} %convert_element_type.18), channel_id=1, source_target_pairs={{0,2},{1,3},{2,0},{3,1},{4,6},{5,7},{6,4},{7,5},{8,10},{9,11},{10,... | collective-permute-start | bytes 196616 | tf_op jit(solution)/shard_map/ppermute | solution.py:153
  32.2 1.8 %collective-permute-start.7 = (bf16[256,128]{1,0:T(8,128)(2,1)S(1)}, bf16[256,128]{1,0:T(8,128)(2,1)S(1)}, u32[]{:S(2)}, u32[]{:S(2)}) collective-permute-start(bf16[256,128]{1,0:T(8,128)(2,1)S(1)} %convert_element_type.18), channel_id=1, source_target_pairs={{0,3},{1,0},{2,1},{3,2},{4,7},{5,4},{6,5},{7,6},{8,11},{9,8},{10,9... | collective-permute-start | bytes 196616 | tf_op jit(solution)/shard_map/ppermute | solution.py:153
  34.0 3.3 %collective-permute-done.6 = bf16[256,128]{1,0:T(8,128)(2,1)S(1)} collective-permute-done((bf16[256,128]{1,0:T(8,128)(2,1)S(1)}, bf16[256,128]{1,0:T(8,128)(2,1)S(1)}, u32[]{:S(2)}, u32[]{:S(2)}) %collective-permute-start.6) | collective-permute-done | bytes 65568 | tf_op jit(solution)/shard_map/ppermute | solution.py:153
  37.3 5.2 %collective-permute-done.8.refs_1_ = bf16[128,1024]{1,0:T(8,128)(2,1)S(1)} collective-permute-done((bf16[128,1024]{1,0:T(8,128)(2,1)S(1)}, bf16[128,1024]{1,0:T(8,128)(2,1)S(1)}, u32[]{:S(2)}, u32[]{:S(2)}) %collective-permute-start.8) | collective-permute-done | bytes 262176 | tf_op jit(solution)/shard_map/ppermute | solution.py:149
  46.5 1.6 %collective-permute-start.15 = (f32[256,128]{1,0:T(8,128)S(1)}, f32[256,128]{1,0:T(8,128)S(1)}, u32[]{:S(2)}, u32[]{:S(2)}) collective-permute-start(f32[256,128]{1,0:T(8,128)S(1)} %get-tuple-element.94), channel_id=1, source_target_pairs={{0,8},{4,12},{8,0},{12,4},{16,24},{20,28},{24,16},{28,20},{1,9},{5... | collective-permute-start | bytes 393224 | tf_op jit(solution)/shard_map/ppermute | solution.py:149
  48.1 1.4 %collective-permute-start.16 = (f32[256,128]{1,0:T(8,128)S(1)}, f32[256,128]{1,0:T(8,128)S(1)}, u32[]{:S(2)}, u32[]{:S(2)}) collective-permute-start(f32[256,128]{1,0:T(8,128)S(1)} %get-tuple-element.96), channel_id=1, source_target_pairs={{0,16},{4,20},{8,24},{12,28},{16,0},{20,4},{24,8},{28,12},{1,17},{... | collective-permute-start | bytes 393224 | tf_op jit(solution)/shard_map/ppermute | solution.py:149
  52.5 3.7 %collective-permute-done.16 = f32[256,128]{1,0:T(8,128)S(1)} collective-permute-done((f32[256,128]{1,0:T(8,128)S(1)}, f32[256,128]{1,0:T(8,128)S(1)}, u32[]{:S(2)}, u32[]{:S(2)}) %collective-permute-start.16) | collective-permute-done | bytes 131104 | tf_op jit(solution)/shard_map/ppermute | solution.py:149
  57.2 1.6 %collective-permute-start.19 = (bf16[256,128]{1,0:T(8,128)(2,1)S(1)}, bf16[256,128]{1,0:T(8,128)(2,1)S(1)}, u32[]{:S(2)}, u32[]{:S(2)}) collective-permute-start(bf16[256,128]{1,0:T(8,128)(2,1)S(1)} %get-tuple-element.86), channel_id=1, source_target_pairs={{0,2},{1,3},{2,0},{3,1},{4,6},{5,7},{6,4},{7,5},{8,10},{9,11},{10,... | collective-permute-start | bytes 196616 | tf_op jit(solution)/shard_map/ppermute | solution.py:153
  58.8 1.8 %collective-permute-start.20 = (bf16[256,128]{1,0:T(8,128)(2,1)S(1)}, bf16[256,128]{1,0:T(8,128)(2,1)S(1)}, u32[]{:S(2)}, u32[]{:S(2)}) collective-permute-start(bf16[256,128]{1,0:T(8,128)(2,1)S(1)} %get-tuple-element.86), channel_id=1, source_target_pairs={{0,3},{1,0},{2,1},{3,2},{4,7},{5,4},{6,5},{7,6},{8,11},{9,8},{10,9... | collective-permute-start | bytes 196616 | tf_op jit(solution)/shard_map/ppermute | solution.py:153
  60.7 1.7 %collective-permute-done.18 = bf16[256,128]{1,0:T(8,128)(2,1)S(1)} collective-permute-done((bf16[256,128]{1,0:T(8,128)(2,1)S(1)}, bf16[256,128]{1,0:T(8,128)(2,1)S(1)}, u32[]{:S(2)}, u32[]{:S(2)}) %collective-permute-start.18) | collective-permute-done | bytes 65568 | tf_op jit(solution)/shard_map/ppermute | solution.py:153
  62.4 1.7 %collective-permute-done.19 = bf16[256,128]{1,0:T(8,128)(2,1)S(1)} collective-permute-done((bf16[256,128]{1,0:T(8,128)(2,1)S(1)}, bf16[256,128]{1,0:T(8,128)(2,1)S(1)}, u32[]{:S(2)}, u32[]{:S(2)}) %collective-permute-start.19) | collective-permute-done | bytes 65568 | tf_op jit(solution)/shard_map/ppermute | solution.py:153
  64.9 1.6 %collective-permute-start.21 = (f32[256,128]{1,0:T(8,128)S(1)}, f32[256,128]{1,0:T(8,128)S(1)}, u32[]{:S(2)}, u32[]{:S(2)}) collective-permute-start(f32[256,128]{1,0:T(8,128)S(1)} %get-tuple-element.91), channel_id=1, source_target_pairs={{0,8},{4,12},{8,0},{12,4},{16,24},{20,28},{24,16},{28,20},{1,9},{5... | collective-permute-start | bytes 393224 | tf_op jit(solution)/shard_map/ppermute | solution.py:149
  68.4 2.2 %collective-permute-done.21 = f32[256,128]{1,0:T(8,128)S(1)} collective-permute-done((f32[256,128]{1,0:T(8,128)S(1)}, f32[256,128]{1,0:T(8,128)S(1)}, u32[]{:S(2)}, u32[]{:S(2)}) %collective-permute-start.21) | collective-permute-done | bytes 131104 | tf_op jit(solution)/shard_map/ppermute | solution.py:149
  71.4 1.7 %collective-permute-done.23 = f32[256,128]{1,0:T(8,128)S(1)} collective-permute-done((f32[256,128]{1,0:T(8,128)S(1)}, f32[256,128]{1,0:T(8,128)S(1)}, u32[]{:S(2)}, u32[]{:S(2)}) %collective-permute-start.23) | collective-permute-done | bytes 131104 | tf_op jit(solution)/shard_map/ppermute | solution.py:149
  73.2 2.3 %collective-permute-start.24 = (bf16[256,128]{1,0:T(8,128)(2,1)S(1)}, bf16[256,128]{1,0:T(8,128)(2,1)S(1)}, u32[]{:S(2)}, u32[]{:S(2)}) collective-permute-start(bf16[256,128]{1,0:T(8,128)(2,1)S(1)} %get-tuple-element.84), channel_id=1, source_target_pairs={{0,1},{1,2},{2,3},{3,0},{4,5},{5,6},{6,7},{7,4},{8,9},{9,10},{10,1... | collective-permute-start | bytes 196616 | tf_op jit(solution)/shard_map/ppermute | solution.py:153
  75.4 1.2 collective-permute-start.25
  76.7 1.2 collective-permute-start.26
  77.8 1.4 %collective-permute-done.24 = bf16[256,128]{1,0:T(8,128)(2,1)S(1)} collective-permute-done((bf16[256,128]{1,0:T(8,128)(2,1)S(1)}, bf16[256,128]{1,0:T(8,128)(2,1)S(1)}, u32[]{:S(2)}, u32[]{:S(2)}) %collective-permute-start.24) | collective-permute-done | bytes 65568 | tf_op jit(solution)/shard_map/ppermute | solution.py:153
  79.3 1.6 %collective-permute-done.25 = bf16[256,128]{1,0:T(8,128)(2,1)S(1)} collective-permute-done((bf16[256,128]{1,0:T(8,128)(2,1)S(1)}, bf16[256,128]{1,0:T(8,128)(2,1)S(1)}, u32[]{:S(2)}, u32[]{:S(2)}) %collective-permute-start.25) | collective-permute-done | bytes 65568 | tf_op jit(solution)/shard_map/ppermute | solution.py:153
  82.9 1.2 collective-permute-start.28
  84.2 1.6 %collective-permute-start.29 = (f32[256,128]{1,0:T(8,128)S(1)}, f32[256,128]{1,0:T(8,128)S(1)}, u32[]{:S(2)}, u32[]{:S(2)}) collective-permute-start(f32[256,128]{1,0:T(8,128)S(1)} %get-tuple-element.89), channel_id=1, source_target_pairs={{0,24},{4,28},{8,16},{12,20},{16,8},{20,12},{24,0},{28,4},{1,25},{... | collective-permute-start | bytes 393224 | tf_op jit(solution)/shard_map/ppermute | solution.py:149
  85.8 1.5 %collective-permute-done.27 = f32[256,128]{1,0:T(8,128)S(1)} collective-permute-done((f32[256,128]{1,0:T(8,128)S(1)}, f32[256,128]{1,0:T(8,128)S(1)}, u32[]{:S(2)}, u32[]{:S(2)}) %collective-permute-start.27) | collective-permute-done | bytes 131104 | tf_op jit(solution)/shard_map/ppermute | solution.py:149
  87.9 2.1 %collective-permute-done.29 = f32[256,128]{1,0:T(8,128)S(1)} collective-permute-done((f32[256,128]{1,0:T(8,128)S(1)}, f32[256,128]{1,0:T(8,128)S(1)}, u32[]{:S(2)}, u32[]{:S(2)}) %collective-permute-start.29) | collective-permute-done | bytes 131104 | tf_op jit(solution)/shard_map/ppermute | solution.py:149
  90.7 2.3 %collective-permute-start.31 = (bf16[256,128]{1,0:T(8,128)(2,1)S(1)}, bf16[256,128]{1,0:T(8,128)(2,1)S(1)}, u32[]{:S(2)}, u32[]{:S(2)}) collective-permute-start(bf16[256,128]{1,0:T(8,128)(2,1)S(1)} %get-tuple-element.82), channel_id=1, source_target_pairs={{0,2},{1,3},{2,0},{3,1},{4,6},{5,7},{6,4},{7,5},{8,10},{9,11},{10,... | collective-permute-start | bytes 196616 | tf_op jit(solution)/shard_map/ppermute | solution.py:153
  94.0 1.3 collective-permute-start.33
  96.4 1.6 %collective-permute-start.35 = (bf16[256,128]{1,0:T(8,128)(2,1)S(1)}, bf16[256,128]{1,0:T(8,128)(2,1)S(1)}, u32[]{:S(2)}, u32[]{:S(2)}) collective-permute-start(bf16[256,128]{1,0:T(8,128)(2,1)S(1)} %get-tuple-element.82), channel_id=1, source_target_pairs={{0,24},{4,28},{8,16},{12,20},{16,8},{20,12},{24,0},{28,4},{1,25},{... | collective-permute-start | bytes 196616 | tf_op jit(solution)/shard_map/ppermute | solution.py:149
  98.3 1.3 collective-permute-done.34
  99.6 1.9 %collective-permute-done.35 = bf16[256,128]{1,0:T(8,128)(2,1)S(1)} collective-permute-done((bf16[256,128]{1,0:T(8,128)(2,1)S(1)}, bf16[256,128]{1,0:T(8,128)(2,1)S(1)}, u32[]{:S(2)}, u32[]{:S(2)}) %collective-permute-start.35) | collective-permute-done | bytes 65568 | tf_op jit(solution)/shard_map/ppermute | solution.py:149
  105.2 1.3 collective-permute-start.38
  107.4 1.4 collective-permute-start.40
  109.6 1.2 collective-permute-done.39
  110.8 1.8 %collective-permute-done.40 = f32[2,64,128]{2,1,0:T(8,128)S(1)} collective-permute-done((f32[2,64,128]{2,1,0:T(8,128)S(1)}, f32[2,64,128]{2,1,0:T(8,128)S(1)}, u32[]{:S(2)}, u32[]{:S(2)}) %collective-permute-start.40) | collective-permute-done | bytes 65568 | tf_op jit(solution)/shard_map/ppermute | solution.py:149
  114.6 1.6 %collective-permute-start.43 = (f32[64,128]{1,0:T(8,128)S(1)}, f32[64,128]{1,0:T(8,128)S(1)}, u32[]{:S(2)}, u32[]{:S(2)}) collective-permute-start(f32[64,128]{1,0:T(8,128)S(1)} %get-tuple-element.123), channel_id=1, source_target_pairs={{0,24},{4,28},{8,16},{12,20},{16,8},{20,12},{24,0},{28,4},{1,25},{... | collective-permute-start | bytes 98312 | tf_op jit(solution)/shard_map/ppermute | solution.py:149
  117.8 2.8 %collective-permute-start.48 = (f32[64,128]{1,0:T(8,128)S(1)}, f32[64,128]{1,0:T(8,128)S(1)}, u32[]{:S(2)}, u32[]{:S(2)}) collective-permute-start(f32[64,128]{1,0:T(8,128)S(1)} %get-tuple-element.122), channel_id=1, source_target_pairs={{0,3},{1,0},{2,1},{3,2},{4,7},{5,4},{6,5},{7,6},{8,11},{9,8},{10,9... | collective-permute-start | bytes 98312 | tf_op jit(solution)/shard_map/ppermute | solution.py:153
  122.5 1.2 collective-permute-start.49
  124.6 1.4 %collective-permute-start.51 = (f32[64,128]{1,0:T(8,128)S(1)}, f32[64,128]{1,0:T(8,128)S(1)}, u32[]{:S(2)}, u32[]{:S(2)}) collective-permute-start(f32[64,128]{1,0:T(8,128)S(1)} %add_add_fusion), channel_id=1, source_target_pairs={{0,24},{4,28},{8,16},{12,20},{16,8},{20,12},{24,0},{28,4},{1,25},{... | collective-permute-start | bytes 98312 | tf_op jit(solution)/shard_map/ppermute | solution.py:149
  126.1 7.9 %factorize.1 = (f32[128,256]{1,0:T(8,128)}, f32[256,256]{1,0:T(8,128)S(1)}) custom-call(f32[256,256]{1,0:T(8,128)S(1)} %maximum_select_fusion.2.gram_ref, f32[128,256]{1,0:T(8,128)S(1)} %maximum_select_fusion.5.y_ref), custom_call_target="tpu_custom_call" | custom-call | bytes 5242880 | tf_op jit(solution)/shard_map/factorize/pallas_call | solution.py:124
  134.3 1.3 collective-permute-done.52
  135.6 1.8 %project.1 = f32[256,256]{1,0:T(8,128)} custom-call(f32[256,256]{1,0:T(8,128)S(1)} %get-tuple-element.75.inverse_ref, f32[256,256]{1,0:T(8,128)S(1)} %maximum_select_fusion.3.cross_ref), custom_call_target="tpu_custom_call" | custom-call | tf_op jit(solution)/shard_map/project/pallas_call | solution.py:138
  (134 shorter events, 34.0 us)
Async XLA Ops:
  4.9 11.1 %collective-permute-start.3 = (f32[128,128]{1,0:T(8,128)S(1)}, f32[128,128]{1,0:T(8,128)S(1)}, u32[]{:S(2)}, u32[]{:S(2)}) collective-permute-start(f32[128,128]{1,0:T(8,128)S(1)} %get-tuple-element.121), channel_id=1, source_target_pairs={{0,4},{4,0},{8,12},{12,8},{16,20},{20,16},{24,28},{28,24},{1,5},{5... | collective-permute-start | bytes 196616 | tf_op jit(solution)/shard_map/ppermute | solution.py:149
  5.5 10.6 %collective-permute-start = (bf16[16,4224]{1,0:T(8,128)(2,1)}, bf16[16,4224]{1,0:T(8,128)(2,1)S(1)}, u32[]{:S(2)}, u32[]{:S(2)}) collective-permute-start(bf16[16,4224]{1,0:T(8,128)(2,1)} %get-tuple-element.44), channel_id=1, source_target_pairs={{0,1},{1,2},{2,3},{3,0},{4,5},{5,6},{6,7},{7,4},{8,9},{9,10},{10,1... | collective-permute-start | bytes 405512 | tf_op jit(solution)/shard_map/ppermute | solution.py:153
  8.1 12.3 %collective-permute-start.1 = (bf16[16,4224]{1,0:T(8,128)(2,1)}, bf16[16,4224]{1,0:T(8,128)(2,1)S(1)}, u32[]{:S(2)}, u32[]{:S(2)}) collective-permute-start(bf16[16,4224]{1,0:T(8,128)(2,1)} %get-tuple-element.45), channel_id=1, source_target_pairs={{0,2},{1,3},{2,0},{3,1},{4,6},{5,7},{6,4},{7,5},{8,10},{9,11},{10,... | collective-permute-start | bytes 405512 | tf_op jit(solution)/shard_map/ppermute | solution.py:153
  10.7 9.7 %collective-permute-start.2 = (bf16[16,4224]{1,0:T(8,128)(2,1)}, bf16[16,4224]{1,0:T(8,128)(2,1)S(1)}, u32[]{:S(2)}, u32[]{:S(2)}) collective-permute-start(bf16[16,4224]{1,0:T(8,128)(2,1)} %get-tuple-element.46), channel_id=1, source_target_pairs={{0,3},{1,0},{2,1},{3,2},{4,7},{5,4},{6,5},{7,6},{8,11},{9,8},{10,9... | collective-permute-start | bytes 405512 | tf_op jit(solution)/shard_map/ppermute | solution.py:153
  20.4 6.8 %collective-permute-start.4 = (bf16[256,128]{1,0:T(8,128)(2,1)S(1)}, bf16[256,128]{1,0:T(8,128)(2,1)S(1)}, u32[]{:S(2)}, u32[]{:S(2)}) collective-permute-start(bf16[256,128]{1,0:T(8,128)(2,1)S(1)} %convert_element_type.18), channel_id=1, source_target_pairs={{0,1},{1,2},{2,3},{3,0},{4,5},{5,6},{6,7},{7,4},{8,9},{9,10},{10,1... | collective-permute-start | bytes 196616 | tf_op jit(solution)/shard_map/ppermute | solution.py:153
  27.2 3.5 %collective-permute-start.5 = (bf16[2,512,512]{2,1,0:T(8,128)(2,1)S(1)}, bf16[2,512,512]{2,1,0:T(8,128)(2,1)S(1)}, u32[]{:S(2)}, u32[]{:S(2)}) collective-permute-start(bf16[2,512,512]{2,1,0:T(8,128)(2,1)S(1)} %mirror.1.mirrored), channel_id=1, source_target_pairs={{0,4},{4,0},{8,12},{12,8},{16,20},{20,16},{24,28},{28,24},{1,5},{5... | collective-permute-start | bytes 3145736 | tf_op jit(solution)/shard_map/ppermute | solution.py:149
  27.2 10.1 %collective-permute-start.10 = (bf16[128,1024]{1,0:T(8,128)(2,1)S(1)}, bf16[128,1024]{1,0:T(8,128)(2,1)S(1)}, u32[]{:S(2)}, u32[]{:S(2)}) collective-permute-start(bf16[128,1024]{1,0:T(8,128)(2,1)S(1)} %get-tuple-element.65), channel_id=1, source_target_pairs={{0,24},{4,28},{8,16},{12,20},{16,8},{20,12},{24,0},{28,4},{1,25},{... | collective-permute-start | bytes 786440 | tf_op jit(solution)/shard_map/ppermute | solution.py:149
  29.6 12.9 %collective-permute-start.8 = (bf16[128,1024]{1,0:T(8,128)(2,1)S(1)}, bf16[128,1024]{1,0:T(8,128)(2,1)S(1)}, u32[]{:S(2)}, u32[]{:S(2)}) collective-permute-start(bf16[128,1024]{1,0:T(8,128)(2,1)S(1)} %get-tuple-element.63), channel_id=1, source_target_pairs={{0,8},{4,12},{8,0},{12,4},{16,24},{20,28},{24,16},{28,20},{1,9},{5... | collective-permute-start | bytes 786440 | tf_op jit(solution)/shard_map/ppermute | solution.py:149
  30.1 12.4 %collective-permute-start.9 = (bf16[128,1024]{1,0:T(8,128)(2,1)S(1)}, bf16[128,1024]{1,0:T(8,128)(2,1)S(1)}, u32[]{:S(2)}, u32[]{:S(2)}) collective-permute-start(bf16[128,1024]{1,0:T(8,128)(2,1)S(1)} %get-tuple-element.64), channel_id=1, source_target_pairs={{0,16},{4,20},{8,24},{12,28},{16,0},{20,4},{24,8},{28,12},{1,17},{... | collective-permute-start | bytes 786440 | tf_op jit(solution)/shard_map/ppermute | solution.py:149
  30.7 6.6 %collective-permute-start.6 = (bf16[256,128]{1,0:T(8,128)(2,1)S(1)}, bf16[256,128]{1,0:T(8,128)(2,1)S(1)}, u32[]{:S(2)}, u32[]{:S(2)}) collective-permute-start(bf16[256,128]{1,0:T(8,128)(2,1)S(1)} %convert_element_type.18), channel_id=1, source_target_pairs={{0,2},{1,3},{2,0},{3,1},{4,6},{5,7},{6,4},{7,5},{8,10},{9,11},{10,... | collective-permute-start | bytes 196616 | tf_op jit(solution)/shard_map/ppermute | solution.py:153
  32.2 5.0 %collective-permute-start.7 = (bf16[256,128]{1,0:T(8,128)(2,1)S(1)}, bf16[256,128]{1,0:T(8,128)(2,1)S(1)}, u32[]{:S(2)}, u32[]{:S(2)}) collective-permute-start(bf16[256,128]{1,0:T(8,128)(2,1)S(1)} %convert_element_type.18), channel_id=1, source_target_pairs={{0,3},{1,0},{2,1},{3,2},{4,7},{5,4},{6,5},{7,6},{8,11},{9,8},{10,9... | collective-permute-start | bytes 196616 | tf_op jit(solution)/shard_map/ppermute | solution.py:153
  43.0 2.1 %collective-permute-start.14 = (bf16[128,1024]{1,0:T(8,128)(2,1)S(1)}, bf16[128,1024]{1,0:T(8,128)(2,1)S(1)}, u32[]{:S(2)}, u32[]{:S(2)}) collective-permute-start(bf16[128,1024]{1,0:T(8,128)(2,1)S(1)} %collective-permute-done.10.refs_3_), channel_id=1, source_target_pairs={{0,4},{4,0},{8,12},{12,8},{16,20},{20,16},{24,28},{28,24},{1,5},{5... | collective-permute-start | bytes 786440 | tf_op jit(solution)/shard_map/ppermute | solution.py:149
  46.5 5.9 %collective-permute-start.15 = (f32[256,128]{1,0:T(8,128)S(1)}, f32[256,128]{1,0:T(8,128)S(1)}, u32[]{:S(2)}, u32[]{:S(2)}) collective-permute-start(f32[256,128]{1,0:T(8,128)S(1)} %get-tuple-element.94), channel_id=1, source_target_pairs={{0,8},{4,12},{8,0},{12,4},{16,24},{20,28},{24,16},{28,20},{1,9},{5... | collective-permute-start | bytes 393224 | tf_op jit(solution)/shard_map/ppermute | solution.py:149
  48.1 8.1 %collective-permute-start.16 = (f32[256,128]{1,0:T(8,128)S(1)}, f32[256,128]{1,0:T(8,128)S(1)}, u32[]{:S(2)}, u32[]{:S(2)}) collective-permute-start(f32[256,128]{1,0:T(8,128)S(1)} %get-tuple-element.96), channel_id=1, source_target_pairs={{0,16},{4,20},{8,24},{12,28},{16,0},{20,4},{24,8},{28,12},{1,17},{... | collective-permute-start | bytes 393224 | tf_op jit(solution)/shard_map/ppermute | solution.py:149
  49.5 6.7 %collective-permute-start.17 = (f32[256,128]{1,0:T(8,128)S(1)}, f32[256,128]{1,0:T(8,128)S(1)}, u32[]{:S(2)}, u32[]{:S(2)}) collective-permute-start(f32[256,128]{1,0:T(8,128)S(1)} %get-tuple-element.95), channel_id=1, source_target_pairs={{0,24},{4,28},{8,16},{12,20},{16,8},{20,12},{24,0},{28,4},{1,25},{... | collective-permute-start | bytes 393224 | tf_op jit(solution)/shard_map/ppermute | solution.py:149
  56.2 6.2 %collective-permute-start.18 = (bf16[256,128]{1,0:T(8,128)(2,1)S(1)}, bf16[256,128]{1,0:T(8,128)(2,1)S(1)}, u32[]{:S(2)}, u32[]{:S(2)}) collective-permute-start(bf16[256,128]{1,0:T(8,128)(2,1)S(1)} %get-tuple-element.86), channel_id=1, source_target_pairs={{0,1},{1,2},{2,3},{3,0},{4,5},{5,6},{6,7},{7,4},{8,9},{9,10},{10,1... | collective-permute-start | bytes 196616 | tf_op jit(solution)/shard_map/ppermute | solution.py:153
  57.2 6.9 %collective-permute-start.19 = (bf16[256,128]{1,0:T(8,128)(2,1)S(1)}, bf16[256,128]{1,0:T(8,128)(2,1)S(1)}, u32[]{:S(2)}, u32[]{:S(2)}) collective-permute-start(bf16[256,128]{1,0:T(8,128)(2,1)S(1)} %get-tuple-element.86), channel_id=1, source_target_pairs={{0,2},{1,3},{2,0},{3,1},{4,6},{5,7},{6,4},{7,5},{8,10},{9,11},{10,... | collective-permute-start | bytes 196616 | tf_op jit(solution)/shard_map/ppermute | solution.py:153
  58.8 5.3 %collective-permute-start.20 = (bf16[256,128]{1,0:T(8,128)(2,1)S(1)}, bf16[256,128]{1,0:T(8,128)(2,1)S(1)}, u32[]{:S(2)}, u32[]{:S(2)}) collective-permute-start(bf16[256,128]{1,0:T(8,128)(2,1)S(1)} %get-tuple-element.86), channel_id=1, source_target_pairs={{0,3},{1,0},{2,1},{3,2},{4,7},{5,4},{6,5},{7,6},{8,11},{9,8},{10,9... | collective-permute-start | bytes 196616 | tf_op jit(solution)/shard_map/ppermute | solution.py:153
  64.9 5.7 %collective-permute-start.21 = (f32[256,128]{1,0:T(8,128)S(1)}, f32[256,128]{1,0:T(8,128)S(1)}, u32[]{:S(2)}, u32[]{:S(2)}) collective-permute-start(f32[256,128]{1,0:T(8,128)S(1)} %get-tuple-element.91), channel_id=1, source_target_pairs={{0,8},{4,12},{8,0},{12,4},{16,24},{20,28},{24,16},{28,20},{1,9},{5... | collective-permute-start | bytes 393224 | tf_op jit(solution)/shard_map/ppermute | solution.py:149
  66.5 5.0 %collective-permute-start.22 = (f32[256,128]{1,0:T(8,128)S(1)}, f32[256,128]{1,0:T(8,128)S(1)}, u32[]{:S(2)}, u32[]{:S(2)}) collective-permute-start(f32[256,128]{1,0:T(8,128)S(1)} %get-tuple-element.93), channel_id=1, source_target_pairs={{0,16},{4,20},{8,24},{12,28},{16,0},{20,4},{24,8},{28,12},{1,17},{... | collective-permute-start | bytes 393224 | tf_op jit(solution)/shard_map/ppermute | solution.py:149
  67.2 5.9 %collective-permute-start.23 = (f32[256,128]{1,0:T(8,128)S(1)}, f32[256,128]{1,0:T(8,128)S(1)}, u32[]{:S(2)}, u32[]{:S(2)}) collective-permute-start(f32[256,128]{1,0:T(8,128)S(1)} %get-tuple-element.92), channel_id=1, source_target_pairs={{0,24},{4,28},{8,16},{12,20},{16,8},{20,12},{24,0},{28,4},{1,25},{... | collective-permute-start | bytes 393224 | tf_op jit(solution)/shard_map/ppermute | solution.py:149
  73.2 6.1 %collective-permute-start.24 = (bf16[256,128]{1,0:T(8,128)(2,1)S(1)}, bf16[256,128]{1,0:T(8,128)(2,1)S(1)}, u32[]{:S(2)}, u32[]{:S(2)}) collective-permute-start(bf16[256,128]{1,0:T(8,128)(2,1)S(1)} %get-tuple-element.84), channel_id=1, source_target_pairs={{0,1},{1,2},{2,3},{3,0},{4,5},{5,6},{6,7},{7,4},{8,9},{9,10},{10,1... | collective-permute-start | bytes 196616 | tf_op jit(solution)/shard_map/ppermute | solution.py:153
  75.4 5.4 %collective-permute-start.25 = (bf16[256,128]{1,0:T(8,128)(2,1)S(1)}, bf16[256,128]{1,0:T(8,128)(2,1)S(1)}, u32[]{:S(2)}, u32[]{:S(2)}) collective-permute-start(bf16[256,128]{1,0:T(8,128)(2,1)S(1)} %get-tuple-element.84), channel_id=1, source_target_pairs={{0,2},{1,3},{2,0},{3,1},{4,6},{5,7},{6,4},{7,5},{8,10},{9,11},{10,... | collective-permute-start | bytes 196616 | tf_op jit(solution)/shard_map/ppermute | solution.py:153
  76.7 4.8 %collective-permute-start.26 = (bf16[256,128]{1,0:T(8,128)(2,1)S(1)}, bf16[256,128]{1,0:T(8,128)(2,1)S(1)}, u32[]{:S(2)}, u32[]{:S(2)}) collective-permute-start(bf16[256,128]{1,0:T(8,128)(2,1)S(1)} %get-tuple-element.84), channel_id=1, source_target_pairs={{0,3},{1,0},{2,1},{3,2},{4,7},{5,4},{6,5},{7,6},{8,11},{9,8},{10,9... | collective-permute-start | bytes 196616 | tf_op jit(solution)/shard_map/ppermute | solution.py:153
  82.2 5.0 %collective-permute-start.27 = (f32[256,128]{1,0:T(8,128)S(1)}, f32[256,128]{1,0:T(8,128)S(1)}, u32[]{:S(2)}, u32[]{:S(2)}) collective-permute-start(f32[256,128]{1,0:T(8,128)S(1)} %get-tuple-element.88), channel_id=1, source_target_pairs={{0,8},{4,12},{8,0},{12,4},{16,24},{20,28},{24,16},{28,20},{1,9},{5... | collective-permute-start | bytes 393224 | tf_op jit(solution)/shard_map/ppermute | solution.py:149
  82.9 5.0 %collective-permute-start.28 = (f32[256,128]{1,0:T(8,128)S(1)}, f32[256,128]{1,0:T(8,128)S(1)}, u32[]{:S(2)}, u32[]{:S(2)}) collective-permute-start(f32[256,128]{1,0:T(8,128)S(1)} %get-tuple-element.90), channel_id=1, source_target_pairs={{0,16},{4,20},{8,24},{12,28},{16,0},{20,4},{24,8},{28,12},{1,17},{... | collective-permute-start | bytes 393224 | tf_op jit(solution)/shard_map/ppermute | solution.py:149
  84.2 5.9 %collective-permute-start.29 = (f32[256,128]{1,0:T(8,128)S(1)}, f32[256,128]{1,0:T(8,128)S(1)}, u32[]{:S(2)}, u32[]{:S(2)}) collective-permute-start(f32[256,128]{1,0:T(8,128)S(1)} %get-tuple-element.89), channel_id=1, source_target_pairs={{0,24},{4,28},{8,16},{12,20},{16,8},{20,12},{24,0},{28,4},{1,25},{... | collective-permute-start | bytes 393224 | tf_op jit(solution)/shard_map/ppermute | solution.py:149
  90.1 6.3 %collective-permute-start.30 = (bf16[256,128]{1,0:T(8,128)(2,1)S(1)}, bf16[256,128]{1,0:T(8,128)(2,1)S(1)}, u32[]{:S(2)}, u32[]{:S(2)}) collective-permute-start(bf16[256,128]{1,0:T(8,128)(2,1)S(1)} %get-tuple-element.82), channel_id=1, source_target_pairs={{0,1},{1,2},{2,3},{3,0},{4,5},{5,6},{6,7},{7,4},{8,9},{9,10},{10,1... | collective-permute-start | bytes 196616 | tf_op jit(solution)/shard_map/ppermute | solution.py:153
  90.7 7.2 %collective-permute-start.31 = (bf16[256,128]{1,0:T(8,128)(2,1)S(1)}, bf16[256,128]{1,0:T(8,128)(2,1)S(1)}, u32[]{:S(2)}, u32[]{:S(2)}) collective-permute-start(bf16[256,128]{1,0:T(8,128)(2,1)S(1)} %get-tuple-element.82), channel_id=1, source_target_pairs={{0,2},{1,3},{2,0},{3,1},{4,6},{5,7},{6,4},{7,5},{8,10},{9,11},{10,... | collective-permute-start | bytes 196616 | tf_op jit(solution)/shard_map/ppermute | solution.py:153
  93.0 4.9 %collective-permute-start.32 = (bf16[256,128]{1,0:T(8,128)(2,1)S(1)}, bf16[256,128]{1,0:T(8,128)(2,1)S(1)}, u32[]{:S(2)}, u32[]{:S(2)}) collective-permute-start(bf16[256,128]{1,0:T(8,128)(2,1)S(1)} %get-tuple-element.82), channel_id=1, source_target_pairs={{0,3},{1,0},{2,1},{3,2},{4,7},{5,4},{6,5},{7,6},{8,11},{9,8},{10,9... | collective-permute-start | bytes 196616 | tf_op jit(solution)/shard_map/ppermute | solution.py:153
  94.0 4.3 %collective-permute-start.33 = (bf16[256,128]{1,0:T(8,128)(2,1)S(1)}, bf16[256,128]{1,0:T(8,128)(2,1)S(1)}, u32[]{:S(2)}, u32[]{:S(2)}) collective-permute-start(bf16[256,128]{1,0:T(8,128)(2,1)S(1)} %get-tuple-element.82), channel_id=1, source_target_pairs={{0,8},{4,12},{8,0},{12,4},{16,24},{20,28},{24,16},{28,20},{1,9},{5... | collective-permute-start | bytes 196616 | tf_op jit(solution)/shard_map/ppermute | solution.py:149
  95.3 4.3 %collective-permute-start.34 = (bf16[256,128]{1,0:T(8,128)(2,1)S(1)}, bf16[256,128]{1,0:T(8,128)(2,1)S(1)}, u32[]{:S(2)}, u32[]{:S(2)}) collective-permute-start(bf16[256,128]{1,0:T(8,128)(2,1)S(1)} %get-tuple-element.82), channel_id=1, source_target_pairs={{0,16},{4,20},{8,24},{12,28},{16,0},{20,4},{24,8},{28,12},{1,17},{... | collective-permute-start | bytes 196616 | tf_op jit(solution)/shard_map/ppermute | solution.py:149
  96.4 5.2 %collective-permute-start.35 = (bf16[256,128]{1,0:T(8,128)(2,1)S(1)}, bf16[256,128]{1,0:T(8,128)(2,1)S(1)}, u32[]{:S(2)}, u32[]{:S(2)}) collective-permute-start(bf16[256,128]{1,0:T(8,128)(2,1)S(1)} %get-tuple-element.82), channel_id=1, source_target_pairs={{0,24},{4,28},{8,16},{12,20},{16,8},{20,12},{24,0},{28,4},{1,25},{... | collective-permute-start | bytes 196616 | tf_op jit(solution)/shard_map/ppermute | solution.py:149
  101.6 2.1 %collective-permute-start.36 = (bf16[1024,128]{1,0:T(8,128)(2,1)S(1)}, bf16[1024,128]{1,0:T(8,128)(2,1)S(1)}, u32[]{:S(2)}, u32[]{:S(2)}) collective-permute-start(bf16[1024,128]{1,0:T(8,128)(2,1)S(1)} %get-tuple-element.71), channel_id=1, source_target_pairs={{0,4},{4,0},{8,12},{12,8},{16,20},{20,16},{24,28},{28,24},{1,5},{5... | collective-permute-start | bytes 786440 | tf_op jit(solution)/shard_map/ppermute | solution.py:149
  105.2 4.4 %collective-permute-start.38 = (f32[2,64,128]{2,1,0:T(8,128)S(1)}, f32[2,64,128]{2,1,0:T(8,128)S(1)}, u32[]{:S(2)}, u32[]{:S(2)}) collective-permute-start(f32[2,64,128]{2,1,0:T(8,128)S(1)} %get-tuple-element.97), channel_id=1, source_target_pairs={{0,8},{4,12},{8,0},{12,4},{16,24},{20,28},{24,16},{28,20},{1,9},{5... | collective-permute-start | bytes 196616 | tf_op jit(solution)/shard_map/ppermute | solution.py:149
  106.5 4.3 %collective-permute-start.39 = (f32[2,64,128]{2,1,0:T(8,128)S(1)}, f32[2,64,128]{2,1,0:T(8,128)S(1)}, u32[]{:S(2)}, u32[]{:S(2)}) collective-permute-start(f32[2,64,128]{2,1,0:T(8,128)S(1)} %get-tuple-element.99), channel_id=1, source_target_pairs={{0,16},{4,20},{8,24},{12,28},{16,0},{20,4},{24,8},{28,12},{1,17},{... | collective-permute-start | bytes 196616 | tf_op jit(solution)/shard_map/ppermute | solution.py:149
  107.4 5.2 %collective-permute-start.40 = (f32[2,64,128]{2,1,0:T(8,128)S(1)}, f32[2,64,128]{2,1,0:T(8,128)S(1)}, u32[]{:S(2)}, u32[]{:S(2)}) collective-permute-start(f32[2,64,128]{2,1,0:T(8,128)S(1)} %get-tuple-element.98), channel_id=1, source_target_pairs={{0,24},{4,28},{8,16},{12,20},{16,8},{20,12},{24,0},{28,4},{1,25},{... | collective-permute-start | bytes 196616 | tf_op jit(solution)/shard_map/ppermute | solution.py:149
  108.7 7.4 %collective-permute-start.45 = (f32[128,128]{1,0:T(8,128)S(1)}, f32[128,128]{1,0:T(8,128)S(1)}, u32[]{:S(2)}, u32[]{:S(2)}) collective-permute-start(f32[128,128]{1,0:T(8,128)S(1)} %get-tuple-element.113), channel_id=1, source_target_pairs={{0,4},{4,0},{8,12},{12,8},{16,20},{20,16},{24,28},{28,24},{1,5},{5... | collective-permute-start | bytes 196616 | tf_op jit(solution)/shard_map/ppermute | solution.py:149
  112.6 5.3 %collective-permute-start.41 = (f32[64,128]{1,0:T(8,128)S(1)}, f32[64,128]{1,0:T(8,128)S(1)}, u32[]{:S(2)}, u32[]{:S(2)}) collective-permute-start(f32[64,128]{1,0:T(8,128)S(1)} %get-tuple-element.123), channel_id=1, source_target_pairs={{0,8},{4,12},{8,0},{12,4},{16,24},{20,28},{24,16},{28,20},{1,9},{5... | collective-permute-start | bytes 98312 | tf_op jit(solution)/shard_map/ppermute | solution.py:149
  113.5 7.2 %collective-permute-start.42 = (f32[64,128]{1,0:T(8,128)S(1)}, f32[64,128]{1,0:T(8,128)S(1)}, u32[]{:S(2)}, u32[]{:S(2)}) collective-permute-start(f32[64,128]{1,0:T(8,128)S(1)} %get-tuple-element.123), channel_id=1, source_target_pairs={{0,16},{4,20},{8,24},{12,28},{16,0},{20,4},{24,8},{28,12},{1,17},{... | collective-permute-start | bytes 98312 | tf_op jit(solution)/shard_map/ppermute | solution.py:149
  114.6 6.1 %collective-permute-start.43 = (f32[64,128]{1,0:T(8,128)S(1)}, f32[64,128]{1,0:T(8,128)S(1)}, u32[]{:S(2)}, u32[]{:S(2)}) collective-permute-start(f32[64,128]{1,0:T(8,128)S(1)} %get-tuple-element.123), channel_id=1, source_target_pairs={{0,24},{4,28},{8,16},{12,20},{16,8},{20,12},{24,0},{28,4},{1,25},{... | collective-permute-start | bytes 98312 | tf_op jit(solution)/shard_map/ppermute | solution.py:149
  116.1 5.8 %collective-permute-start.46 = (f32[64,128]{1,0:T(8,128)S(1)}, f32[64,128]{1,0:T(8,128)S(1)}, u32[]{:S(2)}, u32[]{:S(2)}) collective-permute-start(f32[64,128]{1,0:T(8,128)S(1)} %get-tuple-element.122), channel_id=1, source_target_pairs={{0,1},{1,2},{2,3},{3,0},{4,5},{5,6},{6,7},{7,4},{8,9},{9,10},{10,1... | collective-permute-start | bytes 98312 | tf_op jit(solution)/shard_map/ppermute | solution.py:153
  116.8 5.2 %collective-permute-start.47 = (f32[64,128]{1,0:T(8,128)S(1)}, f32[64,128]{1,0:T(8,128)S(1)}, u32[]{:S(2)}, u32[]{:S(2)}) collective-permute-start(f32[64,128]{1,0:T(8,128)S(1)} %get-tuple-element.122), channel_id=1, source_target_pairs={{0,2},{1,3},{2,0},{3,1},{4,6},{5,7},{6,4},{7,5},{8,10},{9,11},{10,... | collective-permute-start | bytes 98312 | tf_op jit(solution)/shard_map/ppermute | solution.py:153
  117.8 4.6 %collective-permute-start.48 = (f32[64,128]{1,0:T(8,128)S(1)}, f32[64,128]{1,0:T(8,128)S(1)}, u32[]{:S(2)}, u32[]{:S(2)}) collective-permute-start(f32[64,128]{1,0:T(8,128)S(1)} %get-tuple-element.122), channel_id=1, source_target_pairs={{0,3},{1,0},{2,1},{3,2},{4,7},{5,4},{6,5},{7,6},{8,11},{9,8},{10,9... | collective-permute-start | bytes 98312 | tf_op jit(solution)/shard_map/ppermute | solution.py:153
  120.9 5.2 %collective-permute-start.44 = (f32[256,128]{1,0:T(8,128)S(1)}, f32[256,128]{1,0:T(8,128)S(1)}, u32[]{:S(2)}, u32[]{:S(2)}) collective-permute-start(f32[256,128]{1,0:T(8,128)S(1)} %maximum_select_fusion.4), channel_id=1, source_target_pairs={{0,4},{4,0},{8,12},{12,8},{16,20},{20,16},{24,28},{28,24},{1,5},{5... | collective-permute-start | bytes 393224 | tf_op jit(solution)/shard_map/ppermute | solution.py:149
  122.5 11.5 %collective-permute-start.49 = (f32[64,128]{1,0:T(8,128)S(1)}, f32[64,128]{1,0:T(8,128)S(1)}, u32[]{:S(2)}, u32[]{:S(2)}) collective-permute-start(f32[64,128]{1,0:T(8,128)S(1)} %add_add_fusion), channel_id=1, source_target_pairs={{0,8},{4,12},{8,0},{12,4},{16,24},{20,28},{24,16},{28,20},{1,9},{5... | collective-permute-start | bytes 98312 | tf_op jit(solution)/shard_map/ppermute | solution.py:149
  123.7 10.3 %collective-permute-start.50 = (f32[64,128]{1,0:T(8,128)S(1)}, f32[64,128]{1,0:T(8,128)S(1)}, u32[]{:S(2)}, u32[]{:S(2)}) collective-permute-start(f32[64,128]{1,0:T(8,128)S(1)} %add_add_fusion), channel_id=1, source_target_pairs={{0,16},{4,20},{8,24},{12,28},{16,0},{20,4},{24,8},{28,12},{1,17},{... | collective-permute-start | bytes 98312 | tf_op jit(solution)/shard_map/ppermute | solution.py:149
  124.6 9.4 %collective-permute-start.51 = (f32[64,128]{1,0:T(8,128)S(1)}, f32[64,128]{1,0:T(8,128)S(1)}, u32[]{:S(2)}, u32[]{:S(2)}) collective-permute-start(f32[64,128]{1,0:T(8,128)S(1)} %add_add_fusion), channel_id=1, source_target_pairs={{0,24},{4,28},{8,16},{12,20},{16,8},{20,12},{24,0},{28,4},{1,25},{... | collective-permute-start | bytes 98312 | tf_op jit(solution)/shard_map/ppermute | solution.py:149
  (9 other events, 55.0 us)

commit v6 on v4

--- a/solution.py
+++ b/solution.py
@@ -173,8 +173,16 @@
 
 
 def places_of(places_ref, owner):
-    ids = lax.broadcasted_iota(jnp.int32, places_ref.shape, 0)
-    return jnp.sum(jnp.where(ids == owner, places_ref[...], 0.0), 0, keepdims=True)
+    height, slots = places_ref.shape
+    width = PB * slots
+    slot = lax.broadcasted_iota(jnp.int32, (slots, width), 0)
+    lane = lax.broadcasted_iota(jnp.int32, (slots, width), 1)
+    repeat = (lane % slots == slot).astype(jnp.float32)
+    copies = jnp.dot(places_ref[...], repeat, precision=HI, preferred_element_type=jnp.float32)
+    row = lax.broadcasted_iota(jnp.int32, (height, width), 0)
+    block = lax.broadcasted_iota(jnp.int32, (height, width), 1) // slots
+    taken = row == owner * PB + block
+    return jnp.sum(jnp.where(taken, copies, 0.0), 0, keepdims=True)
 
 
 def pack_kernel(col_ref, blocks_ref, places_ref, *piece_refs):
@@ -182,7 +190,7 @@
     for s, piece in enumerate(piece_refs, 1):
         owner = lax.rem(col_ref[0] + s, cols)
         piece[:, : BS * BS] = blocks_ref[owner]
-        count = places_ref.shape[1]
+        count = piece.shape[0]
         row = jnp.broadcast_to(places_of(places_ref, owner), (piece.shape[0], count))
         piece[:, BS * BS : BS * BS + count] = row.astype(jnp.bfloat16)
 
@@ -347,7 +355,6 @@
     apart = (device % 2) ^ core
     distance = (device // 2) ^ chip
     places = jnp.where(live, (distance * 2 + apart) * PB + block, -1).astype(jnp.float32)
-    places = places.reshape(cols, PB * slots)
     block_row = jnp.arange(row_blocks, dtype=jnp.int32)[:, None]
     near_row = (col - block_row // PB) % cols * PB + block_row % PB
     groups = rows * row_blocks
@@ -391,7 +398,16 @@
     direct = direct_rows(col[None], by_owner, places, pieces, rows, slots)
     mirrored, direct = lax.optimization_barrier((mirrored, direct))
     mirrored_other = core_swap(mirrored, rows)
-    direct = [chip_swap(direct[s], rows, s) if s else direct[s] for s in range(chips)]
+    direct = [
+        lax.ppermute(
+            direct[s],
+            "row",
+            [(i, i ^ (2 * s)) for i in range(rows) if i ^ (2 * s) > i],
+        )
+        if s
+        else direct[s]
+        for s in range(chips)
+    ]
     first, mirrored_other = lax.optimization_barrier(
         (start.astype(jnp.bfloat16), mirrored_other)
     )

time: 135 us -> 139 us (1.030)
  starting transfers between devices: 63.3 us -> 67.7 us
    ppermute x0 -> x3, starting transfers between devices: none -> 8.14 us  [local(): lax.ppermute(direct[s], 'row', [(i, i ^ 2 * s) for i in range(rows) if i...]
    ppermute x35 -> x32, starting transfers between devices: 30.8 us -> 27.3 us  [exchanged(): return lax.ppermute(x, axis, [(i, i ^ apart) for i in range(size)])]
    ppermute x35 -> x32, waiting for transfers between devices: 23.9 us -> 23.3 us  [exchanged(): return lax.ppermute(x, axis, [(i, i ^ apart) for i in range(size)])]
  transfers between devices with their start and end apart: 53 -> 53, of which waited for: 31 -> 30; matrix products, arithmetic and copies ran while one was open for 1% -> 1% of each run, Pallas kernels for 8% -> 7%
where the time goes in v6:
time: 139 us
  starting transfers between devices  67.7 us (49%)
  waiting for transfers between devices  41.8 us (30%)
  Pallas kernels  17.6 us (13%)
  matrix products  4.24 us (3%)
  other arithmetic  2.98 us (2%)
  between operations  2.57 us (2%)
  local copies, waits for them, and re-layouts  2.12 us (2%)
    ppermute x18, starting transfers between devices, shifted(): return lax.ppermute(x, axis, [(i, (i + step) % size) for i in range(size)])  32.3 us
    ppermute x32, starting transfers between devices, exchanged(): return lax.ppermute(x, axis, [(i, i ^ apart) for i in range(size)])  27.3 us
    ppermute x32, waiting for transfers between devices, exchanged(): return lax.ppermute(x, axis, [(i, i ^ apart) for i in range(size)])  23.3 us
    ppermute x18, waiting for transfers between devices, shifted(): return lax.ppermute(x, axis, [(i, (i + step) % size) for i in range(size)])  18.4 us
    ppermute x3, starting transfers between devices, local(): lax.ppermute(direct[s], 'row', [(i, i ^ 2 * s) for i in range(rows) if i...  8.14 us
    pallas_call x1, Pallas kernels, factorize(): pl.pallas_call(functools.partial(factor_kernel, total_rows), out_shape=(j...  7.94 us
    pallas_call x1, Pallas kernels, direct_rows(): pl.pallas_call(functools.partial(direct_kernel, rows, slots), out_shape=(...  3.1 us
    dot_general x4, matrix products, partial_product(): return jnp.dot(tile, gathered, preferred_element_type=jnp.float32)  2.82 us
  transfers between devices with their start and end apart: 53, of which 30 were waited for; matrix products, arithmetic and copies ran while one was open for 1% of the time, Pallas kernels for 7%

profile of v6, /device:TPU:0, one launch (start us, length us, event | category | flops | bytes accessed | tf_op | source)
XLA Modules:
  0.0 139.0 jit_solution(12916257999567760808)
XLA Ops:
  0.7 1.4 %select_convert_fusion = (f32[8,8]{1,0:T(8,128)}, s32[8,8]{1,0:T(8,128)S(1)}) fusion(s32[8]{0:T(128)} %bitcast.128, s32[8,8]{1,0:T(8,128)} %param.9, s32[]{:T(128)S(6)} %select_n.201, s32[]{:T(128)S(6)} %select_n.204, s32[8]{0:T(128)S(1)} %fusion.50), kind=kLoop, calls=%fused_computation.96 | loop fusion | flops 3456 | bytes 840 | tf_op jit(solution)/shard_map/convert_element_type | solution.py:357
  3.1 1.9 %pack.1 = (bf16[16,4224]{1,0:T(8,128)(2,1)}, bf16[16,4224]{1,0:T(8,128)(2,1)}, bf16[16,4224]{1,0:T(8,128)(2,1)}) custom-call(s32[1]{0:T(128)} %bitcast.1.col_ref, bf16[4,16,4096]{2,1,0:T(8,128)(2,1)} %bitcast.91, f32[8,8]{1,0:T(8,128)} %get-tuple-element.123.places_ref), custom_call_target="tpu_custom_call" | custom-call | tf_op jit(solution)/shard_map/pack/pallas_call | solution.py:201
  5.5 2.6 %collective-permute-start = (bf16[16,4224]{1,0:T(8,128)(2,1)}, bf16[16,4224]{1,0:T(8,128)(2,1)S(1)}, u32[]{:S(2)}, u32[]{:S(2)}) collective-permute-start(bf16[16,4224]{1,0:T(8,128)(2,1)} %get-tuple-element.43), channel_id=1, source_target_pairs={{0,1},{1,2},{2,3},{3,0},{4,5},{5,6},{6,7},{7,4},{8,9},{9,10},{10,1... | collective-permute-start | bytes 405512 | tf_op jit(solution)/shard_map/ppermute | solution.py:153
  8.0 2.6 %collective-permute-start.1 = (bf16[16,4224]{1,0:T(8,128)(2,1)}, bf16[16,4224]{1,0:T(8,128)(2,1)S(1)}, u32[]{:S(2)}, u32[]{:S(2)}) collective-permute-start(bf16[16,4224]{1,0:T(8,128)(2,1)} %get-tuple-element.44), channel_id=1, source_target_pairs={{0,2},{1,3},{2,0},{3,1},{4,6},{5,7},{6,4},{7,5},{8,10},{9,11},{10,... | collective-permute-start | bytes 405512 | tf_op jit(solution)/shard_map/ppermute | solution.py:153
  10.6 1.3 collective-permute-start.2
  13.7 2.3 %mirror.1.mirrored = bf16[2,512,512]{2,1,0:T(8,128)(2,1)S(1)} custom-call(s32[1,64]{1,0:T(1,128)S(1)} %reshape.248.key_ref, bf16[64,4096]{1,0:T(8,128)(2,1)S(1)} %bitcast.92, bf16[2,4096]{1,0:T(2,128)(2,1)S(1)} %copy-done.3), custom_call_target="tpu_custom_call" | custom-call | flops 67108864 | bytes 786432 | tf_op jit(solution)/shard_map/mirror/pallas_call | solution.py:241
  16.0 4.3 %collective-permute-done.1.refs_1_ = bf16[16,4224]{1,0:T(8,128)(2,1)S(1)} collective-permute-done((bf16[16,4224]{1,0:T(8,128)(2,1)}, bf16[16,4224]{1,0:T(8,128)(2,1)S(1)}, u32[]{:S(2)}, u32[]{:S(2)}) %collective-permute-start.1) | collective-permute-done | bytes 135200 | tf_op jit(solution)/shard_map/ppermute | solution.py:153
  20.4 3.1 %direct_rows.1 = (bf16[128,1024]{1,0:T(8,128)(2,1)S(1)}, bf16[128,1024]{1,0:T(8,128)(2,1)S(1)}, bf16[128,1024]{1,0:T(8,128)(2,1)S(1)}, bf16[128,1024]{1,0:T(8,128)(2,1)S(1)}) custom-call(s32[1]{0:T(128)} %bitcast.1.col_ref, bf16[4,16,4096]{2,1,0:T(8,128)(2,1)S(1)} %bitcast.93, f32[8,8]{1,0:T(8,128)S(1)} %copy-done.2, ...), custom_call_target="tpu_custom_call" | custom-call | tf_op jit(solution)/shard_map/direct_rows/pallas_call | solution.py:293
  23.6 4.4 %collective-permute-start.10 = (bf16[128,1024]{1,0:T(8,128)(2,1)S(1)}, bf16[128,1024]{1,0:T(8,128)(2,1)S(1)}, u32[]{:S(2)}, u32[]{:S(2)}) collective-permute-start(bf16[128,1024]{1,0:T(8,128)(2,1)S(1)} %get-tuple-element.61), channel_id=1, source_target_pairs={{0,24},{4,28},{8,16},{12,20},{1,25},{5,29},{9,17},{13,21},{2,26},{... | collective-permute-start | bytes 786440 | tf_op jit(solution)/shard_map/ppermute | solution.py:402
  27.9 2.5 %collective-permute-start.8 = (bf16[128,1024]{1,0:T(8,128)(2,1)S(1)}, bf16[128,1024]{1,0:T(8,128)(2,1)S(1)}, u32[]{:S(2)}, u32[]{:S(2)}) collective-permute-start(bf16[128,1024]{1,0:T(8,128)(2,1)S(1)} %get-tuple-element.59), channel_id=1, source_target_pairs={{0,8},{4,12},{16,24},{20,28},{1,9},{5,13},{17,25},{21,29},{2,10},{... | collective-permute-start | bytes 786440 | tf_op jit(solution)/shard_map/ppermute | solution.py:402
  30.4 1.3 collective-permute-start.9
  31.8 3.5 %collective-permute-start.5 = (bf16[256,128]{1,0:T(8,128)(2,1)S(1)}, bf16[256,128]{1,0:T(8,128)(2,1)S(1)}, u32[]{:S(2)}, u32[]{:S(2)}) collective-permute-start(bf16[256,128]{1,0:T(8,128)(2,1)S(1)} %convert_element_type.18), channel_id=1, source_target_pairs={{0,1},{1,2},{2,3},{3,0},{4,5},{5,6},{6,7},{7,4},{8,9},{9,10},{10,1... | collective-permute-start | bytes 196616 | tf_op jit(solution)/shard_map/ppermute | solution.py:153
  35.2 1.6 %collective-permute-start.6 = (bf16[256,128]{1,0:T(8,128)(2,1)S(1)}, bf16[256,128]{1,0:T(8,128)(2,1)S(1)}, u32[]{:S(2)}, u32[]{:S(2)}) collective-permute-start(bf16[256,128]{1,0:T(8,128)(2,1)S(1)} %convert_element_type.18), channel_id=1, source_target_pairs={{0,2},{1,3},{2,0},{3,1},{4,6},{5,7},{6,4},{7,5},{8,10},{9,11},{10,... | collective-permute-start | bytes 196616 | tf_op jit(solution)/shard_map/ppermute | solution.py:153
  36.8 2.1 %collective-permute-done.5 = bf16[256,128]{1,0:T(8,128)(2,1)S(1)} collective-permute-done((bf16[256,128]{1,0:T(8,128)(2,1)S(1)}, bf16[256,128]{1,0:T(8,128)(2,1)S(1)}, u32[]{:S(2)}, u32[]{:S(2)}) %collective-permute-start.5) | collective-permute-done | bytes 65568 | tf_op jit(solution)/shard_map/ppermute | solution.py:153
  39.0 2.6 %collective-permute-start.7 = (bf16[256,128]{1,0:T(8,128)(2,1)S(1)}, bf16[256,128]{1,0:T(8,128)(2,1)S(1)}, u32[]{:S(2)}, u32[]{:S(2)}) collective-permute-start(bf16[256,128]{1,0:T(8,128)(2,1)S(1)} %convert_element_type.18), channel_id=1, source_target_pairs={{0,3},{1,0},{2,1},{3,2},{4,7},{5,4},{6,5},{7,6},{8,11},{9,8},{10,9... | collective-permute-start | bytes 196616 | tf_op jit(solution)/shard_map/ppermute | solution.py:153
  41.6 1.9 %collective-permute-done.7 = bf16[256,128]{1,0:T(8,128)(2,1)S(1)} collective-permute-done((bf16[256,128]{1,0:T(8,128)(2,1)S(1)}, bf16[256,128]{1,0:T(8,128)(2,1)S(1)}, u32[]{:S(2)}, u32[]{:S(2)}) %collective-permute-start.7) | collective-permute-done | bytes 65568 | tf_op jit(solution)/shard_map/ppermute | solution.py:153
  47.8 3.4 %collective-permute-start.17 = (f32[256,128]{1,0:T(8,128)S(1)}, f32[256,128]{1,0:T(8,128)S(1)}, u32[]{:S(2)}, u32[]{:S(2)}) collective-permute-start(f32[256,128]{1,0:T(8,128)S(1)} %get-tuple-element.91), channel_id=1, source_target_pairs={{0,24},{4,28},{8,16},{12,20},{16,8},{20,12},{24,0},{28,4},{1,25},{... | collective-permute-start | bytes 393224 | tf_op jit(solution)/shard_map/ppermute | solution.py:149
  52.5 1.5 %collective-permute-done.15 = f32[256,128]{1,0:T(8,128)S(1)} collective-permute-done((f32[256,128]{1,0:T(8,128)S(1)}, f32[256,128]{1,0:T(8,128)S(1)}, u32[]{:S(2)}, u32[]{:S(2)}) %collective-permute-start.15) | collective-permute-done | bytes 131104 | tf_op jit(solution)/shard_map/ppermute | solution.py:149
  54.1 2.1 %collective-permute-done.16 = f32[256,128]{1,0:T(8,128)S(1)} collective-permute-done((f32[256,128]{1,0:T(8,128)S(1)}, f32[256,128]{1,0:T(8,128)S(1)}, u32[]{:S(2)}, u32[]{:S(2)}) %collective-permute-start.16) | collective-permute-done | bytes 131104 | tf_op jit(solution)/shard_map/ppermute | solution.py:149
  56.2 1.7 %collective-permute-start.18 = (bf16[256,128]{1,0:T(8,128)(2,1)S(1)}, bf16[256,128]{1,0:T(8,128)(2,1)S(1)}, u32[]{:S(2)}, u32[]{:S(2)}) collective-permute-start(bf16[256,128]{1,0:T(8,128)(2,1)S(1)} %get-tuple-element.82), channel_id=1, source_target_pairs={{0,1},{1,2},{2,3},{3,0},{4,5},{5,6},{6,7},{7,4},{8,9},{9,10},{10,1... | collective-permute-start | bytes 196616 | tf_op jit(solution)/shard_map/ppermute | solution.py:153
  57.9 3.1 %collective-permute-start.19 = (bf16[256,128]{1,0:T(8,128)(2,1)S(1)}, bf16[256,128]{1,0:T(8,128)(2,1)S(1)}, u32[]{:S(2)}, u32[]{:S(2)}) collective-permute-start(bf16[256,128]{1,0:T(8,128)(2,1)S(1)} %get-tuple-element.82), channel_id=1, source_target_pairs={{0,2},{1,3},{2,0},{3,1},{4,6},{5,7},{6,4},{7,5},{8,10},{9,11},{10,... | collective-permute-start | bytes 196616 | tf_op jit(solution)/shard_map/ppermute | solution.py:153
  61.0 2.4 %collective-permute-done.18 = bf16[256,128]{1,0:T(8,128)(2,1)S(1)} collective-permute-done((bf16[256,128]{1,0:T(8,128)(2,1)S(1)}, bf16[256,128]{1,0:T(8,128)(2,1)S(1)}, u32[]{:S(2)}, u32[]{:S(2)}) %collective-permute-start.18) | collective-permute-done | bytes 65568 | tf_op jit(solution)/shard_map/ppermute | solution.py:153
  63.4 1.6 %collective-permute-done.19 = bf16[256,128]{1,0:T(8,128)(2,1)S(1)} collective-permute-done((bf16[256,128]{1,0:T(8,128)(2,1)S(1)}, bf16[256,128]{1,0:T(8,128)(2,1)S(1)}, u32[]{:S(2)}, u32[]{:S(2)}) %collective-permute-start.19) | collective-permute-done | bytes 65568 | tf_op jit(solution)/shard_map/ppermute | solution.py:153
  66.3 1.8 %collective-permute-start.21 = (f32[256,128]{1,0:T(8,128)S(1)}, f32[256,128]{1,0:T(8,128)S(1)}, u32[]{:S(2)}, u32[]{:S(2)}) collective-permute-start(f32[256,128]{1,0:T(8,128)S(1)} %get-tuple-element.87), channel_id=1, source_target_pairs={{0,8},{4,12},{8,0},{12,4},{16,24},{20,28},{24,16},{28,20},{1,9},{5... | collective-permute-start | bytes 393224 | tf_op jit(solution)/shard_map/ppermute | solution.py:149
  68.3 1.5 %collective-permute-start.23 = (f32[256,128]{1,0:T(8,128)S(1)}, f32[256,128]{1,0:T(8,128)S(1)}, u32[]{:S(2)}, u32[]{:S(2)}) collective-permute-start(f32[256,128]{1,0:T(8,128)S(1)} %get-tuple-element.88), channel_id=1, source_target_pairs={{0,24},{4,28},{8,16},{12,20},{16,8},{20,12},{24,0},{28,4},{1,25},{... | collective-permute-start | bytes 393224 | tf_op jit(solution)/shard_map/ppermute | solution.py:149
  69.8 2.6 %collective-permute-done.21 = f32[256,128]{1,0:T(8,128)S(1)} collective-permute-done((f32[256,128]{1,0:T(8,128)S(1)}, f32[256,128]{1,0:T(8,128)S(1)}, u32[]{:S(2)}, u32[]{:S(2)}) %collective-permute-start.21) | collective-permute-done | bytes 131104 | tf_op jit(solution)/shard_map/ppermute | solution.py:149
  72.4 2.5 %collective-permute-done.22 = f32[256,128]{1,0:T(8,128)S(1)} collective-permute-done((f32[256,128]{1,0:T(8,128)S(1)}, f32[256,128]{1,0:T(8,128)S(1)}, u32[]{:S(2)}, u32[]{:S(2)}) %collective-permute-start.22) | collective-permute-done | bytes 131104 | tf_op jit(solution)/shard_map/ppermute | solution.py:149
  75.0 1.9 %collective-permute-start.24 = (bf16[256,128]{1,0:T(8,128)(2,1)S(1)}, bf16[256,128]{1,0:T(8,128)(2,1)S(1)}, u32[]{:S(2)}, u32[]{:S(2)}) collective-permute-start(bf16[256,128]{1,0:T(8,128)(2,1)S(1)} %get-tuple-element.80), channel_id=1, source_target_pairs={{0,1},{1,2},{2,3},{3,0},{4,5},{5,6},{6,7},{7,4},{8,9},{9,10},{10,1... | collective-permute-start | bytes 196616 | tf_op jit(solution)/shard_map/ppermute | solution.py:153
  77.3 2.1 %collective-permute-start.26 = (bf16[256,128]{1,0:T(8,128)(2,1)S(1)}, bf16[256,128]{1,0:T(8,128)(2,1)S(1)}, u32[]{:S(2)}, u32[]{:S(2)}) collective-permute-start(bf16[256,128]{1,0:T(8,128)(2,1)S(1)} %get-tuple-element.80), channel_id=1, source_target_pairs={{0,3},{1,0},{2,1},{3,2},{4,7},{5,4},{6,5},{7,6},{8,11},{9,8},{10,9... | collective-permute-start | bytes 196616 | tf_op jit(solution)/shard_map/ppermute | solution.py:153
  79.3 2.2 %collective-permute-done.24 = bf16[256,128]{1,0:T(8,128)(2,1)S(1)} collective-permute-done((bf16[256,128]{1,0:T(8,128)(2,1)S(1)}, bf16[256,128]{1,0:T(8,128)(2,1)S(1)}, u32[]{:S(2)}, u32[]{:S(2)}) %collective-permute-start.24) | collective-permute-done | bytes 65568 | tf_op jit(solution)/shard_map/ppermute | solution.py:153
  81.5 1.3 collective-permute-done.25
  85.4 1.7 %collective-permute-start.29 = (f32[256,128]{1,0:T(8,128)S(1)}, f32[256,128]{1,0:T(8,128)S(1)}, u32[]{:S(2)}, u32[]{:S(2)}) collective-permute-start(f32[256,128]{1,0:T(8,128)S(1)} %get-tuple-element.85), channel_id=1, source_target_pairs={{0,24},{4,28},{8,16},{12,20},{16,8},{20,12},{24,0},{28,4},{1,25},{... | collective-permute-start | bytes 393224 | tf_op jit(solution)/shard_map/ppermute | solution.py:149
  87.1 1.5 %collective-permute-done.27 = f32[256,128]{1,0:T(8,128)S(1)} collective-permute-done((f32[256,128]{1,0:T(8,128)S(1)}, f32[256,128]{1,0:T(8,128)S(1)}, u32[]{:S(2)}, u32[]{:S(2)}) %collective-permute-start.27) | collective-permute-done | bytes 131104 | tf_op jit(solution)/shard_map/ppermute | solution.py:149
  89.4 1.9 %collective-permute-done.29 = f32[256,128]{1,0:T(8,128)S(1)} collective-permute-done((f32[256,128]{1,0:T(8,128)S(1)}, f32[256,128]{1,0:T(8,128)S(1)}, u32[]{:S(2)}, u32[]{:S(2)}) %collective-permute-start.29) | collective-permute-done | bytes 131104 | tf_op jit(solution)/shard_map/ppermute | solution.py:149
  92.6 2.1 %collective-permute-start.31 = (bf16[256,128]{1,0:T(8,128)(2,1)S(1)}, bf16[256,128]{1,0:T(8,128)(2,1)S(1)}, u32[]{:S(2)}, u32[]{:S(2)}) collective-permute-start(bf16[256,128]{1,0:T(8,128)(2,1)S(1)} %get-tuple-element.78), channel_id=1, source_target_pairs={{0,2},{1,3},{2,0},{3,1},{4,6},{5,7},{6,4},{7,5},{8,10},{9,11},{10,... | collective-permute-start | bytes 196616 | tf_op jit(solution)/shard_map/ppermute | solution.py:153
  96.3 1.5 %collective-permute-start.34 = (bf16[256,128]{1,0:T(8,128)(2,1)S(1)}, bf16[256,128]{1,0:T(8,128)(2,1)S(1)}, u32[]{:S(2)}, u32[]{:S(2)}) collective-permute-start(bf16[256,128]{1,0:T(8,128)(2,1)S(1)} %get-tuple-element.78), channel_id=1, source_target_pairs={{0,16},{4,20},{8,24},{12,28},{16,0},{20,4},{24,8},{28,12},{1,17},{... | collective-permute-start | bytes 196616 | tf_op jit(solution)/shard_map/ppermute | solution.py:149
  97.9 1.4 %collective-permute-start.35 = (bf16[256,128]{1,0:T(8,128)(2,1)S(1)}, bf16[256,128]{1,0:T(8,128)(2,1)S(1)}, u32[]{:S(2)}, u32[]{:S(2)}) collective-permute-start(bf16[256,128]{1,0:T(8,128)(2,1)S(1)} %get-tuple-element.78), channel_id=1, source_target_pairs={{0,24},{4,28},{8,16},{12,20},{16,8},{20,12},{24,0},{28,4},{1,25},{... | collective-permute-start | bytes 196616 | tf_op jit(solution)/shard_map/ppermute | solution.py:149
  100.6 2.4 %collective-permute-done.35 = bf16[256,128]{1,0:T(8,128)(2,1)S(1)} collective-permute-done((bf16[256,128]{1,0:T(8,128)(2,1)S(1)}, bf16[256,128]{1,0:T(8,128)(2,1)S(1)}, u32[]{:S(2)}, u32[]{:S(2)}) %collective-permute-start.35) | collective-permute-done | bytes 65568 | tf_op jit(solution)/shard_map/ppermute | solution.py:149
  108.7 1.5 %collective-permute-start.40 = (f32[2,64,128]{2,1,0:T(8,128)S(1)}, f32[2,64,128]{2,1,0:T(8,128)S(1)}, u32[]{:S(2)}, u32[]{:S(2)}) collective-permute-start(f32[2,64,128]{2,1,0:T(8,128)S(1)} %get-tuple-element.94), channel_id=1, source_target_pairs={{0,24},{4,28},{8,16},{12,20},{16,8},{20,12},{24,0},{28,4},{1,25},{... | collective-permute-start | bytes 196616 | tf_op jit(solution)/shard_map/ppermute | solution.py:149
  111.8 2.1 %collective-permute-done.40 = f32[2,64,128]{2,1,0:T(8,128)S(1)} collective-permute-done((f32[2,64,128]{2,1,0:T(8,128)S(1)}, f32[2,64,128]{2,1,0:T(8,128)S(1)}, u32[]{:S(2)}, u32[]{:S(2)}) %collective-permute-start.40) | collective-permute-done | bytes 65568 | tf_op jit(solution)/shard_map/ppermute | solution.py:149
  114.7 1.4 collective-permute-start.42
  116.0 1.4 %collective-permute-start.43 = (f32[64,128]{1,0:T(8,128)S(1)}, f32[64,128]{1,0:T(8,128)S(1)}, u32[]{:S(2)}, u32[]{:S(2)}) collective-permute-start(f32[64,128]{1,0:T(8,128)S(1)} %get-tuple-element.119), channel_id=1, source_target_pairs={{0,24},{4,28},{8,16},{12,20},{16,8},{20,12},{24,0},{28,4},{1,25},{... | collective-permute-start | bytes 98312 | tf_op jit(solution)/shard_map/ppermute | solution.py:149
  119.4 2.6 %collective-permute-start.48 = (f32[64,128]{1,0:T(8,128)S(1)}, f32[64,128]{1,0:T(8,128)S(1)}, u32[]{:S(2)}, u32[]{:S(2)}) collective-permute-start(f32[64,128]{1,0:T(8,128)S(1)} %get-tuple-element.118), channel_id=1, source_target_pairs={{0,3},{1,0},{2,1},{3,2},{4,7},{5,4},{6,5},{7,6},{8,11},{9,8},{10,9... | collective-permute-start | bytes 98312 | tf_op jit(solution)/shard_map/ppermute | solution.py:153
  124.8 1.4 collective-permute-start.50
  126.1 1.5 %collective-permute-start.51 = (f32[64,128]{1,0:T(8,128)S(1)}, f32[64,128]{1,0:T(8,128)S(1)}, u32[]{:S(2)}, u32[]{:S(2)}) collective-permute-start(f32[64,128]{1,0:T(8,128)S(1)} %add_add_fusion), channel_id=1, source_target_pairs={{0,24},{4,28},{8,16},{12,20},{16,8},{20,12},{24,0},{28,4},{1,25},{... | collective-permute-start | bytes 98312 | tf_op jit(solution)/shard_map/ppermute | solution.py:149
  127.6 7.9 %factorize.1 = (f32[128,256]{1,0:T(8,128)}, f32[256,256]{1,0:T(8,128)S(1)}) custom-call(f32[256,256]{1,0:T(8,128)S(1)} %maximum_select_fusion.2.gram_ref, f32[128,256]{1,0:T(8,128)S(1)} %maximum_select_fusion.5.y_ref), custom_call_target="tpu_custom_call" | custom-call | bytes 5242880 | tf_op jit(solution)/shard_map/factorize/pallas_call | solution.py:124
  135.8 1.3 collective-permute-done.52
  137.2 1.8 %project.1 = f32[256,256]{1,0:T(8,128)} custom-call(f32[256,256]{1,0:T(8,128)S(1)} %get-tuple-element.71.inverse_ref, f32[256,256]{1,0:T(8,128)S(1)} %maximum_select_fusion.3.cross_ref), custom_call_target="tpu_custom_call" | custom-call | tf_op jit(solution)/shard_map/project/pallas_call | solution.py:138
  (133 shorter events, 29.8 us)
Async XLA Ops:
  5.0 11.0 %collective-permute-start.3 = (f32[128,128]{1,0:T(8,128)S(1)}, f32[128,128]{1,0:T(8,128)S(1)}, u32[]{:S(2)}, u32[]{:S(2)}) collective-permute-start(f32[128,128]{1,0:T(8,128)S(1)} %get-tuple-element.46), channel_id=1, source_target_pairs={{0,4},{4,0},{8,12},{12,8},{16,20},{20,16},{24,28},{28,24},{1,5},{5... | collective-permute-start | bytes 196616 | tf_op jit(solution)/shard_map/ppermute | solution.py:149
  5.5 10.6 %collective-permute-start = (bf16[16,4224]{1,0:T(8,128)(2,1)}, bf16[16,4224]{1,0:T(8,128)(2,1)S(1)}, u32[]{:S(2)}, u32[]{:S(2)}) collective-permute-start(bf16[16,4224]{1,0:T(8,128)(2,1)} %get-tuple-element.43), channel_id=1, source_target_pairs={{0,1},{1,2},{2,3},{3,0},{4,5},{5,6},{6,7},{7,4},{8,9},{9,10},{10,1... | collective-permute-start | bytes 405512 | tf_op jit(solution)/shard_map/ppermute | solution.py:153
  8.0 12.3 %collective-permute-start.1 = (bf16[16,4224]{1,0:T(8,128)(2,1)}, bf16[16,4224]{1,0:T(8,128)(2,1)S(1)}, u32[]{:S(2)}, u32[]{:S(2)}) collective-permute-start(bf16[16,4224]{1,0:T(8,128)(2,1)} %get-tuple-element.44), channel_id=1, source_target_pairs={{0,2},{1,3},{2,0},{3,1},{4,6},{5,7},{6,4},{7,5},{8,10},{9,11},{10,... | collective-permute-start | bytes 405512 | tf_op jit(solution)/shard_map/ppermute | solution.py:153
  10.6 9.8 %collective-permute-start.2 = (bf16[16,4224]{1,0:T(8,128)(2,1)}, bf16[16,4224]{1,0:T(8,128)(2,1)S(1)}, u32[]{:S(2)}, u32[]{:S(2)}) collective-permute-start(bf16[16,4224]{1,0:T(8,128)(2,1)} %get-tuple-element.45), channel_id=1, source_target_pairs={{0,3},{1,0},{2,1},{3,2},{4,7},{5,4},{6,5},{7,6},{8,11},{9,8},{10,9... | collective-permute-start | bytes 405512 | tf_op jit(solution)/shard_map/ppermute | solution.py:153
  23.5 8.3 %collective-permute-start.4 = (bf16[2,512,512]{2,1,0:T(8,128)(2,1)S(1)}, bf16[2,512,512]{2,1,0:T(8,128)(2,1)S(1)}, u32[]{:S(2)}, u32[]{:S(2)}) collective-permute-start(bf16[2,512,512]{2,1,0:T(8,128)(2,1)S(1)} %mirror.1.mirrored), channel_id=1, source_target_pairs={{0,4},{4,0},{8,12},{12,8},{16,20},{20,16},{24,28},{28,24},{1,5},{5... | collective-permute-start | bytes 3145736 | tf_op jit(solution)/shard_map/ppermute | solution.py:149
  23.6 20.0 %collective-permute-start.10 = (bf16[128,1024]{1,0:T(8,128)(2,1)S(1)}, bf16[128,1024]{1,0:T(8,128)(2,1)S(1)}, u32[]{:S(2)}, u32[]{:S(2)}) collective-permute-start(bf16[128,1024]{1,0:T(8,128)(2,1)S(1)} %get-tuple-element.61), channel_id=1, source_target_pairs={{0,24},{4,28},{8,16},{12,20},{1,25},{5,29},{9,17},{13,21},{2,26},{... | collective-permute-start | bytes 786440 | tf_op jit(solution)/shard_map/ppermute | solution.py:402
  27.9 15.6 %collective-permute-start.8 = (bf16[128,1024]{1,0:T(8,128)(2,1)S(1)}, bf16[128,1024]{1,0:T(8,128)(2,1)S(1)}, u32[]{:S(2)}, u32[]{:S(2)}) collective-permute-start(bf16[128,1024]{1,0:T(8,128)(2,1)S(1)} %get-tuple-element.59), channel_id=1, source_target_pairs={{0,8},{4,12},{16,24},{20,28},{1,9},{5,13},{17,25},{21,29},{2,10},{... | collective-permute-start | bytes 786440 | tf_op jit(solution)/shard_map/ppermute | solution.py:402
  30.4 13.2 %collective-permute-start.9 = (bf16[128,1024]{1,0:T(8,128)(2,1)S(1)}, bf16[128,1024]{1,0:T(8,128)(2,1)S(1)}, u32[]{:S(2)}, u32[]{:S(2)}) collective-permute-start(bf16[128,1024]{1,0:T(8,128)(2,1)S(1)} %get-tuple-element.60), channel_id=1, source_target_pairs={{0,16},{4,20},{8,24},{12,28},{1,17},{5,21},{9,25},{13,29},{2,18},{... | collective-permute-start | bytes 786440 | tf_op jit(solution)/shard_map/ppermute | solution.py:402
  31.8 7.2 %collective-permute-start.5 = (bf16[256,128]{1,0:T(8,128)(2,1)S(1)}, bf16[256,128]{1,0:T(8,128)(2,1)S(1)}, u32[]{:S(2)}, u32[]{:S(2)}) collective-permute-start(bf16[256,128]{1,0:T(8,128)(2,1)S(1)} %convert_element_type.18), channel_id=1, source_target_pairs={{0,1},{1,2},{2,3},{3,0},{4,5},{5,6},{6,7},{7,4},{8,9},{9,10},{10,1... | collective-permute-start | bytes 196616 | tf_op jit(solution)/shard_map/ppermute | solution.py:153
  35.2 6.4 %collective-permute-start.6 = (bf16[256,128]{1,0:T(8,128)(2,1)S(1)}, bf16[256,128]{1,0:T(8,128)(2,1)S(1)}, u32[]{:S(2)}, u32[]{:S(2)}) collective-permute-start(bf16[256,128]{1,0:T(8,128)(2,1)S(1)} %convert_element_type.18), channel_id=1, source_target_pairs={{0,2},{1,3},{2,0},{3,1},{4,6},{5,7},{6,4},{7,5},{8,10},{9,11},{10,... | collective-permute-start | bytes 196616 | tf_op jit(solution)/shard_map/ppermute | solution.py:153
  39.0 4.6 %collective-permute-start.7 = (bf16[256,128]{1,0:T(8,128)(2,1)S(1)}, bf16[256,128]{1,0:T(8,128)(2,1)S(1)}, u32[]{:S(2)}, u32[]{:S(2)}) collective-permute-start(bf16[256,128]{1,0:T(8,128)(2,1)S(1)} %convert_element_type.18), channel_id=1, source_target_pairs={{0,3},{1,0},{2,1},{3,2},{4,7},{5,4},{6,5},{7,6},{8,11},{9,8},{10,9... | collective-permute-start | bytes 196616 | tf_op jit(solution)/shard_map/ppermute | solution.py:153
  44.2 2.1 %collective-permute-start.14 = (bf16[128,1024]{1,0:T(8,128)(2,1)S(1)}, bf16[128,1024]{1,0:T(8,128)(2,1)S(1)}, u32[]{:S(2)}, u32[]{:S(2)}) collective-permute-start(bf16[128,1024]{1,0:T(8,128)(2,1)S(1)} %collective-permute-done.10.refs_3_), channel_id=1, source_target_pairs={{0,4},{4,0},{8,12},{12,8},{16,20},{20,16},{24,28},{28,24},{1,5},{5... | collective-permute-start | bytes 786440 | tf_op jit(solution)/shard_map/ppermute | solution.py:149
  47.7 6.4 %collective-permute-start.15 = (f32[256,128]{1,0:T(8,128)S(1)}, f32[256,128]{1,0:T(8,128)S(1)}, u32[]{:S(2)}, u32[]{:S(2)}) collective-permute-start(f32[256,128]{1,0:T(8,128)S(1)} %get-tuple-element.90), channel_id=1, source_target_pairs={{0,8},{4,12},{8,0},{12,4},{16,24},{20,28},{24,16},{28,20},{1,9},{5... | collective-permute-start | bytes 393224 | tf_op jit(solution)/shard_map/ppermute | solution.py:149
  47.8 8.4 %collective-permute-start.16 = (f32[256,128]{1,0:T(8,128)S(1)}, f32[256,128]{1,0:T(8,128)S(1)}, u32[]{:S(2)}, u32[]{:S(2)}) collective-permute-start(f32[256,128]{1,0:T(8,128)S(1)} %get-tuple-element.92), channel_id=1, source_target_pairs={{0,16},{4,20},{8,24},{12,28},{16,0},{20,4},{24,8},{28,12},{1,17},{... | collective-permute-start | bytes 393224 | tf_op jit(solution)/shard_map/ppermute | solution.py:149
  47.8 8.3 %collective-permute-start.17 = (f32[256,128]{1,0:T(8,128)S(1)}, f32[256,128]{1,0:T(8,128)S(1)}, u32[]{:S(2)}, u32[]{:S(2)}) collective-permute-start(f32[256,128]{1,0:T(8,128)S(1)} %get-tuple-element.91), channel_id=1, source_target_pairs={{0,24},{4,28},{8,16},{12,20},{16,8},{20,12},{24,0},{28,4},{1,25},{... | collective-permute-start | bytes 393224 | tf_op jit(solution)/shard_map/ppermute | solution.py:149
  56.2 7.2 %collective-permute-start.18 = (bf16[256,128]{1,0:T(8,128)(2,1)S(1)}, bf16[256,128]{1,0:T(8,128)(2,1)S(1)}, u32[]{:S(2)}, u32[]{:S(2)}) collective-permute-start(bf16[256,128]{1,0:T(8,128)(2,1)S(1)} %get-tuple-element.82), channel_id=1, source_target_pairs={{0,1},{1,2},{2,3},{3,0},{4,5},{5,6},{6,7},{7,4},{8,9},{9,10},{10,1... | collective-permute-start | bytes 196616 | tf_op jit(solution)/shard_map/ppermute | solution.py:153
  57.9 7.1 %collective-permute-start.19 = (bf16[256,128]{1,0:T(8,128)(2,1)S(1)}, bf16[256,128]{1,0:T(8,128)(2,1)S(1)}, u32[]{:S(2)}, u32[]{:S(2)}) collective-permute-start(bf16[256,128]{1,0:T(8,128)(2,1)S(1)} %get-tuple-element.82), channel_id=1, source_target_pairs={{0,2},{1,3},{2,0},{3,1},{4,6},{5,7},{6,4},{7,5},{8,10},{9,11},{10,... | collective-permute-start | bytes 196616 | tf_op jit(solution)/shard_map/ppermute | solution.py:153
  61.0 4.5 %collective-permute-start.20 = (bf16[256,128]{1,0:T(8,128)(2,1)S(1)}, bf16[256,128]{1,0:T(8,128)(2,1)S(1)}, u32[]{:S(2)}, u32[]{:S(2)}) collective-permute-start(bf16[256,128]{1,0:T(8,128)(2,1)S(1)} %get-tuple-element.82), channel_id=1, source_target_pairs={{0,3},{1,0},{2,1},{3,2},{4,7},{5,4},{6,5},{7,6},{8,11},{9,8},{10,9... | collective-permute-start | bytes 196616 | tf_op jit(solution)/shard_map/ppermute | solution.py:153
  66.3 6.2 %collective-permute-start.21 = (f32[256,128]{1,0:T(8,128)S(1)}, f32[256,128]{1,0:T(8,128)S(1)}, u32[]{:S(2)}, u32[]{:S(2)}) collective-permute-start(f32[256,128]{1,0:T(8,128)S(1)} %get-tuple-element.87), channel_id=1, source_target_pairs={{0,8},{4,12},{8,0},{12,4},{16,24},{20,28},{24,16},{28,20},{1,9},{5... | collective-permute-start | bytes 393224 | tf_op jit(solution)/shard_map/ppermute | solution.py:149
  68.0 6.9 %collective-permute-start.22 = (f32[256,128]{1,0:T(8,128)S(1)}, f32[256,128]{1,0:T(8,128)S(1)}, u32[]{:S(2)}, u32[]{:S(2)}) collective-permute-start(f32[256,128]{1,0:T(8,128)S(1)} %get-tuple-element.89), channel_id=1, source_target_pairs={{0,16},{4,20},{8,24},{12,28},{16,0},{20,4},{24,8},{28,12},{1,17},{... | collective-permute-start | bytes 393224 | tf_op jit(solution)/shard_map/ppermute | solution.py:149
  68.3 6.7 %collective-permute-start.23 = (f32[256,128]{1,0:T(8,128)S(1)}, f32[256,128]{1,0:T(8,128)S(1)}, u32[]{:S(2)}, u32[]{:S(2)}) collective-permute-start(f32[256,128]{1,0:T(8,128)S(1)} %get-tuple-element.88), channel_id=1, source_target_pairs={{0,24},{4,28},{8,16},{12,20},{16,8},{20,12},{24,0},{28,4},{1,25},{... | collective-permute-start | bytes 393224 | tf_op jit(solution)/shard_map/ppermute | solution.py:149
  75.0 6.5 %collective-permute-start.24 = (bf16[256,128]{1,0:T(8,128)(2,1)S(1)}, bf16[256,128]{1,0:T(8,128)(2,1)S(1)}, u32[]{:S(2)}, u32[]{:S(2)}) collective-permute-start(bf16[256,128]{1,0:T(8,128)(2,1)S(1)} %get-tuple-element.80), channel_id=1, source_target_pairs={{0,1},{1,2},{2,3},{3,0},{4,5},{5,6},{6,7},{7,4},{8,9},{9,10},{10,1... | collective-permute-start | bytes 196616 | tf_op jit(solution)/shard_map/ppermute | solution.py:153
  76.9 5.9 %collective-permute-start.25 = (bf16[256,128]{1,0:T(8,128)(2,1)S(1)}, bf16[256,128]{1,0:T(8,128)(2,1)S(1)}, u32[]{:S(2)}, u32[]{:S(2)}) collective-permute-start(bf16[256,128]{1,0:T(8,128)(2,1)S(1)} %get-tuple-element.80), channel_id=1, source_target_pairs={{0,2},{1,3},{2,0},{3,1},{4,6},{5,7},{6,4},{7,5},{8,10},{9,11},{10,... | collective-permute-start | bytes 196616 | tf_op jit(solution)/shard_map/ppermute | solution.py:153
  77.3 5.5 %collective-permute-start.26 = (bf16[256,128]{1,0:T(8,128)(2,1)S(1)}, bf16[256,128]{1,0:T(8,128)(2,1)S(1)}, u32[]{:S(2)}, u32[]{:S(2)}) collective-permute-start(bf16[256,128]{1,0:T(8,128)(2,1)S(1)} %get-tuple-element.80), channel_id=1, source_target_pairs={{0,3},{1,0},{2,1},{3,2},{4,7},{5,4},{6,5},{7,6},{8,11},{9,8},{10,9... | collective-permute-start | bytes 196616 | tf_op jit(solution)/shard_map/ppermute | solution.py:153
  83.6 5.0 %collective-permute-start.27 = (f32[256,128]{1,0:T(8,128)S(1)}, f32[256,128]{1,0:T(8,128)S(1)}, u32[]{:S(2)}, u32[]{:S(2)}) collective-permute-start(f32[256,128]{1,0:T(8,128)S(1)} %get-tuple-element.84), channel_id=1, source_target_pairs={{0,8},{4,12},{8,0},{12,4},{16,24},{20,28},{24,16},{28,20},{1,9},{5... | collective-permute-start | bytes 393224 | tf_op jit(solution)/shard_map/ppermute | solution.py:149
  84.4 5.0 %collective-permute-start.28 = (f32[256,128]{1,0:T(8,128)S(1)}, f32[256,128]{1,0:T(8,128)S(1)}, u32[]{:S(2)}, u32[]{:S(2)}) collective-permute-start(f32[256,128]{1,0:T(8,128)S(1)} %get-tuple-element.86), channel_id=1, source_target_pairs={{0,16},{4,20},{8,24},{12,28},{16,0},{20,4},{24,8},{28,12},{1,17},{... | collective-permute-start | bytes 393224 | tf_op jit(solution)/shard_map/ppermute | solution.py:149
  85.4 5.9 %collective-permute-start.29 = (f32[256,128]{1,0:T(8,128)S(1)}, f32[256,128]{1,0:T(8,128)S(1)}, u32[]{:S(2)}, u32[]{:S(2)}) collective-permute-start(f32[256,128]{1,0:T(8,128)S(1)} %get-tuple-element.85), channel_id=1, source_target_pairs={{0,24},{4,28},{8,16},{12,20},{16,8},{20,12},{24,0},{28,4},{1,25},{... | collective-permute-start | bytes 393224 | tf_op jit(solution)/shard_map/ppermute | solution.py:149
  91.3 6.5 %collective-permute-start.30 = (bf16[256,128]{1,0:T(8,128)(2,1)S(1)}, bf16[256,128]{1,0:T(8,128)(2,1)S(1)}, u32[]{:S(2)}, u32[]{:S(2)}) collective-permute-start(bf16[256,128]{1,0:T(8,128)(2,1)S(1)} %get-tuple-element.78), channel_id=1, source_target_pairs={{0,1},{1,2},{2,3},{3,0},{4,5},{5,6},{6,7},{7,4},{8,9},{9,10},{10,1... | collective-permute-start | bytes 196616 | tf_op jit(solution)/shard_map/ppermute | solution.py:153
  92.6 6.7 %collective-permute-start.31 = (bf16[256,128]{1,0:T(8,128)(2,1)S(1)}, bf16[256,128]{1,0:T(8,128)(2,1)S(1)}, u32[]{:S(2)}, u32[]{:S(2)}) collective-permute-start(bf16[256,128]{1,0:T(8,128)(2,1)S(1)} %get-tuple-element.78), channel_id=1, source_target_pairs={{0,2},{1,3},{2,0},{3,1},{4,6},{5,7},{6,4},{7,5},{8,10},{9,11},{10,... | collective-permute-start | bytes 196616 | tf_op jit(solution)/shard_map/ppermute | solution.py:153
  94.8 4.8 %collective-permute-start.32 = (bf16[256,128]{1,0:T(8,128)(2,1)S(1)}, bf16[256,128]{1,0:T(8,128)(2,1)S(1)}, u32[]{:S(2)}, u32[]{:S(2)}) collective-permute-start(bf16[256,128]{1,0:T(8,128)(2,1)S(1)} %get-tuple-element.78), channel_id=1, source_target_pairs={{0,3},{1,0},{2,1},{3,2},{4,7},{5,4},{6,5},{7,6},{8,11},{9,8},{10,9... | collective-permute-start | bytes 196616 | tf_op jit(solution)/shard_map/ppermute | solution.py:153
  95.8 4.3 %collective-permute-start.33 = (bf16[256,128]{1,0:T(8,128)(2,1)S(1)}, bf16[256,128]{1,0:T(8,128)(2,1)S(1)}, u32[]{:S(2)}, u32[]{:S(2)}) collective-permute-start(bf16[256,128]{1,0:T(8,128)(2,1)S(1)} %get-tuple-element.78), channel_id=1, source_target_pairs={{0,8},{4,12},{8,0},{12,4},{16,24},{20,28},{24,16},{28,20},{1,9},{5... | collective-permute-start | bytes 196616 | tf_op jit(solution)/shard_map/ppermute | solution.py:149
  96.3 4.3 %collective-permute-start.34 = (bf16[256,128]{1,0:T(8,128)(2,1)S(1)}, bf16[256,128]{1,0:T(8,128)(2,1)S(1)}, u32[]{:S(2)}, u32[]{:S(2)}) collective-permute-start(bf16[256,128]{1,0:T(8,128)(2,1)S(1)} %get-tuple-element.78), channel_id=1, source_target_pairs={{0,16},{4,20},{8,24},{12,28},{16,0},{20,4},{24,8},{28,12},{1,17},{... | collective-permute-start | bytes 196616 | tf_op jit(solution)/shard_map/ppermute | solution.py:149
  97.9 5.2 %collective-permute-start.35 = (bf16[256,128]{1,0:T(8,128)(2,1)S(1)}, bf16[256,128]{1,0:T(8,128)(2,1)S(1)}, u32[]{:S(2)}, u32[]{:S(2)}) collective-permute-start(bf16[256,128]{1,0:T(8,128)(2,1)S(1)} %get-tuple-element.78), channel_id=1, source_target_pairs={{0,24},{4,28},{8,16},{12,20},{16,8},{20,12},{24,0},{28,4},{1,25},{... | collective-permute-start | bytes 196616 | tf_op jit(solution)/shard_map/ppermute | solution.py:149
  103.1 2.1 %collective-permute-start.36 = (bf16[1024,128]{1,0:T(8,128)(2,1)S(1)}, bf16[1024,128]{1,0:T(8,128)(2,1)S(1)}, u32[]{:S(2)}, u32[]{:S(2)}) collective-permute-start(bf16[1024,128]{1,0:T(8,128)(2,1)S(1)} %get-tuple-element.67), channel_id=1, source_target_pairs={{0,4},{4,0},{8,12},{12,8},{16,20},{20,16},{24,28},{28,24},{1,5},{5... | collective-permute-start | bytes 786440 | tf_op jit(solution)/shard_map/ppermute | solution.py:149
  106.7 4.4 %collective-permute-start.38 = (f32[2,64,128]{2,1,0:T(8,128)S(1)}, f32[2,64,128]{2,1,0:T(8,128)S(1)}, u32[]{:S(2)}, u32[]{:S(2)}) collective-permute-start(f32[2,64,128]{2,1,0:T(8,128)S(1)} %get-tuple-element.93), channel_id=1, source_target_pairs={{0,8},{4,12},{8,0},{12,4},{16,24},{20,28},{24,16},{28,20},{1,9},{5... | collective-permute-start | bytes 196616 | tf_op jit(solution)/shard_map/ppermute | solution.py:149
  107.5 4.3 %collective-permute-start.39 = (f32[2,64,128]{2,1,0:T(8,128)S(1)}, f32[2,64,128]{2,1,0:T(8,128)S(1)}, u32[]{:S(2)}, u32[]{:S(2)}) collective-permute-start(f32[2,64,128]{2,1,0:T(8,128)S(1)} %get-tuple-element.95), channel_id=1, source_target_pairs={{0,16},{4,20},{8,24},{12,28},{16,0},{20,4},{24,8},{28,12},{1,17},{... | collective-permute-start | bytes 196616 | tf_op jit(solution)/shard_map/ppermute | solution.py:149
  108.7 5.2 %collective-permute-start.40 = (f32[2,64,128]{2,1,0:T(8,128)S(1)}, f32[2,64,128]{2,1,0:T(8,128)S(1)}, u32[]{:S(2)}, u32[]{:S(2)}) collective-permute-start(f32[2,64,128]{2,1,0:T(8,128)S(1)} %get-tuple-element.94), channel_id=1, source_target_pairs={{0,24},{4,28},{8,16},{12,20},{16,8},{20,12},{24,0},{28,4},{1,25},{... | collective-permute-start | bytes 196616 | tf_op jit(solution)/shard_map/ppermute | solution.py:149
  110.2 7.3 %collective-permute-start.45 = (f32[128,128]{1,0:T(8,128)S(1)}, f32[128,128]{1,0:T(8,128)S(1)}, u32[]{:S(2)}, u32[]{:S(2)}) collective-permute-start(f32[128,128]{1,0:T(8,128)S(1)} %get-tuple-element.109), channel_id=1, source_target_pairs={{0,4},{4,0},{8,12},{12,8},{16,20},{20,16},{24,28},{28,24},{1,5},{5... | collective-permute-start | bytes 196616 | tf_op jit(solution)/shard_map/ppermute | solution.py:149
  113.9 5.4 %collective-permute-start.41 = (f32[64,128]{1,0:T(8,128)S(1)}, f32[64,128]{1,0:T(8,128)S(1)}, u32[]{:S(2)}, u32[]{:S(2)}) collective-permute-start(f32[64,128]{1,0:T(8,128)S(1)} %get-tuple-element.119), channel_id=1, source_target_pairs={{0,8},{4,12},{8,0},{12,4},{16,24},{20,28},{24,16},{28,20},{1,9},{5... | collective-permute-start | bytes 98312 | tf_op jit(solution)/shard_map/ppermute | solution.py:149
  114.7 7.2 %collective-permute-start.42 = (f32[64,128]{1,0:T(8,128)S(1)}, f32[64,128]{1,0:T(8,128)S(1)}, u32[]{:S(2)}, u32[]{:S(2)}) collective-permute-start(f32[64,128]{1,0:T(8,128)S(1)} %get-tuple-element.119), channel_id=1, source_target_pairs={{0,16},{4,20},{8,24},{12,28},{16,0},{20,4},{24,8},{28,12},{1,17},{... | collective-permute-start | bytes 98312 | tf_op jit(solution)/shard_map/ppermute | solution.py:149
  116.0 5.9 %collective-permute-start.43 = (f32[64,128]{1,0:T(8,128)S(1)}, f32[64,128]{1,0:T(8,128)S(1)}, u32[]{:S(2)}, u32[]{:S(2)}) collective-permute-start(f32[64,128]{1,0:T(8,128)S(1)} %get-tuple-element.119), channel_id=1, source_target_pairs={{0,24},{4,28},{8,16},{12,20},{16,8},{20,12},{24,0},{28,4},{1,25},{... | collective-permute-start | bytes 98312 | tf_op jit(solution)/shard_map/ppermute | solution.py:149
  117.5 5.8 %collective-permute-start.46 = (f32[64,128]{1,0:T(8,128)S(1)}, f32[64,128]{1,0:T(8,128)S(1)}, u32[]{:S(2)}, u32[]{:S(2)}) collective-permute-start(f32[64,128]{1,0:T(8,128)S(1)} %get-tuple-element.118), channel_id=1, source_target_pairs={{0,1},{1,2},{2,3},{3,0},{4,5},{5,6},{6,7},{7,4},{8,9},{9,10},{10,1... | collective-permute-start | bytes 98312 | tf_op jit(solution)/shard_map/ppermute | solution.py:153
  118.5 5.5 %collective-permute-start.47 = (f32[64,128]{1,0:T(8,128)S(1)}, f32[64,128]{1,0:T(8,128)S(1)}, u32[]{:S(2)}, u32[]{:S(2)}) collective-permute-start(f32[64,128]{1,0:T(8,128)S(1)} %get-tuple-element.118), channel_id=1, source_target_pairs={{0,2},{1,3},{2,0},{3,1},{4,6},{5,7},{6,4},{7,5},{8,10},{9,11},{10,... | collective-permute-start | bytes 98312 | tf_op jit(solution)/shard_map/ppermute | solution.py:153
  119.4 4.7 %collective-permute-start.48 = (f32[64,128]{1,0:T(8,128)S(1)}, f32[64,128]{1,0:T(8,128)S(1)}, u32[]{:S(2)}, u32[]{:S(2)}) collective-permute-start(f32[64,128]{1,0:T(8,128)S(1)} %get-tuple-element.118), channel_id=1, source_target_pairs={{0,3},{1,0},{2,1},{3,2},{4,7},{5,4},{6,5},{7,6},{8,11},{9,8},{10,9... | collective-permute-start | bytes 98312 | tf_op jit(solution)/shard_map/ppermute | solution.py:153
  122.1 5.5 %collective-permute-start.44 = (f32[256,128]{1,0:T(8,128)S(1)}, f32[256,128]{1,0:T(8,128)S(1)}, u32[]{:S(2)}, u32[]{:S(2)}) collective-permute-start(f32[256,128]{1,0:T(8,128)S(1)} %maximum_select_fusion.4), channel_id=1, source_target_pairs={{0,4},{4,0},{8,12},{12,8},{16,20},{20,16},{24,28},{28,24},{1,5},{5... | collective-permute-start | bytes 393224 | tf_op jit(solution)/shard_map/ppermute | solution.py:149
  124.0 11.5 %collective-permute-start.49 = (f32[64,128]{1,0:T(8,128)S(1)}, f32[64,128]{1,0:T(8,128)S(1)}, u32[]{:S(2)}, u32[]{:S(2)}) collective-permute-start(f32[64,128]{1,0:T(8,128)S(1)} %add_add_fusion), channel_id=1, source_target_pairs={{0,8},{4,12},{8,0},{12,4},{16,24},{20,28},{24,16},{28,20},{1,9},{5... | collective-permute-start | bytes 98312 | tf_op jit(solution)/shard_map/ppermute | solution.py:149
  124.8 10.8 %collective-permute-start.50 = (f32[64,128]{1,0:T(8,128)S(1)}, f32[64,128]{1,0:T(8,128)S(1)}, u32[]{:S(2)}, u32[]{:S(2)}) collective-permute-start(f32[64,128]{1,0:T(8,128)S(1)} %add_add_fusion), channel_id=1, source_target_pairs={{0,16},{4,20},{8,24},{12,28},{16,0},{20,4},{24,8},{28,12},{1,17},{... | collective-permute-start | bytes 98312 | tf_op jit(solution)/shard_map/ppermute | solution.py:149
  126.1 9.5 %collective-permute-start.51 = (f32[64,128]{1,0:T(8,128)S(1)}, f32[64,128]{1,0:T(8,128)S(1)}, u32[]{:S(2)}, u32[]{:S(2)}) collective-permute-start(f32[64,128]{1,0:T(8,128)S(1)} %add_add_fusion), channel_id=1, source_target_pairs={{0,24},{4,28},{8,16},{12,20},{16,8},{20,12},{24,0},{28,4},{1,25},{... | collective-permute-start | bytes 98312 | tf_op jit(solution)/shard_map/ppermute | solution.py:149
  (9 other events, 48.2 us)

commit v7 on v4

--- a/solution.py
+++ b/solution.py
@@ -365,14 +365,10 @@
         ordered = jnp.concatenate([own, other], axis), jnp.concatenate([other, own], axis)
         return jnp.where(first_core, *ordered)
 
-    own, other = halves(orbitals_in)
-
     by_owner = hblocks.reshape(cols, PB * slots, BS * BS)
     pieces = pack(col[None], by_owner, places)
-    key, pieces, other = lax.optimization_barrier((key, pieces, other))
-    start = jnp.concatenate([own, core_swap(other, rows)], 0)
+    key, pieces = lax.optimization_barrier((key, pieces))
     pieces = [shifted(piece, "col", cols, s) for s, piece in enumerate(pieces, 1)]
-    pieces, start = lax.optimization_barrier((pieces, start))
 
     def gather(v):
         return jnp.concatenate([v] + [shifted(v, "col", cols, s) for s in range(1, cols)], 0)
@@ -387,6 +383,10 @@
     mirrored = mirror(
         key, hblocks.reshape(row_blocks * slots, BS * BS), onsite, rows, row_blocks
     )
+
+    orbitals_in, mirrored = lax.optimization_barrier((orbitals_in, mirrored))
+    own, other = halves(orbitals_in)
+    start = jnp.concatenate([own, core_swap(other, rows)], 0)
 
     direct = direct_rows(col[None], by_owner, places, pieces, rows, slots)
     mirrored, direct = lax.optimization_barrier((mirrored, direct))

time: 135 us -> 135 us (level)
  local copies, waits for them, and re-layouts: 2.78 us -> 4.98 us
    unnamed x8 -> x14, local copies, waits for them, and re-layouts: 1.77 us -> 3.97 us
  transfers between devices with their start and end apart: 53 -> 53, of which waited for: 31 -> 34; matrix products, arithmetic and copies ran while one was open for 1% -> 1% of each run, Pallas kernels for 8% -> 8%
where the time goes in v7:
time: 135 us
  starting transfers between devices  62.8 us (47%)
  waiting for transfers between devices  41.6 us (31%)
  Pallas kernels  17.5 us (13%)
  local copies, waits for them, and re-layouts  4.98 us (4%)
  matrix products  4.23 us (3%)
  between operations  2.54 us (2%)
  other arithmetic  1.56 us (1%)
    ppermute x18, starting transfers between devices, shifted(): return lax.ppermute(x, axis, [(i, (i + step) % size) for i in range(size)])  31.9 us
    ppermute x35, starting transfers between devices, exchanged(): return lax.ppermute(x, axis, [(i, i ^ apart) for i in range(size)])  30.9 us
    ppermute x35, waiting for transfers between devices, exchanged(): return lax.ppermute(x, axis, [(i, i ^ apart) for i in range(size)])  23.8 us
    ppermute x18, waiting for transfers between devices, shifted(): return lax.ppermute(x, axis, [(i, (i + step) % size) for i in range(size)])  17.8 us
    pallas_call x1, Pallas kernels, factorize(): pl.pallas_call(functools.partial(factor_kernel, total_rows), out_shape=(j...  7.94 us
    unnamed x14, local copies, waits for them, and re-layouts  3.97 us
    pallas_call x1, Pallas kernels, direct_rows(): pl.pallas_call(functools.partial(direct_kernel, rows, slots), out_shape=(...  3.07 us
    dot_general x4, matrix products, partial_product(): return jnp.dot(tile, gathered, preferred_element_type=jnp.float32)  2.81 us
  transfers between devices with their start and end apart: 53, of which 34 were waited for; matrix products, arithmetic and copies ran while one was open for 1% of the time, Pallas kernels for 8%

profile of v7, /device:TPU:0, one launch (start us, length us, event | category | flops | bytes accessed | tf_op | source)
XLA Modules:
  0.0 135.1 jit_solution(6456335193353294707)
XLA Ops:
  2.3 1.8 %pack.1 = (bf16[16,4224]{1,0:T(8,128)(2,1)}, bf16[16,4224]{1,0:T(8,128)(2,1)}, bf16[16,4224]{1,0:T(8,128)(2,1)}) custom-call(s32[1]{0:T(128)} %bitcast.1.col_ref, bf16[4,16,4096]{2,1,0:T(8,128)(2,1)} %bitcast.91, f32[4,16]{1,0:T(4,128)} %reshape.253.places_ref), custom_call_target="tpu_custom_call" | custom-call | tf_op jit(solution)/shard_map/pack/pallas_call | solution.py:193
  4.1 3.0 %collective-permute-start = (bf16[16,4224]{1,0:T(8,128)(2,1)}, bf16[16,4224]{1,0:T(8,128)(2,1)S(1)}, u32[]{:S(2)}, u32[]{:S(2)}) collective-permute-start(bf16[16,4224]{1,0:T(8,128)(2,1)} %get-tuple-element.41), channel_id=1, source_target_pairs={{0,1},{1,2},{2,3},{3,0},{4,5},{5,6},{6,7},{7,4},{8,9},{9,10},{10,1... | collective-permute-start | bytes 405512 | tf_op jit(solution)/shard_map/ppermute | solution.py:153
  7.1 2.6 %collective-permute-start.1 = (bf16[16,4224]{1,0:T(8,128)(2,1)}, bf16[16,4224]{1,0:T(8,128)(2,1)S(1)}, u32[]{:S(2)}, u32[]{:S(2)}) collective-permute-start(bf16[16,4224]{1,0:T(8,128)(2,1)} %get-tuple-element.42), channel_id=1, source_target_pairs={{0,2},{1,3},{2,0},{3,1},{4,6},{5,7},{6,4},{7,5},{8,10},{9,11},{10,... | collective-permute-start | bytes 405512 | tf_op jit(solution)/shard_map/ppermute | solution.py:153
  9.7 1.3 collective-permute-start.2
  12.8 2.3 %mirror.1.mirrored = bf16[2,512,512]{2,1,0:T(8,128)(2,1)S(1)} custom-call(s32[1,64]{1,0:T(1,128)S(1)} %reshape.251.key_ref, bf16[64,4096]{1,0:T(8,128)(2,1)S(1)} %bitcast.92, bf16[2,4096]{1,0:T(2,128)(2,1)S(1)} %copy-done.5), custom_call_target="tpu_custom_call" | custom-call | flops 67108864 | bytes 786432 | tf_op jit(solution)/shard_map/mirror/pallas_call | solution.py:233
  15.1 3.7 %collective-permute-done.1.refs_1_ = bf16[16,4224]{1,0:T(8,128)(2,1)S(1)} collective-permute-done((bf16[16,4224]{1,0:T(8,128)(2,1)}, bf16[16,4224]{1,0:T(8,128)(2,1)S(1)}, u32[]{:S(2)}, u32[]{:S(2)}) %collective-permute-start.1) | collective-permute-done | bytes 135200 | tf_op jit(solution)/shard_map/ppermute | solution.py:153
  18.8 3.1 %direct_rows.1 = (bf16[128,1024]{1,0:T(8,128)(2,1)S(1)}, bf16[128,1024]{1,0:T(8,128)(2,1)S(1)}, bf16[128,1024]{1,0:T(8,128)(2,1)S(1)}, bf16[128,1024]{1,0:T(8,128)(2,1)S(1)}) custom-call(s32[1]{0:T(128)} %bitcast.1.col_ref, bf16[4,16,4096]{2,1,0:T(8,128)(2,1)S(1)} %bitcast.93, f32[4,16]{1,0:T(4,128)S(1)} %copy-done.4, ...), custom_call_target="tpu_custom_call" | custom-call | tf_op jit(solution)/shard_map/direct_rows/pallas_call | solution.py:285
  22.5 2.5 %collective-permute-start.10 = (bf16[128,1024]{1,0:T(8,128)(2,1)S(1)}, bf16[128,1024]{1,0:T(8,128)(2,1)S(1)}, u32[]{:S(2)}, u32[]{:S(2)}) collective-permute-start(bf16[128,1024]{1,0:T(8,128)(2,1)S(1)} %get-tuple-element.55), channel_id=1, source_target_pairs={{0,24},{4,28},{8,16},{12,20},{16,8},{20,12},{24,0},{28,4},{1,25},{... | collective-permute-start | bytes 786440 | tf_op jit(solution)/shard_map/ppermute | solution.py:149
  27.0 3.4 %collective-permute-start.5 = (bf16[256,128]{1,0:T(8,128)(2,1)S(1)}, bf16[256,128]{1,0:T(8,128)(2,1)S(1)}, u32[]{:S(2)}, u32[]{:S(2)}) collective-permute-start(bf16[256,128]{1,0:T(8,128)(2,1)S(1)} %fusion.41), channel_id=1, source_target_pairs={{0,1},{1,2},{2,3},{3,0},{4,5},{5,6},{6,7},{7,4},{8,9},{9,10},{10,1... | collective-permute-start | bytes 196616 | tf_op jit(solution)/shard_map/ppermute | solution.py:153
  30.4 1.6 %collective-permute-start.6 = (bf16[256,128]{1,0:T(8,128)(2,1)S(1)}, bf16[256,128]{1,0:T(8,128)(2,1)S(1)}, u32[]{:S(2)}, u32[]{:S(2)}) collective-permute-start(bf16[256,128]{1,0:T(8,128)(2,1)S(1)} %fusion.41), channel_id=1, source_target_pairs={{0,2},{1,3},{2,0},{3,1},{4,6},{5,7},{6,4},{7,5},{8,10},{9,11},{10,... | collective-permute-start | bytes 196616 | tf_op jit(solution)/shard_map/ppermute | solution.py:153
  32.0 2.0 %collective-permute-done.5 = bf16[256,128]{1,0:T(8,128)(2,1)S(1)} collective-permute-done((bf16[256,128]{1,0:T(8,128)(2,1)S(1)}, bf16[256,128]{1,0:T(8,128)(2,1)S(1)}, u32[]{:S(2)}, u32[]{:S(2)}) %collective-permute-start.5) | collective-permute-done | bytes 65568 | tf_op jit(solution)/shard_map/ppermute | solution.py:153
  34.1 1.9 %collective-permute-start.7 = (bf16[256,128]{1,0:T(8,128)(2,1)S(1)}, bf16[256,128]{1,0:T(8,128)(2,1)S(1)}, u32[]{:S(2)}, u32[]{:S(2)}) collective-permute-start(bf16[256,128]{1,0:T(8,128)(2,1)S(1)} %fusion.41), channel_id=1, source_target_pairs={{0,3},{1,0},{2,1},{3,2},{4,7},{5,4},{6,5},{7,6},{8,11},{9,8},{10,9... | collective-permute-start | bytes 196616 | tf_op jit(solution)/shard_map/ppermute | solution.py:153
  36.4 1.9 %collective-permute-done.7 = bf16[256,128]{1,0:T(8,128)(2,1)S(1)} collective-permute-done((bf16[256,128]{1,0:T(8,128)(2,1)S(1)}, bf16[256,128]{1,0:T(8,128)(2,1)S(1)}, u32[]{:S(2)}, u32[]{:S(2)}) %collective-permute-start.7) | collective-permute-done | bytes 65568 | tf_op jit(solution)/shard_map/ppermute | solution.py:153
  41.1 1.2 copy-done.3
  43.7 1.6 %collective-permute-start.15 = (f32[256,128]{1,0:T(8,128)S(1)}, f32[256,128]{1,0:T(8,128)S(1)}, u32[]{:S(2)}, u32[]{:S(2)}) collective-permute-start(f32[256,128]{1,0:T(8,128)S(1)} %get-tuple-element.84), channel_id=1, source_target_pairs={{0,8},{4,12},{8,0},{12,4},{16,24},{20,28},{24,16},{28,20},{1,9},{5... | collective-permute-start | bytes 393224 | tf_op jit(solution)/shard_map/ppermute | solution.py:149
  45.2 1.5 %collective-permute-start.16 = (f32[256,128]{1,0:T(8,128)S(1)}, f32[256,128]{1,0:T(8,128)S(1)}, u32[]{:S(2)}, u32[]{:S(2)}) collective-permute-start(f32[256,128]{1,0:T(8,128)S(1)} %get-tuple-element.86), channel_id=1, source_target_pairs={{0,16},{4,20},{8,24},{12,28},{16,0},{20,4},{24,8},{28,12},{1,17},{... | collective-permute-start | bytes 393224 | tf_op jit(solution)/shard_map/ppermute | solution.py:149
  49.6 3.7 %collective-permute-done.16 = f32[256,128]{1,0:T(8,128)S(1)} collective-permute-done((f32[256,128]{1,0:T(8,128)S(1)}, f32[256,128]{1,0:T(8,128)S(1)}, u32[]{:S(2)}, u32[]{:S(2)}) %collective-permute-start.16) | collective-permute-done | bytes 131104 | tf_op jit(solution)/shard_map/ppermute | solution.py:149
  53.4 2.4 %collective-permute-start.18 = (bf16[256,128]{1,0:T(8,128)(2,1)S(1)}, bf16[256,128]{1,0:T(8,128)(2,1)S(1)}, u32[]{:S(2)}, u32[]{:S(2)}) collective-permute-start(bf16[256,128]{1,0:T(8,128)(2,1)S(1)} %get-tuple-element.76), channel_id=1, source_target_pairs={{0,1},{1,2},{2,3},{3,0},{4,5},{5,6},{6,7},{7,4},{8,9},{9,10},{10,1... | collective-permute-start | bytes 196616 | tf_op jit(solution)/shard_map/ppermute | solution.py:153
  55.8 1.9 %collective-permute-start.19 = (bf16[256,128]{1,0:T(8,128)(2,1)S(1)}, bf16[256,128]{1,0:T(8,128)(2,1)S(1)}, u32[]{:S(2)}, u32[]{:S(2)}) collective-permute-start(bf16[256,128]{1,0:T(8,128)(2,1)S(1)} %get-tuple-element.76), channel_id=1, source_target_pairs={{0,2},{1,3},{2,0},{3,1},{4,6},{5,7},{6,4},{7,5},{8,10},{9,11},{10,... | collective-permute-start | bytes 196616 | tf_op jit(solution)/shard_map/ppermute | solution.py:153
  58.2 1.8 %collective-permute-done.18 = bf16[256,128]{1,0:T(8,128)(2,1)S(1)} collective-permute-done((bf16[256,128]{1,0:T(8,128)(2,1)S(1)}, bf16[256,128]{1,0:T(8,128)(2,1)S(1)}, u32[]{:S(2)}, u32[]{:S(2)}) %collective-permute-start.18) | collective-permute-done | bytes 65568 | tf_op jit(solution)/shard_map/ppermute | solution.py:153
  60.0 1.9 %collective-permute-done.19 = bf16[256,128]{1,0:T(8,128)(2,1)S(1)} collective-permute-done((bf16[256,128]{1,0:T(8,128)(2,1)S(1)}, bf16[256,128]{1,0:T(8,128)(2,1)S(1)}, u32[]{:S(2)}, u32[]{:S(2)}) %collective-permute-start.19) | collective-permute-done | bytes 65568 | tf_op jit(solution)/shard_map/ppermute | solution.py:153
  63.2 1.2 collective-permute-start.21
  65.3 1.5 %collective-permute-start.23 = (f32[256,128]{1,0:T(8,128)S(1)}, f32[256,128]{1,0:T(8,128)S(1)}, u32[]{:S(2)}, u32[]{:S(2)}) collective-permute-start(f32[256,128]{1,0:T(8,128)S(1)} %get-tuple-element.82), channel_id=1, source_target_pairs={{0,24},{4,28},{8,16},{12,20},{16,8},{20,12},{24,0},{28,4},{1,25},{... | collective-permute-start | bytes 393224 | tf_op jit(solution)/shard_map/ppermute | solution.py:149
  66.8 2.6 %collective-permute-done.21 = f32[256,128]{1,0:T(8,128)S(1)} collective-permute-done((f32[256,128]{1,0:T(8,128)S(1)}, f32[256,128]{1,0:T(8,128)S(1)}, u32[]{:S(2)}, u32[]{:S(2)}) %collective-permute-start.21) | collective-permute-done | bytes 131104 | tf_op jit(solution)/shard_map/ppermute | solution.py:149
  69.6 1.5 %collective-permute-done.23 = f32[256,128]{1,0:T(8,128)S(1)} collective-permute-done((f32[256,128]{1,0:T(8,128)S(1)}, f32[256,128]{1,0:T(8,128)S(1)}, u32[]{:S(2)}, u32[]{:S(2)}) %collective-permute-start.23) | collective-permute-done | bytes 131104 | tf_op jit(solution)/shard_map/ppermute | solution.py:149
  71.2 1.9 %collective-permute-start.24 = (bf16[256,128]{1,0:T(8,128)(2,1)S(1)}, bf16[256,128]{1,0:T(8,128)(2,1)S(1)}, u32[]{:S(2)}, u32[]{:S(2)}) collective-permute-start(bf16[256,128]{1,0:T(8,128)(2,1)S(1)} %get-tuple-element.74), channel_id=1, source_target_pairs={{0,1},{1,2},{2,3},{3,0},{4,5},{5,6},{6,7},{7,4},{8,9},{9,10},{10,1... | collective-permute-start | bytes 196616 | tf_op jit(solution)/shard_map/ppermute | solution.py:153
  74.1 1.4 %collective-permute-start.26 = (bf16[256,128]{1,0:T(8,128)(2,1)S(1)}, bf16[256,128]{1,0:T(8,128)(2,1)S(1)}, u32[]{:S(2)}, u32[]{:S(2)}) collective-permute-start(bf16[256,128]{1,0:T(8,128)(2,1)S(1)} %get-tuple-element.74), channel_id=1, source_target_pairs={{0,3},{1,0},{2,1},{3,2},{4,7},{5,4},{6,5},{7,6},{8,11},{9,8},{10,9... | collective-permute-start | bytes 196616 | tf_op jit(solution)/shard_map/ppermute | solution.py:153
  75.5 1.8 %collective-permute-done.24 = bf16[256,128]{1,0:T(8,128)(2,1)S(1)} collective-permute-done((bf16[256,128]{1,0:T(8,128)(2,1)S(1)}, bf16[256,128]{1,0:T(8,128)(2,1)S(1)}, u32[]{:S(2)}, u32[]{:S(2)}) %collective-permute-start.24) | collective-permute-done | bytes 65568 | tf_op jit(solution)/shard_map/ppermute | solution.py:153
  77.3 1.5 %collective-permute-done.25 = bf16[256,128]{1,0:T(8,128)(2,1)S(1)} collective-permute-done((bf16[256,128]{1,0:T(8,128)(2,1)S(1)}, bf16[256,128]{1,0:T(8,128)(2,1)S(1)}, u32[]{:S(2)}, u32[]{:S(2)}) %collective-permute-start.25) | collective-permute-done | bytes 65568 | tf_op jit(solution)/shard_map/ppermute | solution.py:153
  79.8 1.4 %collective-permute-start.27 = (f32[256,128]{1,0:T(8,128)S(1)}, f32[256,128]{1,0:T(8,128)S(1)}, u32[]{:S(2)}, u32[]{:S(2)}) collective-permute-start(f32[256,128]{1,0:T(8,128)S(1)} %get-tuple-element.78), channel_id=1, source_target_pairs={{0,8},{4,12},{8,0},{12,4},{16,24},{20,28},{24,16},{28,20},{1,9},{5... | collective-permute-start | bytes 393224 | tf_op jit(solution)/shard_map/ppermute | solution.py:149
  81.8 1.6 %collective-permute-start.29 = (f32[256,128]{1,0:T(8,128)S(1)}, f32[256,128]{1,0:T(8,128)S(1)}, u32[]{:S(2)}, u32[]{:S(2)}) collective-permute-start(f32[256,128]{1,0:T(8,128)S(1)} %get-tuple-element.79), channel_id=1, source_target_pairs={{0,24},{4,28},{8,16},{12,20},{16,8},{20,12},{24,0},{28,4},{1,25},{... | collective-permute-start | bytes 393224 | tf_op jit(solution)/shard_map/ppermute | solution.py:149
  83.4 1.5 %collective-permute-done.27 = f32[256,128]{1,0:T(8,128)S(1)} collective-permute-done((f32[256,128]{1,0:T(8,128)S(1)}, f32[256,128]{1,0:T(8,128)S(1)}, u32[]{:S(2)}, u32[]{:S(2)}) %collective-permute-start.27) | collective-permute-done | bytes 131104 | tf_op jit(solution)/shard_map/ppermute | solution.py:149
  84.8 1.3 collective-permute-done.28
  86.2 1.5 %collective-permute-done.29 = f32[256,128]{1,0:T(8,128)S(1)} collective-permute-done((f32[256,128]{1,0:T(8,128)S(1)}, f32[256,128]{1,0:T(8,128)S(1)}, u32[]{:S(2)}, u32[]{:S(2)}) %collective-permute-start.29) | collective-permute-done | bytes 131104 | tf_op jit(solution)/shard_map/ppermute | solution.py:149
  88.9 2.1 %collective-permute-start.31 = (bf16[256,128]{1,0:T(8,128)(2,1)S(1)}, bf16[256,128]{1,0:T(8,128)(2,1)S(1)}, u32[]{:S(2)}, u32[]{:S(2)}) collective-permute-start(bf16[256,128]{1,0:T(8,128)(2,1)S(1)} %get-tuple-element.72), channel_id=1, source_target_pairs={{0,2},{1,3},{2,0},{3,1},{4,6},{5,7},{6,4},{7,5},{8,10},{9,11},{10,... | collective-permute-start | bytes 196616 | tf_op jit(solution)/shard_map/ppermute | solution.py:153
  94.1 1.4 %collective-permute-start.35 = (bf16[256,128]{1,0:T(8,128)(2,1)S(1)}, bf16[256,128]{1,0:T(8,128)(2,1)S(1)}, u32[]{:S(2)}, u32[]{:S(2)}) collective-permute-start(bf16[256,128]{1,0:T(8,128)(2,1)S(1)} %get-tuple-element.72), channel_id=1, source_target_pairs={{0,24},{4,28},{8,16},{12,20},{16,8},{20,12},{24,0},{28,4},{1,25},{... | collective-permute-start | bytes 196616 | tf_op jit(solution)/shard_map/ppermute | solution.py:149
  97.4 1.9 %collective-permute-done.35 = bf16[256,128]{1,0:T(8,128)(2,1)S(1)} collective-permute-done((bf16[256,128]{1,0:T(8,128)(2,1)S(1)}, bf16[256,128]{1,0:T(8,128)(2,1)S(1)}, u32[]{:S(2)}, u32[]{:S(2)}) %collective-permute-start.35) | collective-permute-done | bytes 65568 | tf_op jit(solution)/shard_map/ppermute | solution.py:149
  102.9 1.4 %collective-permute-start.38 = (f32[2,64,128]{2,1,0:T(8,128)S(1)}, f32[2,64,128]{2,1,0:T(8,128)S(1)}, u32[]{:S(2)}, u32[]{:S(2)}) collective-permute-start(f32[2,64,128]{2,1,0:T(8,128)S(1)} %get-tuple-element.87), channel_id=1, source_target_pairs={{0,8},{4,12},{8,0},{12,4},{16,24},{20,28},{24,16},{28,20},{1,9},{5... | collective-permute-start | bytes 196616 | tf_op jit(solution)/shard_map/ppermute | solution.py:149
  104.9 1.5 %collective-permute-start.40 = (f32[2,64,128]{2,1,0:T(8,128)S(1)}, f32[2,64,128]{2,1,0:T(8,128)S(1)}, u32[]{:S(2)}, u32[]{:S(2)}) collective-permute-start(f32[2,64,128]{2,1,0:T(8,128)S(1)} %get-tuple-element.88), channel_id=1, source_target_pairs={{0,24},{4,28},{8,16},{12,20},{16,8},{20,12},{24,0},{28,4},{1,25},{... | collective-permute-start | bytes 196616 | tf_op jit(solution)/shard_map/ppermute | solution.py:149
  107.3 1.9 %collective-permute-done.39 = f32[2,64,128]{2,1,0:T(8,128)S(1)} collective-permute-done((f32[2,64,128]{2,1,0:T(8,128)S(1)}, f32[2,64,128]{2,1,0:T(8,128)S(1)}, u32[]{:S(2)}, u32[]{:S(2)}) %collective-permute-start.39) | collective-permute-done | bytes 65568 | tf_op jit(solution)/shard_map/ppermute | solution.py:149
  110.1 1.4 %collective-permute-start.41 = (f32[64,128]{1,0:T(8,128)S(1)}, f32[64,128]{1,0:T(8,128)S(1)}, u32[]{:S(2)}, u32[]{:S(2)}) collective-permute-start(f32[64,128]{1,0:T(8,128)S(1)} %get-tuple-element.113), channel_id=1, source_target_pairs={{0,8},{4,12},{8,0},{12,4},{16,24},{20,28},{24,16},{28,20},{1,9},{5... | collective-permute-start | bytes 98312 | tf_op jit(solution)/shard_map/ppermute | solution.py:149
  112.3 1.4 %collective-permute-start.43 = (f32[64,128]{1,0:T(8,128)S(1)}, f32[64,128]{1,0:T(8,128)S(1)}, u32[]{:S(2)}, u32[]{:S(2)}) collective-permute-start(f32[64,128]{1,0:T(8,128)S(1)} %get-tuple-element.113), channel_id=1, source_target_pairs={{0,24},{4,28},{8,16},{12,20},{16,8},{20,12},{24,0},{28,4},{1,25},{... | collective-permute-start | bytes 98312 | tf_op jit(solution)/shard_map/ppermute | solution.py:149
  115.6 2.8 %collective-permute-start.48 = (f32[64,128]{1,0:T(8,128)S(1)}, f32[64,128]{1,0:T(8,128)S(1)}, u32[]{:S(2)}, u32[]{:S(2)}) collective-permute-start(f32[64,128]{1,0:T(8,128)S(1)} %get-tuple-element.112), channel_id=1, source_target_pairs={{0,3},{1,0},{2,1},{3,2},{4,7},{5,4},{6,5},{7,6},{8,11},{9,8},{10,9... | collective-permute-start | bytes 98312 | tf_op jit(solution)/shard_map/ppermute | solution.py:153
  120.2 1.4 %collective-permute-start.49 = (f32[64,128]{1,0:T(8,128)S(1)}, f32[64,128]{1,0:T(8,128)S(1)}, u32[]{:S(2)}, u32[]{:S(2)}) collective-permute-start(f32[64,128]{1,0:T(8,128)S(1)} %add_add_fusion), channel_id=1, source_target_pairs={{0,8},{4,12},{8,0},{12,4},{16,24},{20,28},{24,16},{28,20},{1,9},{5... | collective-permute-start | bytes 98312 | tf_op jit(solution)/shard_map/ppermute | solution.py:149
  122.3 1.4 %collective-permute-start.51 = (f32[64,128]{1,0:T(8,128)S(1)}, f32[64,128]{1,0:T(8,128)S(1)}, u32[]{:S(2)}, u32[]{:S(2)}) collective-permute-start(f32[64,128]{1,0:T(8,128)S(1)} %add_add_fusion), channel_id=1, source_target_pairs={{0,24},{4,28},{8,16},{12,20},{16,8},{20,12},{24,0},{28,4},{1,25},{... | collective-permute-start | bytes 98312 | tf_op jit(solution)/shard_map/ppermute | solution.py:149
  123.8 7.9 %factorize.1 = (f32[128,256]{1,0:T(8,128)}, f32[256,256]{1,0:T(8,128)S(1)}) custom-call(f32[256,256]{1,0:T(8,128)S(1)} %maximum_select_fusion.2.gram_ref, f32[128,256]{1,0:T(8,128)S(1)} %maximum_select_fusion.5.y_ref), custom_call_target="tpu_custom_call" | custom-call | bytes 5242880 | tf_op jit(solution)/shard_map/factorize/pallas_call | solution.py:124
  132.0 1.3 collective-permute-done.52
  133.3 1.8 %project.1 = f32[256,256]{1,0:T(8,128)} custom-call(f32[256,256]{1,0:T(8,128)S(1)} %get-tuple-element.65.inverse_ref, f32[256,256]{1,0:T(8,128)S(1)} %maximum_select_fusion.3.cross_ref), custom_call_target="tpu_custom_call" | custom-call | tf_op jit(solution)/shard_map/project/pallas_call | solution.py:138
  (139 shorter events, 35.1 us)
Async XLA Ops:
  4.1 11.0 %collective-permute-start = (bf16[16,4224]{1,0:T(8,128)(2,1)}, bf16[16,4224]{1,0:T(8,128)(2,1)S(1)}, u32[]{:S(2)}, u32[]{:S(2)}) collective-permute-start(bf16[16,4224]{1,0:T(8,128)(2,1)} %get-tuple-element.41), channel_id=1, source_target_pairs={{0,1},{1,2},{2,3},{3,0},{4,5},{5,6},{6,7},{7,4},{8,9},{9,10},{10,1... | collective-permute-start | bytes 405512 | tf_op jit(solution)/shard_map/ppermute | solution.py:153
  7.1 11.7 %collective-permute-start.1 = (bf16[16,4224]{1,0:T(8,128)(2,1)}, bf16[16,4224]{1,0:T(8,128)(2,1)S(1)}, u32[]{:S(2)}, u32[]{:S(2)}) collective-permute-start(bf16[16,4224]{1,0:T(8,128)(2,1)} %get-tuple-element.42), channel_id=1, source_target_pairs={{0,2},{1,3},{2,0},{3,1},{4,6},{5,7},{6,4},{7,5},{8,10},{9,11},{10,... | collective-permute-start | bytes 405512 | tf_op jit(solution)/shard_map/ppermute | solution.py:153
  9.7 9.1 %collective-permute-start.2 = (bf16[16,4224]{1,0:T(8,128)(2,1)}, bf16[16,4224]{1,0:T(8,128)(2,1)S(1)}, u32[]{:S(2)}, u32[]{:S(2)}) collective-permute-start(bf16[16,4224]{1,0:T(8,128)(2,1)} %get-tuple-element.43), channel_id=1, source_target_pairs={{0,3},{1,0},{2,1},{3,2},{4,7},{5,4},{6,5},{7,6},{8,11},{9,8},{10,9... | collective-permute-start | bytes 405512 | tf_op jit(solution)/shard_map/ppermute | solution.py:153
  21.9 4.2 %collective-permute-start.4 = (bf16[2,512,512]{2,1,0:T(8,128)(2,1)S(1)}, bf16[2,512,512]{2,1,0:T(8,128)(2,1)S(1)}, u32[]{:S(2)}, u32[]{:S(2)}) collective-permute-start(bf16[2,512,512]{2,1,0:T(8,128)(2,1)S(1)} %mirror.1.mirrored), channel_id=1, source_target_pairs={{0,4},{4,0},{8,12},{12,8},{16,20},{20,16},{24,28},{28,24},{1,5},{5... | collective-permute-start | bytes 3145736 | tf_op jit(solution)/shard_map/ppermute | solution.py:149
  22.0 4.0 %collective-permute-start.3 = (f32[128,128]{1,0:T(8,128)S(1)}, f32[128,128]{1,0:T(8,128)S(1)}, u32[]{:S(2)}, u32[]{:S(2)}) collective-permute-start(f32[128,128]{1,0:T(8,128)S(1)} %get-tuple-element.111), channel_id=1, source_target_pairs={{0,4},{4,0},{8,12},{12,8},{16,20},{20,16},{24,28},{28,24},{1,5},{5... | collective-permute-start | bytes 196616 | tf_op jit(solution)/shard_map/ppermute | solution.py:149
  22.5 15.8 %collective-permute-start.10 = (bf16[128,1024]{1,0:T(8,128)(2,1)S(1)}, bf16[128,1024]{1,0:T(8,128)(2,1)S(1)}, u32[]{:S(2)}, u32[]{:S(2)}) collective-permute-start(bf16[128,1024]{1,0:T(8,128)(2,1)S(1)} %get-tuple-element.55), channel_id=1, source_target_pairs={{0,24},{4,28},{8,16},{12,20},{16,8},{20,12},{24,0},{28,4},{1,25},{... | collective-permute-start | bytes 786440 | tf_op jit(solution)/shard_map/ppermute | solution.py:149
  25.0 13.4 %collective-permute-start.8 = (bf16[128,1024]{1,0:T(8,128)(2,1)S(1)}, bf16[128,1024]{1,0:T(8,128)(2,1)S(1)}, u32[]{:S(2)}, u32[]{:S(2)}) collective-permute-start(bf16[128,1024]{1,0:T(8,128)(2,1)S(1)} %get-tuple-element.53), channel_id=1, source_target_pairs={{0,8},{4,12},{8,0},{12,4},{16,24},{20,28},{24,16},{28,20},{1,9},{5... | collective-permute-start | bytes 786440 | tf_op jit(solution)/shard_map/ppermute | solution.py:149
  25.5 12.9 %collective-permute-start.9 = (bf16[128,1024]{1,0:T(8,128)(2,1)S(1)}, bf16[128,1024]{1,0:T(8,128)(2,1)S(1)}, u32[]{:S(2)}, u32[]{:S(2)}) collective-permute-start(bf16[128,1024]{1,0:T(8,128)(2,1)S(1)} %get-tuple-element.54), channel_id=1, source_target_pairs={{0,16},{4,20},{8,24},{12,28},{16,0},{20,4},{24,8},{28,12},{1,17},{... | collective-permute-start | bytes 786440 | tf_op jit(solution)/shard_map/ppermute | solution.py:149
  27.0 7.0 %collective-permute-start.5 = (bf16[256,128]{1,0:T(8,128)(2,1)S(1)}, bf16[256,128]{1,0:T(8,128)(2,1)S(1)}, u32[]{:S(2)}, u32[]{:S(2)}) collective-permute-start(bf16[256,128]{1,0:T(8,128)(2,1)S(1)} %fusion.41), channel_id=1, source_target_pairs={{0,1},{1,2},{2,3},{3,0},{4,5},{5,6},{6,7},{7,4},{8,9},{9,10},{10,1... | collective-permute-start | bytes 196616 | tf_op jit(solution)/shard_map/ppermute | solution.py:153
  30.4 6.0 %collective-permute-start.6 = (bf16[256,128]{1,0:T(8,128)(2,1)S(1)}, bf16[256,128]{1,0:T(8,128)(2,1)S(1)}, u32[]{:S(2)}, u32[]{:S(2)}) collective-permute-start(bf16[256,128]{1,0:T(8,128)(2,1)S(1)} %fusion.41), channel_id=1, source_target_pairs={{0,2},{1,3},{2,0},{3,1},{4,6},{5,7},{6,4},{7,5},{8,10},{9,11},{10,... | collective-permute-start | bytes 196616 | tf_op jit(solution)/shard_map/ppermute | solution.py:153
  34.1 4.3 %collective-permute-start.7 = (bf16[256,128]{1,0:T(8,128)(2,1)S(1)}, bf16[256,128]{1,0:T(8,128)(2,1)S(1)}, u32[]{:S(2)}, u32[]{:S(2)}) collective-permute-start(bf16[256,128]{1,0:T(8,128)(2,1)S(1)} %fusion.41), channel_id=1, source_target_pairs={{0,3},{1,0},{2,1},{3,2},{4,7},{5,4},{6,5},{7,6},{8,11},{9,8},{10,9... | collective-permute-start | bytes 196616 | tf_op jit(solution)/shard_map/ppermute | solution.py:153
  39.0 2.1 %collective-permute-start.14 = (bf16[128,1024]{1,0:T(8,128)(2,1)S(1)}, bf16[128,1024]{1,0:T(8,128)(2,1)S(1)}, u32[]{:S(2)}, u32[]{:S(2)}) collective-permute-start(bf16[128,1024]{1,0:T(8,128)(2,1)S(1)} %collective-permute-done.10.refs_3_), channel_id=1, source_target_pairs={{0,4},{4,0},{8,12},{12,8},{16,20},{20,16},{24,28},{28,24},{1,5},{5... | collective-permute-start | bytes 786440 | tf_op jit(solution)/shard_map/ppermute | solution.py:149
  43.7 6.0 %collective-permute-start.15 = (f32[256,128]{1,0:T(8,128)S(1)}, f32[256,128]{1,0:T(8,128)S(1)}, u32[]{:S(2)}, u32[]{:S(2)}) collective-permute-start(f32[256,128]{1,0:T(8,128)S(1)} %get-tuple-element.84), channel_id=1, source_target_pairs={{0,8},{4,12},{8,0},{12,4},{16,24},{20,28},{24,16},{28,20},{1,9},{5... | collective-permute-start | bytes 393224 | tf_op jit(solution)/shard_map/ppermute | solution.py:149
  45.2 8.1 %collective-permute-start.16 = (f32[256,128]{1,0:T(8,128)S(1)}, f32[256,128]{1,0:T(8,128)S(1)}, u32[]{:S(2)}, u32[]{:S(2)}) collective-permute-start(f32[256,128]{1,0:T(8,128)S(1)} %get-tuple-element.86), channel_id=1, source_target_pairs={{0,16},{4,20},{8,24},{12,28},{16,0},{20,4},{24,8},{28,12},{1,17},{... | collective-permute-start | bytes 393224 | tf_op jit(solution)/shard_map/ppermute | solution.py:149
  46.7 6.5 %collective-permute-start.17 = (f32[256,128]{1,0:T(8,128)S(1)}, f32[256,128]{1,0:T(8,128)S(1)}, u32[]{:S(2)}, u32[]{:S(2)}) collective-permute-start(f32[256,128]{1,0:T(8,128)S(1)} %get-tuple-element.85), channel_id=1, source_target_pairs={{0,24},{4,28},{8,16},{12,20},{16,8},{20,12},{24,0},{28,4},{1,25},{... | collective-permute-start | bytes 393224 | tf_op jit(solution)/shard_map/ppermute | solution.py:149
  53.4 6.7 %collective-permute-start.18 = (bf16[256,128]{1,0:T(8,128)(2,1)S(1)}, bf16[256,128]{1,0:T(8,128)(2,1)S(1)}, u32[]{:S(2)}, u32[]{:S(2)}) collective-permute-start(bf16[256,128]{1,0:T(8,128)(2,1)S(1)} %get-tuple-element.76), channel_id=1, source_target_pairs={{0,1},{1,2},{2,3},{3,0},{4,5},{5,6},{6,7},{7,4},{8,9},{9,10},{10,1... | collective-permute-start | bytes 196616 | tf_op jit(solution)/shard_map/ppermute | solution.py:153
  55.8 6.1 %collective-permute-start.19 = (bf16[256,128]{1,0:T(8,128)(2,1)S(1)}, bf16[256,128]{1,0:T(8,128)(2,1)S(1)}, u32[]{:S(2)}, u32[]{:S(2)}) collective-permute-start(bf16[256,128]{1,0:T(8,128)(2,1)S(1)} %get-tuple-element.76), channel_id=1, source_target_pairs={{0,2},{1,3},{2,0},{3,1},{4,6},{5,7},{6,4},{7,5},{8,10},{9,11},{10,... | collective-permute-start | bytes 196616 | tf_op jit(solution)/shard_map/ppermute | solution.py:153
  57.7 4.8 %collective-permute-start.20 = (bf16[256,128]{1,0:T(8,128)(2,1)S(1)}, bf16[256,128]{1,0:T(8,128)(2,1)S(1)}, u32[]{:S(2)}, u32[]{:S(2)}) collective-permute-start(bf16[256,128]{1,0:T(8,128)(2,1)S(1)} %get-tuple-element.76), channel_id=1, source_target_pairs={{0,3},{1,0},{2,1},{3,2},{4,7},{5,4},{6,5},{7,6},{8,11},{9,8},{10,9... | collective-permute-start | bytes 196616 | tf_op jit(solution)/shard_map/ppermute | solution.py:153
  63.2 6.1 %collective-permute-start.21 = (f32[256,128]{1,0:T(8,128)S(1)}, f32[256,128]{1,0:T(8,128)S(1)}, u32[]{:S(2)}, u32[]{:S(2)}) collective-permute-start(f32[256,128]{1,0:T(8,128)S(1)} %get-tuple-element.81), channel_id=1, source_target_pairs={{0,8},{4,12},{8,0},{12,4},{16,24},{20,28},{24,16},{28,20},{1,9},{5... | collective-permute-start | bytes 393224 | tf_op jit(solution)/shard_map/ppermute | solution.py:149
  64.4 5.2 %collective-permute-start.22 = (f32[256,128]{1,0:T(8,128)S(1)}, f32[256,128]{1,0:T(8,128)S(1)}, u32[]{:S(2)}, u32[]{:S(2)}) collective-permute-start(f32[256,128]{1,0:T(8,128)S(1)} %get-tuple-element.83), channel_id=1, source_target_pairs={{0,16},{4,20},{8,24},{12,28},{16,0},{20,4},{24,8},{28,12},{1,17},{... | collective-permute-start | bytes 393224 | tf_op jit(solution)/shard_map/ppermute | solution.py:149
  65.3 5.9 %collective-permute-start.23 = (f32[256,128]{1,0:T(8,128)S(1)}, f32[256,128]{1,0:T(8,128)S(1)}, u32[]{:S(2)}, u32[]{:S(2)}) collective-permute-start(f32[256,128]{1,0:T(8,128)S(1)} %get-tuple-element.82), channel_id=1, source_target_pairs={{0,24},{4,28},{8,16},{12,20},{16,8},{20,12},{24,0},{28,4},{1,25},{... | collective-permute-start | bytes 393224 | tf_op jit(solution)/shard_map/ppermute | solution.py:149
  71.2 6.1 %collective-permute-start.24 = (bf16[256,128]{1,0:T(8,128)(2,1)S(1)}, bf16[256,128]{1,0:T(8,128)(2,1)S(1)}, u32[]{:S(2)}, u32[]{:S(2)}) collective-permute-start(bf16[256,128]{1,0:T(8,128)(2,1)S(1)} %get-tuple-element.74), channel_id=1, source_target_pairs={{0,1},{1,2},{2,3},{3,0},{4,5},{5,6},{6,7},{7,4},{8,9},{9,10},{10,1... | collective-permute-start | bytes 196616 | tf_op jit(solution)/shard_map/ppermute | solution.py:153
  73.1 5.7 %collective-permute-start.25 = (bf16[256,128]{1,0:T(8,128)(2,1)S(1)}, bf16[256,128]{1,0:T(8,128)(2,1)S(1)}, u32[]{:S(2)}, u32[]{:S(2)}) collective-permute-start(bf16[256,128]{1,0:T(8,128)(2,1)S(1)} %get-tuple-element.74), channel_id=1, source_target_pairs={{0,2},{1,3},{2,0},{3,1},{4,6},{5,7},{6,4},{7,5},{8,10},{9,11},{10,... | collective-permute-start | bytes 196616 | tf_op jit(solution)/shard_map/ppermute | solution.py:153
  74.1 5.0 %collective-permute-start.26 = (bf16[256,128]{1,0:T(8,128)(2,1)S(1)}, bf16[256,128]{1,0:T(8,128)(2,1)S(1)}, u32[]{:S(2)}, u32[]{:S(2)}) collective-permute-start(bf16[256,128]{1,0:T(8,128)(2,1)S(1)} %get-tuple-element.74), channel_id=1, source_target_pairs={{0,3},{1,0},{2,1},{3,2},{4,7},{5,4},{6,5},{7,6},{8,11},{9,8},{10,9... | collective-permute-start | bytes 196616 | tf_op jit(solution)/shard_map/ppermute | solution.py:153
  79.8 5.0 %collective-permute-start.27 = (f32[256,128]{1,0:T(8,128)S(1)}, f32[256,128]{1,0:T(8,128)S(1)}, u32[]{:S(2)}, u32[]{:S(2)}) collective-permute-start(f32[256,128]{1,0:T(8,128)S(1)} %get-tuple-element.78), channel_id=1, source_target_pairs={{0,8},{4,12},{8,0},{12,4},{16,24},{20,28},{24,16},{28,20},{1,9},{5... | collective-permute-start | bytes 393224 | tf_op jit(solution)/shard_map/ppermute | solution.py:149
  81.2 5.0 %collective-permute-start.28 = (f32[256,128]{1,0:T(8,128)S(1)}, f32[256,128]{1,0:T(8,128)S(1)}, u32[]{:S(2)}, u32[]{:S(2)}) collective-permute-start(f32[256,128]{1,0:T(8,128)S(1)} %get-tuple-element.80), channel_id=1, source_target_pairs={{0,16},{4,20},{8,24},{12,28},{16,0},{20,4},{24,8},{28,12},{1,17},{... | collective-permute-start | bytes 393224 | tf_op jit(solution)/shard_map/ppermute | solution.py:149
  81.8 5.9 %collective-permute-start.29 = (f32[256,128]{1,0:T(8,128)S(1)}, f32[256,128]{1,0:T(8,128)S(1)}, u32[]{:S(2)}, u32[]{:S(2)}) collective-permute-start(f32[256,128]{1,0:T(8,128)S(1)} %get-tuple-element.79), channel_id=1, source_target_pairs={{0,24},{4,28},{8,16},{12,20},{16,8},{20,12},{24,0},{28,4},{1,25},{... | collective-permute-start | bytes 393224 | tf_op jit(solution)/shard_map/ppermute | solution.py:149
  87.7 6.3 %collective-permute-start.30 = (bf16[256,128]{1,0:T(8,128)(2,1)S(1)}, bf16[256,128]{1,0:T(8,128)(2,1)S(1)}, u32[]{:S(2)}, u32[]{:S(2)}) collective-permute-start(bf16[256,128]{1,0:T(8,128)(2,1)S(1)} %get-tuple-element.72), channel_id=1, source_target_pairs={{0,1},{1,2},{2,3},{3,0},{4,5},{5,6},{6,7},{7,4},{8,9},{9,10},{10,1... | collective-permute-start | bytes 196616 | tf_op jit(solution)/shard_map/ppermute | solution.py:153
  88.9 6.6 %collective-permute-start.31 = (bf16[256,128]{1,0:T(8,128)(2,1)S(1)}, bf16[256,128]{1,0:T(8,128)(2,1)S(1)}, u32[]{:S(2)}, u32[]{:S(2)}) collective-permute-start(bf16[256,128]{1,0:T(8,128)(2,1)S(1)} %get-tuple-element.72), channel_id=1, source_target_pairs={{0,2},{1,3},{2,0},{3,1},{4,6},{5,7},{6,4},{7,5},{8,10},{9,11},{10,... | collective-permute-start | bytes 196616 | tf_op jit(solution)/shard_map/ppermute | solution.py:153
  90.9 4.9 %collective-permute-start.32 = (bf16[256,128]{1,0:T(8,128)(2,1)S(1)}, bf16[256,128]{1,0:T(8,128)(2,1)S(1)}, u32[]{:S(2)}, u32[]{:S(2)}) collective-permute-start(bf16[256,128]{1,0:T(8,128)(2,1)S(1)} %get-tuple-element.72), channel_id=1, source_target_pairs={{0,3},{1,0},{2,1},{3,2},{4,7},{5,4},{6,5},{7,6},{8,11},{9,8},{10,9... | collective-permute-start | bytes 196616 | tf_op jit(solution)/shard_map/ppermute | solution.py:153
  92.0 4.3 %collective-permute-start.33 = (bf16[256,128]{1,0:T(8,128)(2,1)S(1)}, bf16[256,128]{1,0:T(8,128)(2,1)S(1)}, u32[]{:S(2)}, u32[]{:S(2)}) collective-permute-start(bf16[256,128]{1,0:T(8,128)(2,1)S(1)} %get-tuple-element.72), channel_id=1, source_target_pairs={{0,8},{4,12},{8,0},{12,4},{16,24},{20,28},{24,16},{28,20},{1,9},{5... | collective-permute-start | bytes 196616 | tf_op jit(solution)/shard_map/ppermute | solution.py:149
  93.1 4.3 %collective-permute-start.34 = (bf16[256,128]{1,0:T(8,128)(2,1)S(1)}, bf16[256,128]{1,0:T(8,128)(2,1)S(1)}, u32[]{:S(2)}, u32[]{:S(2)}) collective-permute-start(bf16[256,128]{1,0:T(8,128)(2,1)S(1)} %get-tuple-element.72), channel_id=1, source_target_pairs={{0,16},{4,20},{8,24},{12,28},{16,0},{20,4},{24,8},{28,12},{1,17},{... | collective-permute-start | bytes 196616 | tf_op jit(solution)/shard_map/ppermute | solution.py:149
  94.1 5.2 %collective-permute-start.35 = (bf16[256,128]{1,0:T(8,128)(2,1)S(1)}, bf16[256,128]{1,0:T(8,128)(2,1)S(1)}, u32[]{:S(2)}, u32[]{:S(2)}) collective-permute-start(bf16[256,128]{1,0:T(8,128)(2,1)S(1)} %get-tuple-element.72), channel_id=1, source_target_pairs={{0,24},{4,28},{8,16},{12,20},{16,8},{20,12},{24,0},{28,4},{1,25},{... | collective-permute-start | bytes 196616 | tf_op jit(solution)/shard_map/ppermute | solution.py:149
  99.3 2.1 %collective-permute-start.36 = (bf16[1024,128]{1,0:T(8,128)(2,1)S(1)}, bf16[1024,128]{1,0:T(8,128)(2,1)S(1)}, u32[]{:S(2)}, u32[]{:S(2)}) collective-permute-start(bf16[1024,128]{1,0:T(8,128)(2,1)S(1)} %get-tuple-element.61), channel_id=1, source_target_pairs={{0,4},{4,0},{8,12},{12,8},{16,20},{20,16},{24,28},{28,24},{1,5},{5... | collective-permute-start | bytes 786440 | tf_op jit(solution)/shard_map/ppermute | solution.py:149
  102.9 4.4 %collective-permute-start.38 = (f32[2,64,128]{2,1,0:T(8,128)S(1)}, f32[2,64,128]{2,1,0:T(8,128)S(1)}, u32[]{:S(2)}, u32[]{:S(2)}) collective-permute-start(f32[2,64,128]{2,1,0:T(8,128)S(1)} %get-tuple-element.87), channel_id=1, source_target_pairs={{0,8},{4,12},{8,0},{12,4},{16,24},{20,28},{24,16},{28,20},{1,9},{5... | collective-permute-start | bytes 196616 | tf_op jit(solution)/shard_map/ppermute | solution.py:149
  104.3 5.0 %collective-permute-start.39 = (f32[2,64,128]{2,1,0:T(8,128)S(1)}, f32[2,64,128]{2,1,0:T(8,128)S(1)}, u32[]{:S(2)}, u32[]{:S(2)}) collective-permute-start(f32[2,64,128]{2,1,0:T(8,128)S(1)} %get-tuple-element.89), channel_id=1, source_target_pairs={{0,16},{4,20},{8,24},{12,28},{16,0},{20,4},{24,8},{28,12},{1,17},{... | collective-permute-start | bytes 196616 | tf_op jit(solution)/shard_map/ppermute | solution.py:149
  104.9 5.2 %collective-permute-start.40 = (f32[2,64,128]{2,1,0:T(8,128)S(1)}, f32[2,64,128]{2,1,0:T(8,128)S(1)}, u32[]{:S(2)}, u32[]{:S(2)}) collective-permute-start(f32[2,64,128]{2,1,0:T(8,128)S(1)} %get-tuple-element.88), channel_id=1, source_target_pairs={{0,24},{4,28},{8,16},{12,20},{16,8},{20,12},{24,0},{28,4},{1,25},{... | collective-permute-start | bytes 196616 | tf_op jit(solution)/shard_map/ppermute | solution.py:149
  106.4 7.2 %collective-permute-start.45 = (f32[128,128]{1,0:T(8,128)S(1)}, f32[128,128]{1,0:T(8,128)S(1)}, u32[]{:S(2)}, u32[]{:S(2)}) collective-permute-start(f32[128,128]{1,0:T(8,128)S(1)} %get-tuple-element.103), channel_id=1, source_target_pairs={{0,4},{4,0},{8,12},{12,8},{16,20},{20,16},{24,28},{28,24},{1,5},{5... | collective-permute-start | bytes 196616 | tf_op jit(solution)/shard_map/ppermute | solution.py:149
  110.1 5.5 %collective-permute-start.41 = (f32[64,128]{1,0:T(8,128)S(1)}, f32[64,128]{1,0:T(8,128)S(1)}, u32[]{:S(2)}, u32[]{:S(2)}) collective-permute-start(f32[64,128]{1,0:T(8,128)S(1)} %get-tuple-element.113), channel_id=1, source_target_pairs={{0,8},{4,12},{8,0},{12,4},{16,24},{20,28},{24,16},{28,20},{1,9},{5... | collective-permute-start | bytes 98312 | tf_op jit(solution)/shard_map/ppermute | solution.py:149
  111.5 6.8 %collective-permute-start.42 = (f32[64,128]{1,0:T(8,128)S(1)}, f32[64,128]{1,0:T(8,128)S(1)}, u32[]{:S(2)}, u32[]{:S(2)}) collective-permute-start(f32[64,128]{1,0:T(8,128)S(1)} %get-tuple-element.113), channel_id=1, source_target_pairs={{0,16},{4,20},{8,24},{12,28},{16,0},{20,4},{24,8},{28,12},{1,17},{... | collective-permute-start | bytes 98312 | tf_op jit(solution)/shard_map/ppermute | solution.py:149
  112.3 6.1 %collective-permute-start.43 = (f32[64,128]{1,0:T(8,128)S(1)}, f32[64,128]{1,0:T(8,128)S(1)}, u32[]{:S(2)}, u32[]{:S(2)}) collective-permute-start(f32[64,128]{1,0:T(8,128)S(1)} %get-tuple-element.113), channel_id=1, source_target_pairs={{0,24},{4,28},{8,16},{12,20},{16,8},{20,12},{24,0},{28,4},{1,25},{... | collective-permute-start | bytes 98312 | tf_op jit(solution)/shard_map/ppermute | solution.py:149
  113.7 5.8 %collective-permute-start.46 = (f32[64,128]{1,0:T(8,128)S(1)}, f32[64,128]{1,0:T(8,128)S(1)}, u32[]{:S(2)}, u32[]{:S(2)}) collective-permute-start(f32[64,128]{1,0:T(8,128)S(1)} %get-tuple-element.112), channel_id=1, source_target_pairs={{0,1},{1,2},{2,3},{3,0},{4,5},{5,6},{6,7},{7,4},{8,9},{9,10},{10,1... | collective-permute-start | bytes 98312 | tf_op jit(solution)/shard_map/ppermute | solution.py:153
  114.7 5.1 %collective-permute-start.47 = (f32[64,128]{1,0:T(8,128)S(1)}, f32[64,128]{1,0:T(8,128)S(1)}, u32[]{:S(2)}, u32[]{:S(2)}) collective-permute-start(f32[64,128]{1,0:T(8,128)S(1)} %get-tuple-element.112), channel_id=1, source_target_pairs={{0,2},{1,3},{2,0},{3,1},{4,6},{5,7},{6,4},{7,5},{8,10},{9,11},{10,... | collective-permute-start | bytes 98312 | tf_op jit(solution)/shard_map/ppermute | solution.py:153
  115.6 4.6 %collective-permute-start.48 = (f32[64,128]{1,0:T(8,128)S(1)}, f32[64,128]{1,0:T(8,128)S(1)}, u32[]{:S(2)}, u32[]{:S(2)}) collective-permute-start(f32[64,128]{1,0:T(8,128)S(1)} %get-tuple-element.112), channel_id=1, source_target_pairs={{0,3},{1,0},{2,1},{3,2},{4,7},{5,4},{6,5},{7,6},{8,11},{9,8},{10,9... | collective-permute-start | bytes 98312 | tf_op jit(solution)/shard_map/ppermute | solution.py:153
  118.5 5.2 %collective-permute-start.44 = (f32[256,128]{1,0:T(8,128)S(1)}, f32[256,128]{1,0:T(8,128)S(1)}, u32[]{:S(2)}, u32[]{:S(2)}) collective-permute-start(f32[256,128]{1,0:T(8,128)S(1)} %maximum_select_fusion.4), channel_id=1, source_target_pairs={{0,4},{4,0},{8,12},{12,8},{16,20},{20,16},{24,28},{28,24},{1,5},{5... | collective-permute-start | bytes 393224 | tf_op jit(solution)/shard_map/ppermute | solution.py:149
  120.2 11.5 %collective-permute-start.49 = (f32[64,128]{1,0:T(8,128)S(1)}, f32[64,128]{1,0:T(8,128)S(1)}, u32[]{:S(2)}, u32[]{:S(2)}) collective-permute-start(f32[64,128]{1,0:T(8,128)S(1)} %add_add_fusion), channel_id=1, source_target_pairs={{0,8},{4,12},{8,0},{12,4},{16,24},{20,28},{24,16},{28,20},{1,9},{5... | collective-permute-start | bytes 98312 | tf_op jit(solution)/shard_map/ppermute | solution.py:149
  121.6 10.1 %collective-permute-start.50 = (f32[64,128]{1,0:T(8,128)S(1)}, f32[64,128]{1,0:T(8,128)S(1)}, u32[]{:S(2)}, u32[]{:S(2)}) collective-permute-start(f32[64,128]{1,0:T(8,128)S(1)} %add_add_fusion), channel_id=1, source_target_pairs={{0,16},{4,20},{8,24},{12,28},{16,0},{20,4},{24,8},{28,12},{1,17},{... | collective-permute-start | bytes 98312 | tf_op jit(solution)/shard_map/ppermute | solution.py:149
  122.3 9.4 %collective-permute-start.51 = (f32[64,128]{1,0:T(8,128)S(1)}, f32[64,128]{1,0:T(8,128)S(1)}, u32[]{:S(2)}, u32[]{:S(2)}) collective-permute-start(f32[64,128]{1,0:T(8,128)S(1)} %add_add_fusion), channel_id=1, source_target_pairs={{0,24},{4,28},{8,16},{12,20},{16,8},{20,12},{24,0},{28,4},{1,25},{... | collective-permute-start | bytes 98312 | tf_op jit(solution)/shard_map/ppermute | solution.py:149
  (12 other events, 56.3 us)
